TPU v7x, 512 devices: a whole 4x4x16 slice. The times are simulated.
512 devices in a mesh: dp: 64 (over x, z_hi, y, core), expert: 8 (over z_lo).
Axes of the slice: x: 4, y: 4, z: 16 (z_hi: 2, z_lo: 8; z = z_hi * 8 + z_lo), core: 2. Of those that a mesh axis runs over, the one named last changes fastest.
Arguments:
- tokens_in: bfloat16 [131072, 2560], P(('dp', 'expert')), may hold values from -6 to 6
- cotangent: bfloat16 [131072, 2560], P(('dp', 'expert')), may hold values from -0.29882812 to 0.29882812
- routes: int32 [131072, 6], P(('dp', 'expert')), may hold values from 0 to 159, as said below
- gate_weights: bfloat16 [131072, 6], P(('dp', 'expert')), may hold values from 0.5 to 8
- gate_proj: bfloat16 [8, 2560, 768], P('expert', 'dp'), may hold values from -0.125 to 0.125
- up_proj: bfloat16 [8, 2560, 768], P('expert', 'dp'), may hold values from -0.125 to 0.125
- down_proj: bfloat16 [8, 2560, 768], P('expert', 'dp'), may hold values from -0.21875 to 0.21875
Outputs:
- grad_tokens: bfloat16 [131072, 2560], P(('dp', 'expert'))
- grad_gates: bfloat16 [131072, 6], P(('dp', 'expert'))
Inputs may be any that keep to these rules, and one draw needn't show every extreme that they name: `routes`: each row holds 6 different expert numbers, at most one of them below 8. Within the 256 rows of one device no number below 8 is named by more than 32 rows, and in every draw, for each group of devices along expert, some number below 8 is named by exactly 32 rows on every device of that group.
All inputs are finite; a program needn't handle non-finite values.
Results may differ from a plain program's by a relative error of at most 0.024.
Values may be sent and summed in bfloat16 or wider, within the bound.
No kernel may reach another device: no remote copies, remote signals or barrier semaphores. Data moves between devices by JAX's collectives and lax.ppermute only.
A program may use at most 64 MiB of HBM per device.

v0:
```python
import jax
import jax.numpy as jnp
from jax import lax
from jax.sharding import PartitionSpec as P


def expert_rows(row_block, cotangent_rows, gate_column, gate_full, up_full, down_full):
    pre_gate = jnp.dot(row_block, gate_full, preferred_element_type=jnp.float32)
    pre_up = jnp.dot(row_block, up_full, preferred_element_type=jnp.float32)
    sigmoid_gate = jax.nn.sigmoid(pre_gate)
    activation = pre_gate * sigmoid_gate
    hidden = (activation * pre_up).astype(jnp.bfloat16)
    expert_out = jnp.dot(hidden, down_full.T, preferred_element_type=jnp.float32)
    score_rows = jnp.sum(cotangent_rows.astype(jnp.float32) * expert_out, axis=1).astype(
        jnp.bfloat16
    )
    back_hidden = jnp.dot(cotangent_rows, down_full, preferred_element_type=jnp.float32)
    scaled = gate_column.astype(jnp.float32)[:, None] * back_hidden
    silu_slope = sigmoid_gate * (1.0 + pre_gate * (1.0 - sigmoid_gate))
    grad_gate_pre = (scaled * pre_up * silu_slope).astype(jnp.bfloat16)
    grad_up_pre = (scaled * activation).astype(jnp.bfloat16)
    grad_rows = jnp.dot(grad_gate_pre, gate_full.T, preferred_element_type=jnp.float32)
    grad_rows = grad_rows + jnp.dot(grad_up_pre, up_full.T, preferred_element_type=jnp.float32)
    return (grad_rows.astype(jnp.bfloat16), score_rows)


def expert_block(row_block, cotangent_rows, gate_column, gate_full, up_full, down_full):
    sources, slots, width = row_block.shape
    grad_rows, score_rows = expert_rows(
        row_block.reshape(sources * slots, width),
        cotangent_rows.reshape(sources * slots, width),
        gate_column.reshape(sources * slots),
        gate_full,
        up_full,
        down_full,
    )
    return (grad_rows.reshape(sources, slots, width), score_rows.reshape(sources, slots))


def on_device(tokens_in, cotangent, routes, gate_weights, gate_proj, up_proj, down_proj):
    experts = lax.axis_size("expert")
    local_rows = tokens_in.shape[0]
    capacity = local_rows // 8
    window = routes < experts
    owner_id = jnp.sum(jnp.where(window, routes, 0), axis=1)
    routed = jnp.any(window, axis=1)
    onehot = ((owner_id[:, None] == jnp.arange(experts)[None, :]) & routed[:, None]).astype(
        jnp.float32
    )
    slot_rank = jnp.cumsum(onehot, axis=0) - 1.0
    token_slot = jnp.sum(slot_rank * onehot, axis=1)
    selector = onehot.T[:, None, :] * (
        token_slot[None, None, :] == jnp.arange(capacity, dtype=jnp.float32)[None, :, None]
    ).astype(jnp.float32)
    selector_half = selector.astype(jnp.bfloat16)
    send_rows = jnp.einsum(
        "ect,td->ecd", selector_half, tokens_in, preferred_element_type=jnp.float32
    ).astype(jnp.bfloat16)
    send_cotangent = jnp.einsum(
        "ect,td->ecd", selector_half, cotangent, preferred_element_type=jnp.float32
    ).astype(jnp.bfloat16)
    token_gate = jnp.sum(jnp.where(window, gate_weights.astype(jnp.float32), 0.0), axis=1)
    send_gate = jnp.einsum("ect,t->ec", selector, token_gate).astype(jnp.bfloat16)
    gate_full, up_full, down_full = (
        lax.all_gather(gate_proj, "dp", axis=1, tiled=True),
        lax.all_gather(up_proj, "dp", axis=1, tiled=True),
        lax.all_gather(down_proj, "dp", axis=1, tiled=True),
    )
    gate_full = gate_full[0]
    up_full = up_full[0]
    down_full = down_full[0]
    row_block, gate_column = (
        lax.all_to_all(send_rows, "expert", split_axis=0, concat_axis=0, tiled=True),
        lax.all_to_all(send_gate, "expert", split_axis=0, concat_axis=0, tiled=True),
    )
    cotangent_rows = lax.all_to_all(
        send_cotangent, "expert", split_axis=0, concat_axis=0, tiled=True
    )
    grad_rows, score_rows = expert_block(
        row_block, cotangent_rows, gate_column, gate_full, up_full, down_full
    )
    back_grad, back_score = (
        lax.all_to_all(grad_rows, "expert", split_axis=0, concat_axis=0, tiled=True),
        lax.all_to_all(score_rows, "expert", split_axis=0, concat_axis=0, tiled=True),
    )
    grad_tokens = jnp.einsum(
        "ect,ecd->td", selector_half, back_grad, preferred_element_type=jnp.float32
    ).astype(jnp.bfloat16)
    token_score = jnp.einsum("ect,ec->t", selector, back_score.astype(jnp.float32))
    grad_gates = jnp.where(window, token_score[:, None], 0.0).astype(jnp.bfloat16)
    return (grad_tokens, grad_gates)


def solution(mesh):
    return jax.shard_map(
        on_device,
        mesh=mesh,
        in_specs=(
            P(("dp", "expert"), None),
            P(("dp", "expert"), None),
            P(("dp", "expert"), None),
            P(("dp", "expert"), None),
            P("expert", "dp", None),
            P("expert", "dp", None),
            P("expert", "dp", None),
        ),
        out_specs=(P(("dp", "expert"), None), P(("dp", "expert"), None)),
        check_vma=False,
    )
```

profile of v0, /device:TPU:1, one launch (start us, length us, event | category | flops | bytes accessed | tf_op | source)
XLA Modules:
  0.0 552.9 jit_solution(2953650666727684968)
XLA Ops:
  7.2 0.7 all-gather.8.cloned.1.call-update
  8.0 0.7 all-gather.6.cloned.1.call-update
  8.7 0.7 select_reduce_fusion
  9.4 0.7 select_reduce_fusion.1
  10.1 0.6 reduce-window.6
  11.0 0.2 fusion.25
  11.2 0.6 copy.10
  11.9 13.1 %all-to-all-start = ((bf16[8,1,32]{2,1,0:T(2,128)(2,1)}), bf16[8,1,32]{2,1,0:T(2,128)(2,1)S(1)}, u32[]{:S(2)}, u32[]{:S(2)}) async-start(bf16[8,1,32]{2,1,0:T(2,128)(2,1)} %copy.10), calls=%async_computation | async-start | bytes 8192 | tf_op jit(solution)/shard_map/all_to_all | solution.py:74
  25.0 1.6 convolution_convert_fusion
  26.5 7.6 %all-to-all-done = bf16[8,1,32]{2,1,0:T(2,128)(2,1)S(1)} async-done(((bf16[8,1,32]{2,1,0:T(2,128)(2,1)}), bf16[8,1,32]{2,1,0:T(2,128)(2,1)S(1)}, u32[]{:S(2)}, u32[]{:S(2)}) %all-to-all-start) | async-done | bytes 544 | tf_op jit(solution)/shard_map/all_to_all | solution.py:74
  34.1 4.3 all-to-all-start.2
  38.4 0.7 all-gather.4.cloned.1.call-update
  39.1 1.6 convolution_convert_fusion.1
  40.7 66.5 %all-to-all-done.2 = bf16[8,32,2560]{2,1,0:T(8,128)(2,1)} async-done(((bf16[8,32,2560]{2,1,0:T(8,128)(2,1)}), bf16[8,32,2560]{2,1,0:T(8,128)(2,1)}, u32[]{:S(2)}, u32[]{:S(2)}) %all-to-all-start.2) | async-done | bytes 1310752 | tf_op jit(solution)/shard_map/all_to_all | solution.py:73
  107.2 5.4 all-to-all-start.1
  112.7 51.1 %all-gather.8.cloned.1.call-done = bf16[1,2560,768]{2,1,0:T(8,128)(2,1)} async-done(((bf16[1,40,768]{2,1,0:T(8,128)(2,1)}), bf16[1,2560,768]{2,1,0:T(8,128)(2,1)}) %all-gather.8.cloned.1.call-update) | async-done | bytes 3932176 | tf_op jit(solution)/shard_map/all_gather | solution.py:65
  163.8 3.7 fusion.2
  167.5 167.0 %all-gather.6.cloned.1.call-done = bf16[1,2560,768]{2,1,0:T(8,128)(2,1)} async-done(((bf16[1,40,768]{2,1,0:T(8,128)(2,1)}), bf16[1,2560,768]{2,1,0:T(8,128)(2,1)}) %all-gather.6.cloned.1.call-update) | async-done | bytes 3932176 | tf_op jit(solution)/shard_map/all_gather | solution.py:66
  334.5 4.6 fusion.5
  339.1 119.1 %all-gather.4.cloned.1.call-done = bf16[1,2560,768]{2,1,0:T(8,128)(2,1)} async-done(((bf16[1,40,768]{2,1,0:T(8,128)(2,1)}), bf16[1,2560,768]{2,1,0:T(8,128)(2,1)}) %all-gather.4.cloned.1.call-update) | async-done | bytes 3932176 | tf_op jit(solution)/shard_map/all_gather | solution.py:67
  458.2 3.7 fusion.14
  461.8 0.7 convert_element_type.101
  462.5 3.3 all-to-all-start.4
  465.9 3.4 fusion.19
  469.3 1.4 fusion
  470.8 0.7 copy-done.3
  471.4 2.4 fusion.10
  473.8 1.1 all-to-all-done.4
  474.9 8.2 %all-to-all-start.3 = ((bf16[8,32,2560]{2,1,0:T(8,128)(2,1)}), bf16[8,32,2560]{2,1,0:T(8,128)(2,1)S(1)}, u32[]{:S(2)}, u32[]{:S(2)}) async-start(bf16[8,32,2560]{2,1,0:T(8,128)(2,1)} %bitcast.15), calls=%async_computation.3 | async-start | bytes 2621440 | tf_op jit(solution)/shard_map/all_to_all | solution.py:83
  483.3 0.6 select_convert_fusion
  483.9 60.9 %all-to-all-done.3 = bf16[8,32,2560]{2,1,0:T(8,128)(2,1)S(1)} async-done(((bf16[8,32,2560]{2,1,0:T(8,128)(2,1)}), bf16[8,32,2560]{2,1,0:T(8,128)(2,1)S(1)}, u32[]{:S(2)}, u32[]{:S(2)}) %all-to-all-start.3) | async-done | bytes 1310752 | tf_op jit(solution)/shard_map/all_to_all | solution.py:83
  544.8 1.6 fusion.13
  (25 shorter events, 0.8 us)
Async XLA Ops:
  7.2 17.8 %copy-start = (bf16[256,2560]{1,0:T(8,128)(2,1)S(1)}, bf16[256,2560]{1,0:T(8,128)(2,1)}, u32[]{:S(2)}) copy-start(bf16[256,2560]{1,0:T(8,128)(2,1)} %param.7) | copy-start | bytes 3932164
  7.2 156.6 %all-gather.8.cloned.1.call-start = ((), (), s32[]{:S(2)}) async-start(), calls=%async_computation.7 | async-start | bytes 3993600 | tf_op jit(solution)/shard_map/all_gather | solution.py:65
  7.9 326.6 %all-gather.6.cloned.1.call-start = ((), (), s32[]{:S(2)}) async-start(), calls=%async_computation.6 | async-start | bytes 3993600 | tf_op jit(solution)/shard_map/all_gather | solution.py:66
  11.9 22.2 %all-to-all-start = ((bf16[8,1,32]{2,1,0:T(2,128)(2,1)}), bf16[8,1,32]{2,1,0:T(2,128)(2,1)S(1)}, u32[]{:S(2)}, u32[]{:S(2)}) async-start(bf16[8,1,32]{2,1,0:T(2,128)(2,1)} %copy.10), calls=%async_computation | async-start | bytes 8192 | tf_op jit(solution)/shard_map/all_to_all | solution.py:74
  24.9 14.2 %copy-start.1 = (bf16[256,2560]{1,0:T(8,128)(2,1)S(1)}, bf16[256,2560]{1,0:T(8,128)(2,1)}, u32[]{:S(2)}) copy-start(bf16[256,2560]{1,0:T(8,128)(2,1)} %param.8) | copy-start | bytes 3932164
  34.1 73.1 %all-to-all-start.2 = ((bf16[8,32,2560]{2,1,0:T(8,128)(2,1)}), bf16[8,32,2560]{2,1,0:T(8,128)(2,1)}, u32[]{:S(2)}, u32[]{:S(2)}) async-start(bf16[8,32,2560]{2,1,0:T(8,128)(2,1)} %convolution_convert_fusion), calls=%async_computation.2 | async-start | bytes 2621440 | tf_op jit(solution)/shard_map/all_to_all | solution.py:73
  38.4 419.8 %all-gather.4.cloned.1.call-start = ((), (), s32[]{:S(2)}) async-start(), calls=%async_computation.5 | async-start | bytes 3993600 | tf_op jit(solution)/shard_map/all_gather | solution.py:67
  107.2 231.9 %all-to-all-start.1 = ((bf16[8,32,2560]{2,1,0:T(8,128)(2,1)}), bf16[8,32,2560]{2,1,0:T(8,128)(2,1)S(1)}, u32[]{:S(2)}, u32[]{:S(2)}) async-start(bf16[8,32,2560]{2,1,0:T(8,128)(2,1)} %convolution_convert_fusion.1), calls=%async_computation.1 | async-start | bytes 2621440 | tf_op jit(solution)/shard_map/all_to_all | solution.py:76
  462.5 12.4 %all-to-all-start.4 = ((bf16[8,1,32]{2,1,0:T(2,128)(2,1)}), bf16[8,1,32]{2,1,0:T(2,128)(2,1)S(1)}, u32[]{:S(2)}, u32[]{:S(2)}) async-start(bf16[8,1,32]{2,1,0:T(2,128)(2,1)} %convert_element_type.101), calls=%async_computation.4 | async-start | bytes 8192 | tf_op jit(solution)/shard_map/all_to_all | solution.py:84
  465.8 3.5 copy-start.2
  465.8 3.5 copy-start.4
  469.3 2.1 copy-start.3
  474.9 69.9 %all-to-all-start.3 = ((bf16[8,32,2560]{2,1,0:T(8,128)(2,1)}), bf16[8,32,2560]{2,1,0:T(8,128)(2,1)S(1)}, u32[]{:S(2)}, u32[]{:S(2)}) async-start(bf16[8,32,2560]{2,1,0:T(8,128)(2,1)} %bitcast.15), calls=%async_computation.3 | async-start | bytes 2621440 | tf_op jit(solution)/shard_map/all_to_all | solution.py:83
Sparse Core Ops, SparseCore 0:
  12.4 151.3 all-gather.7
  168.2 166.2 all-gather.5
  338.9 119.1 all-gather.3
where the time goes:
time: 553 us
  waiting for transfers between devices  475 us (86%)
  starting transfers between devices  34.3 us (6%)
  matrix products  24.2 us (4%)
  between operations  13.9 us (3%)
    all_gather x1, waiting for transfers between devices, on_device(): lax.all_gather(up_proj, 'dp', axis=1, tiled=True)  167 us
    all_gather x1, waiting for transfers between devices, on_device(): lax.all_gather(down_proj, 'dp', axis=1, tiled=True)  119 us
    all_to_all x1, waiting for transfers between devices, on_device(): lax.all_to_all(send_rows, 'expert', split_axis=0, concat_axis=0, tiled=True)  66.5 us
    all_to_all x1, waiting for transfers between devices, on_device(): lax.all_to_all(grad_rows, 'expert', split_axis=0, concat_axis=0, tiled=True)  60.9 us
    all_gather x1, waiting for transfers between devices, on_device(): lax.all_gather(gate_proj, 'dp', axis=1, tiled=True)  51.1 us
    all_to_all x1, starting transfers between devices, on_device(): lax.all_to_all(send_gate, 'expert', split_axis=0, concat_axis=0, tiled=True)  13.1 us
  transfers between devices with their start and end apart: 8, of which 7 were waited for; matrix products, arithmetic and copies ran while one was open for 4% of the time, Pallas kernels for 0%

commit v1 on v0

v1 whole, which is shorter than its diff:
```python
import jax
import jax.numpy as jnp
from jax import lax
from jax.experimental import pallas as pl
from jax.experimental.pallas import tpu as pltpu
from jax.sharding import Mesh, PartitionSpec as P

BF = jnp.bfloat16
F32 = jnp.float32
AXES = ("x", "zh", "y", "c", "zq", "zr")
SPLIT = 128
PAD = 128


def route_place(routes, slots):
    tokens = routes.shape[0]
    window = routes < 8
    owner = jnp.sum(jnp.where(window, routes, 0), axis=1, keepdims=True)
    routed = jnp.sum(jnp.where(window, 1, 0), axis=1, keepdims=True) > 0
    lane = lax.broadcasted_iota(jnp.int32, (tokens, 128), 1)
    onehot = jnp.where((lane == owner) & routed, 1.0, 0.0)
    row = lax.broadcasted_iota(jnp.int32, (tokens, tokens), 0)
    col = lax.broadcasted_iota(jnp.int32, (tokens, tokens), 1)
    lower = jnp.where(col <= row, 1.0, 0.0).astype(BF)
    rank = jnp.dot(lower, onehot.astype(BF), preferred_element_type=F32)
    slot = jnp.sum(rank * onehot, axis=1, keepdims=True).astype(jnp.int32) - 1
    return jnp.where(routed, owner * slots + slot, -1)


def dispatch_kernel(routes_ref, tok_ref, cot_ref, out_ref, sel_ref):
    tokens, width = tok_ref.shape
    place = route_place(routes_ref[...], 32)
    lane = lax.broadcasted_iota(jnp.int32, (tokens, 256), 1)
    sel = jnp.where(lane == place, 1.0, 0.0).astype(BF)
    sel_ref[...] = sel
    step = 512

    @pl.loop(0, width // step)
    def _(i):
        cols = pl.ds(pl.multiple_of(i * step, step), step)
        for source, first in ((tok_ref, 0), (cot_ref, 32)):
            rows = lax.dot_general(
                sel, source[:, cols], (((0,), (0,)), ((), ())), preferred_element_type=F32
            ).astype(BF)
            out_ref[:, first : first + 32, cols] = rows.reshape(8, 32, step)


def combine_kernel(routes_ref, gates_ref, sel_ref, back_ref, grad_ref, score_ref):
    width = grad_ref.shape[1]
    window = routes_ref[...] < 8
    gate = jnp.sum(jnp.where(window, gates_ref[...].astype(F32), 0.0), axis=1, keepdims=True)
    sel = sel_ref[...]
    step = 512

    @pl.loop(0, width // step)
    def _(i):
        cols = pl.ds(pl.multiple_of(i * step, step), step)
        rows = back_ref[:, :, cols].reshape(256, step)
        grad_ref[:, cols] = (jnp.dot(sel, rows, preferred_element_type=F32) * gate).astype(BF)

    tail = back_ref[:, :, width : width + PAD].reshape(256, PAD)
    score = jnp.dot(sel, tail, preferred_element_type=F32)[:, 0:1]
    score_ref[...] = jnp.where(window, score, 0.0).astype(BF)


def expert_kernel(where_ref, rows_ref, *refs):
    pieces = refs[:10]
    out_ref = refs[10]
    gate_w, up_w, down_w, grad_a, grad_b, pre_g, pre_u, sems = refs[11:]
    weights = (gate_w, up_w, down_w)
    my_x, my_y = where_ref[0], where_ref[1]

    copies = ([], [], [])

    def place(src, src_row, block, half, xx, yy):
        target = ((xx * 2 + block) * 4 + yy) * 80
        for m in range(3):
            lo, hi = max(80 * m, half[0]), min(80 * m + 80, half[1])
            if lo < hi:
                copies[m].append(
                    pltpu.make_async_copy(
                        src.at[pl.ds(src_row + lo - half[0], hi - lo), :],
                        weights[m].at[pl.ds(pl.multiple_of(target + lo - 80 * m, 16), hi - lo), :],
                        sems.at[m],
                    )
                )

    whole = (0, 240)
    offs = (0, 3, 1, 2)
    for block in range(2):
        own, low, high, opp0, opp1 = pieces[5 * block : 5 * block + 5]
        for outer, (src, first, inner) in enumerate(
            ((own, 0, (0, 1, 2, 3)), (low, 0, (0, 1, 2, 3)), (high, 0, (0, 1, 2, 3)),
             (opp0, 0, (0, 1)), (opp1, 2, (2, 3)))
        ):
            far = offs[min(outer, 3)]
            for k in inner:
                near = offs[k]
                if block == 0:
                    xx, yy = lax.rem(my_x + far, 4), lax.rem(my_y + near, 4)
                else:
                    xx, yy = lax.rem(my_x + near, 4), lax.rem(my_y + far, 4)
                place(src, (k - first) * 240, block, whole, xx, yy)
    for m in range(3):
        for copy in copies[m]:
            copy.start()

    width = gate_w.shape[0]
    hidden_width = gate_w.shape[1]
    cstep = 256

    for copy in copies[0]:
        copy.wait()

    tok = rows_ref[:, 0:32, :].reshape(256, width)

    @pl.loop(0, hidden_width // cstep)
    def _(i):
        cols = pl.ds(pl.multiple_of(i * cstep, cstep), cstep)
        pre_g[:, cols] = jnp.dot(tok, gate_w[:, cols], preferred_element_type=F32)

    for copy in copies[1]:
        copy.wait()

    @pl.loop(0, hidden_width // cstep)
    def _(i):
        cols = pl.ds(pl.multiple_of(i * cstep, cstep), cstep)
        pre_u[:, cols] = jnp.dot(tok, up_w[:, cols], preferred_element_type=F32)

    for copy in copies[2]:
        copy.wait()

    cot = rows_ref[:, 32:64, :].reshape(256, width)

    def back(i, score):
        cols = pl.ds(pl.multiple_of(i * cstep, cstep), cstep)
        back_hidden = jnp.dot(cot, down_w[:, cols], preferred_element_type=F32)
        gate, up = pre_g[:, cols], pre_u[:, cols]
        sig = jax.nn.sigmoid(gate)
        act = gate * sig
        hidden = (act * up).astype(BF).astype(F32)
        grad_a[:, cols] = (back_hidden * up * (sig * (1.0 + gate * (1.0 - sig)))).astype(BF)
        grad_b[:, cols] = (back_hidden * act).astype(BF)
        return score + jnp.sum(hidden * back_hidden, axis=1, keepdims=True)

    score = lax.fori_loop(0, hidden_width // cstep, back, jnp.zeros((256, 1), F32))
    out_ref[:, :, width : width + PAD] = (
        jnp.broadcast_to(score, (256, PAD)).astype(BF).reshape(8, 32, PAD)
    )

    a, b = grad_a[...], grad_b[...]
    dims = (((1,), (1,)), ((), ()))
    dstep = 256

    @pl.loop(0, width // dstep)
    def _(i):
        part = pl.ds(pl.multiple_of(i * dstep, dstep), dstep)
        rows = lax.dot_general(a, gate_w[part, :], dims, preferred_element_type=F32)
        rows = rows + lax.dot_general(b, up_w[part, :], dims, preferred_element_type=F32)
        out_ref[:, :, part] = rows.astype(BF).reshape(8, 32, dstep)


def params():
    return pltpu.CompilerParams(vmem_limit_bytes=48 * 1024 * 1024)


def cost(flops, moved):
    return pl.CostEstimate(flops=flops, bytes_accessed=moved, transcendentals=0)


VM = pl.BlockSpec(memory_space=pltpu.VMEM)
ANY = pl.BlockSpec(memory_space=pl.ANY)


def shift(v, axis, by):
    return lax.ppermute(v, axis, [(i, (i + by) % 4) for i in range(4)])


def ring_first(v, axis):
    return shift(v, axis, 1), shift(v, axis, -1)


def ring_second(low, high, axis, cut):
    return shift(low[:cut], axis, 1), shift(high[cut:], axis, -1)


def on_device(tokens_in, cotangent, routes, gate_weights, gate_proj, up_proj, down_proj):
    width = tokens_in.shape[1]
    hidden_width = gate_proj.shape[2]
    ix, iy, ic = lax.axis_index("x"), lax.axis_index("y"), lax.axis_index("c")
    zh, zq = lax.axis_index("zh"), lax.axis_index("zq")
    ring = zh * 2 + zq

    shard = jnp.concatenate([gate_proj, up_proj, down_proj], axis=0)
    other = lax.ppermute(shard, ("c", "zq"), [(2, 0), (1, 3)])
    pair = jnp.stack([jnp.where(ic == 0, shard, other), jnp.where(ic == 0, other, shard)], axis=1)
    pair = pair.reshape(240, hidden_width)

    def at(c, p):
        return (p // 2 * 2 + c) * 2 + p % 2

    def zmove(v, source, by):
        pairs = [(at(c, p), at(c, (p + by) % 4)) for c in range(2) for p in range(4) if (p % 2 == c) == source]
        return lax.ppermute(v, ("zh", "c", "zq"), pairs)

    low, high = zmove(pair, True, 1), zmove(pair, True, -1)
    far0, far1 = zmove(low[:SPLIT], False, 1), zmove(high[SPLIT:], False, -1)
    far = jnp.concatenate([far0, far1], axis=0)
    source = ic == zq
    swapped = (ring == 0) | (ring == 3)
    block_a = jnp.where(source, jnp.where(zh == 0, pair, far), jnp.where(swapped, high, low))
    block_b = jnp.where(source, jnp.where(zh == 0, far, pair), jnp.where(swapped, low, high))

    payload, sel = pl.pallas_call(
        dispatch_kernel,
        out_shape=(
            jax.ShapeDtypeStruct((8, 64, width), BF),
            jax.ShapeDtypeStruct((256, 256), BF),
        ),
        in_specs=[VM] * 3,
        out_specs=(VM, VM),
        compiler_params=params(),
        cost_estimate=cost(2 * 256 * 512 * width, 8 * 256 * width),
    )(routes, tokens_in, cotangent)

    payload, block_a, block_b = lax.optimization_barrier((payload, block_a, block_b))
    rows = lax.all_to_all(payload, ("c", "zr"), split_axis=0, concat_axis=0, tiled=True)

    a_low, a_high = ring_first(block_a, "y")
    b_low, b_high = ring_first(block_b, "x")
    a_far = ring_second(a_low, a_high, "y", SPLIT)
    b_far = ring_second(b_low, b_high, "x", SPLIT)
    line_a = jnp.concatenate([block_a, a_low, a_high, *a_far], axis=0)
    line_b = jnp.concatenate([block_b, b_low, b_high, *b_far], axis=0)
    al, ah = ring_first(line_a, "x")
    bl, bh = ring_first(line_b, "y")
    af = ring_second(al, ah, "x", 480)
    bf = ring_second(bl, bh, "y", 480)

    back = pl.pallas_call(
        expert_kernel,
        out_shape=jax.ShapeDtypeStruct((8, 32, width + PAD), BF),
        in_specs=[pl.BlockSpec(memory_space=pltpu.SMEM), VM] + [ANY] * 10,
        out_specs=VM,
        scratch_shapes=[pltpu.VMEM((width, hidden_width), BF)] * 3
        + [pltpu.VMEM((256, hidden_width), BF)] * 2
        + [pltpu.VMEM((256, hidden_width), F32)] * 2
        + [pltpu.SemaphoreType.DMA((3,))],
        compiler_params=params(),
        cost_estimate=cost(10 * 256 * width * hidden_width, 6 * width * hidden_width),
    )(jnp.stack([ix, iy]).astype(jnp.int32), rows, line_a, al, ah, *af, line_b, bl, bh, *bf)

    home = lax.all_to_all(back, ("c", "zr"), split_axis=0, concat_axis=0, tiled=True)

    return pl.pallas_call(
        combine_kernel,
        out_shape=(
            jax.ShapeDtypeStruct(tokens_in.shape, BF),
            jax.ShapeDtypeStruct(gate_weights.shape, BF),
        ),
        in_specs=[VM] * 4,
        out_specs=(VM, VM),
        compiler_params=params(),
        cost_estimate=cost(2 * 256 * 256 * width, 4 * 256 * width),
    )(routes, gate_weights, sel, home)


def solution(mesh):
    fine = Mesh(mesh.devices.reshape(4, 2, 4, 2, 2, 4), AXES)
    rows = P(AXES, None)
    proj = P(("zq", "zr"), ("x", "zh", "y", "c"), None)
    return jax.shard_map(
        on_device,
        mesh=fine,
        in_specs=(rows, rows, rows, rows, proj, proj, proj),
        out_specs=(rows, rows),
        check_vma=False,
    )
```

time: 553 us -> 219 us (0.40)
  waiting for transfers between devices: 475 us -> 88.2 us
  starting transfers between devices: 34.3 us -> 94.6 us
  matrix products: 24.2 us -> 0 us
  Pallas kernels: 0 us -> 21.4 us
  between operations: 13.9 us -> 1.19 us
  local copies, waits for them, and re-layouts: 2.28 us -> 11.3 us
    all_gather x3 -> x0, waiting for transfers between devices: 337 us -> none  [the longest x1 167 us: on_device(): lax.all_gather(up_proj, 'dp', axis=1, tiled=True)]
    all_to_all x5 -> x2, waiting for transfers between devices: 136 us -> 32.8 us  [the longest x1 32.8 us: on_device(): lax.all_to_all(back, ('c', 'zr'), split_axis=0, concat_axis=0, tiled=True)]
    ppermute x0 -> x21, starting transfers between devices: none -> 77.7 us  [the longest x16 50.2 us: shift(): return lax.ppermute(v, axis, [(i, (i + by) % 4) for i in range(4)])]
    ppermute x0 -> x21, waiting for transfers between devices: none -> 55.4 us  [the longest x16 41.7 us: shift(): return lax.ppermute(v, axis, [(i, (i + by) % 4) for i in range(4)])]
    dot_general x11 -> x0, matrix products: 24.2 us -> none  [the longest x1 4.57 us: expert_rows(): pre_up = jnp.dot(row_block, up_full, preferred_element_type=jnp.float32)]
    pallas_call x0 -> x3, Pallas kernels: none -> 21.4 us  [the longest x1 15.4 us: on_device(): pl.pallas_call(expert_kernel, out_shape=jax.ShapeDtypeStruct((8, 32, widt...]
    all_to_all x5 -> x2, starting transfers between devices: 34.2 us -> 16.9 us  [the longest x1 8.69 us: on_device(): lax.all_to_all(back, ('c', 'zr'), split_axis=0, concat_axis=0, tiled=True)]
  transfers between devices with their start and end apart: 8 -> 23, of which waited for: 7 -> 10; matrix products, arithmetic and copies ran while one was open for 4% -> 3% of each run, Pallas kernels for 0% -> 2%
where the time goes in v1:
time: 219 us; the launch traced here: 218 us
  starting transfers between devices  94.6 us (43%)
  waiting for transfers between devices  88.2 us (40%)
  Pallas kernels  21.4 us (10%)
  local copies, waits for them, and re-layouts  11.3 us (5%)
    ppermute x16, starting transfers between devices, shift(): return lax.ppermute(v, axis, [(i, (i + by) % 4) for i in range(4)])  50.2 us
    ppermute x16, waiting for transfers between devices, shift(): return lax.ppermute(v, axis, [(i, (i + by) % 4) for i in range(4)])  41.7 us
    all_to_all x1, waiting for transfers between devices, on_device(): lax.all_to_all(back, ('c', 'zr'), split_axis=0, concat_axis=0, tiled=True)  32.8 us
    ppermute x4, starting transfers between devices, zmove(): return lax.ppermute(v, ('zh', 'c', 'zq'), pairs)  18.8 us
    pallas_call x1, Pallas kernels, on_device(): pl.pallas_call(expert_kernel, out_shape=jax.ShapeDtypeStruct((8, 32, widt...  15.4 us
    ppermute x4, waiting for transfers between devices, zmove(): return lax.ppermute(v, ('zh', 'c', 'zq'), pairs)  12.6 us
    ppermute x1, starting transfers between devices, on_device(): other = lax.ppermute(shard, ('c', 'zq'), [(2, 0), (1, 3)])  8.78 us
    all_to_all x1, starting transfers between devices, on_device(): lax.all_to_all(back, ('c', 'zr'), split_axis=0, concat_axis=0, tiled=True)  8.69 us
  transfers between devices with their start and end apart: 23, of which 10 were waited for; matrix products, arithmetic and copies ran while one was open for 3% of the time, Pallas kernels for 2%

profile of v1, /device:TPU:1, one launch (start us, length us, event | category | flops | bytes accessed | tf_op | source)
XLA Modules:
  0.0 217.9 jit_solution(12481200871918947035)
XLA Ops:
  3.1 8.8 %collective-permute-start = (bf16[3,40,768]{2,1,0:T(8,128)(2,1)S(1)}, bf16[3,40,768]{2,1,0:T(8,128)(2,1)S(1)}, u32[]{:S(2)}, u32[]{:S(2)}) collective-permute-start(bf16[3,40,768]{2,1,0:T(8,128)(2,1)S(1)} %constant_dynamic-update-slice_fusion), channel_id=1, source_target_pairs={{8,0},{4,12},{9,1},{5,13},{10,2},{6,14},{11,3},{7,15},{24,16},{20,... | collective-permute-start | bytes 552968 | tf_op jit(solution)/shard_map/ppermute | solution.py:195
  13.1 1.3 collective-permute-start.1
  15.7 11.5 %collective-permute-done.1 = bf16[240,768]{1,0:T(8,128)(2,1)S(1)} collective-permute-done((bf16[240,768]{1,0:T(8,128)(2,1)S(1)}, bf16[240,768]{1,0:T(8,128)(2,1)S(1)}, u32[]{:S(2)}, u32[]{:S(2)}) %collective-permute-start.1) | collective-permute-done | bytes 368672 | tf_op jit(solution)/shard_map/ppermute | solution.py:204
  28.6 14.8 %collective-permute-start.2 = (bf16[128,768]{1,0:T(8,128)(2,1)}, bf16[128,768]{1,0:T(8,128)(2,1)S(1)}, u32[]{:S(2)}, u32[]{:S(2)}) collective-permute-start(bf16[128,768]{1,0:T(8,128)(2,1)} %slice.40), channel_id=1, source_target_pairs={{4,64},{68,0},{8,12},{72,76},{5,65},{69,1},{9,13},{73,77},{6,66},{... | collective-permute-start | bytes 589832 | tf_op jit(solution)/shard_map/ppermute | solution.py:204
  44.5 1.4 collective-permute-start.4
  46.0 3.6 %shard_map.86 = (bf16[8,64,2560]{2,1,0:T(8,128)(2,1)}, bf16[256,256]{1,0:T(8,128)(2,1)S(1)}) custom-call(s32[256,6]{1,0:T(8,128)S(1)} %copy.11.routes_ref, bf16[256,2560]{1,0:T(8,128)(2,1)S(1)} %copy-done, bf16[256,2560]{1,0:T(8,128)(2,1)S(1)} %copy-done.1), custom_call_target="tpu_custom_call" | custom-call | flops 671088640 | bytes 5242880 | tf_op jit(solution)/shard_map/pallas_call | solution.py:214
  51.8 8.2 %all-to-all-start = ((bf16[8,64,2560]{2,1,0:T(8,128)(2,1)}), bf16[8,64,2560]{2,1,0:T(8,128)(2,1)}, u32[]{:S(2)}, u32[]{:S(2)}) async-start(bf16[8,64,2560]{2,1,0:T(8,128)(2,1)} %get-tuple-element.9), calls=%async_computation | async-start | bytes 5242880 | tf_op jit(solution)/shard_map/all_to_all | solution.py:227
  60.0 4.6 %collective-permute-start.6 = (bf16[240,768]{1,0:T(8,128)(2,1)S(1)}, bf16[240,768]{1,0:T(8,128)(2,1)S(1)}, u32[]{:S(2)}, u32[]{:S(2)}) collective-permute-start(bf16[240,768]{1,0:T(8,128)(2,1)S(1)} %get-tuple-element.10), channel_id=1, source_target_pairs={{0,48},{16,0},{32,16},{48,32},{1,49},{17,1},{33,17},{49,33},{2,50}... | collective-permute-start | bytes 1105928 | tf_op jit(solution)/shard_map/ppermute | solution.py:176
  64.7 1.9 collective-permute-start.5
  66.6 4.4 %collective-permute-start.14 = (bf16[240,768]{1,0:T(8,128)(2,1)S(1)}, bf16[240,768]{1,0:T(8,128)(2,1)S(1)}, u32[]{:S(2)}, u32[]{:S(2)}) collective-permute-start(bf16[240,768]{1,0:T(8,128)(2,1)S(1)} %get-tuple-element.11), channel_id=1, source_target_pairs={{0,384},{128,0},{256,128},{384,256},{1,385},{129,1},{257,129},{385... | collective-permute-start | bytes 1105928 | tf_op jit(solution)/shard_map/ppermute | solution.py:176
  71.0 1.9 collective-permute-start.13
  73.0 5.0 %collective-permute-start.8 = (bf16[112,768]{1,0:T(8,128)(2,1)S(1)}, bf16[112,768]{1,0:T(8,128)(2,1)S(1)}, u32[]{:S(2)}, u32[]{:S(2)}) collective-permute-start(bf16[112,768]{1,0:T(8,128)(2,1)S(1)} %slice.43), channel_id=1, source_target_pairs={{0,48},{16,0},{32,16},{48,32},{1,49},{17,1},{33,17},{49,33},{2,50}... | collective-permute-start | bytes 516104 | tf_op jit(solution)/shard_map/ppermute | solution.py:176
  78.1 1.9 collective-permute-start.7
  80.0 4.4 %collective-permute-start.16 = (bf16[112,768]{1,0:T(8,128)(2,1)S(1)}, bf16[112,768]{1,0:T(8,128)(2,1)S(1)}, u32[]{:S(2)}, u32[]{:S(2)}) collective-permute-start(bf16[112,768]{1,0:T(8,128)(2,1)S(1)} %slice.47), channel_id=1, source_target_pairs={{0,384},{128,0},{256,128},{384,256},{1,385},{129,1},{257,129},{385... | collective-permute-start | bytes 516104 | tf_op jit(solution)/shard_map/ppermute | solution.py:176
  84.4 1.9 collective-permute-start.15
  86.5 6.0 %collective-permute-done.15 = bf16[128,768]{1,0:T(8,128)(2,1)S(1)} collective-permute-done((bf16[128,768]{1,0:T(8,128)(2,1)S(1)}, bf16[128,768]{1,0:T(8,128)(2,1)S(1)}, u32[]{:S(2)}, u32[]{:S(2)}) %collective-permute-start.15) | collective-permute-done | bytes 196640 | tf_op jit(solution)/shard_map/ppermute | solution.py:176
  92.6 4.4 %collective-permute-start.18 = (bf16[960,768]{1,0:T(8,128)(2,1)S(1)}, bf16[960,768]{1,0:T(8,128)(2,1)S(1)}, u32[]{:S(2)}, u32[]{:S(2)}) collective-permute-start(bf16[960,768]{1,0:T(8,128)(2,1)S(1)} %constant_dynamic-update-slice_fusion.10.refs_5_), channel_id=1, source_target_pairs={{0,48},{16,0},{32,16},{48,32},{1,49},{17,1},{33,17},{49,33},{2,50}... | collective-permute-start | bytes 4423688 | tf_op jit(solution)/shard_map/ppermute | solution.py:176
  97.0 1.9 collective-permute-start.17
  99.0 1.9 collective-permute-start.10
  100.9 3.4 %collective-permute-start.9 = (bf16[960,768]{1,0:T(8,128)(2,1)S(1)}, bf16[960,768]{1,0:T(8,128)(2,1)S(1)}, u32[]{:S(2)}, u32[]{:S(2)}) collective-permute-start(bf16[960,768]{1,0:T(8,128)(2,1)S(1)} %constant_dynamic-update-slice_fusion.5.refs_0_), channel_id=1, source_target_pairs={{0,128},{128,256},{256,384},{384,0},{1,129},{129,257},{257,385},{3... | collective-permute-start | bytes 4423688 | tf_op jit(solution)/shard_map/ppermute | solution.py:176
  104.2 21.6 %collective-permute-done.18.refs_7_ = bf16[960,768]{1,0:T(8,128)(2,1)S(1)} collective-permute-done((bf16[960,768]{1,0:T(8,128)(2,1)S(1)}, bf16[960,768]{1,0:T(8,128)(2,1)S(1)}, u32[]{:S(2)}, u32[]{:S(2)}) %collective-permute-start.18) | collective-permute-done | bytes 1474592 | tf_op jit(solution)/shard_map/ppermute | solution.py:176
  126.9 5.3 %collective-permute-start.20 = (bf16[480,768]{1,0:T(8,128)(2,1)}, bf16[480,768]{1,0:T(8,128)(2,1)S(1)}, u32[]{:S(2)}, u32[]{:S(2)}) collective-permute-start(bf16[480,768]{1,0:T(8,128)(2,1)} %slice.49), channel_id=1, source_target_pairs={{0,48},{16,0},{32,16},{48,32},{1,49},{17,1},{33,17},{49,33},{2,50}... | collective-permute-start | bytes 2211848 | tf_op jit(solution)/shard_map/ppermute | solution.py:176
  133.2 1.9 collective-permute-start.19
  136.1 1.9 collective-permute-start.12
  140.2 3.4 %collective-permute-start.11 = (bf16[480,768]{1,0:T(8,128)(2,1)}, bf16[480,768]{1,0:T(8,128)(2,1)}, u32[]{:S(2)}, u32[]{:S(2)}) collective-permute-start(bf16[480,768]{1,0:T(8,128)(2,1)} %slice.44), channel_id=1, source_target_pairs={{0,128},{128,256},{256,384},{384,0},{1,129},{129,257},{257,385},{3... | collective-permute-start | bytes 2211848 | tf_op jit(solution)/shard_map/ppermute | solution.py:176
  144.7 6.1 %collective-permute-done.19.refs_8_ = bf16[480,768]{1,0:T(8,128)(2,1)} collective-permute-done((bf16[480,768]{1,0:T(8,128)(2,1)}, bf16[480,768]{1,0:T(8,128)(2,1)}, u32[]{:S(2)}, u32[]{:S(2)}) %collective-permute-start.19) | collective-permute-done | bytes 737312 | tf_op jit(solution)/shard_map/ppermute | solution.py:176
  150.8 1.7 collective-permute-done.12.refs_4_
  152.5 5.2 %collective-permute-done.11.refs_3_ = bf16[480,768]{1,0:T(8,128)(2,1)} collective-permute-done((bf16[480,768]{1,0:T(8,128)(2,1)}, bf16[480,768]{1,0:T(8,128)(2,1)}, u32[]{:S(2)}, u32[]{:S(2)}) %collective-permute-start.11) | collective-permute-done | bytes 737312 | tf_op jit(solution)/shard_map/ppermute | solution.py:176
  157.7 15.4 %shard_map.87 = bf16[8,32,2688]{2,1,0:T(8,128)(2,1)} custom-call(s32[2]{0:T(128)S(1)} %pad_add_fusion.where_ref, bf16[8,64,2560]{2,1,0:T(8,128)(2,1)} %all-to-all-done.rows_ref, bf16[960,768]{1,0:T(8,128)(2,1)S(1)} %constant_dynamic-update-slice_fusion.5.refs_0_, bf16[960,768]{1,0:T(8,128)(2,1)} %copy-done.7, bf16[960,768]{1,0:T(8,128)(2,1)} %copy-done.6, ...), custom_call_target="tpu_custom_call" | custom-call | flops 5033164800 | bytes 11796480 | tf_op jit(solution)/shard_map/pallas_call | solution.py:240
  173.2 8.7 %all-to-all-start.1 = ((bf16[8,32,2688]{2,1,0:T(8,128)(2,1)}), bf16[8,32,2688]{2,1,0:T(8,128)(2,1)S(1)}, u32[]{:S(2)}, u32[]{:S(2)}) async-start(bf16[8,32,2688]{2,1,0:T(8,128)(2,1)} %shard_map.87), calls=%async_computation.1 | async-start | bytes 2752512 | tf_op jit(solution)/shard_map/all_to_all | solution.py:253
  182.0 32.8 %all-to-all-done.1.back_ref = bf16[8,32,2688]{2,1,0:T(8,128)(2,1)S(1)} async-done(((bf16[8,32,2688]{2,1,0:T(8,128)(2,1)}), bf16[8,32,2688]{2,1,0:T(8,128)(2,1)S(1)}, u32[]{:S(2)}, u32[]{:S(2)}) %all-to-all-start.1) | async-done | bytes 1376288 | tf_op jit(solution)/shard_map/all_to_all | solution.py:253
  214.8 2.3 %shard_map.88 = (bf16[256,2560]{1,0:T(8,128)(2,1)}, bf16[256,6]{1,0:T(8,128)(2,1)S(1)}) custom-call(s32[256,6]{1,0:T(8,128)S(1)} %copy.11.routes_ref, bf16[256,6]{1,0:T(8,128)(2,1)S(1)} %copy.12.gates_ref, bf16[256,256]{1,0:T(8,128)(2,1)S(1)} %get-tuple-element.7.sel_ref, bf16[8,32,2688]{2,1,0:T(8,128)(2,1)S(1)} %all-to-all-done.1.back_ref), custom_call_target="tpu_custom_call" | custom-call | flops 335544320 | bytes 2621440 | tf_op jit(solution)/shard_map/pallas_call | solution.py:255
  (71 shorter events, 17.0 us)
Async XLA Ops:
  1.5 41.9 %copy-start.9 = (s32[256,6]{0,1:T(8,128)S(1)}, s32[256,6]{0,1:T(8,128)}, u32[]{:S(2)}) copy-start(s32[256,6]{0,1:T(8,128)} %param.9) | copy-start | bytes 18436
  3.1 9.8 %collective-permute-start = (bf16[3,40,768]{2,1,0:T(8,128)(2,1)S(1)}, bf16[3,40,768]{2,1,0:T(8,128)(2,1)S(1)}, u32[]{:S(2)}, u32[]{:S(2)}) collective-permute-start(bf16[3,40,768]{2,1,0:T(8,128)(2,1)S(1)} %constant_dynamic-update-slice_fusion), channel_id=1, source_target_pairs={{8,0},{4,12},{9,1},{5,13},{10,2},{6,14},{11,3},{7,15},{24,16},{20,... | collective-permute-start | bytes 552968 | tf_op jit(solution)/shard_map/ppermute | solution.py:195
  11.9 34.0 %copy-start = (bf16[256,2560]{1,0:T(8,128)(2,1)S(1)}, bf16[256,2560]{1,0:T(8,128)(2,1)}, u32[]{:S(2)}) copy-start(bf16[256,2560]{1,0:T(8,128)(2,1)} %tok_ref.1) | copy-start | bytes 3932164
  12.0 34.0 %copy-start.1 = (bf16[256,2560]{1,0:T(8,128)(2,1)S(1)}, bf16[256,2560]{1,0:T(8,128)(2,1)}, u32[]{:S(2)}) copy-start(bf16[256,2560]{1,0:T(8,128)(2,1)} %cot_ref.1) | copy-start | bytes 3932164
  13.1 14.1 %collective-permute-start.1 = (bf16[240,768]{1,0:T(8,128)(2,1)S(1)}, bf16[240,768]{1,0:T(8,128)(2,1)S(1)}, u32[]{:S(2)}, u32[]{:S(2)}) collective-permute-start(bf16[240,768]{1,0:T(8,128)(2,1)S(1)} %bitcast.9), channel_id=1, source_target_pairs={{0,4},{64,68},{12,72},{76,8},{1,5},{65,69},{13,73},{77,9},{2,6},{6... | collective-permute-start | bytes 1105928 | tf_op jit(solution)/shard_map/ppermute | solution.py:204
  14.4 29.2 %collective-permute-start.3 = (bf16[240,768]{1,0:T(8,128)(2,1)S(1)}, bf16[240,768]{1,0:T(8,128)(2,1)}, u32[]{:S(2)}, u32[]{:S(2)}) collective-permute-start(bf16[240,768]{1,0:T(8,128)(2,1)S(1)} %bitcast.10), channel_id=1, source_target_pairs={{0,68},{64,4},{12,8},{76,72},{1,69},{65,5},{13,9},{77,73},{2,70},{... | collective-permute-start | bytes 1105928 | tf_op jit(solution)/shard_map/ppermute | solution.py:204
  28.6 22.1 %collective-permute-start.2 = (bf16[128,768]{1,0:T(8,128)(2,1)}, bf16[128,768]{1,0:T(8,128)(2,1)S(1)}, u32[]{:S(2)}, u32[]{:S(2)}) collective-permute-start(bf16[128,768]{1,0:T(8,128)(2,1)} %slice.40), channel_id=1, source_target_pairs={{4,64},{68,0},{8,12},{72,76},{5,65},{69,1},{9,13},{73,77},{6,66},{... | collective-permute-start | bytes 589832 | tf_op jit(solution)/shard_map/ppermute | solution.py:204
  44.5 6.2 %copy-start.3 = (bf16[240,768]{1,0:T(8,128)(2,1)S(1)}, bf16[240,768]{1,0:T(8,128)(2,1)}, u32[]{:S(2)}) copy-start(bf16[240,768]{1,0:T(8,128)(2,1)} %copy-done.2) | copy-start | bytes 1105924
  44.5 6.2 %collective-permute-start.4 = (bf16[112,768]{1,0:T(8,128)(2,1)S(1)}, bf16[112,768]{1,0:T(8,128)(2,1)S(1)}, u32[]{:S(2)}, u32[]{:S(2)}) collective-permute-start(bf16[112,768]{1,0:T(8,128)(2,1)S(1)} %slice.41), channel_id=1, source_target_pairs={{4,0},{68,64},{8,76},{72,12},{5,1},{69,65},{9,77},{73,13},{6,2},{7... | collective-permute-start | bytes 516104 | tf_op jit(solution)/shard_map/ppermute | solution.py:204
  51.8 105.9 %all-to-all-start = ((bf16[8,64,2560]{2,1,0:T(8,128)(2,1)}), bf16[8,64,2560]{2,1,0:T(8,128)(2,1)}, u32[]{:S(2)}, u32[]{:S(2)}) async-start(bf16[8,64,2560]{2,1,0:T(8,128)(2,1)} %get-tuple-element.9), calls=%async_computation | async-start | bytes 5242880 | tf_op jit(solution)/shard_map/all_to_all | solution.py:227
  60.0 13.0 %collective-permute-start.6 = (bf16[240,768]{1,0:T(8,128)(2,1)S(1)}, bf16[240,768]{1,0:T(8,128)(2,1)S(1)}, u32[]{:S(2)}, u32[]{:S(2)}) collective-permute-start(bf16[240,768]{1,0:T(8,128)(2,1)S(1)} %get-tuple-element.10), channel_id=1, source_target_pairs={{0,48},{16,0},{32,16},{48,32},{1,49},{17,1},{33,17},{49,33},{2,50}... | collective-permute-start | bytes 1105928 | tf_op jit(solution)/shard_map/ppermute | solution.py:176
  64.7 13.3 %collective-permute-start.5 = (bf16[240,768]{1,0:T(8,128)(2,1)S(1)}, bf16[240,768]{1,0:T(8,128)(2,1)S(1)}, u32[]{:S(2)}, u32[]{:S(2)}) collective-permute-start(bf16[240,768]{1,0:T(8,128)(2,1)S(1)} %get-tuple-element.10), channel_id=1, source_target_pairs={{0,16},{16,32},{32,48},{48,0},{1,17},{17,33},{33,49},{49,1},{2,18}... | collective-permute-start | bytes 1105928 | tf_op jit(solution)/shard_map/ppermute | solution.py:176
  66.6 13.4 %collective-permute-start.14 = (bf16[240,768]{1,0:T(8,128)(2,1)S(1)}, bf16[240,768]{1,0:T(8,128)(2,1)S(1)}, u32[]{:S(2)}, u32[]{:S(2)}) collective-permute-start(bf16[240,768]{1,0:T(8,128)(2,1)S(1)} %get-tuple-element.11), channel_id=1, source_target_pairs={{0,384},{128,0},{256,128},{384,256},{1,385},{129,1},{257,129},{385... | collective-permute-start | bytes 1105928 | tf_op jit(solution)/shard_map/ppermute | solution.py:176
  71.0 13.4 %collective-permute-start.13 = (bf16[240,768]{1,0:T(8,128)(2,1)S(1)}, bf16[240,768]{1,0:T(8,128)(2,1)S(1)}, u32[]{:S(2)}, u32[]{:S(2)}) collective-permute-start(bf16[240,768]{1,0:T(8,128)(2,1)S(1)} %get-tuple-element.11), channel_id=1, source_target_pairs={{0,128},{128,256},{256,384},{384,0},{1,129},{129,257},{257,385},{3... | collective-permute-start | bytes 1105928 | tf_op jit(solution)/shard_map/ppermute | solution.py:176
  73.0 25.9 %collective-permute-start.8 = (bf16[112,768]{1,0:T(8,128)(2,1)S(1)}, bf16[112,768]{1,0:T(8,128)(2,1)S(1)}, u32[]{:S(2)}, u32[]{:S(2)}) collective-permute-start(bf16[112,768]{1,0:T(8,128)(2,1)S(1)} %slice.43), channel_id=1, source_target_pairs={{0,48},{16,0},{32,16},{48,32},{1,49},{17,1},{33,17},{49,33},{2,50}... | collective-permute-start | bytes 516104 | tf_op jit(solution)/shard_map/ppermute | solution.py:176
  78.1 20.8 %collective-permute-start.7 = (bf16[128,768]{1,0:T(8,128)(2,1)S(1)}, bf16[128,768]{1,0:T(8,128)(2,1)S(1)}, u32[]{:S(2)}, u32[]{:S(2)}) collective-permute-start(bf16[128,768]{1,0:T(8,128)(2,1)S(1)} %slice.42), channel_id=1, source_target_pairs={{0,16},{16,32},{32,48},{48,0},{1,17},{17,33},{33,49},{49,1},{2,18}... | collective-permute-start | bytes 589832 | tf_op jit(solution)/shard_map/ppermute | solution.py:176
  80.0 12.5 %collective-permute-start.16 = (bf16[112,768]{1,0:T(8,128)(2,1)S(1)}, bf16[112,768]{1,0:T(8,128)(2,1)S(1)}, u32[]{:S(2)}, u32[]{:S(2)}) collective-permute-start(bf16[112,768]{1,0:T(8,128)(2,1)S(1)} %slice.47), channel_id=1, source_target_pairs={{0,384},{128,0},{256,128},{384,256},{1,385},{129,1},{257,129},{385... | collective-permute-start | bytes 516104 | tf_op jit(solution)/shard_map/ppermute | solution.py:176
  84.4 8.0 %collective-permute-start.15 = (bf16[128,768]{1,0:T(8,128)(2,1)S(1)}, bf16[128,768]{1,0:T(8,128)(2,1)S(1)}, u32[]{:S(2)}, u32[]{:S(2)}) collective-permute-start(bf16[128,768]{1,0:T(8,128)(2,1)S(1)} %slice.46), channel_id=1, source_target_pairs={{0,128},{128,256},{256,384},{384,0},{1,129},{129,257},{257,385},{3... | collective-permute-start | bytes 589832 | tf_op jit(solution)/shard_map/ppermute | solution.py:176
  92.5 47.6 %copy-start.8 = (bf16[960,768]{1,0:T(8,128)(2,1)}, bf16[960,768]{1,0:T(8,128)(2,1)S(1)}, u32[]{:S(2)}) copy-start(bf16[960,768]{1,0:T(8,128)(2,1)S(1)} %constant_dynamic-update-slice_fusion.10.refs_5_) | copy-start | bytes 4423684
  92.6 33.3 %collective-permute-start.18 = (bf16[960,768]{1,0:T(8,128)(2,1)S(1)}, bf16[960,768]{1,0:T(8,128)(2,1)S(1)}, u32[]{:S(2)}, u32[]{:S(2)}) collective-permute-start(bf16[960,768]{1,0:T(8,128)(2,1)S(1)} %constant_dynamic-update-slice_fusion.10.refs_5_), channel_id=1, source_target_pairs={{0,48},{16,0},{32,16},{48,32},{1,49},{17,1},{33,17},{49,33},{2,50}... | collective-permute-start | bytes 4423688 | tf_op jit(solution)/shard_map/ppermute | solution.py:176
  97.0 35.2 %collective-permute-start.17 = (bf16[960,768]{1,0:T(8,128)(2,1)S(1)}, bf16[960,768]{1,0:T(8,128)(2,1)S(1)}, u32[]{:S(2)}, u32[]{:S(2)}) collective-permute-start(bf16[960,768]{1,0:T(8,128)(2,1)S(1)} %constant_dynamic-update-slice_fusion.10.refs_5_), channel_id=1, source_target_pairs={{0,16},{16,32},{32,48},{48,0},{1,17},{17,33},{33,49},{49,1},{2,18}... | collective-permute-start | bytes 4423688 | tf_op jit(solution)/shard_map/ppermute | solution.py:176
  99.0 36.2 %collective-permute-start.10 = (bf16[960,768]{1,0:T(8,128)(2,1)S(1)}, bf16[960,768]{1,0:T(8,128)(2,1)S(1)}, u32[]{:S(2)}, u32[]{:S(2)}) collective-permute-start(bf16[960,768]{1,0:T(8,128)(2,1)S(1)} %constant_dynamic-update-slice_fusion.5.refs_0_), channel_id=1, source_target_pairs={{0,384},{128,0},{256,128},{384,256},{1,385},{129,1},{257,129},{385... | collective-permute-start | bytes 4423688 | tf_op jit(solution)/shard_map/ppermute | solution.py:176
  100.9 37.2 %collective-permute-start.9 = (bf16[960,768]{1,0:T(8,128)(2,1)S(1)}, bf16[960,768]{1,0:T(8,128)(2,1)S(1)}, u32[]{:S(2)}, u32[]{:S(2)}) collective-permute-start(bf16[960,768]{1,0:T(8,128)(2,1)S(1)} %constant_dynamic-update-slice_fusion.5.refs_0_), channel_id=1, source_target_pairs={{0,128},{128,256},{256,384},{384,0},{1,129},{129,257},{257,385},{3... | collective-permute-start | bytes 4423688 | tf_op jit(solution)/shard_map/ppermute | solution.py:176
  125.9 7.3 %copy-start.4 = (bf16[960,768]{1,0:T(8,128)(2,1)}, bf16[960,768]{1,0:T(8,128)(2,1)S(1)}, u32[]{:S(2)}) copy-start(bf16[960,768]{1,0:T(8,128)(2,1)S(1)} %collective-permute-done.18.refs_7_) | copy-start | bytes 4423684
  126.9 17.8 %collective-permute-start.20 = (bf16[480,768]{1,0:T(8,128)(2,1)}, bf16[480,768]{1,0:T(8,128)(2,1)S(1)}, u32[]{:S(2)}, u32[]{:S(2)}) collective-permute-start(bf16[480,768]{1,0:T(8,128)(2,1)} %slice.49), channel_id=1, source_target_pairs={{0,48},{16,0},{32,16},{48,32},{1,49},{17,1},{33,17},{49,33},{2,50}... | collective-permute-start | bytes 2211848 | tf_op jit(solution)/shard_map/ppermute | solution.py:176
  132.2 4.0 %copy-start.5 = (bf16[960,768]{1,0:T(8,128)(2,1)}, bf16[960,768]{1,0:T(8,128)(2,1)S(1)}, u32[]{:S(2)}) copy-start(bf16[960,768]{1,0:T(8,128)(2,1)S(1)} %collective-permute-done.17.refs_6_) | copy-start | bytes 4423684
  133.2 17.6 %collective-permute-start.19 = (bf16[480,768]{1,0:T(8,128)(2,1)}, bf16[480,768]{1,0:T(8,128)(2,1)}, u32[]{:S(2)}, u32[]{:S(2)}) collective-permute-start(bf16[480,768]{1,0:T(8,128)(2,1)} %slice.48), channel_id=1, source_target_pairs={{0,16},{16,32},{32,48},{48,0},{1,17},{17,33},{33,49},{49,1},{2,18}... | collective-permute-start | bytes 2211848 | tf_op jit(solution)/shard_map/ppermute | solution.py:176
  135.1 5.0 %copy-start.6 = (bf16[960,768]{1,0:T(8,128)(2,1)}, bf16[960,768]{1,0:T(8,128)(2,1)S(1)}, u32[]{:S(2)}) copy-start(bf16[960,768]{1,0:T(8,128)(2,1)S(1)} %collective-permute-done.10.refs_2_) | copy-start | bytes 4423684
  136.1 16.3 %collective-permute-start.12 = (bf16[480,768]{1,0:T(8,128)(2,1)}, bf16[480,768]{1,0:T(8,128)(2,1)}, u32[]{:S(2)}, u32[]{:S(2)}) collective-permute-start(bf16[480,768]{1,0:T(8,128)(2,1)} %slice.45), channel_id=1, source_target_pairs={{0,384},{128,0},{256,128},{384,256},{1,385},{129,1},{257,129},{385... | collective-permute-start | bytes 2211848 | tf_op jit(solution)/shard_map/ppermute | solution.py:176
  140.2 17.6 %collective-permute-start.11 = (bf16[480,768]{1,0:T(8,128)(2,1)}, bf16[480,768]{1,0:T(8,128)(2,1)}, u32[]{:S(2)}, u32[]{:S(2)}) collective-permute-start(bf16[480,768]{1,0:T(8,128)(2,1)} %slice.44), channel_id=1, source_target_pairs={{0,128},{128,256},{256,384},{384,0},{1,129},{129,257},{257,385},{3... | collective-permute-start | bytes 2211848 | tf_op jit(solution)/shard_map/ppermute | solution.py:176
  173.2 8.7 %copy-start.10 = (bf16[256,6]{0,1:T(8,128)(2,1)S(1)}, bf16[256,6]{0,1:T(8,128)(2,1)}, u32[]{:S(2)}) copy-start(bf16[256,6]{0,1:T(8,128)(2,1)} %param.10) | copy-start | bytes 9220
  173.2 41.6 %all-to-all-start.1 = ((bf16[8,32,2688]{2,1,0:T(8,128)(2,1)}), bf16[8,32,2688]{2,1,0:T(8,128)(2,1)S(1)}, u32[]{:S(2)}, u32[]{:S(2)}) async-start(bf16[8,32,2688]{2,1,0:T(8,128)(2,1)} %shard_map.87), calls=%async_computation.1 | async-start | bytes 2752512 | tf_op jit(solution)/shard_map/all_to_all | solution.py:253
  (2 other events, 1.9 us)

commit v2 on v1

--- a/solution.py
+++ b/solution.py
@@ -1,3 +1,5 @@
+import functools
+
 import jax
 import jax.numpy as jnp
 from jax import lax
@@ -63,44 +65,30 @@
     score_ref[...] = jnp.where(window, score, 0.0).astype(BF)
 
 
-def expert_kernel(where_ref, rows_ref, *refs):
-    pieces = refs[:10]
-    out_ref = refs[10]
-    gate_w, up_w, down_w, grad_a, grad_b, pre_g, pre_u, sems = refs[11:]
+def stack_kernel(gate_ref, up_ref, down_ref, out_ref):
+    for m, ref in enumerate((gate_ref, up_ref, down_ref)):
+        out_ref[m] = ref[0]
+
+
+def expert_kernel(pieces, where_ref, rows_ref, *refs):
+    sources = refs[: len(refs) - 9]
+    out_ref = refs[-9]
+    gate_w, up_w, down_w, grad_a, grad_b, pre_g, pre_u, sems = refs[-8:]
     weights = (gate_w, up_w, down_w)
     my_x, my_y = where_ref[0], where_ref[1]
 
     copies = ([], [], [])
-
-    def place(src, src_row, block, half, xx, yy):
-        target = ((xx * 2 + block) * 4 + yy) * 80
+    for number, row, block, dx, dy in pieces:
+        xx, yy = lax.rem(my_x + dx, 4), lax.rem(my_y + dy, 4)
+        target = pl.multiple_of(((xx * 2 + block) * 4 + yy) * 80, 16)
         for m in range(3):
-            lo, hi = max(80 * m, half[0]), min(80 * m + 80, half[1])
-            if lo < hi:
-                copies[m].append(
-                    pltpu.make_async_copy(
-                        src.at[pl.ds(src_row + lo - half[0], hi - lo), :],
-                        weights[m].at[pl.ds(pl.multiple_of(target + lo - 80 * m, 16), hi - lo), :],
-                        sems.at[m],
-                    )
+            copies[m].append(
+                pltpu.make_async_copy(
+                    sources[number].at[pl.ds(row + 80 * m, 80), :],
+                    weights[m].at[pl.ds(target, 80), :],
+                    sems.at[m],
                 )
-
-    whole = (0, 240)
-    offs = (0, 3, 1, 2)
-    for block in range(2):
-        own, low, high, opp0, opp1 = pieces[5 * block : 5 * block + 5]
-        for outer, (src, first, inner) in enumerate(
-            ((own, 0, (0, 1, 2, 3)), (low, 0, (0, 1, 2, 3)), (high, 0, (0, 1, 2, 3)),
-             (opp0, 0, (0, 1)), (opp1, 2, (2, 3)))
-        ):
-            far = offs[min(outer, 3)]
-            for k in inner:
-                near = offs[k]
-                if block == 0:
-                    xx, yy = lax.rem(my_x + far, 4), lax.rem(my_y + near, 4)
-                else:
-                    xx, yy = lax.rem(my_x + near, 4), lax.rem(my_y + far, 4)
-                place(src, (k - first) * 240, block, whole, xx, yy)
+            )
     for m in range(3):
         for copy in copies[m]:
             copy.start()
@@ -160,8 +148,8 @@
         out_ref[:, :, part] = rows.astype(BF).reshape(8, 32, dstep)
 
 
-def params():
-    return pltpu.CompilerParams(vmem_limit_bytes=48 * 1024 * 1024)
+def params(mib=16):
+    return pltpu.CompilerParams(vmem_limit_bytes=mib * 1024 * 1024)
 
 
 def cost(flops, moved):
@@ -176,12 +164,78 @@
     return lax.ppermute(v, axis, [(i, (i + by) % 4) for i in range(4)])
 
 
-def ring_first(v, axis):
-    return shift(v, axis, 1), shift(v, axis, -1)
-
-
-def ring_second(low, high, axis, cut):
-    return shift(low[:cut], axis, 1), shift(high[cut:], axis, -1)
+def diagonal(v, by):
+    pairs = [(i * 4 + j, (i + by) % 4 * 4 + (j + by) % 4) for i in range(4) for j in range(4)]
+    return lax.ppermute(v, ("x", "y"), pairs)
+
+
+def join_kernel(plan, inputs, *refs):
+    sources, targets, sem = refs[:inputs], refs[inputs:-1], refs[-1]
+    copies = [
+        pltpu.make_async_copy(
+            sources[i].at[pl.ds(row, count), :], targets[o].at[pl.ds(at, count), :], sem
+        )
+        for i, row, count, o, at in plan
+    ]
+    for copy in copies:
+        copy.start()
+    for copy in copies:
+        copy.wait()
+
+
+def join(rows, plan, *arrays):
+    width = arrays[0].shape[1]
+    moved = 4 * sum(rows) * width
+    return pl.pallas_call(
+        functools.partial(join_kernel, plan, len(arrays)),
+        out_shape=[jax.ShapeDtypeStruct((r, width), BF) for r in rows],
+        in_specs=[ANY] * len(arrays),
+        out_specs=[ANY] * len(rows),
+        scratch_shapes=[pltpu.SemaphoreType.DMA],
+        compiler_params=params(),
+        cost_estimate=cost(0, moved),
+    )(*arrays)
+
+
+def torus_gather(own):
+    full = own.shape[0]
+    half = full // 2
+    y0, y1 = shift(own, "y", 1), shift(own, "y", -1)
+    x0, x1 = shift(own, "x", 1), shift(own, "x", -1)
+    ya, yb, xa, xb = join(
+        [full + half] * 4,
+        (
+            (2, 0, full, 0, 0), (0, 0, half, 0, full),
+            (3, 0, full, 1, 0), (1, half, half, 1, full),
+            (1, 0, full, 2, 0), (2, 0, half, 2, full),
+            (0, 0, full, 3, 0), (3, half, half, 3, full),
+        ),
+        y0, y1, x0, x1,
+    )
+    ya, yb = shift(ya, "y", 1), shift(yb, "y", -1)
+    xa, xb = shift(xa, "x", 1), shift(xb, "x", -1)
+    y_far, x_far, c0, c1 = join(
+        [full, full, half, half],
+        (
+            (0, full, half, 0, 0), (1, full, half, 0, half),
+            (2, full, half, 1, 0), (3, full, half, 1, half),
+            (0, 0, half, 2, 0), (1, half, half, 3, 0),
+        ),
+        ya, yb, xa, xb,
+    )
+    yc, yd = shift(x_far, "y", 1), shift(x_far, "y", -1)
+    xc, xd = shift(y_far, "x", 1), shift(y_far, "x", -1)
+    c0, c1 = diagonal(c0, 1), diagonal(c1, -1)
+    arrays = (own, y0, y1, x0, x1, ya, yb, xa, xb, yc, yd, xc, xd, c0, c1)
+    places = (
+        (0, 0), (0, 3), (0, 1), (3, 0), (1, 0), (3, 3), (1, 1), (3, 1), (1, 3),
+        (2, 3), (2, 1), (3, 2), (1, 2),
+    )
+    pieces = [(n, h * half, h, dx, dy) for n, (dx, dy) in enumerate(places) for h in range(2)]
+    pieces += [(5, full, 0, 0, 2), (6, full, 1, 0, 2)]
+    pieces += [(7, full, 0, 2, 0), (8, full, 1, 2, 0)]
+    pieces += [(13, 0, 0, 2, 2), (14, 0, 1, 2, 2)]
+    return arrays, pieces
 
 
 def on_device(tokens_in, cotangent, routes, gate_weights, gate_proj, up_proj, down_proj):
@@ -191,10 +245,16 @@
     zh, zq = lax.axis_index("zh"), lax.axis_index("zq")
     ring = zh * 2 + zq
 
-    shard = jnp.concatenate([gate_proj, up_proj, down_proj], axis=0)
+    shard = pl.pallas_call(
+        stack_kernel,
+        out_shape=jax.ShapeDtypeStruct((3, *gate_proj.shape[1:]), BF),
+        in_specs=[VM] * 3,
+        out_specs=VM,
+    )(gate_proj, up_proj, down_proj)
     other = lax.ppermute(shard, ("c", "zq"), [(2, 0), (1, 3)])
     pair = jnp.stack([jnp.where(ic == 0, shard, other), jnp.where(ic == 0, other, shard)], axis=1)
     pair = pair.reshape(240, hidden_width)
+    top, bottom = pair[:SPLIT], pair[SPLIT:]
 
     def at(c, p):
         return (p // 2 * 2 + c) * 2 + p % 2
@@ -203,13 +263,20 @@
         pairs = [(at(c, p), at(c, (p + by) % 4)) for c in range(2) for p in range(4) if (p % 2 == c) == source]
         return lax.ppermute(v, ("zh", "c", "zq"), pairs)
 
-    low, high = zmove(pair, True, 1), zmove(pair, True, -1)
-    far0, far1 = zmove(low[:SPLIT], False, 1), zmove(high[SPLIT:], False, -1)
-    far = jnp.concatenate([far0, far1], axis=0)
+    low0, high1 = zmove(top, True, 1), zmove(bottom, True, -1)
+    low1, high0 = zmove(bottom, True, 1), zmove(top, True, -1)
+    far0, far1 = zmove(low0, False, 1), zmove(high1, False, -1)
     source = ic == zq
     swapped = (ring == 0) | (ring == 3)
-    block_a = jnp.where(source, jnp.where(zh == 0, pair, far), jnp.where(swapped, high, low))
-    block_b = jnp.where(source, jnp.where(zh == 0, far, pair), jnp.where(swapped, low, high))
+
+    def pick(mine, far, low, high):
+        return (
+            jnp.where(source, jnp.where(zh == 0, mine, far), jnp.where(swapped, high, low)),
+            jnp.where(source, jnp.where(zh == 0, far, mine), jnp.where(swapped, low, high)),
+        )
+
+    (a0, b0), (a1, b1) = pick(top, far0, low0, high0), pick(bottom, far1, low1, high1)
+    block = jnp.concatenate([a0, a1, b0, b1], axis=0)
 
     payload, sel = pl.pallas_call(
         dispatch_kernel,
@@ -223,32 +290,22 @@
         cost_estimate=cost(2 * 256 * 512 * width, 8 * 256 * width),
     )(routes, tokens_in, cotangent)
 
-    payload, block_a, block_b = lax.optimization_barrier((payload, block_a, block_b))
+    payload, block = lax.optimization_barrier((payload, block))
+    arrays, pieces = torus_gather(block)
     rows = lax.all_to_all(payload, ("c", "zr"), split_axis=0, concat_axis=0, tiled=True)
 
-    a_low, a_high = ring_first(block_a, "y")
-    b_low, b_high = ring_first(block_b, "x")
-    a_far = ring_second(a_low, a_high, "y", SPLIT)
-    b_far = ring_second(b_low, b_high, "x", SPLIT)
-    line_a = jnp.concatenate([block_a, a_low, a_high, *a_far], axis=0)
-    line_b = jnp.concatenate([block_b, b_low, b_high, *b_far], axis=0)
-    al, ah = ring_first(line_a, "x")
-    bl, bh = ring_first(line_b, "y")
-    af = ring_second(al, ah, "x", 480)
-    bf = ring_second(bl, bh, "y", 480)
-
     back = pl.pallas_call(
-        expert_kernel,
+        functools.partial(expert_kernel, pieces),
         out_shape=jax.ShapeDtypeStruct((8, 32, width + PAD), BF),
-        in_specs=[pl.BlockSpec(memory_space=pltpu.SMEM), VM] + [ANY] * 10,
+        in_specs=[pl.BlockSpec(memory_space=pltpu.SMEM), VM] + [ANY] * len(arrays),
         out_specs=VM,
         scratch_shapes=[pltpu.VMEM((width, hidden_width), BF)] * 3
         + [pltpu.VMEM((256, hidden_width), BF)] * 2
         + [pltpu.VMEM((256, hidden_width), F32)] * 2
         + [pltpu.SemaphoreType.DMA((3,))],
-        compiler_params=params(),
+        compiler_params=params(56),
         cost_estimate=cost(10 * 256 * width * hidden_width, 6 * width * hidden_width),
-    )(jnp.stack([ix, iy]).astype(jnp.int32), rows, line_a, al, ah, *af, line_b, bl, bh, *bf)
+    )(jnp.stack([ix, iy]).astype(jnp.int32), rows, *arrays)
 
     home = lax.all_to_all(back, ("c", "zr"), split_axis=0, concat_axis=0, tiled=True)
 

time: 219 us -> 226 us (1.032)
  waiting for transfers between devices: 88.2 us -> 96.5 us
  local copies, waits for them, and re-layouts: 11.3 us -> 4.41 us
  Pallas kernels: 21.4 us -> 24.9 us
    ppermute x16 -> x12, starting transfers between devices: 50.2 us -> 36.6 us  [shift(): return lax.ppermute(v, axis, [(i, (i + by) % 4) for i in range(4)])]
    ppermute x0 -> x2, waiting for transfers between devices: none -> 9.69 us  [diagonal(): return lax.ppermute(v, ('x', 'y'), pairs)]
    ppermute x0 -> x2, starting transfers between devices: none -> 8.87 us  [diagonal(): return lax.ppermute(v, ('x', 'y'), pairs)]
    slice x10 -> x2, local copies, waits for them, and re-layouts: 5.58 us -> 0.7 us  [on_device(): top, bottom = (pair[:SPLIT], pair[SPLIT:])]
    all_to_all x1, starting transfers between devices: 8.22 us -> 11.9 us  [on_device(): lax.all_to_all(payload, ('c', 'zr'), split_axis=0, concat_axis=0, tiled=T...]
    pallas_call x1 -> x4, Pallas kernels: 15.4 us -> 19 us  [the longest x1 14.3 us: on_device(): pl.pallas_call(functools.partial(expert_kernel, pieces), out_shape=jax.Sh...]
    ppermute x16 -> x12, waiting for transfers between devices: 41.7 us -> 40.1 us  [shift(): return lax.ppermute(v, axis, [(i, (i + by) % 4) for i in range(4)])]
    ppermute x4 -> x6, starting transfers between devices: 18.8 us -> 19.4 us  [zmove(): return lax.ppermute(v, ('zh', 'c', 'zq'), pairs)]
  transfers between devices with their start and end apart: 23 -> 23, of which waited for: 10 -> 14; matrix products, arithmetic and copies ran while one was open for 3% -> 1% of each run, Pallas kernels for 2% -> 3%
where the time goes in v2:
time: 226 us; the launch traced here: 224 us
  waiting for transfers between devices  96.5 us (43%)
  starting transfers between devices  94.2 us (42%)
  Pallas kernels  24.9 us (11%)
  local copies, waits for them, and re-layouts  4.41 us (2%)
  other arithmetic  2.82 us (1%)
    ppermute x12, waiting for transfers between devices, shift(): return lax.ppermute(v, axis, [(i, (i + by) % 4) for i in range(4)])  40.1 us
    ppermute x12, starting transfers between devices, shift(): return lax.ppermute(v, axis, [(i, (i + by) % 4) for i in range(4)])  36.6 us
    all_to_all x1, waiting for transfers between devices, on_device(): lax.all_to_all(back, ('c', 'zr'), split_axis=0, concat_axis=0, tiled=True)  32.8 us
    ppermute x6, starting transfers between devices, zmove(): return lax.ppermute(v, ('zh', 'c', 'zq'), pairs)  19.4 us
    pallas_call x1, Pallas kernels, on_device(): pl.pallas_call(functools.partial(expert_kernel, pieces), out_shape=jax.Sh...  14.3 us
    ppermute x6, waiting for transfers between devices, zmove(): return lax.ppermute(v, ('zh', 'c', 'zq'), pairs)  12.7 us
    all_to_all x1, starting transfers between devices, on_device(): lax.all_to_all(payload, ('c', 'zr'), split_axis=0, concat_axis=0, tiled=T...  11.9 us
    ppermute x2, waiting for transfers between devices, diagonal(): return lax.ppermute(v, ('x', 'y'), pairs)  9.69 us
  transfers between devices with their start and end apart: 23, of which 14 were waited for; matrix products, arithmetic and copies ran while one was open for 1% of the time, Pallas kernels for 3%

profile of v2, /device:TPU:1, one launch (start us, length us, event | category | flops | bytes accessed | tf_op | source)
XLA Modules:
  0.0 223.9 jit_solution(8781097223664816898)
XLA Ops:
  2.2 8.8 %collective-permute-start = (bf16[3,40,768]{2,1,0:T(8,128)(2,1)}, bf16[3,40,768]{2,1,0:T(8,128)(2,1)S(1)}, u32[]{:S(2)}, u32[]{:S(2)}) collective-permute-start(bf16[3,40,768]{2,1,0:T(8,128)(2,1)} %shard_map.87), channel_id=1, source_target_pairs={{8,0},{4,12},{9,1},{5,13},{10,2},{6,14},{11,3},{7,15},{24,16},{20,... | collective-permute-start | bytes 552968 | tf_op jit(solution)/shard_map/ppermute | solution.py:254
  17.9 8.8 %collective-permute-done.4 = bf16[112,768]{1,0:T(8,128)(2,1)} collective-permute-done((bf16[112,768]{1,0:T(8,128)(2,1)}, bf16[112,768]{1,0:T(8,128)(2,1)}, u32[]{:S(2)}, u32[]{:S(2)}) %collective-permute-start.4) | collective-permute-done | bytes 172064 | tf_op jit(solution)/shard_map/ppermute | solution.py:264
  26.6 6.3 %collective-permute-start.5 = (bf16[112,768]{1,0:T(8,128)(2,1)}, bf16[112,768]{1,0:T(8,128)(2,1)}, u32[]{:S(2)}, u32[]{:S(2)}) collective-permute-start(bf16[112,768]{1,0:T(8,128)(2,1)} %collective-permute-done.4), channel_id=1, source_target_pairs={{4,0},{68,64},{8,76},{72,12},{5,1},{69,65},{9,77},{73,13},{6,2},{7... | collective-permute-start | bytes 516104 | tf_op jit(solution)/shard_map/ppermute | solution.py:264
  33.1 3.6 %shard_map.86 = (bf16[8,64,2560]{2,1,0:T(8,128)(2,1)}, bf16[256,256]{1,0:T(8,128)(2,1)S(1)}) custom-call(s32[256,6]{1,0:T(8,128)S(1)} %copy.11.routes_ref, bf16[256,2560]{1,0:T(8,128)(2,1)S(1)} %copy-done, bf16[256,2560]{1,0:T(8,128)(2,1)S(1)} %copy-done.1), custom_call_target="tpu_custom_call" | custom-call | flops 671088640 | bytes 5242880 | tf_op jit(solution)/shard_map/pallas_call | solution.py:281
  38.6 7.9 %collective-permute-start.2 = (bf16[128,768]{1,0:T(8,128)(2,1)S(1)}, bf16[128,768]{1,0:T(8,128)(2,1)S(1)}, u32[]{:S(2)}, u32[]{:S(2)}) collective-permute-start(bf16[128,768]{1,0:T(8,128)(2,1)S(1)} %collective-permute-done.1), channel_id=1, source_target_pairs={{4,64},{68,0},{8,12},{72,76},{5,65},{69,1},{9,13},{73,77},{6,66},{... | collective-permute-start | bytes 589832 | tf_op jit(solution)/shard_map/ppermute | solution.py:264
  49.0 2.7 %collective-permute-done.2 = bf16[128,768]{1,0:T(8,128)(2,1)S(1)} collective-permute-done((bf16[128,768]{1,0:T(8,128)(2,1)S(1)}, bf16[128,768]{1,0:T(8,128)(2,1)S(1)}, u32[]{:S(2)}, u32[]{:S(2)}) %collective-permute-start.2) | collective-permute-done | bytes 196640 | tf_op jit(solution)/shard_map/ppermute | solution.py:264
  51.8 11.9 %all-to-all-start = ((bf16[8,64,2560]{2,1,0:T(8,128)(2,1)}), bf16[8,64,2560]{2,1,0:T(8,128)(2,1)}, u32[]{:S(2)}, u32[]{:S(2)}) async-start(bf16[8,64,2560]{2,1,0:T(8,128)(2,1)} %get-tuple-element.16), calls=%async_computation | async-start | bytes 5242880 | tf_op jit(solution)/shard_map/all_to_all | solution.py:295
  63.7 2.4 %collective-permute-start.10 = (bf16[480,768]{1,0:T(8,128)(2,1)S(1)}, bf16[480,768]{1,0:T(8,128)(2,1)S(1)}, u32[]{:S(2)}, u32[]{:S(2)}) collective-permute-start(bf16[480,768]{1,0:T(8,128)(2,1)S(1)} %pad_maximum_fusion.refs_0_), channel_id=1, source_target_pairs={{0,384},{128,0},{256,128},{384,256},{1,385},{129,1},{257,129},{385... | collective-permute-start | bytes 2211848 | tf_op jit(solution)/shard_map/ppermute | solution.py:164
  66.1 2.9 %collective-permute-start.9 = (bf16[480,768]{1,0:T(8,128)(2,1)S(1)}, bf16[480,768]{1,0:T(8,128)(2,1)S(1)}, u32[]{:S(2)}, u32[]{:S(2)}) collective-permute-start(bf16[480,768]{1,0:T(8,128)(2,1)S(1)} %pad_maximum_fusion.refs_0_), channel_id=1, source_target_pairs={{0,128},{128,256},{256,384},{384,0},{1,129},{129,257},{257,385},{3... | collective-permute-start | bytes 2211848 | tf_op jit(solution)/shard_map/ppermute | solution.py:164
  69.0 3.7 %collective-permute-start.8 = (bf16[480,768]{1,0:T(8,128)(2,1)S(1)}, bf16[480,768]{1,0:T(8,128)(2,1)S(1)}, u32[]{:S(2)}, u32[]{:S(2)}) collective-permute-start(bf16[480,768]{1,0:T(8,128)(2,1)S(1)} %pad_maximum_fusion.refs_0_), channel_id=1, source_target_pairs={{0,48},{16,0},{32,16},{48,32},{1,49},{17,1},{33,17},{49,33},{2,50}... | collective-permute-start | bytes 2211848 | tf_op jit(solution)/shard_map/ppermute | solution.py:164
  72.7 1.9 collective-permute-start.7
  74.6 9.2 %collective-permute-done.10.refs_3_.refs_4_ = bf16[480,768]{1,0:T(8,128)(2,1)S(1)} collective-permute-done((bf16[480,768]{1,0:T(8,128)(2,1)S(1)}, bf16[480,768]{1,0:T(8,128)(2,1)S(1)}, u32[]{:S(2)}, u32[]{:S(2)}) %collective-permute-start.10) | collective-permute-done | bytes 737312 | tf_op jit(solution)/shard_map/ppermute | solution.py:164
  83.8 3.2 %collective-permute-done.9.refs_2_.refs_3_ = bf16[480,768]{1,0:T(8,128)(2,1)S(1)} collective-permute-done((bf16[480,768]{1,0:T(8,128)(2,1)S(1)}, bf16[480,768]{1,0:T(8,128)(2,1)S(1)}, u32[]{:S(2)}, u32[]{:S(2)}) %collective-permute-start.9) | collective-permute-done | bytes 737312 | tf_op jit(solution)/shard_map/ppermute | solution.py:164
  88.4 4.8 %collective-permute-done.7.refs_0_.refs_1_ = bf16[480,768]{1,0:T(8,128)(2,1)S(1)} collective-permute-done((bf16[480,768]{1,0:T(8,128)(2,1)S(1)}, bf16[480,768]{1,0:T(8,128)(2,1)S(1)}, u32[]{:S(2)}, u32[]{:S(2)}) %collective-permute-start.7) | collective-permute-done | bytes 737312 | tf_op jit(solution)/shard_map/ppermute | solution.py:164
  93.3 1.9 shard_map.88
  95.2 1.9 collective-permute-start.11
  97.1 4.6 %collective-permute-start.12 = (bf16[720,768]{1,0:T(8,128)(2,1)S(1)}, bf16[720,768]{1,0:T(8,128)(2,1)S(1)}, u32[]{:S(2)}, u32[]{:S(2)}) collective-permute-start(bf16[720,768]{1,0:T(8,128)(2,1)S(1)} %get-tuple-element.19), channel_id=1, source_target_pairs={{0,48},{16,0},{32,16},{48,32},{1,49},{17,1},{33,17},{49,33},{2,50}... | collective-permute-start | bytes 3317768 | tf_op jit(solution)/shard_map/ppermute | solution.py:164
  101.7 1.9 collective-permute-start.13
  103.6 4.6 %collective-permute-start.14 = (bf16[720,768]{1,0:T(8,128)(2,1)S(1)}, bf16[720,768]{1,0:T(8,128)(2,1)S(1)}, u32[]{:S(2)}, u32[]{:S(2)}) collective-permute-start(bf16[720,768]{1,0:T(8,128)(2,1)S(1)} %get-tuple-element.21), channel_id=1, source_target_pairs={{0,384},{128,0},{256,128},{384,256},{1,385},{129,1},{257,129},{385... | collective-permute-start | bytes 3317768 | tf_op jit(solution)/shard_map/ppermute | solution.py:164
  108.2 14.5 %collective-permute-done.11.refs_0_.refs_5_ = bf16[720,768]{1,0:T(8,128)(2,1)S(1)} collective-permute-done((bf16[720,768]{1,0:T(8,128)(2,1)S(1)}, bf16[720,768]{1,0:T(8,128)(2,1)S(1)}, u32[]{:S(2)}, u32[]{:S(2)}) %collective-permute-start.11) | collective-permute-done | bytes 1105952 | tf_op jit(solution)/shard_map/ppermute | solution.py:164
  123.6 5.0 %collective-permute-done.13.refs_2_.refs_7_ = bf16[720,768]{1,0:T(8,128)(2,1)S(1)} collective-permute-done((bf16[720,768]{1,0:T(8,128)(2,1)S(1)}, bf16[720,768]{1,0:T(8,128)(2,1)S(1)}, u32[]{:S(2)}, u32[]{:S(2)}) %collective-permute-start.13) | collective-permute-done | bytes 1105952 | tf_op jit(solution)/shard_map/ppermute | solution.py:164
  130.9 1.9 collective-permute-start.19
  132.9 5.5 %collective-permute-start.16 = (bf16[480,768]{1,0:T(8,128)(2,1)}, bf16[480,768]{1,0:T(8,128)(2,1)S(1)}, u32[]{:S(2)}, u32[]{:S(2)}) collective-permute-start(bf16[480,768]{1,0:T(8,128)(2,1)} %get-tuple-element.22), channel_id=1, source_target_pairs={{0,48},{16,0},{32,16},{48,32},{1,49},{17,1},{33,17},{49,33},{2,50}... | collective-permute-start | bytes 2211848 | tf_op jit(solution)/shard_map/ppermute | solution.py:164
  138.4 1.9 collective-permute-start.15
  140.3 3.3 %collective-permute-start.18 = (bf16[480,768]{1,0:T(8,128)(2,1)S(1)}, bf16[480,768]{1,0:T(8,128)(2,1)S(1)}, u32[]{:S(2)}, u32[]{:S(2)}) collective-permute-start(bf16[480,768]{1,0:T(8,128)(2,1)S(1)} %get-tuple-element.23), channel_id=1, source_target_pairs={{0,384},{128,0},{256,128},{384,256},{1,385},{129,1},{257,129},{385... | collective-permute-start | bytes 2211848 | tf_op jit(solution)/shard_map/ppermute | solution.py:164
  143.7 1.9 collective-permute-start.17
  146.4 6.9 %collective-permute-start.20 = (bf16[240,768]{1,0:T(8,128)(2,1)S(1)}, bf16[240,768]{1,0:T(8,128)(2,1)}, u32[]{:S(2)}, u32[]{:S(2)}) collective-permute-start(bf16[240,768]{1,0:T(8,128)(2,1)S(1)} %get-tuple-element.25), channel_id=1, source_target_pairs={{0,432},{16,384},{32,400},{48,416},{128,48},{144,0},{160,16},{176,... | collective-permute-start | bytes 1105928 | tf_op jit(solution)/shard_map/ppermute | solution.py:169
  153.9 9.7 %collective-permute-done.20.refs_14_ = bf16[240,768]{1,0:T(8,128)(2,1)} collective-permute-done((bf16[240,768]{1,0:T(8,128)(2,1)S(1)}, bf16[240,768]{1,0:T(8,128)(2,1)}, u32[]{:S(2)}, u32[]{:S(2)}) %collective-permute-start.20) | collective-permute-done | bytes 368672 | tf_op jit(solution)/shard_map/ppermute | solution.py:169
  164.9 14.3 %shard_map.90 = bf16[8,32,2688]{2,1,0:T(8,128)(2,1)} custom-call(s32[2]{0:T(128)} %pad_add_fusion.where_ref, bf16[8,64,2560]{2,1,0:T(8,128)(2,1)} %all-to-all-done.rows_ref, bf16[480,768]{1,0:T(8,128)(2,1)} %copy-done.12, bf16[480,768]{1,0:T(8,128)(2,1)} %copy-done.9, bf16[480,768]{1,0:T(8,128)(2,1)} %copy-done.8, bf16[480,768]{1,0:T(8,128)(2,1)} %copy-done.7, ...), custom_call_target="tpu_custom_call" | custom-call | flops 5033164800 | bytes 11796480 | tf_op jit(solution)/shard_map/pallas_call | solution.py:297
  179.2 8.7 %all-to-all-start.1 = ((bf16[8,32,2688]{2,1,0:T(8,128)(2,1)}), bf16[8,32,2688]{2,1,0:T(8,128)(2,1)S(1)}, u32[]{:S(2)}, u32[]{:S(2)}) async-start(bf16[8,32,2688]{2,1,0:T(8,128)(2,1)} %shard_map.90), calls=%async_computation.1 | async-start | bytes 2752512 | tf_op jit(solution)/shard_map/all_to_all | solution.py:310
  188.1 32.8 %all-to-all-done.1.back_ref = bf16[8,32,2688]{2,1,0:T(8,128)(2,1)S(1)} async-done(((bf16[8,32,2688]{2,1,0:T(8,128)(2,1)}), bf16[8,32,2688]{2,1,0:T(8,128)(2,1)S(1)}, u32[]{:S(2)}, u32[]{:S(2)}) %all-to-all-start.1) | async-done | bytes 1376288 | tf_op jit(solution)/shard_map/all_to_all | solution.py:310
  220.9 2.3 %shard_map.91 = (bf16[256,2560]{1,0:T(8,128)(2,1)}, bf16[256,6]{1,0:T(8,128)(2,1)S(1)}) custom-call(s32[256,6]{1,0:T(8,128)S(1)} %copy.11.routes_ref, bf16[256,6]{1,0:T(8,128)(2,1)S(1)} %copy.12.gates_ref, bf16[256,256]{1,0:T(8,128)(2,1)S(1)} %copy-done.11, bf16[8,32,2688]{2,1,0:T(8,128)(2,1)S(1)} %all-to-all-done.1.back_ref), custom_call_target="tpu_custom_call" | custom-call | flops 335544320 | bytes 2621440 | tf_op jit(solution)/shard_map/pallas_call | solution.py:312
  (70 shorter events, 21.0 us)
Async XLA Ops:
  2.2 10.0 %collective-permute-start = (bf16[3,40,768]{2,1,0:T(8,128)(2,1)}, bf16[3,40,768]{2,1,0:T(8,128)(2,1)S(1)}, u32[]{:S(2)}, u32[]{:S(2)}) collective-permute-start(bf16[3,40,768]{2,1,0:T(8,128)(2,1)} %shard_map.87), channel_id=1, source_target_pairs={{8,0},{4,12},{9,1},{5,13},{10,2},{6,14},{11,3},{7,15},{24,16},{20,... | collective-permute-start | bytes 552968 | tf_op jit(solution)/shard_map/ppermute | solution.py:254
  11.0 21.9 %copy-start.13 = (s32[256,6]{0,1:T(8,128)S(1)}, s32[256,6]{0,1:T(8,128)}, u32[]{:S(2)}) copy-start(s32[256,6]{0,1:T(8,128)} %param.9) | copy-start | bytes 18436
  11.0 22.1 %copy-start = (bf16[256,2560]{1,0:T(8,128)(2,1)S(1)}, bf16[256,2560]{1,0:T(8,128)(2,1)}, u32[]{:S(2)}) copy-start(bf16[256,2560]{1,0:T(8,128)(2,1)} %tok_ref.1) | copy-start | bytes 3932164
  11.0 22.1 %copy-start.1 = (bf16[256,2560]{1,0:T(8,128)(2,1)S(1)}, bf16[256,2560]{1,0:T(8,128)(2,1)}, u32[]{:S(2)}) copy-start(bf16[256,2560]{1,0:T(8,128)(2,1)} %cot_ref.1) | copy-start | bytes 3932164
  13.9 12.7 %collective-permute-start.4 = (bf16[112,768]{1,0:T(8,128)(2,1)}, bf16[112,768]{1,0:T(8,128)(2,1)}, u32[]{:S(2)}, u32[]{:S(2)}) collective-permute-start(bf16[112,768]{1,0:T(8,128)(2,1)} %slice.9), channel_id=1, source_target_pairs={{0,68},{64,4},{12,8},{76,72},{1,69},{65,5},{13,9},{77,73},{2,70},{... | collective-permute-start | bytes 516104 | tf_op jit(solution)/shard_map/ppermute | solution.py:264
  15.3 23.4 %collective-permute-start.1 = (bf16[128,768]{1,0:T(8,128)(2,1)S(1)}, bf16[128,768]{1,0:T(8,128)(2,1)S(1)}, u32[]{:S(2)}, u32[]{:S(2)}) collective-permute-start(bf16[128,768]{1,0:T(8,128)(2,1)S(1)} %slice.8), channel_id=1, source_target_pairs={{0,4},{64,68},{12,72},{76,8},{1,5},{65,69},{13,73},{77,9},{2,6},{6... | collective-permute-start | bytes 589832 | tf_op jit(solution)/shard_map/ppermute | solution.py:264
  16.6 30.0 %collective-permute-start.6 = (bf16[112,768]{1,0:T(8,128)(2,1)}, bf16[112,768]{1,0:T(8,128)(2,1)}, u32[]{:S(2)}, u32[]{:S(2)}) collective-permute-start(bf16[112,768]{1,0:T(8,128)(2,1)} %slice.9), channel_id=1, source_target_pairs={{0,4},{64,68},{12,72},{76,8},{1,5},{65,69},{13,73},{77,9},{2,6},{6... | collective-permute-start | bytes 516104 | tf_op jit(solution)/shard_map/ppermute | solution.py:264
  26.6 19.9 %collective-permute-start.5 = (bf16[112,768]{1,0:T(8,128)(2,1)}, bf16[112,768]{1,0:T(8,128)(2,1)}, u32[]{:S(2)}, u32[]{:S(2)}) collective-permute-start(bf16[112,768]{1,0:T(8,128)(2,1)} %collective-permute-done.4), channel_id=1, source_target_pairs={{4,0},{68,64},{8,76},{72,12},{5,1},{69,65},{9,77},{73,13},{6,2},{7... | collective-permute-start | bytes 516104 | tf_op jit(solution)/shard_map/ppermute | solution.py:264
  37.3 11.6 %collective-permute-start.3 = (bf16[128,768]{1,0:T(8,128)(2,1)S(1)}, bf16[128,768]{1,0:T(8,128)(2,1)S(1)}, u32[]{:S(2)}, u32[]{:S(2)}) collective-permute-start(bf16[128,768]{1,0:T(8,128)(2,1)S(1)} %slice.8), channel_id=1, source_target_pairs={{0,68},{64,4},{12,8},{76,72},{1,69},{65,5},{13,9},{77,73},{2,70},{... | collective-permute-start | bytes 589832 | tf_op jit(solution)/shard_map/ppermute | solution.py:264
  38.6 13.0 %collective-permute-start.2 = (bf16[128,768]{1,0:T(8,128)(2,1)S(1)}, bf16[128,768]{1,0:T(8,128)(2,1)S(1)}, u32[]{:S(2)}, u32[]{:S(2)}) collective-permute-start(bf16[128,768]{1,0:T(8,128)(2,1)S(1)} %collective-permute-done.1), channel_id=1, source_target_pairs={{4,64},{68,0},{8,12},{72,76},{5,65},{69,1},{9,13},{73,77},{6,66},{... | collective-permute-start | bytes 589832 | tf_op jit(solution)/shard_map/ppermute | solution.py:264
  51.8 20.9 %copy-start.12 = (bf16[480,768]{1,0:T(8,128)(2,1)}, bf16[480,768]{1,0:T(8,128)(2,1)S(1)}, u32[]{:S(2)}) copy-start(bf16[480,768]{1,0:T(8,128)(2,1)S(1)} %pad_maximum_fusion.refs_0_) | copy-start | bytes 2211844
  51.8 111.9 %all-to-all-start = ((bf16[8,64,2560]{2,1,0:T(8,128)(2,1)}), bf16[8,64,2560]{2,1,0:T(8,128)(2,1)}, u32[]{:S(2)}, u32[]{:S(2)}) async-start(bf16[8,64,2560]{2,1,0:T(8,128)(2,1)} %get-tuple-element.16), calls=%async_computation | async-start | bytes 5242880 | tf_op jit(solution)/shard_map/all_to_all | solution.py:295
  63.7 20.1 %collective-permute-start.10 = (bf16[480,768]{1,0:T(8,128)(2,1)S(1)}, bf16[480,768]{1,0:T(8,128)(2,1)S(1)}, u32[]{:S(2)}, u32[]{:S(2)}) collective-permute-start(bf16[480,768]{1,0:T(8,128)(2,1)S(1)} %pad_maximum_fusion.refs_0_), channel_id=1, source_target_pairs={{0,384},{128,0},{256,128},{384,256},{1,385},{129,1},{257,129},{385... | collective-permute-start | bytes 2211848 | tf_op jit(solution)/shard_map/ppermute | solution.py:164
  66.1 20.9 %collective-permute-start.9 = (bf16[480,768]{1,0:T(8,128)(2,1)S(1)}, bf16[480,768]{1,0:T(8,128)(2,1)S(1)}, u32[]{:S(2)}, u32[]{:S(2)}) collective-permute-start(bf16[480,768]{1,0:T(8,128)(2,1)S(1)} %pad_maximum_fusion.refs_0_), channel_id=1, source_target_pairs={{0,128},{128,256},{256,384},{384,0},{1,129},{129,257},{257,385},{3... | collective-permute-start | bytes 2211848 | tf_op jit(solution)/shard_map/ppermute | solution.py:164
  69.0 19.5 %collective-permute-start.8 = (bf16[480,768]{1,0:T(8,128)(2,1)S(1)}, bf16[480,768]{1,0:T(8,128)(2,1)S(1)}, u32[]{:S(2)}, u32[]{:S(2)}) collective-permute-start(bf16[480,768]{1,0:T(8,128)(2,1)S(1)} %pad_maximum_fusion.refs_0_), channel_id=1, source_target_pairs={{0,48},{16,0},{32,16},{48,32},{1,49},{17,1},{33,17},{49,33},{2,50}... | collective-permute-start | bytes 2211848 | tf_op jit(solution)/shard_map/ppermute | solution.py:164
  72.7 20.6 %collective-permute-start.7 = (bf16[480,768]{1,0:T(8,128)(2,1)S(1)}, bf16[480,768]{1,0:T(8,128)(2,1)S(1)}, u32[]{:S(2)}, u32[]{:S(2)}) collective-permute-start(bf16[480,768]{1,0:T(8,128)(2,1)S(1)} %pad_maximum_fusion.refs_0_), channel_id=1, source_target_pairs={{0,16},{16,32},{32,48},{48,0},{1,17},{17,33},{33,49},{49,1},{2,18}... | collective-permute-start | bytes 2211848 | tf_op jit(solution)/shard_map/ppermute | solution.py:164
  83.8 11.4 %copy-start.6 = (bf16[480,768]{1,0:T(8,128)(2,1)}, bf16[480,768]{1,0:T(8,128)(2,1)S(1)}, u32[]{:S(2)}) copy-start(bf16[480,768]{1,0:T(8,128)(2,1)S(1)} %collective-permute-done.10.refs_3_.refs_4_) | copy-start | bytes 2211844
  87.0 8.1 %copy-start.7 = (bf16[480,768]{1,0:T(8,128)(2,1)}, bf16[480,768]{1,0:T(8,128)(2,1)S(1)}, u32[]{:S(2)}) copy-start(bf16[480,768]{1,0:T(8,128)(2,1)S(1)} %collective-permute-done.9.refs_2_.refs_3_) | copy-start | bytes 2211844
  95.2 27.6 %collective-permute-start.11 = (bf16[720,768]{1,0:T(8,128)(2,1)S(1)}, bf16[720,768]{1,0:T(8,128)(2,1)S(1)}, u32[]{:S(2)}, u32[]{:S(2)}) collective-permute-start(bf16[720,768]{1,0:T(8,128)(2,1)S(1)} %get-tuple-element.18), channel_id=1, source_target_pairs={{0,16},{16,32},{32,48},{48,0},{1,17},{17,33},{33,49},{49,1},{2,18}... | collective-permute-start | bytes 3317768 | tf_op jit(solution)/shard_map/ppermute | solution.py:164
  97.1 26.5 %collective-permute-start.12 = (bf16[720,768]{1,0:T(8,128)(2,1)S(1)}, bf16[720,768]{1,0:T(8,128)(2,1)S(1)}, u32[]{:S(2)}, u32[]{:S(2)}) collective-permute-start(bf16[720,768]{1,0:T(8,128)(2,1)S(1)} %get-tuple-element.19), channel_id=1, source_target_pairs={{0,48},{16,0},{32,16},{48,32},{1,49},{17,1},{33,17},{49,33},{2,50}... | collective-permute-start | bytes 3317768 | tf_op jit(solution)/shard_map/ppermute | solution.py:164
  101.7 27.0 %collective-permute-start.13 = (bf16[720,768]{1,0:T(8,128)(2,1)S(1)}, bf16[720,768]{1,0:T(8,128)(2,1)S(1)}, u32[]{:S(2)}, u32[]{:S(2)}) collective-permute-start(bf16[720,768]{1,0:T(8,128)(2,1)S(1)} %get-tuple-element.20), channel_id=1, source_target_pairs={{0,128},{128,256},{256,384},{384,0},{1,129},{129,257},{257,385},{3... | collective-permute-start | bytes 3317768 | tf_op jit(solution)/shard_map/ppermute | solution.py:164
  103.6 26.0 %collective-permute-start.14 = (bf16[720,768]{1,0:T(8,128)(2,1)S(1)}, bf16[720,768]{1,0:T(8,128)(2,1)S(1)}, u32[]{:S(2)}, u32[]{:S(2)}) collective-permute-start(bf16[720,768]{1,0:T(8,128)(2,1)S(1)} %get-tuple-element.21), channel_id=1, source_target_pairs={{0,384},{128,0},{256,128},{384,256},{1,385},{129,1},{257,129},{385... | collective-permute-start | bytes 3317768 | tf_op jit(solution)/shard_map/ppermute | solution.py:164
  122.7 8.1 %copy-start.2 = (bf16[720,768]{1,0:T(8,128)(2,1)}, bf16[720,768]{1,0:T(8,128)(2,1)S(1)}, u32[]{:S(2)}) copy-start(bf16[720,768]{1,0:T(8,128)(2,1)S(1)} %collective-permute-done.11.refs_0_.refs_5_) | copy-start | bytes 3317764
  130.9 14.7 %collective-permute-start.19 = (bf16[240,768]{1,0:T(8,128)(2,1)S(1)}, bf16[240,768]{1,0:T(8,128)(2,1)S(1)}, u32[]{:S(2)}, u32[]{:S(2)}) collective-permute-start(bf16[240,768]{1,0:T(8,128)(2,1)S(1)} %get-tuple-element.24), channel_id=1, source_target_pairs={{0,144},{16,160},{32,176},{48,128},{128,272},{144,288},{160,304},{... | collective-permute-start | bytes 1105928 | tf_op jit(solution)/shard_map/ppermute | solution.py:169
  132.9 30.7 %collective-permute-start.16 = (bf16[480,768]{1,0:T(8,128)(2,1)}, bf16[480,768]{1,0:T(8,128)(2,1)S(1)}, u32[]{:S(2)}, u32[]{:S(2)}) collective-permute-start(bf16[480,768]{1,0:T(8,128)(2,1)} %get-tuple-element.22), channel_id=1, source_target_pairs={{0,48},{16,0},{32,16},{48,32},{1,49},{17,1},{33,17},{49,33},{2,50}... | collective-permute-start | bytes 2211848 | tf_op jit(solution)/shard_map/ppermute | solution.py:164
  138.4 25.2 %collective-permute-start.15 = (bf16[480,768]{1,0:T(8,128)(2,1)}, bf16[480,768]{1,0:T(8,128)(2,1)S(1)}, u32[]{:S(2)}, u32[]{:S(2)}) collective-permute-start(bf16[480,768]{1,0:T(8,128)(2,1)} %get-tuple-element.22), channel_id=1, source_target_pairs={{0,16},{16,32},{32,48},{48,0},{1,17},{17,33},{33,49},{49,1},{2,18}... | collective-permute-start | bytes 2211848 | tf_op jit(solution)/shard_map/ppermute | solution.py:164
  140.3 23.3 %collective-permute-start.18 = (bf16[480,768]{1,0:T(8,128)(2,1)S(1)}, bf16[480,768]{1,0:T(8,128)(2,1)S(1)}, u32[]{:S(2)}, u32[]{:S(2)}) collective-permute-start(bf16[480,768]{1,0:T(8,128)(2,1)S(1)} %get-tuple-element.23), channel_id=1, source_target_pairs={{0,384},{128,0},{256,128},{384,256},{1,385},{129,1},{257,129},{385... | collective-permute-start | bytes 2211848 | tf_op jit(solution)/shard_map/ppermute | solution.py:164
  143.7 20.0 %collective-permute-start.17 = (bf16[480,768]{1,0:T(8,128)(2,1)S(1)}, bf16[480,768]{1,0:T(8,128)(2,1)}, u32[]{:S(2)}, u32[]{:S(2)}) collective-permute-start(bf16[480,768]{1,0:T(8,128)(2,1)S(1)} %get-tuple-element.23), channel_id=1, source_target_pairs={{0,128},{128,256},{256,384},{384,0},{1,129},{129,257},{257,385},{3... | collective-permute-start | bytes 2211848 | tf_op jit(solution)/shard_map/ppermute | solution.py:164
  146.4 17.2 %collective-permute-start.20 = (bf16[240,768]{1,0:T(8,128)(2,1)S(1)}, bf16[240,768]{1,0:T(8,128)(2,1)}, u32[]{:S(2)}, u32[]{:S(2)}) collective-permute-start(bf16[240,768]{1,0:T(8,128)(2,1)S(1)} %get-tuple-element.25), channel_id=1, source_target_pairs={{0,432},{16,384},{32,400},{48,416},{128,48},{144,0},{160,16},{176,... | collective-permute-start | bytes 1105928 | tf_op jit(solution)/shard_map/ppermute | solution.py:169
  179.2 8.8 %copy-start.14 = (bf16[256,6]{0,1:T(8,128)(2,1)S(1)}, bf16[256,6]{0,1:T(8,128)(2,1)}, u32[]{:S(2)}) copy-start(bf16[256,6]{0,1:T(8,128)(2,1)} %param.10) | copy-start | bytes 9220
  179.2 41.7 %copy-start.11 = (bf16[256,256]{1,0:T(8,128)(2,1)S(1)}, bf16[256,256]{1,0:T(8,128)(2,1)}, u32[]{:S(2)}) copy-start(bf16[256,256]{1,0:T(8,128)(2,1)} %copy-done.10) | copy-start | bytes 393220
  179.2 41.7 %all-to-all-start.1 = ((bf16[8,32,2688]{2,1,0:T(8,128)(2,1)}), bf16[8,32,2688]{2,1,0:T(8,128)(2,1)S(1)}, u32[]{:S(2)}, u32[]{:S(2)}) async-start(bf16[8,32,2688]{2,1,0:T(8,128)(2,1)} %shard_map.90), calls=%async_computation.1 | async-start | bytes 2752512 | tf_op jit(solution)/shard_map/all_to_all | solution.py:310
  (10 other events, 24.1 us)

commit v3 on v2

--- a/solution.py
+++ b/solution.py
@@ -70,16 +70,44 @@
         out_ref[m] = ref[0]
 
 
+def pair_kernel(first_ref, shard_ref, other_ref, top_ref, bottom_ref):
+    swap = first_ref[0] == 0
+    for m in range(3):
+        mine, theirs = shard_ref[m], other_ref[m]
+        for k in range(2):
+            part = jnp.where(swap == (k == 0), mine, theirs)
+            row = 80 * m + 40 * k
+            cut = min(max(SPLIT - row, 0), 40)
+            if cut:
+                top_ref[row : row + cut] = part[:cut]
+            if cut < 40:
+                bottom_ref[row + cut - SPLIT : row + 40 - SPLIT] = part[cut:]
+
+
+def block_kernel(state_ref, top, bottom, low0, low1, high0, high1, far0, far1, out_ref):
+    source, order = state_ref[0] == 1, state_ref[1] == 0
+    row = 0
+    for z in range(2):
+        for mine, low, high, far in ((top, low0, high0, far0), (bottom, low1, high1, far1)):
+            count = mine.shape[0]
+            first = jnp.where(source, mine[...], low[...])
+            second = jnp.where(source, far[...], high[...])
+            pick = order if z == 0 else jnp.logical_not(order)
+            out_ref[row : row + count] = jnp.where(pick, first, second)
+            row += count
+
+
 def expert_kernel(pieces, where_ref, rows_ref, *refs):
     sources = refs[: len(refs) - 9]
     out_ref = refs[-9]
     gate_w, up_w, down_w, grad_a, grad_b, pre_g, pre_u, sems = refs[-8:]
     weights = (gate_w, up_w, down_w)
-    my_x, my_y = where_ref[0], where_ref[1]
+    my_x, my_y, core = where_ref[0], where_ref[1], where_ref[2]
 
     copies = ([], [], [])
-    for number, row, block, dx, dy in pieces:
-        xx, yy = lax.rem(my_x + dx, 4), lax.rem(my_y + dy, 4)
+    for number, row, block, far, near in pieces:
+        xx = lax.rem(my_x + jnp.where(core == 0, far, near), 4)
+        yy = lax.rem(my_y + jnp.where(core == 0, near, far), 4)
         target = pl.multiple_of(((xx * 2 + block) * 4 + yy) * 80, 16)
         for m in range(3):
             copies[m].append(
@@ -160,15 +188,6 @@
 ANY = pl.BlockSpec(memory_space=pl.ANY)
 
 
-def shift(v, axis, by):
-    return lax.ppermute(v, axis, [(i, (i + by) % 4) for i in range(4)])
-
-
-def diagonal(v, by):
-    pairs = [(i * 4 + j, (i + by) % 4 * 4 + (j + by) % 4) for i in range(4) for j in range(4)]
-    return lax.ppermute(v, ("x", "y"), pairs)
-
-
 def join_kernel(plan, inputs, *refs):
     sources, targets, sem = refs[:inputs], refs[inputs:-1], refs[-1]
     copies = [
@@ -197,44 +216,36 @@
     )(*arrays)
 
 
+def shift(v, far, by):
+    pairs = []
+    for x in range(4):
+        for y in range(4):
+            for c in range(2):
+                along_x = (c == 0) == far
+                tx, ty = ((x + by) % 4, y) if along_x else (x, (y + by) % 4)
+                pairs.append(((x * 4 + y) * 2 + c, (tx * 4 + ty) * 2 + c))
+    return lax.ppermute(v, ("x", "y", "c"), pairs)
+
+
 def torus_gather(own):
     full = own.shape[0]
     half = full // 2
-    y0, y1 = shift(own, "y", 1), shift(own, "y", -1)
-    x0, x1 = shift(own, "x", 1), shift(own, "x", -1)
-    ya, yb, xa, xb = join(
-        [full + half] * 4,
-        (
-            (2, 0, full, 0, 0), (0, 0, half, 0, full),
-            (3, 0, full, 1, 0), (1, half, half, 1, full),
-            (1, 0, full, 2, 0), (2, 0, half, 2, full),
-            (0, 0, full, 3, 0), (3, half, half, 3, full),
-        ),
-        y0, y1, x0, x1,
-    )
-    ya, yb = shift(ya, "y", 1), shift(yb, "y", -1)
-    xa, xb = shift(xa, "x", 1), shift(xb, "x", -1)
-    y_far, x_far, c0, c1 = join(
-        [full, full, half, half],
-        (
-            (0, full, half, 0, 0), (1, full, half, 0, half),
-            (2, full, half, 1, 0), (3, full, half, 1, half),
-            (0, 0, half, 2, 0), (1, half, half, 3, 0),
-        ),
-        ya, yb, xa, xb,
-    )
-    yc, yd = shift(x_far, "y", 1), shift(x_far, "y", -1)
-    xc, xd = shift(y_far, "x", 1), shift(y_far, "x", -1)
-    c0, c1 = diagonal(c0, 1), diagonal(c1, -1)
-    arrays = (own, y0, y1, x0, x1, ya, yb, xa, xb, yc, yd, xc, xd, c0, c1)
-    places = (
-        (0, 0), (0, 3), (0, 1), (3, 0), (1, 0), (3, 3), (1, 1), (3, 1), (1, 3),
-        (2, 3), (2, 1), (3, 2), (1, 2),
-    )
-    pieces = [(n, h * half, h, dx, dy) for n, (dx, dy) in enumerate(places) for h in range(2)]
-    pieces += [(5, full, 0, 0, 2), (6, full, 1, 0, 2)]
-    pieces += [(7, full, 0, 2, 0), (8, full, 1, 2, 0)]
-    pieces += [(13, 0, 0, 2, 2), (14, 0, 1, 2, 2)]
+    pair = ((0, 0, full, 0, 0), (1, 0, full, 0, full))
+    low, high = shift(own, False, 1), shift(own, False, -1)
+    opposite = shift(low, False, 1)
+    (early,) = join([2 * full], pair, own, low)
+    early_low, early_high = shift(early, True, 1), shift(early, True, -1)
+    (late,) = join([2 * full], pair, high, opposite)
+    late_low, late_high = shift(late, True, 1), shift(late, True, -1)
+    early_far, late_far = shift(early_low, True, 1), shift(late_high, True, -1)
+    arrays = (early, late, early_low, late_low, early_high, late_high, early_far, late_far)
+    fars = (0, 0, 3, 3, 1, 1, 2, 2)
+    pieces = [
+        (n, i * full + h * half, h, fars[n], (0, 3, 1, 2)[n % 2 * 2 + i])
+        for n in range(8)
+        for i in range(2)
+        for h in range(2)
+    ]
     return arrays, pieces
 
 
@@ -250,11 +261,20 @@
         out_shape=jax.ShapeDtypeStruct((3, *gate_proj.shape[1:]), BF),
         in_specs=[VM] * 3,
         out_specs=VM,
+        compiler_params=params(4),
     )(gate_proj, up_proj, down_proj)
     other = lax.ppermute(shard, ("c", "zq"), [(2, 0), (1, 3)])
-    pair = jnp.stack([jnp.where(ic == 0, shard, other), jnp.where(ic == 0, other, shard)], axis=1)
-    pair = pair.reshape(240, hidden_width)
-    top, bottom = pair[:SPLIT], pair[SPLIT:]
+    smem = pl.BlockSpec(memory_space=pltpu.SMEM)
+    top, bottom = pl.pallas_call(
+        pair_kernel,
+        out_shape=(
+            jax.ShapeDtypeStruct((SPLIT, hidden_width), BF),
+            jax.ShapeDtypeStruct((240 - SPLIT, hidden_width), BF),
+        ),
+        in_specs=[smem, VM, VM],
+        out_specs=(VM, VM),
+        compiler_params=params(4),
+    )(ic.astype(jnp.int32)[None], shard, other)
 
     def at(c, p):
         return (p // 2 * 2 + c) * 2 + p % 2
@@ -267,17 +287,16 @@
     low1, high0 = zmove(bottom, True, 1), zmove(top, True, -1)
     far0, far1 = zmove(low0, False, 1), zmove(high1, False, -1)
     source = ic == zq
-    swapped = (ring == 0) | (ring == 3)
-
-    def pick(mine, far, low, high):
-        return (
-            jnp.where(source, jnp.where(zh == 0, mine, far), jnp.where(swapped, high, low)),
-            jnp.where(source, jnp.where(zh == 0, far, mine), jnp.where(swapped, low, high)),
-        )
-
-    (a0, b0), (a1, b1) = pick(top, far0, low0, high0), pick(bottom, far1, low1, high1)
-    block = jnp.concatenate([a0, a1, b0, b1], axis=0)
-
+    ordered = jnp.where(source, zh == 0, (ring == 1) | (ring == 2))
+    block = pl.pallas_call(
+        block_kernel,
+        out_shape=jax.ShapeDtypeStruct((480, hidden_width), BF),
+        in_specs=[smem] + [VM] * 8,
+        out_specs=VM,
+        compiler_params=params(8),
+    )(jnp.stack([source, jnp.logical_not(ordered)]).astype(jnp.int32), top, bottom, low0, low1, high0, high1, far0, far1)
+
+    (routes_later, _, _) = lax.optimization_barrier((routes, low0, high1))
     payload, sel = pl.pallas_call(
         dispatch_kernel,
         out_shape=(
@@ -288,7 +307,7 @@
         out_specs=(VM, VM),
         compiler_params=params(),
         cost_estimate=cost(2 * 256 * 512 * width, 8 * 256 * width),
-    )(routes, tokens_in, cotangent)
+    )(routes_later, tokens_in, cotangent)
 
     payload, block = lax.optimization_barrier((payload, block))
     arrays, pieces = torus_gather(block)
@@ -297,7 +316,7 @@
     back = pl.pallas_call(
         functools.partial(expert_kernel, pieces),
         out_shape=jax.ShapeDtypeStruct((8, 32, width + PAD), BF),
-        in_specs=[pl.BlockSpec(memory_space=pltpu.SMEM), VM] + [ANY] * len(arrays),
+        in_specs=[smem, VM] + [ANY] * len(arrays),
         out_specs=VM,
         scratch_shapes=[pltpu.VMEM((width, hidden_width), BF)] * 3
         + [pltpu.VMEM((256, hidden_width), BF)] * 2
@@ -305,7 +324,7 @@
         + [pltpu.SemaphoreType.DMA((3,))],
         compiler_params=params(56),
         cost_estimate=cost(10 * 256 * width * hidden_width, 6 * width * hidden_width),
-    )(jnp.stack([ix, iy]).astype(jnp.int32), rows, *arrays)
+    )(jnp.stack([ix, iy, ic]).astype(jnp.int32), rows, *arrays)
 
     home = lax.all_to_all(back, ("c", "zr"), split_axis=0, concat_axis=0, tiled=True)
 

time: 226 us -> 204 us (0.903)
  starting transfers between devices: 94.2 us -> 76.4 us
  local copies, waits for them, and re-layouts: 4.41 us -> 6.92 us
    ppermute x14 -> x9, starting transfers between devices: 45.4 us -> 27.2 us  [shift(): return lax.ppermute(v, ('x', 'y', 'c'), pairs)]
    ppermute x6, waiting for transfers between devices: 12.7 us -> 6.69 us  [zmove(): return lax.ppermute(v, ('zh', 'c', 'zq'), pairs)]
    all_to_all x1, starting transfers between devices: 11.9 us -> 6.31 us  [on_device(): lax.all_to_all(payload, ('c', 'zr'), split_axis=0, concat_axis=0, tiled=T...]
    ppermute x14 -> x9, waiting for transfers between devices: 49.7 us -> 55.1 us  [shift(): return lax.ppermute(v, ('x', 'y', 'c'), pairs)]
    ppermute x6, starting transfers between devices: 19.4 us -> 23.4 us  [zmove(): return lax.ppermute(v, ('zh', 'c', 'zq'), pairs)]
    unnamed x40 -> x20, local copies, waits for them, and re-layouts: 3 us -> 5.4 us
  transfers between devices with their start and end apart: 23 -> 18, of which waited for: 14 -> 10; matrix products, arithmetic and copies ran while one was open for 1% -> 1% of each run, Pallas kernels for 3% -> 3%
where the time goes in v3:
time: 204 us; the launch traced here: 203 us
  waiting for transfers between devices  95.5 us (47%)
  starting transfers between devices  76.4 us (37%)
  Pallas kernels  22.8 us (11%)
  local copies, waits for them, and re-layouts  6.92 us (3%)
    ppermute x9, waiting for transfers between devices, shift(): return lax.ppermute(v, ('x', 'y', 'c'), pairs)  55.1 us
    all_to_all x1, waiting for transfers between devices, on_device(): lax.all_to_all(back, ('c', 'zr'), split_axis=0, concat_axis=0, tiled=True)  32.6 us
    ppermute x9, starting transfers between devices, shift(): return lax.ppermute(v, ('x', 'y', 'c'), pairs)  27.2 us
    ppermute x6, starting transfers between devices, zmove(): return lax.ppermute(v, ('zh', 'c', 'zq'), pairs)  23.4 us
    pallas_call x1, Pallas kernels, on_device(): pl.pallas_call(functools.partial(expert_kernel, pieces), out_shape=jax.Sh...  14.3 us
    all_to_all x1, starting transfers between devices, on_device(): lax.all_to_all(back, ('c', 'zr'), split_axis=0, concat_axis=0, tiled=True)  10.6 us
    ppermute x1, starting transfers between devices, on_device(): other = lax.ppermute(shard, ('c', 'zq'), [(2, 0), (1, 3)])  8.79 us
    ppermute x6, waiting for transfers between devices, zmove(): return lax.ppermute(v, ('zh', 'c', 'zq'), pairs)  6.69 us
  transfers between devices with their start and end apart: 18, of which 10 were waited for; matrix products, arithmetic and copies ran while one was open for 1% of the time, Pallas kernels for 3%

profile of v3, /device:TPU:1, one launch (start us, length us, event | category | flops | bytes accessed | tf_op | source)
XLA Modules:
  0.0 203.2 jit_solution(6268099427706915177)
XLA Ops:
  3.1 8.8 %collective-permute-start = (bf16[3,40,768]{2,1,0:T(8,128)(2,1)S(1)}, bf16[3,40,768]{2,1,0:T(8,128)(2,1)S(1)}, u32[]{:S(2)}, u32[]{:S(2)}) collective-permute-start(bf16[3,40,768]{2,1,0:T(8,128)(2,1)S(1)} %shard_map.86.shard_ref), channel_id=1, source_target_pairs={{8,0},{4,12},{9,1},{5,13},{10,2},{6,14},{11,3},{7,15},{24,16},{20,... | collective-permute-start | bytes 552968 | tf_op jit(solution)/shard_map/ppermute | solution.py:266
  13.0 1.3 collective-permute-start.1
  14.3 1.3 collective-permute-start.2
  15.6 1.3 collective-permute-start.4
  16.9 6.7 %collective-permute-done.1.low0 = bf16[128,768]{1,0:T(8,128)(2,1)S(1)} collective-permute-done((bf16[128,768]{1,0:T(8,128)(2,1)S(1)}, bf16[128,768]{1,0:T(8,128)(2,1)S(1)}, u32[]{:S(2)}, u32[]{:S(2)}) %collective-permute-start.1) | collective-permute-done | bytes 196640 | tf_op jit(solution)/shard_map/ppermute | solution.py:284
  23.6 10.4 %collective-permute-start.5 = (bf16[128,768]{1,0:T(8,128)(2,1)S(1)}, bf16[128,768]{1,0:T(8,128)(2,1)S(1)}, u32[]{:S(2)}, u32[]{:S(2)}) collective-permute-start(bf16[128,768]{1,0:T(8,128)(2,1)S(1)} %collective-permute-done.1.low0), channel_id=1, source_target_pairs={{4,64},{68,0},{8,12},{72,76},{5,65},{69,1},{9,13},{73,77},{6,66},{... | collective-permute-start | bytes 589832 | tf_op jit(solution)/shard_map/ppermute | solution.py:284
  34.0 1.3 collective-permute-start.3
  35.3 7.9 %collective-permute-start.6 = (bf16[112,768]{1,0:T(8,128)(2,1)S(1)}, bf16[112,768]{1,0:T(8,128)(2,1)S(1)}, u32[]{:S(2)}, u32[]{:S(2)}) collective-permute-start(bf16[112,768]{1,0:T(8,128)(2,1)S(1)} %collective-permute-done.2.high1), channel_id=1, source_target_pairs={{4,0},{68,64},{8,76},{72,12},{5,1},{69,65},{9,77},{73,13},{6,2},{7... | collective-permute-start | bytes 516104 | tf_op jit(solution)/shard_map/ppermute | solution.py:284
  44.1 1.3 copy-done.1
  45.5 1.3 copy-done.2
  46.8 3.6 %shard_map.88 = (bf16[8,64,2560]{2,1,0:T(8,128)(2,1)}, bf16[256,256]{1,0:T(8,128)(2,1)S(1)}) custom-call(s32[256,6]{1,0:T(8,128)S(1)} %copy.9.routes_ref, bf16[256,2560]{1,0:T(8,128)(2,1)S(1)} %copy-done.1, bf16[256,2560]{1,0:T(8,128)(2,1)S(1)} %copy-done.2), custom_call_target="tpu_custom_call" | custom-call | flops 671088640 | bytes 5242880 | tf_op jit(solution)/shard_map/pallas_call | solution.py:300
  51.2 6.3 %all-to-all-start = ((bf16[8,64,2560]{2,1,0:T(8,128)(2,1)}), bf16[8,64,2560]{2,1,0:T(8,128)(2,1)}, u32[]{:S(2)}, u32[]{:S(2)}) async-start(bf16[8,64,2560]{2,1,0:T(8,128)(2,1)} %get-tuple-element.14), calls=%async_computation | async-start | bytes 5242880 | tf_op jit(solution)/shard_map/all_to_all | solution.py:314
  57.5 2.8 %collective-permute-start.7 = (bf16[480,768]{1,0:T(8,128)(2,1)S(1)}, bf16[480,768]{1,0:T(8,128)(2,1)S(1)}, u32[]{:S(2)}, u32[]{:S(2)}) collective-permute-start(bf16[480,768]{1,0:T(8,128)(2,1)S(1)} %shard_map.89.refs_0_), channel_id=1, source_target_pairs={{0,16},{8,136},{16,32},{24,152},{32,48},{40,168},{48,0},{56,184},{... | collective-permute-start | bytes 2211848 | tf_op jit(solution)/shard_map/ppermute | solution.py:227
  60.2 3.7 %collective-permute-start.8 = (bf16[480,768]{1,0:T(8,128)(2,1)S(1)}, bf16[480,768]{1,0:T(8,128)(2,1)S(1)}, u32[]{:S(2)}, u32[]{:S(2)}) collective-permute-start(bf16[480,768]{1,0:T(8,128)(2,1)S(1)} %shard_map.89.refs_0_), channel_id=1, source_target_pairs={{0,48},{8,392},{16,0},{24,408},{32,16},{40,424},{48,32},{56,440},{... | collective-permute-start | bytes 2211848 | tf_op jit(solution)/shard_map/ppermute | solution.py:227
  64.0 7.2 %collective-permute-done.7.refs_1_ = bf16[480,768]{1,0:T(8,128)(2,1)S(1)} collective-permute-done((bf16[480,768]{1,0:T(8,128)(2,1)S(1)}, bf16[480,768]{1,0:T(8,128)(2,1)S(1)}, u32[]{:S(2)}, u32[]{:S(2)}) %collective-permute-start.7) | collective-permute-done | bytes 737312 | tf_op jit(solution)/shard_map/ppermute | solution.py:227
  71.2 1.9 collective-permute-start.9
  73.7 3.0 %collective-permute-start.10 = (bf16[960,768]{1,0:T(8,128)(2,1)S(1)}, bf16[960,768]{1,0:T(8,128)(2,1)}, u32[]{:S(2)}, u32[]{:S(2)}) collective-permute-start(bf16[960,768]{1,0:T(8,128)(2,1)S(1)} %shard_map.90.refs_0_), channel_id=1, source_target_pairs={{0,128},{8,24},{16,144},{24,40},{32,160},{40,56},{48,176},{56,8},{... | collective-permute-start | bytes 4423688 | tf_op jit(solution)/shard_map/ppermute | solution.py:227
  76.7 12.1 %collective-permute-done.9.refs_1_ = bf16[480,768]{1,0:T(8,128)(2,1)S(1)} collective-permute-done((bf16[480,768]{1,0:T(8,128)(2,1)S(1)}, bf16[480,768]{1,0:T(8,128)(2,1)S(1)}, u32[]{:S(2)}, u32[]{:S(2)}) %collective-permute-start.9) | collective-permute-done | bytes 737312 | tf_op jit(solution)/shard_map/ppermute | solution.py:227
  90.0 3.7 %collective-permute-start.13 = (bf16[960,768]{1,0:T(8,128)(2,1)}, bf16[960,768]{1,0:T(8,128)(2,1)S(1)}, u32[]{:S(2)}, u32[]{:S(2)}) collective-permute-start(bf16[960,768]{1,0:T(8,128)(2,1)} %shard_map.91.refs_1_), channel_id=1, source_target_pairs={{0,384},{8,56},{16,400},{24,8},{32,416},{40,24},{48,432},{56,40},{... | collective-permute-start | bytes 4423688 | tf_op jit(solution)/shard_map/ppermute | solution.py:227
  93.7 2.4 %collective-permute-start.12 = (bf16[960,768]{1,0:T(8,128)(2,1)S(1)}, bf16[960,768]{1,0:T(8,128)(2,1)}, u32[]{:S(2)}, u32[]{:S(2)}) collective-permute-start(bf16[960,768]{1,0:T(8,128)(2,1)S(1)} %shard_map.90.refs_0_), channel_id=1, source_target_pairs={{0,384},{8,56},{16,400},{24,8},{32,416},{40,24},{48,432},{56,40},{... | collective-permute-start | bytes 4423688 | tf_op jit(solution)/shard_map/ppermute | solution.py:227
  96.2 2.9 %collective-permute-start.11 = (bf16[960,768]{1,0:T(8,128)(2,1)}, bf16[960,768]{1,0:T(8,128)(2,1)}, u32[]{:S(2)}, u32[]{:S(2)}) collective-permute-start(bf16[960,768]{1,0:T(8,128)(2,1)} %shard_map.91.refs_1_), channel_id=1, source_target_pairs={{0,128},{8,24},{16,144},{24,40},{32,160},{40,56},{48,176},{56,8},{... | collective-permute-start | bytes 4423688 | tf_op jit(solution)/shard_map/ppermute | solution.py:227
  99.0 3.2 %collective-permute-done.10.refs_2_ = bf16[960,768]{1,0:T(8,128)(2,1)} collective-permute-done((bf16[960,768]{1,0:T(8,128)(2,1)S(1)}, bf16[960,768]{1,0:T(8,128)(2,1)}, u32[]{:S(2)}, u32[]{:S(2)}) %collective-permute-start.10) | collective-permute-done | bytes 1474592 | tf_op jit(solution)/shard_map/ppermute | solution.py:227
  102.2 1.9 collective-permute-start.14
  104.1 6.6 %collective-permute-done.13.refs_5_ = bf16[960,768]{1,0:T(8,128)(2,1)S(1)} collective-permute-done((bf16[960,768]{1,0:T(8,128)(2,1)}, bf16[960,768]{1,0:T(8,128)(2,1)S(1)}, u32[]{:S(2)}, u32[]{:S(2)}) %collective-permute-start.13) | collective-permute-done | bytes 1474592 | tf_op jit(solution)/shard_map/ppermute | solution.py:227
  110.7 4.9 %collective-permute-start.15 = (bf16[960,768]{1,0:T(8,128)(2,1)S(1)}, bf16[960,768]{1,0:T(8,128)(2,1)}, u32[]{:S(2)}, u32[]{:S(2)}) collective-permute-start(bf16[960,768]{1,0:T(8,128)(2,1)S(1)} %collective-permute-done.13.refs_5_), channel_id=1, source_target_pairs={{0,384},{8,56},{16,400},{24,8},{32,416},{40,24},{48,432},{56,40},{... | collective-permute-start | bytes 4423688 | tf_op jit(solution)/shard_map/ppermute | solution.py:227
  116.2 10.3 %collective-permute-done.12.refs_4_ = bf16[960,768]{1,0:T(8,128)(2,1)} collective-permute-done((bf16[960,768]{1,0:T(8,128)(2,1)S(1)}, bf16[960,768]{1,0:T(8,128)(2,1)}, u32[]{:S(2)}, u32[]{:S(2)}) %collective-permute-start.12) | collective-permute-done | bytes 1474592 | tf_op jit(solution)/shard_map/ppermute | solution.py:227
  126.5 7.4 %collective-permute-done.14.refs_6_ = bf16[960,768]{1,0:T(8,128)(2,1)} collective-permute-done((bf16[960,768]{1,0:T(8,128)(2,1)}, bf16[960,768]{1,0:T(8,128)(2,1)}, u32[]{:S(2)}, u32[]{:S(2)}) %collective-permute-start.14) | collective-permute-done | bytes 1474592 | tf_op jit(solution)/shard_map/ppermute | solution.py:227
  133.9 8.4 %collective-permute-done.15.refs_7_ = bf16[960,768]{1,0:T(8,128)(2,1)} collective-permute-done((bf16[960,768]{1,0:T(8,128)(2,1)S(1)}, bf16[960,768]{1,0:T(8,128)(2,1)}, u32[]{:S(2)}, u32[]{:S(2)}) %collective-permute-start.15) | collective-permute-done | bytes 1474592 | tf_op jit(solution)/shard_map/ppermute | solution.py:227
  142.3 14.3 %shard_map.92 = bf16[8,32,2688]{2,1,0:T(8,128)(2,1)} custom-call(s32[3]{0:T(128)} %pad_add_fusion.where_ref, bf16[8,64,2560]{2,1,0:T(8,128)(2,1)} %all-to-all-done.rows_ref, bf16[960,768]{1,0:T(8,128)(2,1)} %copy-done, bf16[960,768]{1,0:T(8,128)(2,1)} %shard_map.91.refs_1_, bf16[960,768]{1,0:T(8,128)(2,1)} %collective-permute-done.10.refs_2_, ...), custom_call_target="tpu_custom_call" | custom-call | flops 5033164800 | bytes 11796480 | tf_op jit(solution)/shard_map/pallas_call | solution.py:316
  156.6 10.6 %all-to-all-start.1 = ((bf16[8,32,2688]{2,1,0:T(8,128)(2,1)}), bf16[8,32,2688]{2,1,0:T(8,128)(2,1)S(1)}, u32[]{:S(2)}, u32[]{:S(2)}) async-start(bf16[8,32,2688]{2,1,0:T(8,128)(2,1)} %shard_map.92), calls=%async_computation.1 | async-start | bytes 2752512 | tf_op jit(solution)/shard_map/all_to_all | solution.py:329
  167.5 32.6 %all-to-all-done.1.back_ref = bf16[8,32,2688]{2,1,0:T(8,128)(2,1)S(1)} async-done(((bf16[8,32,2688]{2,1,0:T(8,128)(2,1)}), bf16[8,32,2688]{2,1,0:T(8,128)(2,1)S(1)}, u32[]{:S(2)}, u32[]{:S(2)}) %all-to-all-start.1) | async-done | bytes 1376288 | tf_op jit(solution)/shard_map/all_to_all | solution.py:329
  200.1 2.3 %shard_map.93 = (bf16[256,2560]{1,0:T(8,128)(2,1)}, bf16[256,6]{1,0:T(8,128)(2,1)S(1)}) custom-call(s32[256,6]{1,0:T(8,128)S(1)} %copy.10.routes_ref, bf16[256,6]{1,0:T(8,128)(2,1)S(1)} %copy.11.gates_ref, bf16[256,256]{1,0:T(8,128)(2,1)S(1)} %get-tuple-element.12.sel_ref, bf16[8,32,2688]{2,1,0:T(8,128)(2,1)S(1)} %all-to-all-done.1.back_ref), custom_call_target="tpu_custom_call" | custom-call | flops 335544320 | bytes 2621440 | tf_op jit(solution)/shard_map/pallas_call | solution.py:331
  (36 shorter events, 8.6 us)
Async XLA Ops:
  0.6 0.8 copy-start.3
  1.5 0.8 copy-start.4
  2.3 0.8 copy-start.5
  3.1 9.8 %collective-permute-start = (bf16[3,40,768]{2,1,0:T(8,128)(2,1)S(1)}, bf16[3,40,768]{2,1,0:T(8,128)(2,1)S(1)}, u32[]{:S(2)}, u32[]{:S(2)}) collective-permute-start(bf16[3,40,768]{2,1,0:T(8,128)(2,1)S(1)} %shard_map.86.shard_ref), channel_id=1, source_target_pairs={{8,0},{4,12},{9,1},{5,13},{10,2},{6,14},{11,3},{7,15},{24,16},{20,... | collective-permute-start | bytes 552968 | tf_op jit(solution)/shard_map/ppermute | solution.py:266
  13.0 10.6 %collective-permute-start.1 = (bf16[128,768]{1,0:T(8,128)(2,1)S(1)}, bf16[128,768]{1,0:T(8,128)(2,1)S(1)}, u32[]{:S(2)}, u32[]{:S(2)}) collective-permute-start(bf16[128,768]{1,0:T(8,128)(2,1)S(1)} %get-tuple-element.9.top), channel_id=1, source_target_pairs={{0,4},{64,68},{12,72},{76,8},{1,5},{65,69},{13,73},{77,9},{2,6},{6... | collective-permute-start | bytes 589832 | tf_op jit(solution)/shard_map/ppermute | solution.py:284
  14.3 21.0 %collective-permute-start.2 = (bf16[112,768]{1,0:T(8,128)(2,1)S(1)}, bf16[112,768]{1,0:T(8,128)(2,1)S(1)}, u32[]{:S(2)}, u32[]{:S(2)}) collective-permute-start(bf16[112,768]{1,0:T(8,128)(2,1)S(1)} %get-tuple-element.10.bottom), channel_id=1, source_target_pairs={{0,68},{64,4},{12,8},{76,72},{1,69},{65,5},{13,9},{77,73},{2,70},{... | collective-permute-start | bytes 516104 | tf_op jit(solution)/shard_map/ppermute | solution.py:284
  15.6 34.8 %collective-permute-start.4 = (bf16[128,768]{1,0:T(8,128)(2,1)S(1)}, bf16[128,768]{1,0:T(8,128)(2,1)S(1)}, u32[]{:S(2)}, u32[]{:S(2)}) collective-permute-start(bf16[128,768]{1,0:T(8,128)(2,1)S(1)} %get-tuple-element.9.top), channel_id=1, source_target_pairs={{0,68},{64,4},{12,8},{76,72},{1,69},{65,5},{13,9},{77,73},{2,70},{... | collective-permute-start | bytes 589832 | tf_op jit(solution)/shard_map/ppermute | solution.py:284
  23.6 26.8 %collective-permute-start.5 = (bf16[128,768]{1,0:T(8,128)(2,1)S(1)}, bf16[128,768]{1,0:T(8,128)(2,1)S(1)}, u32[]{:S(2)}, u32[]{:S(2)}) collective-permute-start(bf16[128,768]{1,0:T(8,128)(2,1)S(1)} %collective-permute-done.1.low0), channel_id=1, source_target_pairs={{4,64},{68,0},{8,12},{72,76},{5,65},{69,1},{9,13},{73,77},{6,66},{... | collective-permute-start | bytes 589832 | tf_op jit(solution)/shard_map/ppermute | solution.py:284
  34.0 16.4 %collective-permute-start.3 = (bf16[112,768]{1,0:T(8,128)(2,1)S(1)}, bf16[112,768]{1,0:T(8,128)(2,1)S(1)}, u32[]{:S(2)}, u32[]{:S(2)}) collective-permute-start(bf16[112,768]{1,0:T(8,128)(2,1)S(1)} %get-tuple-element.10.bottom), channel_id=1, source_target_pairs={{0,4},{64,68},{12,72},{76,8},{1,5},{65,69},{13,73},{77,9},{2,6},{6... | collective-permute-start | bytes 516104 | tf_op jit(solution)/shard_map/ppermute | solution.py:284
  35.3 15.1 %collective-permute-start.6 = (bf16[112,768]{1,0:T(8,128)(2,1)S(1)}, bf16[112,768]{1,0:T(8,128)(2,1)S(1)}, u32[]{:S(2)}, u32[]{:S(2)}) collective-permute-start(bf16[112,768]{1,0:T(8,128)(2,1)S(1)} %collective-permute-done.2.high1), channel_id=1, source_target_pairs={{4,0},{68,64},{8,76},{72,12},{5,1},{69,65},{9,77},{73,13},{6,2},{7... | collective-permute-start | bytes 516104 | tf_op jit(solution)/shard_map/ppermute | solution.py:284
  44.1 1.3 copy-start.1
  45.4 1.3 copy-start.2
  51.2 91.1 %all-to-all-start = ((bf16[8,64,2560]{2,1,0:T(8,128)(2,1)}), bf16[8,64,2560]{2,1,0:T(8,128)(2,1)}, u32[]{:S(2)}, u32[]{:S(2)}) async-start(bf16[8,64,2560]{2,1,0:T(8,128)(2,1)} %get-tuple-element.14), calls=%async_computation | async-start | bytes 5242880 | tf_op jit(solution)/shard_map/all_to_all | solution.py:314
  57.5 13.7 %collective-permute-start.7 = (bf16[480,768]{1,0:T(8,128)(2,1)S(1)}, bf16[480,768]{1,0:T(8,128)(2,1)S(1)}, u32[]{:S(2)}, u32[]{:S(2)}) collective-permute-start(bf16[480,768]{1,0:T(8,128)(2,1)S(1)} %shard_map.89.refs_0_), channel_id=1, source_target_pairs={{0,16},{8,136},{16,32},{24,152},{32,48},{40,168},{48,0},{56,184},{... | collective-permute-start | bytes 2211848 | tf_op jit(solution)/shard_map/ppermute | solution.py:227
  60.2 16.5 %collective-permute-start.8 = (bf16[480,768]{1,0:T(8,128)(2,1)S(1)}, bf16[480,768]{1,0:T(8,128)(2,1)S(1)}, u32[]{:S(2)}, u32[]{:S(2)}) collective-permute-start(bf16[480,768]{1,0:T(8,128)(2,1)S(1)} %shard_map.89.refs_0_), channel_id=1, source_target_pairs={{0,48},{8,392},{16,0},{24,408},{32,16},{40,424},{48,32},{56,440},{... | collective-permute-start | bytes 2211848 | tf_op jit(solution)/shard_map/ppermute | solution.py:227
  71.2 17.6 %collective-permute-start.9 = (bf16[480,768]{1,0:T(8,128)(2,1)S(1)}, bf16[480,768]{1,0:T(8,128)(2,1)S(1)}, u32[]{:S(2)}, u32[]{:S(2)}) collective-permute-start(bf16[480,768]{1,0:T(8,128)(2,1)S(1)} %collective-permute-done.7.refs_1_), channel_id=1, source_target_pairs={{0,16},{8,136},{16,32},{24,152},{32,48},{40,168},{48,0},{56,184},{... | collective-permute-start | bytes 2211848 | tf_op jit(solution)/shard_map/ppermute | solution.py:227
  73.7 20.0 %copy-start = (bf16[960,768]{1,0:T(8,128)(2,1)}, bf16[960,768]{1,0:T(8,128)(2,1)S(1)}, u32[]{:S(2)}) copy-start(bf16[960,768]{1,0:T(8,128)(2,1)S(1)} %shard_map.90.refs_0_) | copy-start | bytes 4423684
  73.7 28.5 %collective-permute-start.10 = (bf16[960,768]{1,0:T(8,128)(2,1)S(1)}, bf16[960,768]{1,0:T(8,128)(2,1)}, u32[]{:S(2)}, u32[]{:S(2)}) collective-permute-start(bf16[960,768]{1,0:T(8,128)(2,1)S(1)} %shard_map.90.refs_0_), channel_id=1, source_target_pairs={{0,128},{8,24},{16,144},{24,40},{32,160},{40,56},{48,176},{56,8},{... | collective-permute-start | bytes 4423688 | tf_op jit(solution)/shard_map/ppermute | solution.py:227
  90.0 20.7 %collective-permute-start.13 = (bf16[960,768]{1,0:T(8,128)(2,1)}, bf16[960,768]{1,0:T(8,128)(2,1)S(1)}, u32[]{:S(2)}, u32[]{:S(2)}) collective-permute-start(bf16[960,768]{1,0:T(8,128)(2,1)} %shard_map.91.refs_1_), channel_id=1, source_target_pairs={{0,384},{8,56},{16,400},{24,8},{32,416},{40,24},{48,432},{56,40},{... | collective-permute-start | bytes 4423688 | tf_op jit(solution)/shard_map/ppermute | solution.py:227
  93.7 32.8 %collective-permute-start.12 = (bf16[960,768]{1,0:T(8,128)(2,1)S(1)}, bf16[960,768]{1,0:T(8,128)(2,1)}, u32[]{:S(2)}, u32[]{:S(2)}) collective-permute-start(bf16[960,768]{1,0:T(8,128)(2,1)S(1)} %shard_map.90.refs_0_), channel_id=1, source_target_pairs={{0,384},{8,56},{16,400},{24,8},{32,416},{40,24},{48,432},{56,40},{... | collective-permute-start | bytes 4423688 | tf_op jit(solution)/shard_map/ppermute | solution.py:227
  96.2 30.4 %collective-permute-start.11 = (bf16[960,768]{1,0:T(8,128)(2,1)}, bf16[960,768]{1,0:T(8,128)(2,1)}, u32[]{:S(2)}, u32[]{:S(2)}) collective-permute-start(bf16[960,768]{1,0:T(8,128)(2,1)} %shard_map.91.refs_1_), channel_id=1, source_target_pairs={{0,128},{8,24},{16,144},{24,40},{32,160},{40,56},{48,176},{56,8},{... | collective-permute-start | bytes 4423688 | tf_op jit(solution)/shard_map/ppermute | solution.py:227
  102.2 31.7 %collective-permute-start.14 = (bf16[960,768]{1,0:T(8,128)(2,1)}, bf16[960,768]{1,0:T(8,128)(2,1)}, u32[]{:S(2)}, u32[]{:S(2)}) collective-permute-start(bf16[960,768]{1,0:T(8,128)(2,1)} %collective-permute-done.10.refs_2_), channel_id=1, source_target_pairs={{0,128},{8,24},{16,144},{24,40},{32,160},{40,56},{48,176},{56,8},{... | collective-permute-start | bytes 4423688 | tf_op jit(solution)/shard_map/ppermute | solution.py:227
  110.7 31.6 %copy-start.8 = (bf16[960,768]{1,0:T(8,128)(2,1)}, bf16[960,768]{1,0:T(8,128)(2,1)S(1)}, u32[]{:S(2)}) copy-start(bf16[960,768]{1,0:T(8,128)(2,1)S(1)} %collective-permute-done.13.refs_5_) | copy-start | bytes 4423684
  110.7 31.6 %collective-permute-start.15 = (bf16[960,768]{1,0:T(8,128)(2,1)S(1)}, bf16[960,768]{1,0:T(8,128)(2,1)}, u32[]{:S(2)}, u32[]{:S(2)}) collective-permute-start(bf16[960,768]{1,0:T(8,128)(2,1)S(1)} %collective-permute-done.13.refs_5_), channel_id=1, source_target_pairs={{0,384},{8,56},{16,400},{24,8},{32,416},{40,24},{48,432},{56,40},{... | collective-permute-start | bytes 4423688 | tf_op jit(solution)/shard_map/ppermute | solution.py:227
  156.6 10.6 %copy-start.6 = (s32[256,6]{0,1:T(8,128)S(1)}, s32[256,6]{0,1:T(8,128)}, u32[]{:S(2)}) copy-start(s32[256,6]{0,1:T(8,128)} %param.9) | copy-start | bytes 18436
  156.6 10.8 %copy-start.7 = (bf16[256,6]{0,1:T(8,128)(2,1)S(1)}, bf16[256,6]{0,1:T(8,128)(2,1)}, u32[]{:S(2)}) copy-start(bf16[256,6]{0,1:T(8,128)(2,1)} %param.10) | copy-start | bytes 9220
  156.6 43.5 %all-to-all-start.1 = ((bf16[8,32,2688]{2,1,0:T(8,128)(2,1)}), bf16[8,32,2688]{2,1,0:T(8,128)(2,1)S(1)}, u32[]{:S(2)}, u32[]{:S(2)}) async-start(bf16[8,32,2688]{2,1,0:T(8,128)(2,1)} %shard_map.92), calls=%async_computation.1 | async-start | bytes 2752512 | tf_op jit(solution)/shard_map/all_to_all | solution.py:329

commit v4 on v3

--- a/solution.py
+++ b/solution.py
@@ -30,21 +30,20 @@
 
 
 def dispatch_kernel(routes_ref, tok_ref, cot_ref, out_ref, sel_ref):
-    tokens, width = tok_ref.shape
-    place = route_place(routes_ref[...], 32)
-    lane = lax.broadcasted_iota(jnp.int32, (tokens, 256), 1)
-    sel = jnp.where(lane == place, 1.0, 0.0).astype(BF)
-    sel_ref[...] = sel
-    step = 512
-
-    @pl.loop(0, width // step)
-    def _(i):
-        cols = pl.ds(pl.multiple_of(i * step, step), step)
-        for source, first in ((tok_ref, 0), (cot_ref, 32)):
-            rows = lax.dot_general(
-                sel, source[:, cols], (((0,), (0,)), ((), ())), preferred_element_type=F32
-            ).astype(BF)
-            out_ref[:, first : first + 32, cols] = rows.reshape(8, 32, step)
+    tokens, step = tok_ref.shape
+
+    @pl.when(pl.program_id(0) == 0)
+    def _():
+        place = route_place(routes_ref[...], 32)
+        lane = lax.broadcasted_iota(jnp.int32, (tokens, 256), 1)
+        sel_ref[...] = jnp.where(lane == place, 1.0, 0.0).astype(BF)
+
+    sel = sel_ref[...]
+    for source, first in ((tok_ref, 0), (cot_ref, 32)):
+        rows = lax.dot_general(
+            sel, source[...], (((0,), (0,)), ((), ())), preferred_element_type=F32
+        ).astype(BF)
+        out_ref[:, first : first + 32, :] = rows.reshape(8, 32, step)
 
 
 def combine_kernel(routes_ref, gates_ref, sel_ref, back_ref, grad_ref, score_ref):
@@ -65,9 +64,15 @@
     score_ref[...] = jnp.where(window, score, 0.0).astype(BF)
 
 
-def stack_kernel(gate_ref, up_ref, down_ref, out_ref):
-    for m, ref in enumerate((gate_ref, up_ref, down_ref)):
-        out_ref[m] = ref[0]
+def stack_kernel(gate_ref, up_ref, down_ref, out_ref, sems):
+    copies = [
+        pltpu.make_async_copy(ref.at[0], out_ref.at[m], sems.at[m])
+        for m, ref in enumerate((gate_ref, up_ref, down_ref))
+    ]
+    for copy in copies:
+        copy.start()
+    for copy in copies:
+        copy.wait()
 
 
 def pair_kernel(first_ref, shard_ref, other_ref, top_ref, bottom_ref):
@@ -84,74 +89,76 @@
                 bottom_ref[row + cut - SPLIT : row + 40 - SPLIT] = part[cut:]
 
 
-def block_kernel(state_ref, top, bottom, low0, low1, high0, high1, far0, far1, out_ref):
+def block_kernel(state_ref, top, bottom, low0, low1, high0, high1, far0, far1, gu_ref, down_ref):
     source, order = state_ref[0] == 1, state_ref[1] == 0
-    row = 0
+    cut = 160 - SPLIT
     for z in range(2):
+        pick = order if z == 0 else jnp.logical_not(order)
+        parts = []
         for mine, low, high, far in ((top, low0, high0, far0), (bottom, low1, high1, far1)):
-            count = mine.shape[0]
             first = jnp.where(source, mine[...], low[...])
             second = jnp.where(source, far[...], high[...])
-            pick = order if z == 0 else jnp.logical_not(order)
-            out_ref[row : row + count] = jnp.where(pick, first, second)
-            row += count
-
-
-def expert_kernel(pieces, where_ref, rows_ref, *refs):
-    sources = refs[: len(refs) - 9]
-    out_ref = refs[-9]
-    gate_w, up_w, down_w, grad_a, grad_b, pre_g, pre_u, sems = refs[-8:]
-    weights = (gate_w, up_w, down_w)
+            parts.append(jnp.where(pick, first, second))
+        gu_ref[160 * z : 160 * z + SPLIT] = parts[0]
+        gu_ref[160 * z + SPLIT : 160 * z + 160] = parts[1][:cut]
+        down_ref[80 * z : 80 * z + 80] = parts[1][cut:]
+
+
+def expert_kernel(pieces, where_ref, rows_ref, all_down_ref, *refs):
+    sources = refs[: len(pieces) // 4]
+    out_ref = refs[len(sources)]
+    gate_w, up_w, down_w, tok_v, cot_v, result, grad_a, grad_b, pre_g, pre_u, pre_b, sems, out_sems = refs[
+        len(sources) + 1 :
+    ]
     my_x, my_y, core = where_ref[0], where_ref[1], where_ref[2]
-
-    copies = ([], [], [])
+    width, hidden_width = gate_w.shape
+
+    down_copies, gate_copies, up_copies = [], [], []
+    for x in range(4):
+        for y in range(4):
+            for z in range(2):
+                down_copies.append(
+                    pltpu.make_async_copy(
+                        all_down_ref.at[pl.ds(((x * 4 + y) * 2 + z) * 80, 80), :],
+                        down_w.at[pl.ds(((x * 2 + z) * 4 + y) * 80, 80), :],
+                        sems.at[0],
+                    )
+                )
+    down_copies.append(pltpu.make_async_copy(rows_ref.at[:, pl.ds(32, 32), :], cot_v, sems.at[1]))
+    gate_copies.append(pltpu.make_async_copy(rows_ref.at[:, pl.ds(0, 32), :], tok_v, sems.at[2]))
     for number, row, block, far, near in pieces:
         xx = lax.rem(my_x + jnp.where(core == 0, far, near), 4)
         yy = lax.rem(my_y + jnp.where(core == 0, near, far), 4)
         target = pl.multiple_of(((xx * 2 + block) * 4 + yy) * 80, 16)
-        for m in range(3):
-            copies[m].append(
+        for m, (weights, copies) in enumerate(((gate_w, gate_copies), (up_w, up_copies))):
+            copies.append(
                 pltpu.make_async_copy(
                     sources[number].at[pl.ds(row + 80 * m, 80), :],
-                    weights[m].at[pl.ds(target, 80), :],
-                    sems.at[m],
+                    weights.at[pl.ds(target, 80), :],
+                    sems.at[3 + m],
                 )
             )
-    for m in range(3):
-        for copy in copies[m]:
+    for copies in (down_copies, gate_copies, up_copies):
+        for copy in copies:
             copy.start()
 
-    width = gate_w.shape[0]
-    hidden_width = gate_w.shape[1]
+    for copy in down_copies:
+        copy.wait()
+    cot = cot_v[...].reshape(256, width)
+    pre_b[...] = jnp.dot(cot, down_w[...], preferred_element_type=F32)
+    for copy in gate_copies:
+        copy.wait()
+    tok = tok_v[...].reshape(256, width)
+    pre_g[...] = jnp.dot(tok, gate_w[...], preferred_element_type=F32)
+    for copy in up_copies:
+        copy.wait()
+    pre_u[...] = jnp.dot(tok, up_w[...], preferred_element_type=F32)
+
     cstep = 256
 
-    for copy in copies[0]:
-        copy.wait()
-
-    tok = rows_ref[:, 0:32, :].reshape(256, width)
-
-    @pl.loop(0, hidden_width // cstep)
-    def _(i):
+    def middle(i, score):
         cols = pl.ds(pl.multiple_of(i * cstep, cstep), cstep)
-        pre_g[:, cols] = jnp.dot(tok, gate_w[:, cols], preferred_element_type=F32)
-
-    for copy in copies[1]:
-        copy.wait()
-
-    @pl.loop(0, hidden_width // cstep)
-    def _(i):
-        cols = pl.ds(pl.multiple_of(i * cstep, cstep), cstep)
-        pre_u[:, cols] = jnp.dot(tok, up_w[:, cols], preferred_element_type=F32)
-
-    for copy in copies[2]:
-        copy.wait()
-
-    cot = rows_ref[:, 32:64, :].reshape(256, width)
-
-    def back(i, score):
-        cols = pl.ds(pl.multiple_of(i * cstep, cstep), cstep)
-        back_hidden = jnp.dot(cot, down_w[:, cols], preferred_element_type=F32)
-        gate, up = pre_g[:, cols], pre_u[:, cols]
+        gate, up, back_hidden = pre_g[:, cols], pre_u[:, cols], pre_b[:, cols]
         sig = jax.nn.sigmoid(gate)
         act = gate * sig
         hidden = (act * up).astype(BF).astype(F32)
@@ -159,21 +166,24 @@
         grad_b[:, cols] = (back_hidden * act).astype(BF)
         return score + jnp.sum(hidden * back_hidden, axis=1, keepdims=True)
 
-    score = lax.fori_loop(0, hidden_width // cstep, back, jnp.zeros((256, 1), F32))
-    out_ref[:, :, width : width + PAD] = (
+    score = lax.fori_loop(0, hidden_width // cstep, middle, jnp.zeros((256, 1), F32))
+    result[:, :, width : width + PAD] = (
         jnp.broadcast_to(score, (256, PAD)).astype(BF).reshape(8, 32, PAD)
     )
 
     a, b = grad_a[...], grad_b[...]
     dims = (((1,), (1,)), ((), ()))
-    dstep = 256
-
-    @pl.loop(0, width // dstep)
-    def _(i):
-        part = pl.ds(pl.multiple_of(i * dstep, dstep), dstep)
-        rows = lax.dot_general(a, gate_w[part, :], dims, preferred_element_type=F32)
-        rows = rows + lax.dot_general(b, up_w[part, :], dims, preferred_element_type=F32)
-        out_ref[:, :, part] = rows.astype(BF).reshape(8, 32, dstep)
+    dstep = width // 2
+    outs = []
+    for i in range(2):
+        rows = lax.dot_general(a, gate_w[i * dstep : (i + 1) * dstep, :], dims, preferred_element_type=F32)
+        rows = rows + lax.dot_general(b, up_w[i * dstep : (i + 1) * dstep, :], dims, preferred_element_type=F32)
+        result[:, :, i * dstep : (i + 1) * dstep] = rows.astype(BF).reshape(8, 32, dstep)
+        part = pl.ds(i * dstep, dstep if i == 0 else dstep + PAD)
+        outs.append(pltpu.make_async_copy(result.at[:, :, part], out_ref.at[:, :, part], out_sems.at[i]))
+        outs[i].start()
+    for copy in outs:
+        copy.wait()
 
 
 def params(mib=16):
@@ -235,6 +245,7 @@
     opposite = shift(low, False, 1)
     (early,) = join([2 * full], pair, own, low)
     early_low, early_high = shift(early, True, 1), shift(early, True, -1)
+    opposite, early_high = lax.optimization_barrier((opposite, early_high))
     (late,) = join([2 * full], pair, high, opposite)
     late_low, late_high = shift(late, True, 1), shift(late, True, -1)
     early_far, late_far = shift(early_low, True, 1), shift(late_high, True, -1)
@@ -259,9 +270,10 @@
     shard = pl.pallas_call(
         stack_kernel,
         out_shape=jax.ShapeDtypeStruct((3, *gate_proj.shape[1:]), BF),
-        in_specs=[VM] * 3,
-        out_specs=VM,
-        compiler_params=params(4),
+        in_specs=[ANY] * 3,
+        out_specs=ANY,
+        scratch_shapes=[pltpu.SemaphoreType.DMA((3,))],
+        compiler_params=params(56),
     )(gate_proj, up_proj, down_proj)
     other = lax.ppermute(shard, ("c", "zq"), [(2, 0), (1, 3)])
     smem = pl.BlockSpec(memory_space=pltpu.SMEM)
@@ -288,43 +300,55 @@
     far0, far1 = zmove(low0, False, 1), zmove(high1, False, -1)
     source = ic == zq
     ordered = jnp.where(source, zh == 0, (ring == 1) | (ring == 2))
-    block = pl.pallas_call(
+    block, down_block = pl.pallas_call(
         block_kernel,
-        out_shape=jax.ShapeDtypeStruct((480, hidden_width), BF),
+        out_shape=(
+            jax.ShapeDtypeStruct((320, hidden_width), BF),
+            jax.ShapeDtypeStruct((160, hidden_width), BF),
+        ),
         in_specs=[smem] + [VM] * 8,
-        out_specs=VM,
+        out_specs=(VM, VM),
         compiler_params=params(8),
     )(jnp.stack([source, jnp.logical_not(ordered)]).astype(jnp.int32), top, bottom, low0, low1, high0, high1, far0, far1)
 
-    (routes_later, _, _) = lax.optimization_barrier((routes, low0, high1))
+    (routes_later, _, _) = lax.optimization_barrier((routes, low1, high0))
+    step = 512
+    columns = pl.BlockSpec((256, step), lambda i: (0, i))
     payload, sel = pl.pallas_call(
         dispatch_kernel,
+        grid=(width // step,),
         out_shape=(
             jax.ShapeDtypeStruct((8, 64, width), BF),
             jax.ShapeDtypeStruct((256, 256), BF),
         ),
-        in_specs=[VM] * 3,
-        out_specs=(VM, VM),
-        compiler_params=params(),
+        in_specs=[pl.BlockSpec(routes.shape, lambda i: (0, 0)), columns, columns],
+        out_specs=(
+            pl.BlockSpec((8, 64, step), lambda i: (0, 0, i)),
+            pl.BlockSpec((256, 256), lambda i: (0, 0)),
+        ),
+        compiler_params=params(56),
         cost_estimate=cost(2 * 256 * 512 * width, 8 * 256 * width),
     )(routes_later, tokens_in, cotangent)
 
     payload, block = lax.optimization_barrier((payload, block))
+    all_down = lax.all_gather(down_block, ("x", "y"), axis=0, tiled=True)
     arrays, pieces = torus_gather(block)
     rows = lax.all_to_all(payload, ("c", "zr"), split_axis=0, concat_axis=0, tiled=True)
 
     back = pl.pallas_call(
         functools.partial(expert_kernel, pieces),
         out_shape=jax.ShapeDtypeStruct((8, 32, width + PAD), BF),
-        in_specs=[smem, VM] + [ANY] * len(arrays),
-        out_specs=VM,
+        in_specs=[smem] + [ANY] * (2 + len(arrays)),
+        out_specs=ANY,
         scratch_shapes=[pltpu.VMEM((width, hidden_width), BF)] * 3
+        + [pltpu.VMEM((8, 32, width), BF)] * 2
+        + [pltpu.VMEM((8, 32, width + PAD), BF)]
         + [pltpu.VMEM((256, hidden_width), BF)] * 2
-        + [pltpu.VMEM((256, hidden_width), F32)] * 2
-        + [pltpu.SemaphoreType.DMA((3,))],
+        + [pltpu.VMEM((256, hidden_width), F32)] * 3
+        + [pltpu.SemaphoreType.DMA((5,)), pltpu.SemaphoreType.DMA((2,))],
         compiler_params=params(56),
         cost_estimate=cost(10 * 256 * width * hidden_width, 6 * width * hidden_width),
-    )(jnp.stack([ix, iy, ic]).astype(jnp.int32), rows, *arrays)
+    )(jnp.stack([ix, iy, ic]).astype(jnp.int32), rows, all_down, *arrays)
 
     home = lax.all_to_all(back, ("c", "zr"), split_axis=0, concat_axis=0, tiled=True)
 

time: 204 us -> 218 us (1.069)
  between operations: 0.93 us -> 14.3 us
  Pallas kernels: 22.8 us -> 29.3 us
  local copies, waits for them, and re-layouts: 6.92 us -> 3.41 us
  starting transfers between devices: 76.4 us -> 73.1 us
    pallas_call x1, Pallas kernels: 0.01 us -> 6.71 us  [on_device(): pl.pallas_call(stack_kernel, out_shape=jax.ShapeDtypeStruct((3, *gate_pro...]
    all_to_all x1, starting transfers between devices: 10.6 us -> 5.69 us  [on_device(): lax.all_to_all(back, ('c', 'zr'), split_axis=0, concat_axis=0, tiled=True)]
    unnamed x20 -> x16, local copies, waits for them, and re-layouts: 5.4 us -> 1.23 us
    ppermute x9, starting transfers between devices: 27.2 us -> 30.9 us  [shift(): return lax.ppermute(v, ('x', 'y', 'c'), pairs)]
    ppermute x6, waiting for transfers between devices: 6.69 us -> 9.88 us  [zmove(): return lax.ppermute(v, ('zh', 'c', 'zq'), pairs)]
    ppermute x9, waiting for transfers between devices: 55.1 us -> 52 us  [shift(): return lax.ppermute(v, ('x', 'y', 'c'), pairs)]
    pallas_call x2, Pallas kernels: 4.38 us -> 7.32 us  [the longest x1 5.96 us: on_device(): pl.pallas_call(dispatch_kernel, grid=(width // step,), out_shape=(jax.Sha...]
    pallas_call x1, Pallas kernels: 14.3 us -> 11.7 us  [on_device(): pl.pallas_call(functools.partial(expert_kernel, pieces), out_shape=jax.Sh...]
  transfers between devices with their start and end apart: 18 -> 19, of which waited for: 10 -> 11; matrix products, arithmetic and copies ran while one was open for 1% -> 1% of each run, Pallas kernels for 3% -> 3%
where the time goes in v4:
time: 218 us; the launch traced here: 217 us
  waiting for transfers between devices  96.4 us (44%)
  starting transfers between devices  73.1 us (34%)
  Pallas kernels  29.3 us (13%)
  between operations  14.3 us (7%)
  local copies, waits for them, and re-layouts  3.41 us (2%)
    ppermute x9, waiting for transfers between devices, shift(): return lax.ppermute(v, ('x', 'y', 'c'), pairs)  52 us
    all_to_all x1, waiting for transfers between devices, on_device(): lax.all_to_all(back, ('c', 'zr'), split_axis=0, concat_axis=0, tiled=True)  32.6 us
    ppermute x9, starting transfers between devices, shift(): return lax.ppermute(v, ('x', 'y', 'c'), pairs)  30.9 us
    ppermute x6, starting transfers between devices, zmove(): return lax.ppermute(v, ('zh', 'c', 'zq'), pairs)  23.3 us
    pallas_call x1, Pallas kernels, on_device(): pl.pallas_call(functools.partial(expert_kernel, pieces), out_shape=jax.Sh...  11.7 us
    ppermute x6, waiting for transfers between devices, zmove(): return lax.ppermute(v, ('zh', 'c', 'zq'), pairs)  9.88 us
    ppermute x1, starting transfers between devices, on_device(): other = lax.ppermute(shard, ('c', 'zq'), [(2, 0), (1, 3)])  8.79 us
    pallas_call x1, Pallas kernels, on_device(): pl.pallas_call(stack_kernel, out_shape=jax.ShapeDtypeStruct((3, *gate_pro...  6.71 us
  transfers between devices with their start and end apart: 19, of which 11 were waited for; matrix products, arithmetic and copies ran while one was open for 1% of the time, Pallas kernels for 3%

profile of v4, /device:TPU:1, one launch (start us, length us, event | category | flops | bytes accessed | tf_op | source)
XLA Modules:
  0.0 217.3 jit_solution(1352585412371045913)
XLA Ops:
  7.2 6.7 %shard_map.86.shard_ref = bf16[3,40,768]{2,1,0:T(8,128)(2,1)} custom-call(bf16[1,40,768]{2,1,0:T(8,128)(2,1)} %gate_ref.1, bf16[1,40,768]{2,1,0:T(8,128)(2,1)} %up_ref.1, bf16[1,40,768]{2,1,0:T(8,128)(2,1)} %down_ref.1), custom_call_target="tpu_custom_call" | custom-call | tf_op jit(solution)/shard_map/pallas_call | solution.py:270
  13.9 8.8 %collective-permute-start = (bf16[3,40,768]{2,1,0:T(8,128)(2,1)}, bf16[3,40,768]{2,1,0:T(8,128)(2,1)S(1)}, u32[]{:S(2)}, u32[]{:S(2)}) collective-permute-start(bf16[3,40,768]{2,1,0:T(8,128)(2,1)} %shard_map.86.shard_ref), channel_id=1, source_target_pairs={{8,0},{4,12},{9,1},{5,13},{10,2},{6,14},{11,3},{7,15},{24,16},{20,... | collective-permute-start | bytes 552968 | tf_op jit(solution)/shard_map/ppermute | solution.py:278
  24.9 1.3 collective-permute-start.3
  26.2 1.3 collective-permute-start.4
  27.5 1.3 collective-permute-start.2
  30.1 5.4 %collective-permute-done.3.low0 = bf16[128,768]{1,0:T(8,128)(2,1)S(1)} collective-permute-done((bf16[128,768]{1,0:T(8,128)(2,1)S(1)}, bf16[128,768]{1,0:T(8,128)(2,1)S(1)}, u32[]{:S(2)}, u32[]{:S(2)}) %collective-permute-start.3) | collective-permute-done | bytes 196640 | tf_op jit(solution)/shard_map/ppermute | solution.py:296
  35.5 16.8 %collective-permute-start.5 = (bf16[128,768]{1,0:T(8,128)(2,1)S(1)}, bf16[128,768]{1,0:T(8,128)(2,1)S(1)}, u32[]{:S(2)}, u32[]{:S(2)}) collective-permute-start(bf16[128,768]{1,0:T(8,128)(2,1)S(1)} %collective-permute-done.3.low0), channel_id=1, source_target_pairs={{4,64},{68,0},{8,12},{72,76},{5,65},{69,1},{9,13},{73,77},{6,66},{... | collective-permute-start | bytes 589832 | tf_op jit(solution)/shard_map/ppermute | solution.py:296
  52.3 1.3 collective-permute-start.6
  54.8 3.4 %collective-permute-done.2.high0 = bf16[128,768]{1,0:T(8,128)(2,1)S(1)} collective-permute-done((bf16[128,768]{1,0:T(8,128)(2,1)S(1)}, bf16[128,768]{1,0:T(8,128)(2,1)S(1)}, u32[]{:S(2)}, u32[]{:S(2)}) %collective-permute-start.2) | collective-permute-done | bytes 196640 | tf_op jit(solution)/shard_map/ppermute | solution.py:296
  58.2 1.5 copy.9.routes_ref
  59.7 6.0 %shard_map.88 = (bf16[8,64,2560]{2,1,0:T(8,128)(2,1)}, bf16[256,256]{1,0:T(8,128)(2,1)}) custom-call(s32[256,6]{1,0:T(8,128)} %copy.9.routes_ref, bf16[256,2560]{1,0:T(8,128)(2,1)} %tok_ref.1, bf16[256,2560]{1,0:T(8,128)(2,1)} %cot_ref.1), custom_call_target="tpu_custom_call" | custom-call | flops 671088640 | bytes 5242880 | tf_op jit(solution)/shard_map/pallas_call | solution.py:317
  65.7 1.4 shard_map.89
  67.0 4.4 %all-to-all-start = ((bf16[8,64,2560]{2,1,0:T(8,128)(2,1)}), bf16[8,64,2560]{2,1,0:T(8,128)(2,1)}, u32[]{:S(2)}, u32[]{:S(2)}) async-start(bf16[8,64,2560]{2,1,0:T(8,128)(2,1)} %get-tuple-element.19), calls=%async_computation | async-start | bytes 5242880 | tf_op jit(solution)/shard_map/all_to_all | solution.py:336
  72.2 3.1 %collective-permute-start.7 = (bf16[320,768]{1,0:T(8,128)(2,1)S(1)}, bf16[320,768]{1,0:T(8,128)(2,1)S(1)}, u32[]{:S(2)}, u32[]{:S(2)}) collective-permute-start(bf16[320,768]{1,0:T(8,128)(2,1)S(1)} %get-tuple-element.21.refs_0_), channel_id=1, source_target_pairs={{0,16},{8,136},{16,32},{24,152},{32,48},{40,168},{48,0},{56,184},{... | collective-permute-start | bytes 1474568 | tf_op jit(solution)/shard_map/ppermute | solution.py:237
  75.3 7.7 %collective-permute-done.7.refs_1_ = bf16[320,768]{1,0:T(8,128)(2,1)S(1)} collective-permute-done((bf16[320,768]{1,0:T(8,128)(2,1)S(1)}, bf16[320,768]{1,0:T(8,128)(2,1)S(1)}, u32[]{:S(2)}, u32[]{:S(2)}) %collective-permute-start.7) | collective-permute-done | bytes 491552 | tf_op jit(solution)/shard_map/ppermute | solution.py:237
  83.6 4.7 %collective-permute-start.10 = (bf16[640,768]{1,0:T(8,128)(2,1)S(1)}, bf16[640,768]{1,0:T(8,128)(2,1)S(1)}, u32[]{:S(2)}, u32[]{:S(2)}) collective-permute-start(bf16[640,768]{1,0:T(8,128)(2,1)S(1)} %shard_map.90.refs_0_), channel_id=1, source_target_pairs={{0,384},{8,56},{16,400},{24,8},{32,416},{40,24},{48,432},{56,40},{... | collective-permute-start | bytes 2949128 | tf_op jit(solution)/shard_map/ppermute | solution.py:237
  88.3 2.3 %collective-permute-start.9 = (bf16[320,768]{1,0:T(8,128)(2,1)S(1)}, bf16[320,768]{1,0:T(8,128)(2,1)S(1)}, u32[]{:S(2)}, u32[]{:S(2)}) collective-permute-start(bf16[320,768]{1,0:T(8,128)(2,1)S(1)} %collective-permute-done.7.refs_1_), channel_id=1, source_target_pairs={{0,16},{8,136},{16,32},{24,152},{32,48},{40,168},{48,0},{56,184},{... | collective-permute-start | bytes 1474568 | tf_op jit(solution)/shard_map/ppermute | solution.py:237
  90.6 4.2 %collective-permute-start.8 = (bf16[320,768]{1,0:T(8,128)(2,1)S(1)}, bf16[320,768]{1,0:T(8,128)(2,1)S(1)}, u32[]{:S(2)}, u32[]{:S(2)}) collective-permute-start(bf16[320,768]{1,0:T(8,128)(2,1)S(1)} %get-tuple-element.21.refs_0_), channel_id=1, source_target_pairs={{0,48},{8,392},{16,0},{24,408},{32,16},{40,424},{48,32},{56,440},{... | collective-permute-start | bytes 1474568 | tf_op jit(solution)/shard_map/ppermute | solution.py:237
  94.8 1.9 collective-permute-start.11
  96.7 7.8 %collective-permute-done.9.refs_1_ = bf16[320,768]{1,0:T(8,128)(2,1)S(1)} collective-permute-done((bf16[320,768]{1,0:T(8,128)(2,1)S(1)}, bf16[320,768]{1,0:T(8,128)(2,1)S(1)}, u32[]{:S(2)}, u32[]{:S(2)}) %collective-permute-start.9) | collective-permute-done | bytes 491552 | tf_op jit(solution)/shard_map/ppermute | solution.py:237
  104.5 4.0 %collective-permute-done.10.refs_4_ = bf16[640,768]{1,0:T(8,128)(2,1)S(1)} collective-permute-done((bf16[640,768]{1,0:T(8,128)(2,1)S(1)}, bf16[640,768]{1,0:T(8,128)(2,1)S(1)}, u32[]{:S(2)}, u32[]{:S(2)}) %collective-permute-start.10) | collective-permute-done | bytes 983072 | tf_op jit(solution)/shard_map/ppermute | solution.py:237
  109.2 5.4 %collective-permute-start.13 = (bf16[640,768]{1,0:T(8,128)(2,1)S(1)}, bf16[640,768]{1,0:T(8,128)(2,1)}, u32[]{:S(2)}, u32[]{:S(2)}) collective-permute-start(bf16[640,768]{1,0:T(8,128)(2,1)S(1)} %shard_map.91.refs_1_), channel_id=1, source_target_pairs={{0,384},{8,56},{16,400},{24,8},{32,416},{40,24},{48,432},{56,40},{... | collective-permute-start | bytes 2949128 | tf_op jit(solution)/shard_map/ppermute | solution.py:237
  114.6 1.9 collective-permute-start.12
  116.5 1.9 collective-permute-start.14
  118.5 15.6 %collective-permute-done.13.refs_5_ = bf16[640,768]{1,0:T(8,128)(2,1)} collective-permute-done((bf16[640,768]{1,0:T(8,128)(2,1)S(1)}, bf16[640,768]{1,0:T(8,128)(2,1)}, u32[]{:S(2)}, u32[]{:S(2)}) %collective-permute-start.13) | collective-permute-done | bytes 983072 | tf_op jit(solution)/shard_map/ppermute | solution.py:237
  134.1 5.4 %collective-permute-start.15 = (bf16[640,768]{1,0:T(8,128)(2,1)}, bf16[640,768]{1,0:T(8,128)(2,1)}, u32[]{:S(2)}, u32[]{:S(2)}) collective-permute-start(bf16[640,768]{1,0:T(8,128)(2,1)} %collective-permute-done.13.refs_5_), channel_id=1, source_target_pairs={{0,384},{8,56},{16,400},{24,8},{32,416},{40,24},{48,432},{56,40},{... | collective-permute-start | bytes 2949128 | tf_op jit(solution)/shard_map/ppermute | solution.py:237
  140.1 3.9 %collective-permute-done.12.refs_3_ = bf16[640,768]{1,0:T(8,128)(2,1)} collective-permute-done((bf16[640,768]{1,0:T(8,128)(2,1)S(1)}, bf16[640,768]{1,0:T(8,128)(2,1)}, u32[]{:S(2)}, u32[]{:S(2)}) %collective-permute-start.12) | collective-permute-done | bytes 983072 | tf_op jit(solution)/shard_map/ppermute | solution.py:237
  144.1 13.0 %collective-permute-done.14.refs_6_ = bf16[640,768]{1,0:T(8,128)(2,1)} collective-permute-done((bf16[640,768]{1,0:T(8,128)(2,1)}, bf16[640,768]{1,0:T(8,128)(2,1)}, u32[]{:S(2)}, u32[]{:S(2)}) %collective-permute-start.14) | collective-permute-done | bytes 983072 | tf_op jit(solution)/shard_map/ppermute | solution.py:237
  157.1 11.7 %shard_map.92 = bf16[8,32,2688]{2,1,0:T(8,128)(2,1)} custom-call(s32[3]{0:T(128)} %pad_add_fusion.where_ref, bf16[8,64,2560]{2,1,0:T(8,128)(2,1)} %all-to-all-done.rows_ref, bf16[2560,768]{1,0:T(8,128)(2,1)} %all-gather.2.cloned.1.call-done.all_down_ref, bf16[640,768]{1,0:T(8,128)(2,1)} %copy-done, bf16[640,768]{1,0:T(8,128)(2,1)} %copy-done.1, ...), custom_call_target="tpu_custom_call" | custom-call | flops 5033164800 | bytes 11796480 | tf_op jit(solution)/shard_map/pallas_call | solution.py:338
  168.8 5.7 %all-to-all-start.1 = ((bf16[8,32,2688]{2,1,0:T(8,128)(2,1)}), bf16[8,32,2688]{2,1,0:T(8,128)(2,1)S(1)}, u32[]{:S(2)}, u32[]{:S(2)}) async-start(bf16[8,32,2688]{2,1,0:T(8,128)(2,1)} %shard_map.92), calls=%async_computation.1 | async-start | bytes 2752512 | tf_op jit(solution)/shard_map/all_to_all | solution.py:353
  174.8 32.6 %all-to-all-done.1.back_ref = bf16[8,32,2688]{2,1,0:T(8,128)(2,1)S(1)} async-done(((bf16[8,32,2688]{2,1,0:T(8,128)(2,1)}), bf16[8,32,2688]{2,1,0:T(8,128)(2,1)S(1)}, u32[]{:S(2)}, u32[]{:S(2)}) %all-to-all-start.1) | async-done | bytes 1376288 | tf_op jit(solution)/shard_map/all_to_all | solution.py:353
  207.4 2.3 %shard_map.93 = (bf16[256,2560]{1,0:T(8,128)(2,1)}, bf16[256,6]{1,0:T(8,128)(2,1)S(1)}) custom-call(s32[256,6]{1,0:T(8,128)S(1)} %copy.10.routes_ref, bf16[256,6]{1,0:T(8,128)(2,1)S(1)} %copy.11.gates_ref, bf16[256,256]{1,0:T(8,128)(2,1)S(1)} %copy-done.3, bf16[8,32,2688]{2,1,0:T(8,128)(2,1)S(1)} %all-to-all-done.1.back_ref), custom_call_target="tpu_custom_call" | custom-call | flops 335544320 | bytes 2621440 | tf_op jit(solution)/shard_map/pallas_call | solution.py:355
  (35 shorter events, 8.3 us)
Async XLA Ops:
  13.9 10.0 %collective-permute-start = (bf16[3,40,768]{2,1,0:T(8,128)(2,1)}, bf16[3,40,768]{2,1,0:T(8,128)(2,1)S(1)}, u32[]{:S(2)}, u32[]{:S(2)}) collective-permute-start(bf16[3,40,768]{2,1,0:T(8,128)(2,1)} %shard_map.86.shard_ref), channel_id=1, source_target_pairs={{8,0},{4,12},{9,1},{5,13},{10,2},{6,14},{11,3},{7,15},{24,16},{20,... | collective-permute-start | bytes 552968 | tf_op jit(solution)/shard_map/ppermute | solution.py:278
  23.9 0.9 copy-start.2
  24.9 10.6 %collective-permute-start.3 = (bf16[128,768]{1,0:T(8,128)(2,1)S(1)}, bf16[128,768]{1,0:T(8,128)(2,1)S(1)}, u32[]{:S(2)}, u32[]{:S(2)}) collective-permute-start(bf16[128,768]{1,0:T(8,128)(2,1)S(1)} %get-tuple-element.14.top), channel_id=1, source_target_pairs={{0,4},{64,68},{12,72},{76,8},{1,5},{65,69},{13,73},{77,9},{2,6},{6... | collective-permute-start | bytes 589832 | tf_op jit(solution)/shard_map/ppermute | solution.py:296
  26.2 26.2 %collective-permute-start.4 = (bf16[112,768]{1,0:T(8,128)(2,1)S(1)}, bf16[112,768]{1,0:T(8,128)(2,1)S(1)}, u32[]{:S(2)}, u32[]{:S(2)}) collective-permute-start(bf16[112,768]{1,0:T(8,128)(2,1)S(1)} %get-tuple-element.13.bottom), channel_id=1, source_target_pairs={{0,68},{64,4},{12,8},{76,72},{1,69},{65,5},{13,9},{77,73},{2,70},{... | collective-permute-start | bytes 516104 | tf_op jit(solution)/shard_map/ppermute | solution.py:296
  27.5 30.7 %collective-permute-start.2 = (bf16[128,768]{1,0:T(8,128)(2,1)S(1)}, bf16[128,768]{1,0:T(8,128)(2,1)S(1)}, u32[]{:S(2)}, u32[]{:S(2)}) collective-permute-start(bf16[128,768]{1,0:T(8,128)(2,1)S(1)} %get-tuple-element.14.top), channel_id=1, source_target_pairs={{0,68},{64,4},{12,8},{76,72},{1,69},{65,5},{13,9},{77,73},{2,70},{... | collective-permute-start | bytes 589832 | tf_op jit(solution)/shard_map/ppermute | solution.py:296
  28.8 26.1 %collective-permute-start.1 = (bf16[112,768]{1,0:T(8,128)(2,1)S(1)}, bf16[112,768]{1,0:T(8,128)(2,1)S(1)}, u32[]{:S(2)}, u32[]{:S(2)}) collective-permute-start(bf16[112,768]{1,0:T(8,128)(2,1)S(1)} %get-tuple-element.13.bottom), channel_id=1, source_target_pairs={{0,4},{64,68},{12,72},{76,8},{1,5},{65,69},{13,73},{77,9},{2,6},{6... | collective-permute-start | bytes 516104 | tf_op jit(solution)/shard_map/ppermute | solution.py:296
  35.5 30.2 %collective-permute-start.5 = (bf16[128,768]{1,0:T(8,128)(2,1)S(1)}, bf16[128,768]{1,0:T(8,128)(2,1)S(1)}, u32[]{:S(2)}, u32[]{:S(2)}) collective-permute-start(bf16[128,768]{1,0:T(8,128)(2,1)S(1)} %collective-permute-done.3.low0), channel_id=1, source_target_pairs={{4,64},{68,0},{8,12},{72,76},{5,65},{69,1},{9,13},{73,77},{6,66},{... | collective-permute-start | bytes 589832 | tf_op jit(solution)/shard_map/ppermute | solution.py:296
  52.3 13.3 %collective-permute-start.6 = (bf16[112,768]{1,0:T(8,128)(2,1)S(1)}, bf16[112,768]{1,0:T(8,128)(2,1)S(1)}, u32[]{:S(2)}, u32[]{:S(2)}) collective-permute-start(bf16[112,768]{1,0:T(8,128)(2,1)S(1)} %collective-permute-done.4.high1), channel_id=1, source_target_pairs={{4,0},{68,64},{8,76},{72,12},{5,1},{69,65},{9,77},{73,13},{6,2},{7... | collective-permute-start | bytes 516104 | tf_op jit(solution)/shard_map/ppermute | solution.py:296
  67.0 90.0 %all-to-all-start = ((bf16[8,64,2560]{2,1,0:T(8,128)(2,1)}), bf16[8,64,2560]{2,1,0:T(8,128)(2,1)}, u32[]{:S(2)}, u32[]{:S(2)}) async-start(bf16[8,64,2560]{2,1,0:T(8,128)(2,1)} %get-tuple-element.19), calls=%async_computation | async-start | bytes 5242880 | tf_op jit(solution)/shard_map/all_to_all | solution.py:336
  71.4 85.7 %all-gather.2.cloned.1.call-start = ((), (), s32[]{:S(2)}) async-start(), calls=%async_computation.2 | async-start | bytes 4177920 | tf_op jit(solution)/shard_map/all_gather | solution.py:334
  72.2 10.8 %collective-permute-start.7 = (bf16[320,768]{1,0:T(8,128)(2,1)S(1)}, bf16[320,768]{1,0:T(8,128)(2,1)S(1)}, u32[]{:S(2)}, u32[]{:S(2)}) collective-permute-start(bf16[320,768]{1,0:T(8,128)(2,1)S(1)} %get-tuple-element.21.refs_0_), channel_id=1, source_target_pairs={{0,16},{8,136},{16,32},{24,152},{32,48},{40,168},{48,0},{56,184},{... | collective-permute-start | bytes 1474568 | tf_op jit(solution)/shard_map/ppermute | solution.py:237
  83.6 73.5 %copy-start = (bf16[640,768]{1,0:T(8,128)(2,1)}, bf16[640,768]{1,0:T(8,128)(2,1)S(1)}, u32[]{:S(2)}) copy-start(bf16[640,768]{1,0:T(8,128)(2,1)S(1)} %shard_map.90.refs_0_) | copy-start | bytes 2949124
  83.6 24.9 %collective-permute-start.10 = (bf16[640,768]{1,0:T(8,128)(2,1)S(1)}, bf16[640,768]{1,0:T(8,128)(2,1)S(1)}, u32[]{:S(2)}, u32[]{:S(2)}) collective-permute-start(bf16[640,768]{1,0:T(8,128)(2,1)S(1)} %shard_map.90.refs_0_), channel_id=1, source_target_pairs={{0,384},{8,56},{16,400},{24,8},{32,416},{40,24},{48,432},{56,40},{... | collective-permute-start | bytes 2949128 | tf_op jit(solution)/shard_map/ppermute | solution.py:237
  88.3 16.2 %collective-permute-start.9 = (bf16[320,768]{1,0:T(8,128)(2,1)S(1)}, bf16[320,768]{1,0:T(8,128)(2,1)S(1)}, u32[]{:S(2)}, u32[]{:S(2)}) collective-permute-start(bf16[320,768]{1,0:T(8,128)(2,1)S(1)} %collective-permute-done.7.refs_1_), channel_id=1, source_target_pairs={{0,16},{8,136},{16,32},{24,152},{32,48},{40,168},{48,0},{56,184},{... | collective-permute-start | bytes 1474568 | tf_op jit(solution)/shard_map/ppermute | solution.py:237
  90.6 17.9 %collective-permute-start.8 = (bf16[320,768]{1,0:T(8,128)(2,1)S(1)}, bf16[320,768]{1,0:T(8,128)(2,1)S(1)}, u32[]{:S(2)}, u32[]{:S(2)}) collective-permute-start(bf16[320,768]{1,0:T(8,128)(2,1)S(1)} %get-tuple-element.21.refs_0_), channel_id=1, source_target_pairs={{0,48},{8,392},{16,0},{24,408},{32,16},{40,424},{48,32},{56,440},{... | collective-permute-start | bytes 1474568 | tf_op jit(solution)/shard_map/ppermute | solution.py:237
  94.8 21.7 %collective-permute-start.11 = (bf16[640,768]{1,0:T(8,128)(2,1)S(1)}, bf16[640,768]{1,0:T(8,128)(2,1)}, u32[]{:S(2)}, u32[]{:S(2)}) collective-permute-start(bf16[640,768]{1,0:T(8,128)(2,1)S(1)} %shard_map.90.refs_0_), channel_id=1, source_target_pairs={{0,128},{8,24},{16,144},{24,40},{32,160},{40,56},{48,176},{56,8},{... | collective-permute-start | bytes 2949128 | tf_op jit(solution)/shard_map/ppermute | solution.py:237
  108.5 48.6 %copy-start.6 = (bf16[640,768]{1,0:T(8,128)(2,1)}, bf16[640,768]{1,0:T(8,128)(2,1)S(1)}, u32[]{:S(2)}) copy-start(bf16[640,768]{1,0:T(8,128)(2,1)S(1)} %collective-permute-done.10.refs_4_) | copy-start | bytes 2949124
  109.1 48.0 %copy-start.1 = (bf16[640,768]{1,0:T(8,128)(2,1)}, bf16[640,768]{1,0:T(8,128)(2,1)S(1)}, u32[]{:S(2)}) copy-start(bf16[640,768]{1,0:T(8,128)(2,1)S(1)} %shard_map.91.refs_1_) | copy-start | bytes 2949124
  109.2 24.9 %collective-permute-start.13 = (bf16[640,768]{1,0:T(8,128)(2,1)S(1)}, bf16[640,768]{1,0:T(8,128)(2,1)}, u32[]{:S(2)}, u32[]{:S(2)}) collective-permute-start(bf16[640,768]{1,0:T(8,128)(2,1)S(1)} %shard_map.91.refs_1_), channel_id=1, source_target_pairs={{0,384},{8,56},{16,400},{24,8},{32,416},{40,24},{48,432},{56,40},{... | collective-permute-start | bytes 2949128 | tf_op jit(solution)/shard_map/ppermute | solution.py:237
  114.6 29.5 %collective-permute-start.12 = (bf16[640,768]{1,0:T(8,128)(2,1)S(1)}, bf16[640,768]{1,0:T(8,128)(2,1)}, u32[]{:S(2)}, u32[]{:S(2)}) collective-permute-start(bf16[640,768]{1,0:T(8,128)(2,1)S(1)} %shard_map.91.refs_1_), channel_id=1, source_target_pairs={{0,128},{8,24},{16,144},{24,40},{32,160},{40,56},{48,176},{56,8},{... | collective-permute-start | bytes 2949128 | tf_op jit(solution)/shard_map/ppermute | solution.py:237
  116.5 40.6 %collective-permute-start.14 = (bf16[640,768]{1,0:T(8,128)(2,1)}, bf16[640,768]{1,0:T(8,128)(2,1)}, u32[]{:S(2)}, u32[]{:S(2)}) collective-permute-start(bf16[640,768]{1,0:T(8,128)(2,1)} %collective-permute-done.11.refs_2_), channel_id=1, source_target_pairs={{0,128},{8,24},{16,144},{24,40},{32,160},{40,56},{48,176},{56,8},{... | collective-permute-start | bytes 2949128 | tf_op jit(solution)/shard_map/ppermute | solution.py:237
  134.1 23.0 %collective-permute-start.15 = (bf16[640,768]{1,0:T(8,128)(2,1)}, bf16[640,768]{1,0:T(8,128)(2,1)}, u32[]{:S(2)}, u32[]{:S(2)}) collective-permute-start(bf16[640,768]{1,0:T(8,128)(2,1)} %collective-permute-done.13.refs_5_), channel_id=1, source_target_pairs={{0,384},{8,56},{16,400},{24,8},{32,416},{40,24},{48,432},{56,40},{... | collective-permute-start | bytes 2949128 | tf_op jit(solution)/shard_map/ppermute | solution.py:237
  168.8 5.7 %copy-start.4 = (s32[256,6]{0,1:T(8,128)S(1)}, s32[256,6]{0,1:T(8,128)}, u32[]{:S(2)}) copy-start(s32[256,6]{0,1:T(8,128)} %param.9) | copy-start | bytes 18436
  168.8 5.9 %copy-start.5 = (bf16[256,6]{0,1:T(8,128)(2,1)S(1)}, bf16[256,6]{0,1:T(8,128)(2,1)}, u32[]{:S(2)}) copy-start(bf16[256,6]{0,1:T(8,128)(2,1)} %param.10) | copy-start | bytes 9220
  168.8 38.6 %copy-start.3 = (bf16[256,256]{1,0:T(8,128)(2,1)S(1)}, bf16[256,256]{1,0:T(8,128)(2,1)}, u32[]{:S(2)}) copy-start(bf16[256,256]{1,0:T(8,128)(2,1)} %get-tuple-element.16.sel_ref) | copy-start | bytes 393220
  168.8 38.6 %all-to-all-start.1 = ((bf16[8,32,2688]{2,1,0:T(8,128)(2,1)}), bf16[8,32,2688]{2,1,0:T(8,128)(2,1)S(1)}, u32[]{:S(2)}, u32[]{:S(2)}) async-start(bf16[8,32,2688]{2,1,0:T(8,128)(2,1)} %shard_map.92), calls=%async_computation.1 | async-start | bytes 2752512 | tf_op jit(solution)/shard_map/all_to_all | solution.py:353
Sparse Core Ops, SparseCore 0:
  75.3 73.2 all-gather.1

commit v5 on v4

--- a/solution.py
+++ b/solution.py
@@ -64,80 +64,58 @@
     score_ref[...] = jnp.where(window, score, 0.0).astype(BF)
 
 
-def stack_kernel(gate_ref, up_ref, down_ref, out_ref, sems):
-    copies = [
-        pltpu.make_async_copy(ref.at[0], out_ref.at[m], sems.at[m])
-        for m, ref in enumerate((gate_ref, up_ref, down_ref))
-    ]
-    for copy in copies:
-        copy.start()
-    for copy in copies:
-        copy.wait()
-
-
-def pair_kernel(first_ref, shard_ref, other_ref, top_ref, bottom_ref):
+def stack_kernel(gate_ref, up_ref, down_ref, out_ref):
+    for m, ref in enumerate((gate_ref, up_ref, down_ref)):
+        out_ref[m] = ref[0]
+
+
+def pair_kernel(first_ref, shard_ref, other_ref, out_ref):
     swap = first_ref[0] == 0
     for m in range(3):
         mine, theirs = shard_ref[m], other_ref[m]
         for k in range(2):
-            part = jnp.where(swap == (k == 0), mine, theirs)
             row = 80 * m + 40 * k
-            cut = min(max(SPLIT - row, 0), 40)
-            if cut:
-                top_ref[row : row + cut] = part[:cut]
-            if cut < 40:
-                bottom_ref[row + cut - SPLIT : row + 40 - SPLIT] = part[cut:]
-
-
-def block_kernel(state_ref, top, bottom, low0, low1, high0, high1, far0, far1, gu_ref, down_ref):
-    source, order = state_ref[0] == 1, state_ref[1] == 0
-    cut = 160 - SPLIT
-    for z in range(2):
-        pick = order if z == 0 else jnp.logical_not(order)
-        parts = []
-        for mine, low, high, far in ((top, low0, high0, far0), (bottom, low1, high1, far1)):
-            first = jnp.where(source, mine[...], low[...])
-            second = jnp.where(source, far[...], high[...])
-            parts.append(jnp.where(pick, first, second))
-        gu_ref[160 * z : 160 * z + SPLIT] = parts[0]
-        gu_ref[160 * z + SPLIT : 160 * z + 160] = parts[1][:cut]
-        down_ref[80 * z : 80 * z + 80] = parts[1][cut:]
-
-
-def expert_kernel(pieces, where_ref, rows_ref, all_down_ref, *refs):
-    sources = refs[: len(pieces) // 4]
+            out_ref[row : row + 40] = jnp.where(swap == (k == 0), mine, theirs)
+
+
+def near_kernel(source_ref, mine, low, out_ref):
+    out_ref[...] = jnp.where(source_ref[0] == 1, mine[...], low[...])
+
+
+def far_kernel(source_ref, top, bottom, high, out_ref):
+    source = source_ref[0] == 1
+    cut = top.shape[0]
+    out_ref[:cut] = jnp.where(source, top[...], high[:cut])
+    out_ref[cut:] = jnp.where(source, bottom[...], high[cut:])
+
+
+def expert_kernel(pieces, where_ref, rows_ref, *refs):
+    sources = refs[: pieces[-1][0] + 1]
     out_ref = refs[len(sources)]
     gate_w, up_w, down_w, tok_v, cot_v, result, grad_a, grad_b, pre_g, pre_u, pre_b, sems, out_sems = refs[
         len(sources) + 1 :
     ]
-    my_x, my_y, core = where_ref[0], where_ref[1], where_ref[2]
+    my_x, my_y, core, first_half = where_ref[0], where_ref[1], where_ref[2], where_ref[3]
     width, hidden_width = gate_w.shape
 
-    down_copies, gate_copies, up_copies = [], [], []
-    for x in range(4):
-        for y in range(4):
-            for z in range(2):
-                down_copies.append(
-                    pltpu.make_async_copy(
-                        all_down_ref.at[pl.ds(((x * 4 + y) * 2 + z) * 80, 80), :],
-                        down_w.at[pl.ds(((x * 2 + z) * 4 + y) * 80, 80), :],
-                        sems.at[0],
-                    )
-                )
-    down_copies.append(pltpu.make_async_copy(rows_ref.at[:, pl.ds(32, 32), :], cot_v, sems.at[1]))
-    gate_copies.append(pltpu.make_async_copy(rows_ref.at[:, pl.ds(0, 32), :], tok_v, sems.at[2]))
-    for number, row, block, far, near in pieces:
+    gate_copies, up_copies, down_copies = [], [], []
+    for number, row, chain, far, near in pieces:
         xx = lax.rem(my_x + jnp.where(core == 0, far, near), 4)
         yy = lax.rem(my_y + jnp.where(core == 0, near, far), 4)
-        target = pl.multiple_of(((xx * 2 + block) * 4 + yy) * 80, 16)
-        for m, (weights, copies) in enumerate(((gate_w, gate_copies), (up_w, up_copies))):
+        half = first_half if chain == 0 else 1 - first_half
+        target = pl.multiple_of(((xx * 2 + half) * 4 + yy) * 80, 16)
+        for m, (weights, copies) in enumerate(
+            ((gate_w, gate_copies), (up_w, up_copies), (down_w, down_copies))
+        ):
             copies.append(
                 pltpu.make_async_copy(
                     sources[number].at[pl.ds(row + 80 * m, 80), :],
                     weights.at[pl.ds(target, 80), :],
-                    sems.at[3 + m],
+                    sems.at[m],
                 )
             )
+    down_copies.append(pltpu.make_async_copy(rows_ref.at[:, pl.ds(32, 32), :], cot_v, sems.at[3]))
+    gate_copies.append(pltpu.make_async_copy(rows_ref.at[:, pl.ds(0, 32), :], tok_v, sems.at[4]))
     for copies in (down_copies, gate_copies, up_copies):
         for copy in copies:
             copy.start()
@@ -237,27 +215,22 @@
     return lax.ppermute(v, ("x", "y", "c"), pairs)
 
 
-def torus_gather(own):
-    full = own.shape[0]
-    half = full // 2
-    pair = ((0, 0, full, 0, 0), (1, 0, full, 0, full))
+def torus_gather(own, chain, first):
+    count = own.shape[0]
     low, high = shift(own, False, 1), shift(own, False, -1)
     opposite = shift(low, False, 1)
-    (early,) = join([2 * full], pair, own, low)
-    early_low, early_high = shift(early, True, 1), shift(early, True, -1)
-    opposite, early_high = lax.optimization_barrier((opposite, early_high))
-    (late,) = join([2 * full], pair, high, opposite)
-    late_low, late_high = shift(late, True, 1), shift(late, True, -1)
-    early_far, late_far = shift(early_low, True, 1), shift(late_high, True, -1)
-    arrays = (early, late, early_low, late_low, early_high, late_high, early_far, late_far)
-    fars = (0, 0, 3, 3, 1, 1, 2, 2)
-    pieces = [
-        (n, i * full + h * half, h, fars[n], (0, 3, 1, 2)[n % 2 * 2 + i])
-        for n in range(8)
-        for i in range(2)
-        for h in range(2)
-    ]
-    return arrays, pieces
+    (line,) = join(
+        [4 * count], [(n, 0, count, 0, n * count) for n in range(4)], own, low, high, opposite
+    )
+    line_low, line_high = shift(line, True, 1), shift(line, True, -1)
+    far0, far1 = join(
+        [2 * count] * 2, [(0, 0, 2 * count, 0, 0), (1, 2 * count, 2 * count, 1, 0)], line_low, line_high
+    )
+    far0, far1 = shift(far0, True, 1), shift(far1, True, -1)
+    near = (0, 3, 1, 2)
+    pieces = [(first + n, k * count, chain, far, near[k]) for n, far in enumerate((0, 3, 1)) for k in range(4)]
+    pieces += [(first + 3 + k // 2, k % 2 * count, chain, 2, near[k]) for k in range(4)]
+    return (line, line_low, line_high, far0, far1), pieces
 
 
 def on_device(tokens_in, cotangent, routes, gate_weights, gate_proj, up_proj, down_proj):
@@ -270,23 +243,22 @@
     shard = pl.pallas_call(
         stack_kernel,
         out_shape=jax.ShapeDtypeStruct((3, *gate_proj.shape[1:]), BF),
-        in_specs=[ANY] * 3,
-        out_specs=ANY,
-        scratch_shapes=[pltpu.SemaphoreType.DMA((3,))],
-        compiler_params=params(56),
+        in_specs=[VM] * 3,
+        out_specs=VM,
     )(gate_proj, up_proj, down_proj)
     other = lax.ppermute(shard, ("c", "zq"), [(2, 0), (1, 3)])
     smem = pl.BlockSpec(memory_space=pltpu.SMEM)
-    top, bottom = pl.pallas_call(
-        pair_kernel,
-        out_shape=(
-            jax.ShapeDtypeStruct((SPLIT, hidden_width), BF),
-            jax.ShapeDtypeStruct((240 - SPLIT, hidden_width), BF),
-        ),
-        in_specs=[smem, VM, VM],
-        out_specs=(VM, VM),
-        compiler_params=params(4),
-    )(ic.astype(jnp.int32)[None], shard, other)
+
+    def small(kernel, flag, *arrays):
+        return pl.pallas_call(
+            kernel,
+            out_shape=jax.ShapeDtypeStruct((240, hidden_width), BF),
+            in_specs=[smem] + [VM] * len(arrays),
+            out_specs=VM,
+            compiler_params=params(4),
+        )(flag.astype(jnp.int32)[None], *arrays)
+
+    pair = small(pair_kernel, ic, shard, other)
 
     def at(c, p):
         return (p // 2 * 2 + c) * 2 + p % 2
@@ -295,23 +267,13 @@
         pairs = [(at(c, p), at(c, (p + by) % 4)) for c in range(2) for p in range(4) if (p % 2 == c) == source]
         return lax.ppermute(v, ("zh", "c", "zq"), pairs)
 
-    low0, high1 = zmove(top, True, 1), zmove(bottom, True, -1)
-    low1, high0 = zmove(bottom, True, 1), zmove(top, True, -1)
-    far0, far1 = zmove(low0, False, 1), zmove(high1, False, -1)
     source = ic == zq
-    ordered = jnp.where(source, zh == 0, (ring == 1) | (ring == 2))
-    block, down_block = pl.pallas_call(
-        block_kernel,
-        out_shape=(
-            jax.ShapeDtypeStruct((320, hidden_width), BF),
-            jax.ShapeDtypeStruct((160, hidden_width), BF),
-        ),
-        in_specs=[smem] + [VM] * 8,
-        out_specs=(VM, VM),
-        compiler_params=params(8),
-    )(jnp.stack([source, jnp.logical_not(ordered)]).astype(jnp.int32), top, bottom, low0, low1, high0, high1, far0, far1)
-
-    (routes_later, _, _) = lax.optimization_barrier((routes, low1, high0))
+    low, high = zmove(pair, True, 1), zmove(pair, True, -1)
+    first = small(near_kernel, source, pair, low)
+    far0, far1 = zmove(low[:SPLIT], False, 1), zmove(high[SPLIT:], False, -1)
+    second = small(far_kernel, source, far0, far1, high)
+    first_half = jnp.where(source, zh, jnp.where((ring == 1) | (ring == 2), 0, 1))
+
     step = 512
     columns = pl.BlockSpec((256, step), lambda i: (0, i))
     payload, sel = pl.pallas_call(
@@ -328,17 +290,19 @@
         ),
         compiler_params=params(56),
         cost_estimate=cost(2 * 256 * 512 * width, 8 * 256 * width),
-    )(routes_later, tokens_in, cotangent)
-
-    payload, block = lax.optimization_barrier((payload, block))
-    all_down = lax.all_gather(down_block, ("x", "y"), axis=0, tiled=True)
-    arrays, pieces = torus_gather(block)
+    )(routes, tokens_in, cotangent)
+
+    payload, low, high = lax.optimization_barrier((payload, low, high))
+    arrays, pieces = torus_gather(first, 0, 0)
+    second, _ = lax.optimization_barrier((second, arrays[0]))
+    more_arrays, more_pieces = torus_gather(second, 1, len(arrays))
     rows = lax.all_to_all(payload, ("c", "zr"), split_axis=0, concat_axis=0, tiled=True)
+    arrays, pieces = arrays + more_arrays, pieces + more_pieces
 
     back = pl.pallas_call(
         functools.partial(expert_kernel, pieces),
         out_shape=jax.ShapeDtypeStruct((8, 32, width + PAD), BF),
-        in_specs=[smem] + [ANY] * (2 + len(arrays)),
+        in_specs=[smem] + [ANY] * (1 + len(arrays)),
         out_specs=ANY,
         scratch_shapes=[pltpu.VMEM((width, hidden_width), BF)] * 3
         + [pltpu.VMEM((8, 32, width), BF)] * 2
@@ -348,7 +312,7 @@
         + [pltpu.SemaphoreType.DMA((5,)), pltpu.SemaphoreType.DMA((2,))],
         compiler_params=params(56),
         cost_estimate=cost(10 * 256 * width * hidden_width, 6 * width * hidden_width),
-    )(jnp.stack([ix, iy, ic]).astype(jnp.int32), rows, all_down, *arrays)
+    )(jnp.stack([ix, iy, ic, first_half]).astype(jnp.int32), rows, *arrays)
 
     home = lax.all_to_all(back, ("c", "zr"), split_axis=0, concat_axis=0, tiled=True)
 

time: 218 us -> 239 us (1.096)
  starting transfers between devices: 73.1 us -> 93.7 us
  waiting for transfers between devices: 96.4 us -> 113 us
  between operations: 14.3 us -> 0.98 us
  Pallas kernels: 29.3 us -> 24.3 us
    ppermute x6 -> x4, waiting for transfers between devices: 9.88 us -> 45.6 us  [zmove(): return lax.ppermute(v, ('zh', 'c', 'zq'), pairs)]
    all_to_all x1, starting transfers between devices: 5.69 us -> 28 us  [on_device(): lax.all_to_all(back, ('c', 'zr'), split_axis=0, concat_axis=0, tiled=True)]
    ppermute x9 -> x14, waiting for transfers between devices: 52 us -> 33.7 us  [shift(): return lax.ppermute(v, ('x', 'y', 'c'), pairs)]
    ppermute x6 -> x4, starting transfers between devices: 23.3 us -> 8.81 us  [zmove(): return lax.ppermute(v, ('zh', 'c', 'zq'), pairs)]
    ppermute x9 -> x14, starting transfers between devices: 30.9 us -> 43.7 us  [shift(): return lax.ppermute(v, ('x', 'y', 'c'), pairs)]
    pallas_call x1, Pallas kernels: 6.71 us -> 1.57 us  [on_device(): pl.pallas_call(stack_kernel, out_shape=jax.ShapeDtypeStruct((3, *gate_pro...]
    unnamed x16 -> x22, local copies, waits for them, and re-layouts: 1.23 us -> 4.64 us
  transfers between devices with their start and end apart: 19 -> 21, of which waited for: 11 -> 13; matrix products, arithmetic and copies ran while one was open for 1% -> 1% of each run, Pallas kernels for 3% -> 4%
where the time goes in v5:
time: 239 us; the launch traced here: 238 us
  waiting for transfers between devices  113 us (47%)
  starting transfers between devices  93.7 us (39%)
  Pallas kernels  24.3 us (10%)
  local copies, waits for them, and re-layouts  5.36 us (2%)
    ppermute x4, waiting for transfers between devices, zmove(): return lax.ppermute(v, ('zh', 'c', 'zq'), pairs)  45.6 us
    ppermute x14, starting transfers between devices, shift(): return lax.ppermute(v, ('x', 'y', 'c'), pairs)  43.7 us
    ppermute x14, waiting for transfers between devices, shift(): return lax.ppermute(v, ('x', 'y', 'c'), pairs)  33.7 us
    all_to_all x1, waiting for transfers between devices, on_device(): lax.all_to_all(back, ('c', 'zr'), split_axis=0, concat_axis=0, tiled=True)  32.8 us
    all_to_all x1, starting transfers between devices, on_device(): lax.all_to_all(back, ('c', 'zr'), split_axis=0, concat_axis=0, tiled=True)  28 us
    pallas_call x1, Pallas kernels, on_device(): pl.pallas_call(functools.partial(expert_kernel, pieces), out_shape=jax.Sh...  11.8 us
    ppermute x4, starting transfers between devices, zmove(): return lax.ppermute(v, ('zh', 'c', 'zq'), pairs)  8.81 us
    ppermute x1, starting transfers between devices, on_device(): other = lax.ppermute(shard, ('c', 'zq'), [(2, 0), (1, 3)])  8.78 us
  transfers between devices with their start and end apart: 21, of which 13 were waited for; matrix products, arithmetic and copies ran while one was open for 1% of the time, Pallas kernels for 4%

profile of v5, /device:TPU:1, one launch (start us, length us, event | category | flops | bytes accessed | tf_op | source)
XLA Modules:
  0.0 238.2 jit_solution(13507266270416105856)
XLA Ops:
  0.6 1.6 shard_map.87.shard_ref
  2.2 8.8 %collective-permute-start = (bf16[3,40,768]{2,1,0:T(8,128)(2,1)}, bf16[3,40,768]{2,1,0:T(8,128)(2,1)S(1)}, u32[]{:S(2)}, u32[]{:S(2)}) collective-permute-start(bf16[3,40,768]{2,1,0:T(8,128)(2,1)} %shard_map.87.shard_ref), channel_id=1, source_target_pairs={{8,0},{4,12},{9,1},{5,13},{10,2},{6,14},{11,3},{7,15},{24,16},{20,... | collective-permute-start | bytes 552968 | tf_op jit(solution)/shard_map/ppermute | solution.py:249
  17.3 5.9 %shard_map.86 = (bf16[8,64,2560]{2,1,0:T(8,128)(2,1)}, bf16[256,256]{1,0:T(8,128)(2,1)}) custom-call(s32[256,6]{1,0:T(8,128)} %copy.10.routes_ref, bf16[256,2560]{1,0:T(8,128)(2,1)} %tok_ref.1, bf16[256,2560]{1,0:T(8,128)(2,1)} %cot_ref.1), custom_call_target="tpu_custom_call" | custom-call | flops 671088640 | bytes 5242880 | tf_op jit(solution)/shard_map/pallas_call | solution.py:279
  23.2 4.1 %collective-permute-done.1.low = bf16[240,768]{1,0:T(8,128)(2,1)S(1)} collective-permute-done((bf16[240,768]{1,0:T(8,128)(2,1)S(1)}, bf16[240,768]{1,0:T(8,128)(2,1)S(1)}, u32[]{:S(2)}, u32[]{:S(2)}) %collective-permute-start.1) | collective-permute-done | bytes 368672 | tf_op jit(solution)/shard_map/ppermute | solution.py:268
  27.3 14.3 %collective-permute-done.2.high = bf16[240,768]{1,0:T(8,128)(2,1)S(1)} collective-permute-done((bf16[240,768]{1,0:T(8,128)(2,1)S(1)}, bf16[240,768]{1,0:T(8,128)(2,1)S(1)}, u32[]{:S(2)}, u32[]{:S(2)}) %collective-permute-start.2) | collective-permute-done | bytes 368672 | tf_op jit(solution)/shard_map/ppermute | solution.py:268
  41.6 4.4 %all-to-all-start = ((bf16[8,64,2560]{2,1,0:T(8,128)(2,1)}), bf16[8,64,2560]{2,1,0:T(8,128)(2,1)}, u32[]{:S(2)}, u32[]{:S(2)}) async-start(bf16[8,64,2560]{2,1,0:T(8,128)(2,1)} %get-tuple-element.12), calls=%async_computation | async-start | bytes 5242880 | tf_op jit(solution)/shard_map/all_to_all | solution.py:299
  46.0 3.1 %collective-permute-start.3 = (bf16[240,768]{1,0:T(8,128)(2,1)S(1)}, bf16[240,768]{1,0:T(8,128)(2,1)S(1)}, u32[]{:S(2)}, u32[]{:S(2)}) collective-permute-start(bf16[240,768]{1,0:T(8,128)(2,1)S(1)} %shard_map.89.refs_0_), channel_id=1, source_target_pairs={{0,16},{8,136},{16,32},{24,152},{32,48},{40,168},{48,0},{56,184},{... | collective-permute-start | bytes 1105928 | tf_op jit(solution)/shard_map/ppermute | solution.py:215
  49.1 3.4 %collective-permute-start.4 = (bf16[240,768]{1,0:T(8,128)(2,1)S(1)}, bf16[240,768]{1,0:T(8,128)(2,1)S(1)}, u32[]{:S(2)}, u32[]{:S(2)}) collective-permute-start(bf16[240,768]{1,0:T(8,128)(2,1)S(1)} %shard_map.89.refs_0_), channel_id=1, source_target_pairs={{0,48},{8,392},{16,0},{24,408},{32,16},{40,424},{48,32},{56,440},{... | collective-permute-start | bytes 1105928 | tf_op jit(solution)/shard_map/ppermute | solution.py:215
  52.5 3.0 %collective-permute-done.3.refs_1_ = bf16[240,768]{1,0:T(8,128)(2,1)S(1)} collective-permute-done((bf16[240,768]{1,0:T(8,128)(2,1)S(1)}, bf16[240,768]{1,0:T(8,128)(2,1)S(1)}, u32[]{:S(2)}, u32[]{:S(2)}) %collective-permute-start.3) | collective-permute-done | bytes 368672 | tf_op jit(solution)/shard_map/ppermute | solution.py:215
  55.5 2.3 collective-permute-start.5
  57.8 4.9 %collective-permute-start.10 = (bf16[128,768]{1,0:T(8,128)(2,1)S(1)}, bf16[128,768]{1,0:T(8,128)(2,1)S(1)}, u32[]{:S(2)}, u32[]{:S(2)}) collective-permute-start(bf16[128,768]{1,0:T(8,128)(2,1)S(1)} %slice.8), channel_id=1, source_target_pairs={{4,64},{68,0},{8,12},{72,76},{5,65},{69,1},{9,13},{73,77},{6,66},{... | collective-permute-start | bytes 589832 | tf_op jit(solution)/shard_map/ppermute | solution.py:268
  64.1 2.5 %collective-permute-done.11.bottom = bf16[112,768]{1,0:T(8,128)(2,1)S(1)} collective-permute-done((bf16[112,768]{1,0:T(8,128)(2,1)S(1)}, bf16[112,768]{1,0:T(8,128)(2,1)S(1)}, u32[]{:S(2)}, u32[]{:S(2)}) %collective-permute-start.11) | collective-permute-done | bytes 172064 | tf_op jit(solution)/shard_map/ppermute | solution.py:268
  66.5 24.7 %collective-permute-done.10.top = bf16[128,768]{1,0:T(8,128)(2,1)S(1)} collective-permute-done((bf16[128,768]{1,0:T(8,128)(2,1)S(1)}, bf16[128,768]{1,0:T(8,128)(2,1)S(1)}, u32[]{:S(2)}, u32[]{:S(2)}) %collective-permute-start.10) | collective-permute-done | bytes 196640 | tf_op jit(solution)/shard_map/ppermute | solution.py:268
  92.0 3.1 %collective-permute-start.12 = (bf16[240,768]{1,0:T(8,128)(2,1)S(1)}, bf16[240,768]{1,0:T(8,128)(2,1)S(1)}, u32[]{:S(2)}, u32[]{:S(2)}) collective-permute-start(bf16[240,768]{1,0:T(8,128)(2,1)S(1)} %shard_map.92.refs_0_), channel_id=1, source_target_pairs={{0,16},{8,136},{16,32},{24,152},{32,48},{40,168},{48,0},{56,184},{... | collective-permute-start | bytes 1105928 | tf_op jit(solution)/shard_map/ppermute | solution.py:215
  95.1 3.4 %collective-permute-start.13 = (bf16[240,768]{1,0:T(8,128)(2,1)S(1)}, bf16[240,768]{1,0:T(8,128)(2,1)S(1)}, u32[]{:S(2)}, u32[]{:S(2)}) collective-permute-start(bf16[240,768]{1,0:T(8,128)(2,1)S(1)} %shard_map.92.refs_0_), channel_id=1, source_target_pairs={{0,48},{8,392},{16,0},{24,408},{32,16},{40,424},{48,32},{56,440},{... | collective-permute-start | bytes 1105928 | tf_op jit(solution)/shard_map/ppermute | solution.py:215
  98.5 3.2 %collective-permute-done.12.refs_1_ = bf16[240,768]{1,0:T(8,128)(2,1)S(1)} collective-permute-done((bf16[240,768]{1,0:T(8,128)(2,1)S(1)}, bf16[240,768]{1,0:T(8,128)(2,1)S(1)}, u32[]{:S(2)}, u32[]{:S(2)}) %collective-permute-start.12) | collective-permute-done | bytes 368672 | tf_op jit(solution)/shard_map/ppermute | solution.py:215
  101.7 2.1 collective-permute-start.14
  103.7 3.2 %collective-permute-start.6 = (bf16[960,768]{1,0:T(8,128)(2,1)S(1)}, bf16[960,768]{1,0:T(8,128)(2,1)S(1)}, u32[]{:S(2)}, u32[]{:S(2)}) collective-permute-start(bf16[960,768]{1,0:T(8,128)(2,1)S(1)} %shard_map.90.refs_0_), channel_id=1, source_target_pairs={{0,128},{8,24},{16,144},{24,40},{32,160},{40,56},{48,176},{56,8},{... | collective-permute-start | bytes 4423688 | tf_op jit(solution)/shard_map/ppermute | solution.py:215
  107.0 3.4 %collective-permute-start.7 = (bf16[960,768]{1,0:T(8,128)(2,1)S(1)}, bf16[960,768]{1,0:T(8,128)(2,1)S(1)}, u32[]{:S(2)}, u32[]{:S(2)}) collective-permute-start(bf16[960,768]{1,0:T(8,128)(2,1)S(1)} %shard_map.90.refs_0_), channel_id=1, source_target_pairs={{0,384},{8,56},{16,400},{24,8},{32,416},{40,24},{48,432},{56,40},{... | collective-permute-start | bytes 4423688 | tf_op jit(solution)/shard_map/ppermute | solution.py:215
  111.8 3.2 %collective-permute-start.15 = (bf16[960,768]{1,0:T(8,128)(2,1)S(1)}, bf16[960,768]{1,0:T(8,128)(2,1)S(1)}, u32[]{:S(2)}, u32[]{:S(2)}) collective-permute-start(bf16[960,768]{1,0:T(8,128)(2,1)S(1)} %shard_map.93.refs_5_), channel_id=1, source_target_pairs={{0,128},{8,24},{16,144},{24,40},{32,160},{40,56},{48,176},{56,8},{... | collective-permute-start | bytes 4423688 | tf_op jit(solution)/shard_map/ppermute | solution.py:215
  115.0 3.7 %collective-permute-start.16 = (bf16[960,768]{1,0:T(8,128)(2,1)S(1)}, bf16[960,768]{1,0:T(8,128)(2,1)S(1)}, u32[]{:S(2)}, u32[]{:S(2)}) collective-permute-start(bf16[960,768]{1,0:T(8,128)(2,1)S(1)} %shard_map.93.refs_5_), channel_id=1, source_target_pairs={{0,384},{8,56},{16,400},{24,8},{32,416},{40,24},{48,432},{56,40},{... | collective-permute-start | bytes 4423688 | tf_op jit(solution)/shard_map/ppermute | solution.py:215
  118.7 11.4 %collective-permute-done.6.refs_0_.refs_1_ = bf16[960,768]{1,0:T(8,128)(2,1)S(1)} collective-permute-done((bf16[960,768]{1,0:T(8,128)(2,1)S(1)}, bf16[960,768]{1,0:T(8,128)(2,1)S(1)}, u32[]{:S(2)}, u32[]{:S(2)}) %collective-permute-start.6) | collective-permute-done | bytes 1474592 | tf_op jit(solution)/shard_map/ppermute | solution.py:215
  131.7 2.0 collective-permute-start.8
  133.7 4.5 %collective-permute-start.9 = (bf16[480,768]{1,0:T(8,128)(2,1)S(1)}, bf16[480,768]{1,0:T(8,128)(2,1)}, u32[]{:S(2)}, u32[]{:S(2)}) collective-permute-start(bf16[480,768]{1,0:T(8,128)(2,1)S(1)} %get-tuple-element.14), channel_id=1, source_target_pairs={{0,384},{8,56},{16,400},{24,8},{32,416},{40,24},{48,432},{56,40},{... | collective-permute-start | bytes 2211848 | tf_op jit(solution)/shard_map/ppermute | solution.py:215
  138.2 7.6 %collective-permute-done.15.refs_0_.refs_6_ = bf16[960,768]{1,0:T(8,128)(2,1)S(1)} collective-permute-done((bf16[960,768]{1,0:T(8,128)(2,1)S(1)}, bf16[960,768]{1,0:T(8,128)(2,1)S(1)}, u32[]{:S(2)}, u32[]{:S(2)}) %collective-permute-start.15) | collective-permute-done | bytes 1474592 | tf_op jit(solution)/shard_map/ppermute | solution.py:215
  147.5 2.0 collective-permute-start.17
  149.5 4.5 %collective-permute-start.18 = (bf16[480,768]{1,0:T(8,128)(2,1)S(1)}, bf16[480,768]{1,0:T(8,128)(2,1)}, u32[]{:S(2)}, u32[]{:S(2)}) collective-permute-start(bf16[480,768]{1,0:T(8,128)(2,1)S(1)} %get-tuple-element.17), channel_id=1, source_target_pairs={{0,384},{8,56},{16,400},{24,8},{32,416},{40,24},{48,432},{56,40},{... | collective-permute-start | bytes 2211848 | tf_op jit(solution)/shard_map/ppermute | solution.py:215
  154.7 7.0 %collective-permute-done.17.refs_8_ = bf16[480,768]{1,0:T(8,128)(2,1)} collective-permute-done((bf16[480,768]{1,0:T(8,128)(2,1)S(1)}, bf16[480,768]{1,0:T(8,128)(2,1)}, u32[]{:S(2)}, u32[]{:S(2)}) %collective-permute-start.17) | collective-permute-done | bytes 737312 | tf_op jit(solution)/shard_map/ppermute | solution.py:215
  162.4 11.8 %shard_map.95 = bf16[8,32,2688]{2,1,0:T(8,128)(2,1)} custom-call(s32[4]{0:T(128)} %pad_add_fusion.where_ref, bf16[8,64,2560]{2,1,0:T(8,128)(2,1)} %all-to-all-done.rows_ref, bf16[960,768]{1,0:T(8,128)(2,1)} %copy-done, bf16[960,768]{1,0:T(8,128)(2,1)} %copy-done.1, bf16[960,768]{1,0:T(8,128)(2,1)} %copy-done.2, ...), custom_call_target="tpu_custom_call" | custom-call | flops 5033164800 | bytes 11796480 | tf_op jit(solution)/shard_map/pallas_call | solution.py:302
  174.2 28.0 %all-to-all-start.1 = ((bf16[8,32,2688]{2,1,0:T(8,128)(2,1)}), bf16[8,32,2688]{2,1,0:T(8,128)(2,1)S(1)}, u32[]{:S(2)}, u32[]{:S(2)}) async-start(bf16[8,32,2688]{2,1,0:T(8,128)(2,1)} %shard_map.95), calls=%async_computation.1 | async-start | bytes 2752512 | tf_op jit(solution)/shard_map/all_to_all | solution.py:317
  202.4 32.8 %all-to-all-done.1.back_ref = bf16[8,32,2688]{2,1,0:T(8,128)(2,1)S(1)} async-done(((bf16[8,32,2688]{2,1,0:T(8,128)(2,1)}), bf16[8,32,2688]{2,1,0:T(8,128)(2,1)S(1)}, u32[]{:S(2)}, u32[]{:S(2)}) %all-to-all-start.1) | async-done | bytes 1376288 | tf_op jit(solution)/shard_map/all_to_all | solution.py:317
  235.2 2.3 shard_map.96
  (47 shorter events, 15.3 us)
Async XLA Ops:
  2.2 10.0 %collective-permute-start = (bf16[3,40,768]{2,1,0:T(8,128)(2,1)}, bf16[3,40,768]{2,1,0:T(8,128)(2,1)S(1)}, u32[]{:S(2)}, u32[]{:S(2)}) collective-permute-start(bf16[3,40,768]{2,1,0:T(8,128)(2,1)} %shard_map.87.shard_ref), channel_id=1, source_target_pairs={{8,0},{4,12},{9,1},{5,13},{10,2},{6,14},{11,3},{7,15},{24,16},{20,... | collective-permute-start | bytes 552968 | tf_op jit(solution)/shard_map/ppermute | solution.py:249
  12.2 0.9 copy-start.7
  13.2 14.1 %collective-permute-start.1 = (bf16[240,768]{1,0:T(8,128)(2,1)S(1)}, bf16[240,768]{1,0:T(8,128)(2,1)S(1)}, u32[]{:S(2)}, u32[]{:S(2)}) collective-permute-start(bf16[240,768]{1,0:T(8,128)(2,1)S(1)} %shard_map.88.mine), channel_id=1, source_target_pairs={{0,4},{64,68},{12,72},{76,8},{1,5},{65,69},{13,73},{77,9},{2,6},{6... | collective-permute-start | bytes 1105928 | tf_op jit(solution)/shard_map/ppermute | solution.py:268
  14.5 27.1 %collective-permute-start.2 = (bf16[240,768]{1,0:T(8,128)(2,1)S(1)}, bf16[240,768]{1,0:T(8,128)(2,1)S(1)}, u32[]{:S(2)}, u32[]{:S(2)}) collective-permute-start(bf16[240,768]{1,0:T(8,128)(2,1)S(1)} %shard_map.88.mine), channel_id=1, source_target_pairs={{0,68},{64,4},{12,8},{76,72},{1,69},{65,5},{13,9},{77,73},{2,70},{... | collective-permute-start | bytes 1105928 | tf_op jit(solution)/shard_map/ppermute | solution.py:268
  41.6 120.8 %all-to-all-start = ((bf16[8,64,2560]{2,1,0:T(8,128)(2,1)}), bf16[8,64,2560]{2,1,0:T(8,128)(2,1)}, u32[]{:S(2)}, u32[]{:S(2)}) async-start(bf16[8,64,2560]{2,1,0:T(8,128)(2,1)} %get-tuple-element.12), calls=%async_computation | async-start | bytes 5242880 | tf_op jit(solution)/shard_map/all_to_all | solution.py:299
  46.0 9.5 %collective-permute-start.3 = (bf16[240,768]{1,0:T(8,128)(2,1)S(1)}, bf16[240,768]{1,0:T(8,128)(2,1)S(1)}, u32[]{:S(2)}, u32[]{:S(2)}) collective-permute-start(bf16[240,768]{1,0:T(8,128)(2,1)S(1)} %shard_map.89.refs_0_), channel_id=1, source_target_pairs={{0,16},{8,136},{16,32},{24,152},{32,48},{40,168},{48,0},{56,184},{... | collective-permute-start | bytes 1105928 | tf_op jit(solution)/shard_map/ppermute | solution.py:215
  49.1 42.2 %collective-permute-start.4 = (bf16[240,768]{1,0:T(8,128)(2,1)S(1)}, bf16[240,768]{1,0:T(8,128)(2,1)S(1)}, u32[]{:S(2)}, u32[]{:S(2)}) collective-permute-start(bf16[240,768]{1,0:T(8,128)(2,1)S(1)} %shard_map.89.refs_0_), channel_id=1, source_target_pairs={{0,48},{8,392},{16,0},{24,408},{32,16},{40,424},{48,32},{56,440},{... | collective-permute-start | bytes 1105928 | tf_op jit(solution)/shard_map/ppermute | solution.py:215
  55.5 35.8 %collective-permute-start.5 = (bf16[240,768]{1,0:T(8,128)(2,1)S(1)}, bf16[240,768]{1,0:T(8,128)(2,1)S(1)}, u32[]{:S(2)}, u32[]{:S(2)}) collective-permute-start(bf16[240,768]{1,0:T(8,128)(2,1)S(1)} %collective-permute-done.3.refs_1_), channel_id=1, source_target_pairs={{0,16},{8,136},{16,32},{24,152},{32,48},{40,168},{48,0},{56,184},{... | collective-permute-start | bytes 1105928 | tf_op jit(solution)/shard_map/ppermute | solution.py:215
  57.8 33.4 %collective-permute-start.10 = (bf16[128,768]{1,0:T(8,128)(2,1)S(1)}, bf16[128,768]{1,0:T(8,128)(2,1)S(1)}, u32[]{:S(2)}, u32[]{:S(2)}) collective-permute-start(bf16[128,768]{1,0:T(8,128)(2,1)S(1)} %slice.8), channel_id=1, source_target_pairs={{4,64},{68,0},{8,12},{72,76},{5,65},{69,1},{9,13},{73,77},{6,66},{... | collective-permute-start | bytes 589832 | tf_op jit(solution)/shard_map/ppermute | solution.py:268
  62.8 3.8 %collective-permute-start.11 = (bf16[112,768]{1,0:T(8,128)(2,1)S(1)}, bf16[112,768]{1,0:T(8,128)(2,1)S(1)}, u32[]{:S(2)}, u32[]{:S(2)}) collective-permute-start(bf16[112,768]{1,0:T(8,128)(2,1)S(1)} %slice.9), channel_id=1, source_target_pairs={{4,0},{68,64},{8,76},{72,12},{5,1},{69,65},{9,77},{73,13},{6,2},{7... | collective-permute-start | bytes 516104 | tf_op jit(solution)/shard_map/ppermute | solution.py:268
  92.0 19.8 %copy-start = (bf16[960,768]{1,0:T(8,128)(2,1)}, bf16[960,768]{1,0:T(8,128)(2,1)S(1)}, u32[]{:S(2)}) copy-start(bf16[960,768]{1,0:T(8,128)(2,1)S(1)} %shard_map.90.refs_0_) | copy-start | bytes 4423684
  92.0 9.7 %collective-permute-start.12 = (bf16[240,768]{1,0:T(8,128)(2,1)S(1)}, bf16[240,768]{1,0:T(8,128)(2,1)S(1)}, u32[]{:S(2)}, u32[]{:S(2)}) collective-permute-start(bf16[240,768]{1,0:T(8,128)(2,1)S(1)} %shard_map.92.refs_0_), channel_id=1, source_target_pairs={{0,16},{8,136},{16,32},{24,152},{32,48},{40,168},{48,0},{56,184},{... | collective-permute-start | bytes 1105928 | tf_op jit(solution)/shard_map/ppermute | solution.py:215
  95.1 15.2 %collective-permute-start.13 = (bf16[240,768]{1,0:T(8,128)(2,1)S(1)}, bf16[240,768]{1,0:T(8,128)(2,1)S(1)}, u32[]{:S(2)}, u32[]{:S(2)}) collective-permute-start(bf16[240,768]{1,0:T(8,128)(2,1)S(1)} %shard_map.92.refs_0_), channel_id=1, source_target_pairs={{0,48},{8,392},{16,0},{24,408},{32,16},{40,424},{48,32},{56,440},{... | collective-permute-start | bytes 1105928 | tf_op jit(solution)/shard_map/ppermute | solution.py:215
  101.7 9.5 %collective-permute-start.14 = (bf16[240,768]{1,0:T(8,128)(2,1)S(1)}, bf16[240,768]{1,0:T(8,128)(2,1)S(1)}, u32[]{:S(2)}, u32[]{:S(2)}) collective-permute-start(bf16[240,768]{1,0:T(8,128)(2,1)S(1)} %collective-permute-done.12.refs_1_), channel_id=1, source_target_pairs={{0,16},{8,136},{16,32},{24,152},{32,48},{40,168},{48,0},{56,184},{... | collective-permute-start | bytes 1105928 | tf_op jit(solution)/shard_map/ppermute | solution.py:215
  103.7 26.3 %collective-permute-start.6 = (bf16[960,768]{1,0:T(8,128)(2,1)S(1)}, bf16[960,768]{1,0:T(8,128)(2,1)S(1)}, u32[]{:S(2)}, u32[]{:S(2)}) collective-permute-start(bf16[960,768]{1,0:T(8,128)(2,1)S(1)} %shard_map.90.refs_0_), channel_id=1, source_target_pairs={{0,128},{8,24},{16,144},{24,40},{32,160},{40,56},{48,176},{56,8},{... | collective-permute-start | bytes 4423688 | tf_op jit(solution)/shard_map/ppermute | solution.py:215
  107.0 23.1 %collective-permute-start.7 = (bf16[960,768]{1,0:T(8,128)(2,1)S(1)}, bf16[960,768]{1,0:T(8,128)(2,1)S(1)}, u32[]{:S(2)}, u32[]{:S(2)}) collective-permute-start(bf16[960,768]{1,0:T(8,128)(2,1)S(1)} %shard_map.90.refs_0_), channel_id=1, source_target_pairs={{0,384},{8,56},{16,400},{24,8},{32,416},{40,24},{48,432},{56,40},{... | collective-permute-start | bytes 4423688 | tf_op jit(solution)/shard_map/ppermute | solution.py:215
  111.8 19.9 %copy-start.3 = (bf16[960,768]{1,0:T(8,128)(2,1)}, bf16[960,768]{1,0:T(8,128)(2,1)S(1)}, u32[]{:S(2)}) copy-start(bf16[960,768]{1,0:T(8,128)(2,1)S(1)} %shard_map.93.refs_5_) | copy-start | bytes 4423684
  111.8 34.0 %collective-permute-start.15 = (bf16[960,768]{1,0:T(8,128)(2,1)S(1)}, bf16[960,768]{1,0:T(8,128)(2,1)S(1)}, u32[]{:S(2)}, u32[]{:S(2)}) collective-permute-start(bf16[960,768]{1,0:T(8,128)(2,1)S(1)} %shard_map.93.refs_5_), channel_id=1, source_target_pairs={{0,128},{8,24},{16,144},{24,40},{32,160},{40,56},{48,176},{56,8},{... | collective-permute-start | bytes 4423688 | tf_op jit(solution)/shard_map/ppermute | solution.py:215
  115.0 30.8 %collective-permute-start.16 = (bf16[960,768]{1,0:T(8,128)(2,1)S(1)}, bf16[960,768]{1,0:T(8,128)(2,1)S(1)}, u32[]{:S(2)}, u32[]{:S(2)}) collective-permute-start(bf16[960,768]{1,0:T(8,128)(2,1)S(1)} %shard_map.93.refs_5_), channel_id=1, source_target_pairs={{0,384},{8,56},{16,400},{24,8},{32,416},{40,24},{48,432},{56,40},{... | collective-permute-start | bytes 4423688 | tf_op jit(solution)/shard_map/ppermute | solution.py:215
  130.0 1.2 copy-start.1
  130.0 1.6 copy-start.2
  131.7 23.0 %collective-permute-start.8 = (bf16[480,768]{1,0:T(8,128)(2,1)S(1)}, bf16[480,768]{1,0:T(8,128)(2,1)}, u32[]{:S(2)}, u32[]{:S(2)}) collective-permute-start(bf16[480,768]{1,0:T(8,128)(2,1)S(1)} %get-tuple-element.13), channel_id=1, source_target_pairs={{0,128},{8,24},{16,144},{24,40},{32,160},{40,56},{48,176},{56,8},{... | collective-permute-start | bytes 2211848 | tf_op jit(solution)/shard_map/ppermute | solution.py:215
  133.7 21.0 %collective-permute-start.9 = (bf16[480,768]{1,0:T(8,128)(2,1)S(1)}, bf16[480,768]{1,0:T(8,128)(2,1)}, u32[]{:S(2)}, u32[]{:S(2)}) collective-permute-start(bf16[480,768]{1,0:T(8,128)(2,1)S(1)} %get-tuple-element.14), channel_id=1, source_target_pairs={{0,384},{8,56},{16,400},{24,8},{32,416},{40,24},{48,432},{56,40},{... | collective-permute-start | bytes 2211848 | tf_op jit(solution)/shard_map/ppermute | solution.py:215
  145.8 1.2 copy-start.4
  145.8 1.7 copy-start.5
  147.5 14.2 %collective-permute-start.17 = (bf16[480,768]{1,0:T(8,128)(2,1)S(1)}, bf16[480,768]{1,0:T(8,128)(2,1)}, u32[]{:S(2)}, u32[]{:S(2)}) collective-permute-start(bf16[480,768]{1,0:T(8,128)(2,1)S(1)} %get-tuple-element.16), channel_id=1, source_target_pairs={{0,128},{8,24},{16,144},{24,40},{32,160},{40,56},{48,176},{56,8},{... | collective-permute-start | bytes 2211848 | tf_op jit(solution)/shard_map/ppermute | solution.py:215
  149.5 12.9 %collective-permute-start.18 = (bf16[480,768]{1,0:T(8,128)(2,1)S(1)}, bf16[480,768]{1,0:T(8,128)(2,1)}, u32[]{:S(2)}, u32[]{:S(2)}) collective-permute-start(bf16[480,768]{1,0:T(8,128)(2,1)S(1)} %get-tuple-element.17), channel_id=1, source_target_pairs={{0,384},{8,56},{16,400},{24,8},{32,416},{40,24},{48,432},{56,40},{... | collective-permute-start | bytes 2211848 | tf_op jit(solution)/shard_map/ppermute | solution.py:215
  174.2 28.0 %copy-start.9 = (bf16[256,6]{0,1:T(8,128)(2,1)S(1)}, bf16[256,6]{0,1:T(8,128)(2,1)}, u32[]{:S(2)}) copy-start(bf16[256,6]{0,1:T(8,128)(2,1)} %param.10) | copy-start | bytes 9220
  174.2 61.0 %copy-start.6 = (s32[256,6]{1,0:T(8,128)S(1)}, s32[256,6]{1,0:T(8,128)}, u32[]{:S(2)}) copy-start(s32[256,6]{1,0:T(8,128)} %copy.10.routes_ref) | copy-start | bytes 18436
  174.2 61.0 %copy-start.8 = (bf16[256,256]{1,0:T(8,128)(2,1)S(1)}, bf16[256,256]{1,0:T(8,128)(2,1)}, u32[]{:S(2)}) copy-start(bf16[256,256]{1,0:T(8,128)(2,1)} %get-tuple-element.10.sel_ref) | copy-start | bytes 393220
  174.2 60.9 %all-to-all-start.1 = ((bf16[8,32,2688]{2,1,0:T(8,128)(2,1)}), bf16[8,32,2688]{2,1,0:T(8,128)(2,1)S(1)}, u32[]{:S(2)}, u32[]{:S(2)}) async-start(bf16[8,32,2688]{2,1,0:T(8,128)(2,1)} %shard_map.95), calls=%async_computation.1 | async-start | bytes 2752512 | tf_op jit(solution)/shard_map/all_to_all | solution.py:317

commit v6 on v5

--- a/solution.py
+++ b/solution.py
@@ -230,7 +230,7 @@
     near = (0, 3, 1, 2)
     pieces = [(first + n, k * count, chain, far, near[k]) for n, far in enumerate((0, 3, 1)) for k in range(4)]
     pieces += [(first + 3 + k // 2, k % 2 * count, chain, 2, near[k]) for k in range(4)]
-    return (line, line_low, line_high, far0, far1), pieces
+    return (line, line_low, line_high, far0, far1), pieces, (low, high)
 
 
 def on_device(tokens_in, cotangent, routes, gate_weights, gate_proj, up_proj, down_proj):
@@ -292,11 +292,11 @@
         cost_estimate=cost(2 * 256 * 512 * width, 8 * 256 * width),
     )(routes, tokens_in, cotangent)
 
-    payload, low, high = lax.optimization_barrier((payload, low, high))
-    arrays, pieces = torus_gather(first, 0, 0)
-    second, _ = lax.optimization_barrier((second, arrays[0]))
-    more_arrays, more_pieces = torus_gather(second, 1, len(arrays))
+    arrays, pieces, near = torus_gather(first, 0, 0)
+    payload, *_ = lax.optimization_barrier((payload, far0, far1, *near))
     rows = lax.all_to_all(payload, ("c", "zr"), split_axis=0, concat_axis=0, tiled=True)
+    second, *_ = lax.optimization_barrier((second, *near))
+    more_arrays, more_pieces, _ = torus_gather(second, 1, len(arrays))
     arrays, pieces = arrays + more_arrays, pieces + more_pieces
 
     back = pl.pallas_call(

time: 239 us -> 190 us (0.79)
  waiting for transfers between devices: 113 us -> 72.4 us
  starting transfers between devices: 93.7 us -> 86.7 us
    ppermute x4, waiting for transfers between devices: 45.6 us -> 11.5 us  [zmove(): return lax.ppermute(v, ('zh', 'c', 'zq'), pairs)]
    all_to_all x1, starting transfers between devices: 28 us -> 8.47 us  [on_device(): lax.all_to_all(back, ('c', 'zr'), split_axis=0, concat_axis=0, tiled=True)]
    ppermute x4, starting transfers between devices: 8.81 us -> 18.2 us  [zmove(): return lax.ppermute(v, ('zh', 'c', 'zq'), pairs)]
    ppermute x14, waiting for transfers between devices: 33.7 us -> 26.9 us  [shift(): return lax.ppermute(v, ('x', 'y', 'c'), pairs)]
  transfers between devices with their start and end apart: 21 -> 21, of which waited for: 13 -> 11; matrix products, arithmetic and copies ran while one was open for 1% -> 1% of each run, Pallas kernels for 4% -> 5%
where the time goes in v6:
time: 190 us; the launch traced here: 189 us
  starting transfers between devices  86.7 us (46%)
  waiting for transfers between devices  72.4 us (38%)
  Pallas kernels  24.3 us (13%)
  local copies, waits for them, and re-layouts  3.68 us (2%)
    ppermute x14, starting transfers between devices, shift(): return lax.ppermute(v, ('x', 'y', 'c'), pairs)  45 us
    all_to_all x1, waiting for transfers between devices, on_device(): lax.all_to_all(back, ('c', 'zr'), split_axis=0, concat_axis=0, tiled=True)  32.8 us
    ppermute x14, waiting for transfers between devices, shift(): return lax.ppermute(v, ('x', 'y', 'c'), pairs)  26.9 us
    ppermute x4, starting transfers between devices, zmove(): return lax.ppermute(v, ('zh', 'c', 'zq'), pairs)  18.2 us
    pallas_call x1, Pallas kernels, on_device(): pl.pallas_call(functools.partial(expert_kernel, pieces), out_shape=jax.Sh...  11.7 us
    ppermute x4, waiting for transfers between devices, zmove(): return lax.ppermute(v, ('zh', 'c', 'zq'), pairs)  11.5 us
    ppermute x1, starting transfers between devices, on_device(): other = lax.ppermute(shard, ('c', 'zq'), [(2, 0), (1, 3)])  8.78 us
    all_to_all x1, starting transfers between devices, on_device(): lax.all_to_all(back, ('c', 'zr'), split_axis=0, concat_axis=0, tiled=True)  8.47 us
  transfers between devices with their start and end apart: 21, of which 11 were waited for; matrix products, arithmetic and copies ran while one was open for 1% of the time, Pallas kernels for 5%

profile of v6, /device:TPU:1, one launch (start us, length us, event | category | flops | bytes accessed | tf_op | source)
XLA Modules:
  0.0 188.7 jit_solution(4904244396042007193)
XLA Ops:
  0.6 1.6 shard_map.87.shard_ref
  2.2 8.8 %collective-permute-start = (bf16[3,40,768]{2,1,0:T(8,128)(2,1)}, bf16[3,40,768]{2,1,0:T(8,128)(2,1)S(1)}, u32[]{:S(2)}, u32[]{:S(2)}) collective-permute-start(bf16[3,40,768]{2,1,0:T(8,128)(2,1)} %shard_map.87.shard_ref), channel_id=1, source_target_pairs={{8,0},{4,12},{9,1},{5,13},{10,2},{6,14},{11,3},{7,15},{24,16},{20,... | collective-permute-start | bytes 552968 | tf_op jit(solution)/shard_map/ppermute | solution.py:249
  11.0 1.2 collective-permute-done.other_ref
  13.2 1.3 collective-permute-start.1
  14.5 1.3 collective-permute-start.3
  15.8 11.5 %collective-permute-done.1.low = bf16[240,768]{1,0:T(8,128)(2,1)S(1)} collective-permute-done((bf16[240,768]{1,0:T(8,128)(2,1)S(1)}, bf16[240,768]{1,0:T(8,128)(2,1)S(1)}, u32[]{:S(2)}, u32[]{:S(2)}) %collective-permute-start.1) | collective-permute-done | bytes 368672 | tf_op jit(solution)/shard_map/ppermute | solution.py:268
  27.3 1.9 %collective-permute-start.5 = (bf16[240,768]{1,0:T(8,128)(2,1)S(1)}, bf16[240,768]{1,0:T(8,128)(2,1)S(1)}, u32[]{:S(2)}, u32[]{:S(2)}) collective-permute-start(bf16[240,768]{1,0:T(8,128)(2,1)S(1)} %shard_map.89.refs_0_), channel_id=1, source_target_pairs={{0,16},{8,136},{16,32},{24,152},{32,48},{40,168},{48,0},{56,184},{... | collective-permute-start | bytes 1105928 | tf_op jit(solution)/shard_map/ppermute | solution.py:215
  29.3 4.6 %collective-permute-start.6 = (bf16[240,768]{1,0:T(8,128)(2,1)S(1)}, bf16[240,768]{1,0:T(8,128)(2,1)S(1)}, u32[]{:S(2)}, u32[]{:S(2)}) collective-permute-start(bf16[240,768]{1,0:T(8,128)(2,1)S(1)} %shard_map.89.refs_0_), channel_id=1, source_target_pairs={{0,48},{8,392},{16,0},{24,408},{32,16},{40,424},{48,32},{56,440},{... | collective-permute-start | bytes 1105928 | tf_op jit(solution)/shard_map/ppermute | solution.py:215
  33.9 14.3 %collective-permute-start.2 = (bf16[128,768]{1,0:T(8,128)(2,1)S(1)}, bf16[128,768]{1,0:T(8,128)(2,1)S(1)}, u32[]{:S(2)}, u32[]{:S(2)}) collective-permute-start(bf16[128,768]{1,0:T(8,128)(2,1)S(1)} %slice.8), channel_id=1, source_target_pairs={{4,64},{68,0},{8,12},{72,76},{5,65},{69,1},{9,13},{73,77},{6,66},{... | collective-permute-start | bytes 589832 | tf_op jit(solution)/shard_map/ppermute | solution.py:268
  48.2 1.3 collective-permute-start.4
  50.3 6.0 %shard_map.86 = (bf16[8,64,2560]{2,1,0:T(8,128)(2,1)}, bf16[256,256]{1,0:T(8,128)(2,1)}) custom-call(s32[256,6]{1,0:T(8,128)} %copy.10.routes_ref, bf16[256,2560]{1,0:T(8,128)(2,1)} %tok_ref.1, bf16[256,2560]{1,0:T(8,128)(2,1)} %cot_ref.1), custom_call_target="tpu_custom_call" | custom-call | flops 671088640 | bytes 5242880 | tf_op jit(solution)/shard_map/pallas_call | solution.py:279
  56.3 6.2 %all-to-all-start = ((bf16[8,64,2560]{2,1,0:T(8,128)(2,1)}), bf16[8,64,2560]{2,1,0:T(8,128)(2,1)}, u32[]{:S(2)}, u32[]{:S(2)}) async-start(bf16[8,64,2560]{2,1,0:T(8,128)(2,1)} %get-tuple-element.12), calls=%async_computation | async-start | bytes 5242880 | tf_op jit(solution)/shard_map/all_to_all | solution.py:297
  62.5 2.6 %collective-permute-start.12 = (bf16[240,768]{1,0:T(8,128)(2,1)S(1)}, bf16[240,768]{1,0:T(8,128)(2,1)S(1)}, u32[]{:S(2)}, u32[]{:S(2)}) collective-permute-start(bf16[240,768]{1,0:T(8,128)(2,1)S(1)} %shard_map.92.refs_0_), channel_id=1, source_target_pairs={{0,16},{8,136},{16,32},{24,152},{32,48},{40,168},{48,0},{56,184},{... | collective-permute-start | bytes 1105928 | tf_op jit(solution)/shard_map/ppermute | solution.py:215
  65.2 3.1 %collective-permute-start.7 = (bf16[240,768]{1,0:T(8,128)(2,1)S(1)}, bf16[240,768]{1,0:T(8,128)(2,1)S(1)}, u32[]{:S(2)}, u32[]{:S(2)}) collective-permute-start(bf16[240,768]{1,0:T(8,128)(2,1)S(1)} %collective-permute-done.5.refs_1_), channel_id=1, source_target_pairs={{0,16},{8,136},{16,32},{24,152},{32,48},{40,168},{48,0},{56,184},{... | collective-permute-start | bytes 1105928 | tf_op jit(solution)/shard_map/ppermute | solution.py:215
  68.3 3.4 %collective-permute-start.13 = (bf16[240,768]{1,0:T(8,128)(2,1)S(1)}, bf16[240,768]{1,0:T(8,128)(2,1)S(1)}, u32[]{:S(2)}, u32[]{:S(2)}) collective-permute-start(bf16[240,768]{1,0:T(8,128)(2,1)S(1)} %shard_map.92.refs_0_), channel_id=1, source_target_pairs={{0,48},{8,392},{16,0},{24,408},{32,16},{40,424},{48,32},{56,440},{... | collective-permute-start | bytes 1105928 | tf_op jit(solution)/shard_map/ppermute | solution.py:215
  72.3 1.9 %collective-permute-start.14 = (bf16[240,768]{1,0:T(8,128)(2,1)S(1)}, bf16[240,768]{1,0:T(8,128)(2,1)S(1)}, u32[]{:S(2)}, u32[]{:S(2)}) collective-permute-start(bf16[240,768]{1,0:T(8,128)(2,1)S(1)} %collective-permute-done.12.refs_1_), channel_id=1, source_target_pairs={{0,16},{8,136},{16,32},{24,152},{32,48},{40,168},{48,0},{56,184},{... | collective-permute-start | bytes 1105928 | tf_op jit(solution)/shard_map/ppermute | solution.py:215
  74.2 2.0 %collective-permute-done.7.refs_3_ = bf16[240,768]{1,0:T(8,128)(2,1)S(1)} collective-permute-done((bf16[240,768]{1,0:T(8,128)(2,1)S(1)}, bf16[240,768]{1,0:T(8,128)(2,1)S(1)}, u32[]{:S(2)}, u32[]{:S(2)}) %collective-permute-start.7) | collective-permute-done | bytes 368672 | tf_op jit(solution)/shard_map/ppermute | solution.py:215
  76.9 2.3 %collective-permute-start.8 = (bf16[960,768]{1,0:T(8,128)(2,1)S(1)}, bf16[960,768]{1,0:T(8,128)(2,1)S(1)}, u32[]{:S(2)}, u32[]{:S(2)}) collective-permute-start(bf16[960,768]{1,0:T(8,128)(2,1)S(1)} %shard_map.90.refs_0_), channel_id=1, source_target_pairs={{0,128},{8,24},{16,144},{24,40},{32,160},{40,56},{48,176},{56,8},{... | collective-permute-start | bytes 4423688 | tf_op jit(solution)/shard_map/ppermute | solution.py:215
  79.2 4.2 %collective-permute-start.9 = (bf16[960,768]{1,0:T(8,128)(2,1)S(1)}, bf16[960,768]{1,0:T(8,128)(2,1)S(1)}, u32[]{:S(2)}, u32[]{:S(2)}) collective-permute-start(bf16[960,768]{1,0:T(8,128)(2,1)S(1)} %shard_map.90.refs_0_), channel_id=1, source_target_pairs={{0,384},{8,56},{16,400},{24,8},{32,416},{40,24},{48,432},{56,40},{... | collective-permute-start | bytes 4423688 | tf_op jit(solution)/shard_map/ppermute | solution.py:215
  84.1 1.9 %collective-permute-start.15 = (bf16[960,768]{1,0:T(8,128)(2,1)S(1)}, bf16[960,768]{1,0:T(8,128)(2,1)S(1)}, u32[]{:S(2)}, u32[]{:S(2)}) collective-permute-start(bf16[960,768]{1,0:T(8,128)(2,1)S(1)} %shard_map.93.refs_5_), channel_id=1, source_target_pairs={{0,128},{8,24},{16,144},{24,40},{32,160},{40,56},{48,176},{56,8},{... | collective-permute-start | bytes 4423688 | tf_op jit(solution)/shard_map/ppermute | solution.py:215
  86.0 4.6 %collective-permute-start.16 = (bf16[960,768]{1,0:T(8,128)(2,1)S(1)}, bf16[960,768]{1,0:T(8,128)(2,1)S(1)}, u32[]{:S(2)}, u32[]{:S(2)}) collective-permute-start(bf16[960,768]{1,0:T(8,128)(2,1)S(1)} %shard_map.93.refs_5_), channel_id=1, source_target_pairs={{0,384},{8,56},{16,400},{24,8},{32,416},{40,24},{48,432},{56,40},{... | collective-permute-start | bytes 4423688 | tf_op jit(solution)/shard_map/ppermute | solution.py:215
  90.6 8.7 %collective-permute-done.8.refs_0_.refs_1_ = bf16[960,768]{1,0:T(8,128)(2,1)S(1)} collective-permute-done((bf16[960,768]{1,0:T(8,128)(2,1)S(1)}, bf16[960,768]{1,0:T(8,128)(2,1)S(1)}, u32[]{:S(2)}, u32[]{:S(2)}) %collective-permute-start.8) | collective-permute-done | bytes 1474592 | tf_op jit(solution)/shard_map/ppermute | solution.py:215
  100.9 3.2 %collective-permute-start.10 = (bf16[480,768]{1,0:T(8,128)(2,1)S(1)}, bf16[480,768]{1,0:T(8,128)(2,1)}, u32[]{:S(2)}, u32[]{:S(2)}) collective-permute-start(bf16[480,768]{1,0:T(8,128)(2,1)S(1)} %get-tuple-element.13), channel_id=1, source_target_pairs={{0,128},{8,24},{16,144},{24,40},{32,160},{40,56},{48,176},{56,8},{... | collective-permute-start | bytes 2211848 | tf_op jit(solution)/shard_map/ppermute | solution.py:215
  104.1 4.1 %collective-permute-start.11 = (bf16[480,768]{1,0:T(8,128)(2,1)S(1)}, bf16[480,768]{1,0:T(8,128)(2,1)}, u32[]{:S(2)}, u32[]{:S(2)}) collective-permute-start(bf16[480,768]{1,0:T(8,128)(2,1)S(1)} %get-tuple-element.14), channel_id=1, source_target_pairs={{0,384},{8,56},{16,400},{24,8},{32,416},{40,24},{48,432},{56,40},{... | collective-permute-start | bytes 2211848 | tf_op jit(solution)/shard_map/ppermute | solution.py:215
  108.2 6.7 %collective-permute-done.15.refs_0_.refs_6_ = bf16[960,768]{1,0:T(8,128)(2,1)S(1)} collective-permute-done((bf16[960,768]{1,0:T(8,128)(2,1)S(1)}, bf16[960,768]{1,0:T(8,128)(2,1)S(1)}, u32[]{:S(2)}, u32[]{:S(2)}) %collective-permute-start.15) | collective-permute-done | bytes 1474592 | tf_op jit(solution)/shard_map/ppermute | solution.py:215
  116.7 3.2 %collective-permute-start.17 = (bf16[480,768]{1,0:T(8,128)(2,1)S(1)}, bf16[480,768]{1,0:T(8,128)(2,1)}, u32[]{:S(2)}, u32[]{:S(2)}) collective-permute-start(bf16[480,768]{1,0:T(8,128)(2,1)S(1)} %get-tuple-element.16), channel_id=1, source_target_pairs={{0,128},{8,24},{16,144},{24,40},{32,160},{40,56},{48,176},{56,8},{... | collective-permute-start | bytes 2211848 | tf_op jit(solution)/shard_map/ppermute | solution.py:215
  119.8 4.1 %collective-permute-start.18 = (bf16[480,768]{1,0:T(8,128)(2,1)S(1)}, bf16[480,768]{1,0:T(8,128)(2,1)}, u32[]{:S(2)}, u32[]{:S(2)}) collective-permute-start(bf16[480,768]{1,0:T(8,128)(2,1)S(1)} %get-tuple-element.17), channel_id=1, source_target_pairs={{0,384},{8,56},{16,400},{24,8},{32,416},{40,24},{48,432},{56,40},{... | collective-permute-start | bytes 2211848 | tf_op jit(solution)/shard_map/ppermute | solution.py:215
  124.7 6.6 %collective-permute-done.17.refs_8_ = bf16[480,768]{1,0:T(8,128)(2,1)} collective-permute-done((bf16[480,768]{1,0:T(8,128)(2,1)S(1)}, bf16[480,768]{1,0:T(8,128)(2,1)}, u32[]{:S(2)}, u32[]{:S(2)}) %collective-permute-start.17) | collective-permute-done | bytes 737312 | tf_op jit(solution)/shard_map/ppermute | solution.py:215
  132.4 11.7 %shard_map.95 = bf16[8,32,2688]{2,1,0:T(8,128)(2,1)} custom-call(s32[4]{0:T(128)} %pad_add_fusion.where_ref, bf16[8,64,2560]{2,1,0:T(8,128)(2,1)} %all-to-all-done.rows_ref, bf16[960,768]{1,0:T(8,128)(2,1)} %copy-done, bf16[960,768]{1,0:T(8,128)(2,1)} %copy-done.1, bf16[960,768]{1,0:T(8,128)(2,1)} %copy-done.2, ...), custom_call_target="tpu_custom_call" | custom-call | flops 5033164800 | bytes 11796480 | tf_op jit(solution)/shard_map/pallas_call | solution.py:302
  144.2 8.5 %all-to-all-start.1 = ((bf16[8,32,2688]{2,1,0:T(8,128)(2,1)}), bf16[8,32,2688]{2,1,0:T(8,128)(2,1)S(1)}, u32[]{:S(2)}, u32[]{:S(2)}) async-start(bf16[8,32,2688]{2,1,0:T(8,128)(2,1)} %shard_map.95), calls=%async_computation.1 | async-start | bytes 2752512 | tf_op jit(solution)/shard_map/all_to_all | solution.py:317
  152.8 32.8 %all-to-all-done.1.back_ref = bf16[8,32,2688]{2,1,0:T(8,128)(2,1)S(1)} async-done(((bf16[8,32,2688]{2,1,0:T(8,128)(2,1)}), bf16[8,32,2688]{2,1,0:T(8,128)(2,1)S(1)}, u32[]{:S(2)}, u32[]{:S(2)}) %all-to-all-start.1) | async-done | bytes 1376288 | tf_op jit(solution)/shard_map/all_to_all | solution.py:317
  185.6 2.3 %shard_map.96 = (bf16[256,2560]{1,0:T(8,128)(2,1)}, bf16[256,6]{1,0:T(8,128)(2,1)S(1)}) custom-call(s32[256,6]{1,0:T(8,128)S(1)} %copy-done.6, bf16[256,6]{1,0:T(8,128)(2,1)S(1)} %copy.11.gates_ref, bf16[256,256]{1,0:T(8,128)(2,1)S(1)} %copy-done.8, bf16[8,32,2688]{2,1,0:T(8,128)(2,1)S(1)} %all-to-all-done.1.back_ref), custom_call_target="tpu_custom_call" | custom-call | flops 335544320 | bytes 2621440 | tf_op jit(solution)/shard_map/pallas_call | solution.py:319
  (49 shorter events, 9.8 us)
Async XLA Ops:
  0.6 48.9 %copy-start.9 = (s32[256,6]{0,1:T(8,128)S(1)}, s32[256,6]{0,1:T(8,128)}, u32[]{:S(2)}) copy-start(s32[256,6]{0,1:T(8,128)} %param.9) | copy-start | bytes 18436
  2.2 10.0 %collective-permute-start = (bf16[3,40,768]{2,1,0:T(8,128)(2,1)}, bf16[3,40,768]{2,1,0:T(8,128)(2,1)S(1)}, u32[]{:S(2)}, u32[]{:S(2)}) collective-permute-start(bf16[3,40,768]{2,1,0:T(8,128)(2,1)} %shard_map.87.shard_ref), channel_id=1, source_target_pairs={{8,0},{4,12},{9,1},{5,13},{10,2},{6,14},{11,3},{7,15},{24,16},{20,... | collective-permute-start | bytes 552968 | tf_op jit(solution)/shard_map/ppermute | solution.py:249
  12.2 0.9 copy-start.7
  13.2 14.1 %collective-permute-start.1 = (bf16[240,768]{1,0:T(8,128)(2,1)S(1)}, bf16[240,768]{1,0:T(8,128)(2,1)S(1)}, u32[]{:S(2)}, u32[]{:S(2)}) collective-permute-start(bf16[240,768]{1,0:T(8,128)(2,1)S(1)} %shard_map.88.mine), channel_id=1, source_target_pairs={{0,4},{64,68},{12,72},{76,8},{1,5},{65,69},{13,73},{77,9},{2,6},{6... | collective-permute-start | bytes 1105928 | tf_op jit(solution)/shard_map/ppermute | solution.py:268
  14.5 33.7 %collective-permute-start.3 = (bf16[240,768]{1,0:T(8,128)(2,1)S(1)}, bf16[240,768]{1,0:T(8,128)(2,1)S(1)}, u32[]{:S(2)}, u32[]{:S(2)}) collective-permute-start(bf16[240,768]{1,0:T(8,128)(2,1)S(1)} %shard_map.88.mine), channel_id=1, source_target_pairs={{0,68},{64,4},{12,8},{76,72},{1,69},{65,5},{13,9},{77,73},{2,70},{... | collective-permute-start | bytes 1105928 | tf_op jit(solution)/shard_map/ppermute | solution.py:268
  27.3 29.0 %collective-permute-start.5 = (bf16[240,768]{1,0:T(8,128)(2,1)S(1)}, bf16[240,768]{1,0:T(8,128)(2,1)S(1)}, u32[]{:S(2)}, u32[]{:S(2)}) collective-permute-start(bf16[240,768]{1,0:T(8,128)(2,1)S(1)} %shard_map.89.refs_0_), channel_id=1, source_target_pairs={{0,16},{8,136},{16,32},{24,152},{32,48},{40,168},{48,0},{56,184},{... | collective-permute-start | bytes 1105928 | tf_op jit(solution)/shard_map/ppermute | solution.py:215
  29.3 27.0 %collective-permute-start.6 = (bf16[240,768]{1,0:T(8,128)(2,1)S(1)}, bf16[240,768]{1,0:T(8,128)(2,1)S(1)}, u32[]{:S(2)}, u32[]{:S(2)}) collective-permute-start(bf16[240,768]{1,0:T(8,128)(2,1)S(1)} %shard_map.89.refs_0_), channel_id=1, source_target_pairs={{0,48},{8,392},{16,0},{24,408},{32,16},{40,424},{48,32},{56,440},{... | collective-permute-start | bytes 1105928 | tf_op jit(solution)/shard_map/ppermute | solution.py:215
  33.9 22.4 %collective-permute-start.2 = (bf16[128,768]{1,0:T(8,128)(2,1)S(1)}, bf16[128,768]{1,0:T(8,128)(2,1)S(1)}, u32[]{:S(2)}, u32[]{:S(2)}) collective-permute-start(bf16[128,768]{1,0:T(8,128)(2,1)S(1)} %slice.8), channel_id=1, source_target_pairs={{4,64},{68,0},{8,12},{72,76},{5,65},{69,1},{9,13},{73,77},{6,66},{... | collective-permute-start | bytes 589832 | tf_op jit(solution)/shard_map/ppermute | solution.py:268
  48.2 8.1 %collective-permute-start.4 = (bf16[112,768]{1,0:T(8,128)(2,1)S(1)}, bf16[112,768]{1,0:T(8,128)(2,1)S(1)}, u32[]{:S(2)}, u32[]{:S(2)}) collective-permute-start(bf16[112,768]{1,0:T(8,128)(2,1)S(1)} %slice.9), channel_id=1, source_target_pairs={{4,0},{68,64},{8,76},{72,12},{5,1},{69,65},{9,77},{73,13},{6,2},{7... | collective-permute-start | bytes 516104 | tf_op jit(solution)/shard_map/ppermute | solution.py:268
  56.3 76.1 %all-to-all-start = ((bf16[8,64,2560]{2,1,0:T(8,128)(2,1)}), bf16[8,64,2560]{2,1,0:T(8,128)(2,1)}, u32[]{:S(2)}, u32[]{:S(2)}) async-start(bf16[8,64,2560]{2,1,0:T(8,128)(2,1)} %get-tuple-element.12), calls=%async_computation | async-start | bytes 5242880 | tf_op jit(solution)/shard_map/all_to_all | solution.py:297
  62.5 9.8 %collective-permute-start.12 = (bf16[240,768]{1,0:T(8,128)(2,1)S(1)}, bf16[240,768]{1,0:T(8,128)(2,1)S(1)}, u32[]{:S(2)}, u32[]{:S(2)}) collective-permute-start(bf16[240,768]{1,0:T(8,128)(2,1)S(1)} %shard_map.92.refs_0_), channel_id=1, source_target_pairs={{0,16},{8,136},{16,32},{24,152},{32,48},{40,168},{48,0},{56,184},{... | collective-permute-start | bytes 1105928 | tf_op jit(solution)/shard_map/ppermute | solution.py:215
  65.2 11.1 %collective-permute-start.7 = (bf16[240,768]{1,0:T(8,128)(2,1)S(1)}, bf16[240,768]{1,0:T(8,128)(2,1)S(1)}, u32[]{:S(2)}, u32[]{:S(2)}) collective-permute-start(bf16[240,768]{1,0:T(8,128)(2,1)S(1)} %collective-permute-done.5.refs_1_), channel_id=1, source_target_pairs={{0,16},{8,136},{16,32},{24,152},{32,48},{40,168},{48,0},{56,184},{... | collective-permute-start | bytes 1105928 | tf_op jit(solution)/shard_map/ppermute | solution.py:215
  68.3 15.1 %collective-permute-start.13 = (bf16[240,768]{1,0:T(8,128)(2,1)S(1)}, bf16[240,768]{1,0:T(8,128)(2,1)S(1)}, u32[]{:S(2)}, u32[]{:S(2)}) collective-permute-start(bf16[240,768]{1,0:T(8,128)(2,1)S(1)} %shard_map.92.refs_0_), channel_id=1, source_target_pairs={{0,48},{8,392},{16,0},{24,408},{32,16},{40,424},{48,32},{56,440},{... | collective-permute-start | bytes 1105928 | tf_op jit(solution)/shard_map/ppermute | solution.py:215
  72.3 11.1 %collective-permute-start.14 = (bf16[240,768]{1,0:T(8,128)(2,1)S(1)}, bf16[240,768]{1,0:T(8,128)(2,1)S(1)}, u32[]{:S(2)}, u32[]{:S(2)}) collective-permute-start(bf16[240,768]{1,0:T(8,128)(2,1)S(1)} %collective-permute-done.12.refs_1_), channel_id=1, source_target_pairs={{0,16},{8,136},{16,32},{24,152},{32,48},{40,168},{48,0},{56,184},{... | collective-permute-start | bytes 1105928 | tf_op jit(solution)/shard_map/ppermute | solution.py:215
  76.9 23.5 %copy-start = (bf16[960,768]{1,0:T(8,128)(2,1)}, bf16[960,768]{1,0:T(8,128)(2,1)S(1)}, u32[]{:S(2)}) copy-start(bf16[960,768]{1,0:T(8,128)(2,1)S(1)} %shard_map.90.refs_0_) | copy-start | bytes 4423684
  76.9 22.4 %collective-permute-start.8 = (bf16[960,768]{1,0:T(8,128)(2,1)S(1)}, bf16[960,768]{1,0:T(8,128)(2,1)S(1)}, u32[]{:S(2)}, u32[]{:S(2)}) collective-permute-start(bf16[960,768]{1,0:T(8,128)(2,1)S(1)} %shard_map.90.refs_0_), channel_id=1, source_target_pairs={{0,128},{8,24},{16,144},{24,40},{32,160},{40,56},{48,176},{56,8},{... | collective-permute-start | bytes 4423688 | tf_op jit(solution)/shard_map/ppermute | solution.py:215
  79.2 20.5 %collective-permute-start.9 = (bf16[960,768]{1,0:T(8,128)(2,1)S(1)}, bf16[960,768]{1,0:T(8,128)(2,1)S(1)}, u32[]{:S(2)}, u32[]{:S(2)}) collective-permute-start(bf16[960,768]{1,0:T(8,128)(2,1)S(1)} %shard_map.90.refs_0_), channel_id=1, source_target_pairs={{0,384},{8,56},{16,400},{24,8},{32,416},{40,24},{48,432},{56,40},{... | collective-permute-start | bytes 4423688 | tf_op jit(solution)/shard_map/ppermute | solution.py:215
  84.1 16.9 %copy-start.3 = (bf16[960,768]{1,0:T(8,128)(2,1)}, bf16[960,768]{1,0:T(8,128)(2,1)S(1)}, u32[]{:S(2)}) copy-start(bf16[960,768]{1,0:T(8,128)(2,1)S(1)} %shard_map.93.refs_5_) | copy-start | bytes 4423684
  84.1 30.9 %collective-permute-start.15 = (bf16[960,768]{1,0:T(8,128)(2,1)S(1)}, bf16[960,768]{1,0:T(8,128)(2,1)S(1)}, u32[]{:S(2)}, u32[]{:S(2)}) collective-permute-start(bf16[960,768]{1,0:T(8,128)(2,1)S(1)} %shard_map.93.refs_5_), channel_id=1, source_target_pairs={{0,128},{8,24},{16,144},{24,40},{32,160},{40,56},{48,176},{56,8},{... | collective-permute-start | bytes 4423688 | tf_op jit(solution)/shard_map/ppermute | solution.py:215
  86.0 29.5 %collective-permute-start.16 = (bf16[960,768]{1,0:T(8,128)(2,1)S(1)}, bf16[960,768]{1,0:T(8,128)(2,1)S(1)}, u32[]{:S(2)}, u32[]{:S(2)}) collective-permute-start(bf16[960,768]{1,0:T(8,128)(2,1)S(1)} %shard_map.93.refs_5_), channel_id=1, source_target_pairs={{0,384},{8,56},{16,400},{24,8},{32,416},{40,24},{48,432},{56,40},{... | collective-permute-start | bytes 4423688 | tf_op jit(solution)/shard_map/ppermute | solution.py:215
  99.3 1.2 copy-start.1
  99.7 1.2 copy-start.2
  100.9 23.7 %collective-permute-start.10 = (bf16[480,768]{1,0:T(8,128)(2,1)S(1)}, bf16[480,768]{1,0:T(8,128)(2,1)}, u32[]{:S(2)}, u32[]{:S(2)}) collective-permute-start(bf16[480,768]{1,0:T(8,128)(2,1)S(1)} %get-tuple-element.13), channel_id=1, source_target_pairs={{0,128},{8,24},{16,144},{24,40},{32,160},{40,56},{48,176},{56,8},{... | collective-permute-start | bytes 2211848 | tf_op jit(solution)/shard_map/ppermute | solution.py:215
  104.1 20.5 %collective-permute-start.11 = (bf16[480,768]{1,0:T(8,128)(2,1)S(1)}, bf16[480,768]{1,0:T(8,128)(2,1)}, u32[]{:S(2)}, u32[]{:S(2)}) collective-permute-start(bf16[480,768]{1,0:T(8,128)(2,1)S(1)} %get-tuple-element.14), channel_id=1, source_target_pairs={{0,384},{8,56},{16,400},{24,8},{32,416},{40,24},{48,432},{56,40},{... | collective-permute-start | bytes 2211848 | tf_op jit(solution)/shard_map/ppermute | solution.py:215
  115.0 1.2 copy-start.4
  115.5 1.1 copy-start.5
  116.7 14.6 %collective-permute-start.17 = (bf16[480,768]{1,0:T(8,128)(2,1)S(1)}, bf16[480,768]{1,0:T(8,128)(2,1)}, u32[]{:S(2)}, u32[]{:S(2)}) collective-permute-start(bf16[480,768]{1,0:T(8,128)(2,1)S(1)} %get-tuple-element.16), channel_id=1, source_target_pairs={{0,128},{8,24},{16,144},{24,40},{32,160},{40,56},{48,176},{56,8},{... | collective-permute-start | bytes 2211848 | tf_op jit(solution)/shard_map/ppermute | solution.py:215
  119.8 12.6 %collective-permute-start.18 = (bf16[480,768]{1,0:T(8,128)(2,1)S(1)}, bf16[480,768]{1,0:T(8,128)(2,1)}, u32[]{:S(2)}, u32[]{:S(2)}) collective-permute-start(bf16[480,768]{1,0:T(8,128)(2,1)S(1)} %get-tuple-element.17), channel_id=1, source_target_pairs={{0,384},{8,56},{16,400},{24,8},{32,416},{40,24},{48,432},{56,40},{... | collective-permute-start | bytes 2211848 | tf_op jit(solution)/shard_map/ppermute | solution.py:215
  144.2 8.5 %copy-start.10 = (bf16[256,6]{0,1:T(8,128)(2,1)S(1)}, bf16[256,6]{0,1:T(8,128)(2,1)}, u32[]{:S(2)}) copy-start(bf16[256,6]{0,1:T(8,128)(2,1)} %param.10) | copy-start | bytes 9220
  144.2 41.4 %copy-start.6 = (s32[256,6]{1,0:T(8,128)S(1)}, s32[256,6]{1,0:T(8,128)}, u32[]{:S(2)}) copy-start(s32[256,6]{1,0:T(8,128)} %copy.10.routes_ref) | copy-start | bytes 18436
  144.2 41.4 %copy-start.8 = (bf16[256,256]{1,0:T(8,128)(2,1)S(1)}, bf16[256,256]{1,0:T(8,128)(2,1)}, u32[]{:S(2)}) copy-start(bf16[256,256]{1,0:T(8,128)(2,1)} %get-tuple-element.10.sel_ref) | copy-start | bytes 393220
  144.2 41.4 %all-to-all-start.1 = ((bf16[8,32,2688]{2,1,0:T(8,128)(2,1)}), bf16[8,32,2688]{2,1,0:T(8,128)(2,1)S(1)}, u32[]{:S(2)}, u32[]{:S(2)}) async-start(bf16[8,32,2688]{2,1,0:T(8,128)(2,1)} %shard_map.95), calls=%async_computation.1 | async-start | bytes 2752512 | tf_op jit(solution)/shard_map/all_to_all | solution.py:317

commit v7 on v6

--- a/solution.py
+++ b/solution.py
@@ -14,19 +14,19 @@
 PAD = 128
 
 
-def route_place(routes, slots):
-    tokens = routes.shape[0]
+def slots_of(routes):
+    tokens = routes.shape[1]
     window = routes < 8
-    owner = jnp.sum(jnp.where(window, routes, 0), axis=1, keepdims=True)
-    routed = jnp.sum(jnp.where(window, 1, 0), axis=1, keepdims=True) > 0
-    lane = lax.broadcasted_iota(jnp.int32, (tokens, 128), 1)
-    onehot = jnp.where((lane == owner) & routed, 1.0, 0.0)
+    owner = jnp.sum(jnp.where(window, routes, 0), axis=0, keepdims=True)
+    routed = jnp.sum(jnp.where(window, 1, 0), axis=0, keepdims=True) > 0
+    expert = lax.broadcasted_iota(jnp.int32, (16, tokens), 0)
+    onehot = jnp.where((expert == owner) & routed, 1.0, 0.0)
     row = lax.broadcasted_iota(jnp.int32, (tokens, tokens), 0)
     col = lax.broadcasted_iota(jnp.int32, (tokens, tokens), 1)
-    lower = jnp.where(col <= row, 1.0, 0.0).astype(BF)
-    rank = jnp.dot(lower, onehot.astype(BF), preferred_element_type=F32)
-    slot = jnp.sum(rank * onehot, axis=1, keepdims=True).astype(jnp.int32) - 1
-    return jnp.where(routed, owner * slots + slot, -1)
+    upto = jnp.where(row <= col, 1.0, 0.0).astype(BF)
+    rank = jnp.dot(onehot.astype(BF), upto, preferred_element_type=F32)
+    slot = jnp.sum(rank * onehot, axis=0, keepdims=True).astype(jnp.int32) - 1
+    return jnp.where(routed, owner * 32 + slot, -1)
 
 
 def dispatch_kernel(routes_ref, tok_ref, cot_ref, out_ref, sel_ref):
@@ -34,33 +34,34 @@
 
     @pl.when(pl.program_id(0) == 0)
     def _():
-        place = route_place(routes_ref[...], 32)
-        lane = lax.broadcasted_iota(jnp.int32, (tokens, 256), 1)
-        sel_ref[...] = jnp.where(lane == place, 1.0, 0.0).astype(BF)
+        slot = lax.broadcasted_iota(jnp.int32, (256, tokens), 0)
+        sel_ref[...] = jnp.where(slot == slots_of(routes_ref[...]), 1.0, 0.0).astype(BF)
 
     sel = sel_ref[...]
     for source, first in ((tok_ref, 0), (cot_ref, 32)):
-        rows = lax.dot_general(
-            sel, source[...], (((0,), (0,)), ((), ())), preferred_element_type=F32
-        ).astype(BF)
+        rows = jnp.dot(sel, source[...], preferred_element_type=F32).astype(BF)
         out_ref[:, first : first + 32, :] = rows.reshape(8, 32, step)
 
 
 def combine_kernel(routes_ref, gates_ref, sel_ref, back_ref, grad_ref, score_ref):
     width = grad_ref.shape[1]
     window = routes_ref[...] < 8
-    gate = jnp.sum(jnp.where(window, gates_ref[...].astype(F32), 0.0), axis=1, keepdims=True)
+    gate = jnp.sum(jnp.where(window, gates_ref[...].astype(F32), 0.0), axis=0, keepdims=True)
     sel = sel_ref[...]
+    scaled = (sel.astype(F32) * gate).astype(BF)
+    down = (((0,), (0,)), ((), ()))
     step = 512
 
     @pl.loop(0, width // step)
     def _(i):
         cols = pl.ds(pl.multiple_of(i * step, step), step)
         rows = back_ref[:, :, cols].reshape(256, step)
-        grad_ref[:, cols] = (jnp.dot(sel, rows, preferred_element_type=F32) * gate).astype(BF)
+        grad_ref[:, cols] = lax.dot_general(
+            scaled, rows, down, preferred_element_type=F32
+        ).astype(BF)
 
     tail = back_ref[:, :, width : width + PAD].reshape(256, PAD)
-    score = jnp.dot(sel, tail, preferred_element_type=F32)[:, 0:1]
+    score = lax.dot_general(tail, sel, down, preferred_element_type=F32)[0:1]
     score_ref[...] = jnp.where(window, score, 0.0).astype(BF)
 
 
@@ -78,7 +79,10 @@
             out_ref[row : row + 40] = jnp.where(swap == (k == 0), mine, theirs)
 
 
-def near_kernel(source_ref, mine, low, out_ref):
+def near_kernel(source_ref, mine, low, high, out_ref, top_ref, bottom_ref):
+    cut = top_ref.shape[0]
+    top_ref[...] = low[:cut]
+    bottom_ref[...] = high[cut:]
     out_ref[...] = jnp.where(source_ref[0] == 1, mine[...], low[...])
 
 
@@ -230,7 +234,7 @@
     near = (0, 3, 1, 2)
     pieces = [(first + n, k * count, chain, far, near[k]) for n, far in enumerate((0, 3, 1)) for k in range(4)]
     pieces += [(first + 3 + k // 2, k % 2 * count, chain, 2, near[k]) for k in range(4)]
-    return (line, line_low, line_high, far0, far1), pieces, (low, high)
+    return (line, line_low, line_high, far0, far1), pieces, (low, high, opposite)
 
 
 def on_device(tokens_in, cotangent, routes, gate_weights, gate_proj, up_proj, down_proj):
@@ -249,16 +253,16 @@
     other = lax.ppermute(shard, ("c", "zq"), [(2, 0), (1, 3)])
     smem = pl.BlockSpec(memory_space=pltpu.SMEM)
 
-    def small(kernel, flag, *arrays):
+    def small(kernel, flag, arrays, rows):
         return pl.pallas_call(
             kernel,
-            out_shape=jax.ShapeDtypeStruct((240, hidden_width), BF),
+            out_shape=[jax.ShapeDtypeStruct((r, hidden_width), BF) for r in rows],
             in_specs=[smem] + [VM] * len(arrays),
-            out_specs=VM,
+            out_specs=[VM] * len(rows),
             compiler_params=params(4),
         )(flag.astype(jnp.int32)[None], *arrays)
 
-    pair = small(pair_kernel, ic, shard, other)
+    (pair,) = small(pair_kernel, ic, (shard, other), (240,))
 
     def at(c, p):
         return (p // 2 * 2 + c) * 2 + p % 2
@@ -269,11 +273,6 @@
 
     source = ic == zq
     low, high = zmove(pair, True, 1), zmove(pair, True, -1)
-    first = small(near_kernel, source, pair, low)
-    far0, far1 = zmove(low[:SPLIT], False, 1), zmove(high[SPLIT:], False, -1)
-    second = small(far_kernel, source, far0, far1, high)
-    first_half = jnp.where(source, zh, jnp.where((ring == 1) | (ring == 2), 0, 1))
-
     step = 512
     columns = pl.BlockSpec((256, step), lambda i: (0, i))
     payload, sel = pl.pallas_call(
@@ -283,20 +282,26 @@
             jax.ShapeDtypeStruct((8, 64, width), BF),
             jax.ShapeDtypeStruct((256, 256), BF),
         ),
-        in_specs=[pl.BlockSpec(routes.shape, lambda i: (0, 0)), columns, columns],
+        in_specs=[pl.BlockSpec((6, 256), lambda i: (0, 0)), columns, columns],
         out_specs=(
             pl.BlockSpec((8, 64, step), lambda i: (0, 0, i)),
             pl.BlockSpec((256, 256), lambda i: (0, 0)),
         ),
         compiler_params=params(56),
         cost_estimate=cost(2 * 256 * 512 * width, 8 * 256 * width),
-    )(routes, tokens_in, cotangent)
+    )(routes.T, tokens_in, cotangent)
+
+    low, high, payload = lax.optimization_barrier((low, high, payload))
+    first, top, bottom = small(near_kernel, source, (pair, low, high), (240, SPLIT, 240 - SPLIT))
+    far0, far1 = zmove(top, False, 1), zmove(bottom, False, -1)
+    (second,) = small(far_kernel, source, (far0, far1, high), (240,))
+    first_half = jnp.where(source, zh, jnp.where((ring == 1) | (ring == 2), 0, 1))
 
     arrays, pieces, near = torus_gather(first, 0, 0)
-    payload, *_ = lax.optimization_barrier((payload, far0, far1, *near))
+    second, *_ = lax.optimization_barrier((second, near[0]))
+    more_arrays, more_pieces, near2 = torus_gather(second, 1, len(arrays))
+    payload, *_ = lax.optimization_barrier((payload, far0, far1, near2[0], arrays[0]))
     rows = lax.all_to_all(payload, ("c", "zr"), split_axis=0, concat_axis=0, tiled=True)
-    second, *_ = lax.optimization_barrier((second, *near))
-    more_arrays, more_pieces, _ = torus_gather(second, 1, len(arrays))
     arrays, pieces = arrays + more_arrays, pieces + more_pieces
 
     back = pl.pallas_call(
@@ -316,17 +321,18 @@
 
     home = lax.all_to_all(back, ("c", "zr"), split_axis=0, concat_axis=0, tiled=True)
 
-    return pl.pallas_call(
+    grad_tokens, grad_gates = pl.pallas_call(
         combine_kernel,
         out_shape=(
             jax.ShapeDtypeStruct(tokens_in.shape, BF),
-            jax.ShapeDtypeStruct(gate_weights.shape, BF),
+            jax.ShapeDtypeStruct((6, 256), BF),
         ),
         in_specs=[VM] * 4,
         out_specs=(VM, VM),
         compiler_params=params(),
         cost_estimate=cost(2 * 256 * 256 * width, 4 * 256 * width),
-    )(routes, gate_weights, sel, home)
+    )(routes.T, gate_weights.T, sel, home)
+    return grad_tokens, grad_gates.T
 
 
 def solution(mesh):

time: 190 us -> 196 us (1.032)
  blocking collectives: 0 us -> 42.1 us
  waiting for transfers between devices: 72.4 us -> 52.7 us
  starting transfers between devices: 86.7 us -> 72.6 us
    all_to_all x0 -> x1, blocking collectives: none -> 42.1 us  [on_device(): lax.all_to_all(back, ('c', 'zr'), split_axis=0, concat_axis=0, tiled=True)]
    all_to_all x1 -> x0, waiting for transfers between devices: 32.8 us -> none  [on_device(): lax.all_to_all(back, ('c', 'zr'), split_axis=0, concat_axis=0, tiled=True)]
    ppermute x14, waiting for transfers between devices: 26.9 us -> 35.7 us  [shift(): return lax.ppermute(v, ('x', 'y', 'c'), pairs)]
    all_to_all x1 -> x0, starting transfers between devices: 8.47 us -> none  [on_device(): lax.all_to_all(back, ('c', 'zr'), split_axis=0, concat_axis=0, tiled=True)]
    ppermute x4, starting transfers between devices: 18.2 us -> 10.9 us  [zmove(): return lax.ppermute(v, ('zh', 'c', 'zq'), pairs)]
    ppermute x4, waiting for transfers between devices: 11.5 us -> 15.8 us  [zmove(): return lax.ppermute(v, ('zh', 'c', 'zq'), pairs)]
    all_to_all x1, starting transfers between devices: 6.18 us -> 10.5 us  [on_device(): lax.all_to_all(payload, ('c', 'zr'), split_axis=0, concat_axis=0, tiled=T...]
    ppermute x14, starting transfers between devices: 45 us -> 42.4 us  [shift(): return lax.ppermute(v, ('x', 'y', 'c'), pairs)]
  transfers between devices with their start and end apart: 21 -> 20, of which waited for: 11 -> 13; matrix products, arithmetic and copies ran while one was open for 1% -> 0% of each run, Pallas kernels for 5% -> 4%
where the time goes in v7:
time: 196 us; the launch traced here: 195 us
  starting transfers between devices  72.6 us (37%)
  waiting for transfers between devices  52.7 us (27%)
  blocking collectives  42.1 us (21%)
  Pallas kernels  23.8 us (12%)
  local copies, waits for them, and re-layouts  2.02 us (1%)
    ppermute x14, starting transfers between devices, shift(): return lax.ppermute(v, ('x', 'y', 'c'), pairs)  42.4 us
    all_to_all x1, blocking collectives, on_device(): lax.all_to_all(back, ('c', 'zr'), split_axis=0, concat_axis=0, tiled=True)  42.1 us
    ppermute x14, waiting for transfers between devices, shift(): return lax.ppermute(v, ('x', 'y', 'c'), pairs)  35.7 us
    ppermute x4, waiting for transfers between devices, zmove(): return lax.ppermute(v, ('zh', 'c', 'zq'), pairs)  15.8 us
    pallas_call x1, Pallas kernels, on_device(): pl.pallas_call(functools.partial(expert_kernel, pieces), out_shape=jax.Sh...  11.7 us
    ppermute x4, starting transfers between devices, zmove(): return lax.ppermute(v, ('zh', 'c', 'zq'), pairs)  10.9 us
    all_to_all x1, starting transfers between devices, on_device(): lax.all_to_all(payload, ('c', 'zr'), split_axis=0, concat_axis=0, tiled=T...  10.5 us
    ppermute x1, starting transfers between devices, on_device(): other = lax.ppermute(shard, ('c', 'zq'), [(2, 0), (1, 3)])  8.78 us
  transfers between devices with their start and end apart: 20, of which 13 were waited for; matrix products, arithmetic and copies ran while one was open for 0% of the time, Pallas kernels for 4%

profile of v7, /device:TPU:1, one launch (start us, length us, event | category | flops | bytes accessed | tf_op | source)
XLA Modules:
  0.0 194.8 jit_solution(16020888955649096236)
XLA Ops:
  2.2 8.8 %collective-permute-start = (bf16[3,40,768]{2,1,0:T(8,128)(2,1)}, bf16[3,40,768]{2,1,0:T(8,128)(2,1)S(1)}, u32[]{:S(2)}, u32[]{:S(2)}) collective-permute-start(bf16[3,40,768]{2,1,0:T(8,128)(2,1)} %shard_map.87.shard_ref), channel_id=1, source_target_pairs={{8,0},{4,12},{9,1},{5,13},{10,2},{6,14},{11,3},{7,15},{24,16},{20,... | collective-permute-start | bytes 552968 | tf_op jit(solution)/shard_map/ppermute | solution.py:253
  15.8 5.6 %shard_map.86 = (bf16[8,64,2560]{2,1,0:T(8,128)(2,1)}, bf16[256,256]{1,0:T(8,128)(2,1)}) custom-call(s32[6,256]{1,0:T(8,128)} %bitcast.8, bf16[256,2560]{1,0:T(8,128)(2,1)} %tok_ref.1, bf16[256,2560]{1,0:T(8,128)(2,1)} %cot_ref.1), custom_call_target="tpu_custom_call" | custom-call | flops 671088640 | bytes 5242880 | tf_op jit(solution)/shard_map/pallas_call | solution.py:278
  21.3 12.7 %collective-permute-done.2.high = bf16[240,768]{1,0:T(8,128)(2,1)S(1)} collective-permute-done((bf16[240,768]{1,0:T(8,128)(2,1)S(1)}, bf16[240,768]{1,0:T(8,128)(2,1)S(1)}, u32[]{:S(2)}, u32[]{:S(2)}) %collective-permute-start.2) | collective-permute-done | bytes 368672 | tf_op jit(solution)/shard_map/ppermute | solution.py:272
  34.8 3.1 %collective-permute-start.5 = (bf16[240,768]{1,0:T(8,128)(2,1)S(1)}, bf16[240,768]{1,0:T(8,128)(2,1)S(1)}, u32[]{:S(2)}, u32[]{:S(2)}) collective-permute-start(bf16[240,768]{1,0:T(8,128)(2,1)S(1)} %get-tuple-element.25.refs_0_), channel_id=1, source_target_pairs={{0,16},{8,136},{16,32},{24,152},{32,48},{40,168},{48,0},{56,184},{... | collective-permute-start | bytes 1105928 | tf_op jit(solution)/shard_map/ppermute | solution.py:219
  37.9 3.0 %collective-permute-start.3 = (bf16[128,768]{1,0:T(8,128)(2,1)S(1)}, bf16[128,768]{1,0:T(8,128)(2,1)S(1)}, u32[]{:S(2)}, u32[]{:S(2)}) collective-permute-start(bf16[128,768]{1,0:T(8,128)(2,1)S(1)} %get-tuple-element.23), channel_id=1, source_target_pairs={{4,64},{68,0},{8,12},{72,76},{5,65},{69,1},{9,13},{73,77},{6,66},{... | collective-permute-start | bytes 589832 | tf_op jit(solution)/shard_map/ppermute | solution.py:272
  41.0 5.2 %collective-permute-start.4 = (bf16[112,768]{1,0:T(8,128)(2,1)S(1)}, bf16[112,768]{1,0:T(8,128)(2,1)S(1)}, u32[]{:S(2)}, u32[]{:S(2)}) collective-permute-start(bf16[112,768]{1,0:T(8,128)(2,1)S(1)} %get-tuple-element.24), channel_id=1, source_target_pairs={{4,0},{68,64},{8,76},{72,12},{5,1},{69,65},{9,77},{73,13},{6,2},{7... | collective-permute-start | bytes 516104 | tf_op jit(solution)/shard_map/ppermute | solution.py:272
  46.2 3.2 %collective-permute-start.7 = (bf16[240,768]{1,0:T(8,128)(2,1)S(1)}, bf16[240,768]{1,0:T(8,128)(2,1)S(1)}, u32[]{:S(2)}, u32[]{:S(2)}) collective-permute-start(bf16[240,768]{1,0:T(8,128)(2,1)S(1)} %get-tuple-element.25.refs_0_), channel_id=1, source_target_pairs={{0,48},{8,392},{16,0},{24,408},{32,16},{40,424},{48,32},{56,440},{... | collective-permute-start | bytes 1105928 | tf_op jit(solution)/shard_map/ppermute | solution.py:219
  49.4 2.4 %collective-permute-done.4.bottom = bf16[112,768]{1,0:T(8,128)(2,1)S(1)} collective-permute-done((bf16[112,768]{1,0:T(8,128)(2,1)S(1)}, bf16[112,768]{1,0:T(8,128)(2,1)S(1)}, u32[]{:S(2)}, u32[]{:S(2)}) %collective-permute-start.4) | collective-permute-done | bytes 172064 | tf_op jit(solution)/shard_map/ppermute | solution.py:272
  51.9 3.1 %collective-permute-start.8 = (bf16[240,768]{1,0:T(8,128)(2,1)S(1)}, bf16[240,768]{1,0:T(8,128)(2,1)S(1)}, u32[]{:S(2)}, u32[]{:S(2)}) collective-permute-start(bf16[240,768]{1,0:T(8,128)(2,1)S(1)} %collective-permute-done.5.refs_1_), channel_id=1, source_target_pairs={{0,16},{8,136},{16,32},{24,152},{32,48},{40,168},{48,0},{56,184},{... | collective-permute-start | bytes 1105928 | tf_op jit(solution)/shard_map/ppermute | solution.py:219
  55.0 3.1 %collective-permute-start.6 = (bf16[240,768]{1,0:T(8,128)(2,1)S(1)}, bf16[240,768]{1,0:T(8,128)(2,1)S(1)}, u32[]{:S(2)}, u32[]{:S(2)}) collective-permute-start(bf16[240,768]{1,0:T(8,128)(2,1)S(1)} %shard_map.90.refs_0_), channel_id=1, source_target_pairs={{0,16},{8,136},{16,32},{24,152},{32,48},{40,168},{48,0},{56,184},{... | collective-permute-start | bytes 1105928 | tf_op jit(solution)/shard_map/ppermute | solution.py:219
  58.2 3.4 %collective-permute-done.8.refs_3_ = bf16[240,768]{1,0:T(8,128)(2,1)S(1)} collective-permute-done((bf16[240,768]{1,0:T(8,128)(2,1)S(1)}, bf16[240,768]{1,0:T(8,128)(2,1)S(1)}, u32[]{:S(2)}, u32[]{:S(2)}) %collective-permute-start.8) | collective-permute-done | bytes 368672 | tf_op jit(solution)/shard_map/ppermute | solution.py:219
  62.2 3.6 %collective-permute-done.6.refs_1_ = bf16[240,768]{1,0:T(8,128)(2,1)S(1)} collective-permute-done((bf16[240,768]{1,0:T(8,128)(2,1)S(1)}, bf16[240,768]{1,0:T(8,128)(2,1)S(1)}, u32[]{:S(2)}, u32[]{:S(2)}) %collective-permute-start.6) | collective-permute-done | bytes 368672 | tf_op jit(solution)/shard_map/ppermute | solution.py:219
  65.8 10.5 %all-to-all-start = ((bf16[8,64,2560]{2,1,0:T(8,128)(2,1)}), bf16[8,64,2560]{2,1,0:T(8,128)(2,1)}, u32[]{:S(2)}, u32[]{:S(2)}) async-start(bf16[8,64,2560]{2,1,0:T(8,128)(2,1)} %get-tuple-element.27), calls=%async_computation | async-start | bytes 5242880 | tf_op jit(solution)/shard_map/all_to_all | solution.py:304
  76.3 4.4 %collective-permute-start.13 = (bf16[240,768]{1,0:T(8,128)(2,1)S(1)}, bf16[240,768]{1,0:T(8,128)(2,1)S(1)}, u32[]{:S(2)}, u32[]{:S(2)}) collective-permute-start(bf16[240,768]{1,0:T(8,128)(2,1)S(1)} %shard_map.90.refs_0_), channel_id=1, source_target_pairs={{0,48},{8,392},{16,0},{24,408},{32,16},{40,424},{48,32},{56,440},{... | collective-permute-start | bytes 1105928 | tf_op jit(solution)/shard_map/ppermute | solution.py:219
  80.7 1.9 collective-permute-start.14
  82.7 2.4 %collective-permute-start.10 = (bf16[960,768]{1,0:T(8,128)(2,1)S(1)}, bf16[960,768]{1,0:T(8,128)(2,1)S(1)}, u32[]{:S(2)}, u32[]{:S(2)}) collective-permute-start(bf16[960,768]{1,0:T(8,128)(2,1)S(1)} %shard_map.91.refs_0_), channel_id=1, source_target_pairs={{0,384},{8,56},{16,400},{24,8},{32,416},{40,24},{48,432},{56,40},{... | collective-permute-start | bytes 4423688 | tf_op jit(solution)/shard_map/ppermute | solution.py:219
  85.1 2.9 %collective-permute-start.9 = (bf16[960,768]{1,0:T(8,128)(2,1)S(1)}, bf16[960,768]{1,0:T(8,128)(2,1)S(1)}, u32[]{:S(2)}, u32[]{:S(2)}) collective-permute-start(bf16[960,768]{1,0:T(8,128)(2,1)S(1)} %shard_map.91.refs_0_), channel_id=1, source_target_pairs={{0,128},{8,24},{16,144},{24,40},{32,160},{40,56},{48,176},{56,8},{... | collective-permute-start | bytes 4423688 | tf_op jit(solution)/shard_map/ppermute | solution.py:219
  88.0 2.3 %collective-permute-done.14.refs_3_ = bf16[240,768]{1,0:T(8,128)(2,1)S(1)} collective-permute-done((bf16[240,768]{1,0:T(8,128)(2,1)S(1)}, bf16[240,768]{1,0:T(8,128)(2,1)S(1)}, u32[]{:S(2)}, u32[]{:S(2)}) %collective-permute-start.14) | collective-permute-done | bytes 368672 | tf_op jit(solution)/shard_map/ppermute | solution.py:219
  90.9 2.3 %collective-permute-start.16 = (bf16[960,768]{1,0:T(8,128)(2,1)S(1)}, bf16[960,768]{1,0:T(8,128)(2,1)S(1)}, u32[]{:S(2)}, u32[]{:S(2)}) collective-permute-start(bf16[960,768]{1,0:T(8,128)(2,1)S(1)} %shard_map.93.refs_5_), channel_id=1, source_target_pairs={{0,384},{8,56},{16,400},{24,8},{32,416},{40,24},{48,432},{56,40},{... | collective-permute-start | bytes 4423688 | tf_op jit(solution)/shard_map/ppermute | solution.py:219
  93.2 2.9 %collective-permute-start.15 = (bf16[960,768]{1,0:T(8,128)(2,1)S(1)}, bf16[960,768]{1,0:T(8,128)(2,1)S(1)}, u32[]{:S(2)}, u32[]{:S(2)}) collective-permute-start(bf16[960,768]{1,0:T(8,128)(2,1)S(1)} %shard_map.93.refs_5_), channel_id=1, source_target_pairs={{0,128},{8,24},{16,144},{24,40},{32,160},{40,56},{48,176},{56,8},{... | collective-permute-start | bytes 4423688 | tf_op jit(solution)/shard_map/ppermute | solution.py:219
  96.2 7.0 %collective-permute-done.10.refs_1_.refs_2_ = bf16[960,768]{1,0:T(8,128)(2,1)S(1)} collective-permute-done((bf16[960,768]{1,0:T(8,128)(2,1)S(1)}, bf16[960,768]{1,0:T(8,128)(2,1)S(1)}, u32[]{:S(2)}, u32[]{:S(2)}) %collective-permute-start.10) | collective-permute-done | bytes 1474592 | tf_op jit(solution)/shard_map/ppermute | solution.py:219
  103.2 3.5 %collective-permute-done.9.refs_0_.refs_1_ = bf16[960,768]{1,0:T(8,128)(2,1)S(1)} collective-permute-done((bf16[960,768]{1,0:T(8,128)(2,1)S(1)}, bf16[960,768]{1,0:T(8,128)(2,1)S(1)}, u32[]{:S(2)}, u32[]{:S(2)}) %collective-permute-start.9) | collective-permute-done | bytes 1474592 | tf_op jit(solution)/shard_map/ppermute | solution.py:219
  107.9 1.9 collective-permute-start.11
  109.8 4.6 %collective-permute-start.12 = (bf16[480,768]{1,0:T(8,128)(2,1)S(1)}, bf16[480,768]{1,0:T(8,128)(2,1)}, u32[]{:S(2)}, u32[]{:S(2)}) collective-permute-start(bf16[480,768]{1,0:T(8,128)(2,1)S(1)} %get-tuple-element.29), channel_id=1, source_target_pairs={{0,384},{8,56},{16,400},{24,8},{32,416},{40,24},{48,432},{56,40},{... | collective-permute-start | bytes 2211848 | tf_op jit(solution)/shard_map/ppermute | solution.py:219
  114.4 4.6 %collective-permute-done.16.refs_1_.refs_7_ = bf16[960,768]{1,0:T(8,128)(2,1)S(1)} collective-permute-done((bf16[960,768]{1,0:T(8,128)(2,1)S(1)}, bf16[960,768]{1,0:T(8,128)(2,1)S(1)}, u32[]{:S(2)}, u32[]{:S(2)}) %collective-permute-start.16) | collective-permute-done | bytes 1474592 | tf_op jit(solution)/shard_map/ppermute | solution.py:219
  119.0 3.6 %collective-permute-done.15.refs_0_.refs_6_ = bf16[960,768]{1,0:T(8,128)(2,1)S(1)} collective-permute-done((bf16[960,768]{1,0:T(8,128)(2,1)S(1)}, bf16[960,768]{1,0:T(8,128)(2,1)S(1)}, u32[]{:S(2)}, u32[]{:S(2)}) %collective-permute-start.15) | collective-permute-done | bytes 1474592 | tf_op jit(solution)/shard_map/ppermute | solution.py:219
  123.7 1.9 collective-permute-start.17
  125.7 4.6 %collective-permute-start.18 = (bf16[480,768]{1,0:T(8,128)(2,1)S(1)}, bf16[480,768]{1,0:T(8,128)(2,1)}, u32[]{:S(2)}, u32[]{:S(2)}) collective-permute-start(bf16[480,768]{1,0:T(8,128)(2,1)S(1)} %get-tuple-element.31), channel_id=1, source_target_pairs={{0,384},{8,56},{16,400},{24,8},{32,416},{40,24},{48,432},{56,40},{... | collective-permute-start | bytes 2211848 | tf_op jit(solution)/shard_map/ppermute | solution.py:219
  130.9 7.5 %collective-permute-done.17.refs_8_ = bf16[480,768]{1,0:T(8,128)(2,1)} collective-permute-done((bf16[480,768]{1,0:T(8,128)(2,1)S(1)}, bf16[480,768]{1,0:T(8,128)(2,1)}, u32[]{:S(2)}, u32[]{:S(2)}) %collective-permute-start.17) | collective-permute-done | bytes 737312 | tf_op jit(solution)/shard_map/ppermute | solution.py:219
  138.6 11.7 %shard_map.95 = bf16[8,32,2688]{2,1,0:T(8,128)(2,1)} custom-call(s32[4]{0:T(128)} %pad_add_fusion.where_ref, bf16[8,64,2560]{2,1,0:T(8,128)(2,1)} %all-to-all-done.rows_ref, bf16[960,768]{1,0:T(8,128)(2,1)} %copy-done, bf16[960,768]{1,0:T(8,128)(2,1)} %copy-done.2, bf16[960,768]{1,0:T(8,128)(2,1)} %copy-done.1, ...), custom_call_target="tpu_custom_call" | custom-call | flops 5033164800 | bytes 11796480 | tf_op jit(solution)/shard_map/pallas_call | solution.py:307
  150.4 42.1 %all_to_all.10.back_ref = bf16[8,32,2688]{2,1,0:T(8,128)(2,1)S(1)} all-to-all(bf16[8,32,2688]{2,1,0:T(8,128)(2,1)} %shard_map.95), channel_id=1, replica_groups=mesh['x'=4,'zh'=2,'y'=4,'c'=2,'zq'=2,'zr'=4] {'c','zr'}, dimensions={0} | all-to-all | bytes 2752512 | tf_op jit(solution)/shard_map/all_to_all | solution.py:322
  192.5 2.3 %shard_map.96 = (bf16[256,2560]{1,0:T(8,128)(2,1)}, bf16[6,256]{1,0:T(8,128)(2,1)}) custom-call(s32[6,256]{1,0:T(8,128)S(1)} %bitcast.9, bf16[6,256]{1,0:T(8,128)(2,1)S(1)} %bitcast.10, bf16[256,256]{1,0:T(8,128)(2,1)S(1)} %copy-done.7, bf16[8,32,2688]{2,1,0:T(8,128)(2,1)S(1)} %all_to_all.10.back_ref), custom_call_target="tpu_custom_call" | custom-call | flops 335544320 | bytes 2621440 | tf_op jit(solution)/shard_map/pallas_call | solution.py:324
  (41 shorter events, 11.6 us)
Async XLA Ops:
  2.2 10.0 %collective-permute-start = (bf16[3,40,768]{2,1,0:T(8,128)(2,1)}, bf16[3,40,768]{2,1,0:T(8,128)(2,1)S(1)}, u32[]{:S(2)}, u32[]{:S(2)}) collective-permute-start(bf16[3,40,768]{2,1,0:T(8,128)(2,1)} %shard_map.87.shard_ref), channel_id=1, source_target_pairs={{8,0},{4,12},{9,1},{5,13},{10,2},{6,14},{11,3},{7,15},{24,16},{20,... | collective-permute-start | bytes 552968 | tf_op jit(solution)/shard_map/ppermute | solution.py:253
  12.2 0.9 copy-start.6
  13.2 20.9 %collective-permute-start.2 = (bf16[240,768]{1,0:T(8,128)(2,1)S(1)}, bf16[240,768]{1,0:T(8,128)(2,1)S(1)}, u32[]{:S(2)}, u32[]{:S(2)}) collective-permute-start(bf16[240,768]{1,0:T(8,128)(2,1)S(1)} %shard_map.88.mine), channel_id=1, source_target_pairs={{0,68},{64,4},{12,8},{76,72},{1,69},{65,5},{13,9},{77,73},{2,70},{... | collective-permute-start | bytes 1105928 | tf_op jit(solution)/shard_map/ppermute | solution.py:272
  14.5 20.3 %collective-permute-start.1 = (bf16[240,768]{1,0:T(8,128)(2,1)S(1)}, bf16[240,768]{1,0:T(8,128)(2,1)S(1)}, u32[]{:S(2)}, u32[]{:S(2)}) collective-permute-start(bf16[240,768]{1,0:T(8,128)(2,1)S(1)} %shard_map.88.mine), channel_id=1, source_target_pairs={{0,4},{64,68},{12,72},{76,8},{1,5},{65,69},{13,73},{77,9},{2,6},{6... | collective-permute-start | bytes 1105928 | tf_op jit(solution)/shard_map/ppermute | solution.py:272
  34.8 17.1 %collective-permute-start.5 = (bf16[240,768]{1,0:T(8,128)(2,1)S(1)}, bf16[240,768]{1,0:T(8,128)(2,1)S(1)}, u32[]{:S(2)}, u32[]{:S(2)}) collective-permute-start(bf16[240,768]{1,0:T(8,128)(2,1)S(1)} %get-tuple-element.25.refs_0_), channel_id=1, source_target_pairs={{0,16},{8,136},{16,32},{24,152},{32,48},{40,168},{48,0},{56,184},{... | collective-permute-start | bytes 1105928 | tf_op jit(solution)/shard_map/ppermute | solution.py:219
  37.9 13.9 %collective-permute-start.3 = (bf16[128,768]{1,0:T(8,128)(2,1)S(1)}, bf16[128,768]{1,0:T(8,128)(2,1)S(1)}, u32[]{:S(2)}, u32[]{:S(2)}) collective-permute-start(bf16[128,768]{1,0:T(8,128)(2,1)S(1)} %get-tuple-element.23), channel_id=1, source_target_pairs={{4,64},{68,0},{8,12},{72,76},{5,65},{69,1},{9,13},{73,77},{6,66},{... | collective-permute-start | bytes 589832 | tf_op jit(solution)/shard_map/ppermute | solution.py:272
  41.0 10.9 %collective-permute-start.4 = (bf16[112,768]{1,0:T(8,128)(2,1)S(1)}, bf16[112,768]{1,0:T(8,128)(2,1)S(1)}, u32[]{:S(2)}, u32[]{:S(2)}) collective-permute-start(bf16[112,768]{1,0:T(8,128)(2,1)S(1)} %get-tuple-element.24), channel_id=1, source_target_pairs={{4,0},{68,64},{8,76},{72,12},{5,1},{69,65},{9,77},{73,13},{6,2},{7... | collective-permute-start | bytes 516104 | tf_op jit(solution)/shard_map/ppermute | solution.py:272
  46.2 11.9 %collective-permute-start.7 = (bf16[240,768]{1,0:T(8,128)(2,1)S(1)}, bf16[240,768]{1,0:T(8,128)(2,1)S(1)}, u32[]{:S(2)}, u32[]{:S(2)}) collective-permute-start(bf16[240,768]{1,0:T(8,128)(2,1)S(1)} %get-tuple-element.25.refs_0_), channel_id=1, source_target_pairs={{0,48},{8,392},{16,0},{24,408},{32,16},{40,424},{48,32},{56,440},{... | collective-permute-start | bytes 1105928 | tf_op jit(solution)/shard_map/ppermute | solution.py:219
  51.9 9.7 %collective-permute-start.8 = (bf16[240,768]{1,0:T(8,128)(2,1)S(1)}, bf16[240,768]{1,0:T(8,128)(2,1)S(1)}, u32[]{:S(2)}, u32[]{:S(2)}) collective-permute-start(bf16[240,768]{1,0:T(8,128)(2,1)S(1)} %collective-permute-done.5.refs_1_), channel_id=1, source_target_pairs={{0,16},{8,136},{16,32},{24,152},{32,48},{40,168},{48,0},{56,184},{... | collective-permute-start | bytes 1105928 | tf_op jit(solution)/shard_map/ppermute | solution.py:219
  55.0 10.8 %collective-permute-start.6 = (bf16[240,768]{1,0:T(8,128)(2,1)S(1)}, bf16[240,768]{1,0:T(8,128)(2,1)S(1)}, u32[]{:S(2)}, u32[]{:S(2)}) collective-permute-start(bf16[240,768]{1,0:T(8,128)(2,1)S(1)} %shard_map.90.refs_0_), channel_id=1, source_target_pairs={{0,16},{8,136},{16,32},{24,152},{32,48},{40,168},{48,0},{56,184},{... | collective-permute-start | bytes 1105928 | tf_op jit(solution)/shard_map/ppermute | solution.py:219
  62.2 22.8 %copy-start = (bf16[960,768]{1,0:T(8,128)(2,1)}, bf16[960,768]{1,0:T(8,128)(2,1)S(1)}, u32[]{:S(2)}) copy-start(bf16[960,768]{1,0:T(8,128)(2,1)S(1)} %shard_map.91.refs_0_) | copy-start | bytes 4423684
  65.8 72.8 %all-to-all-start = ((bf16[8,64,2560]{2,1,0:T(8,128)(2,1)}), bf16[8,64,2560]{2,1,0:T(8,128)(2,1)}, u32[]{:S(2)}, u32[]{:S(2)}) async-start(bf16[8,64,2560]{2,1,0:T(8,128)(2,1)} %get-tuple-element.27), calls=%async_computation | async-start | bytes 5242880 | tf_op jit(solution)/shard_map/all_to_all | solution.py:304
  76.3 11.6 %collective-permute-start.13 = (bf16[240,768]{1,0:T(8,128)(2,1)S(1)}, bf16[240,768]{1,0:T(8,128)(2,1)S(1)}, u32[]{:S(2)}, u32[]{:S(2)}) collective-permute-start(bf16[240,768]{1,0:T(8,128)(2,1)S(1)} %shard_map.90.refs_0_), channel_id=1, source_target_pairs={{0,48},{8,392},{16,0},{24,408},{32,16},{40,424},{48,32},{56,440},{... | collective-permute-start | bytes 1105928 | tf_op jit(solution)/shard_map/ppermute | solution.py:219
  80.7 9.5 %collective-permute-start.14 = (bf16[240,768]{1,0:T(8,128)(2,1)S(1)}, bf16[240,768]{1,0:T(8,128)(2,1)S(1)}, u32[]{:S(2)}, u32[]{:S(2)}) collective-permute-start(bf16[240,768]{1,0:T(8,128)(2,1)S(1)} %collective-permute-done.6.refs_1_), channel_id=1, source_target_pairs={{0,16},{8,136},{16,32},{24,152},{32,48},{40,168},{48,0},{56,184},{... | collective-permute-start | bytes 1105928 | tf_op jit(solution)/shard_map/ppermute | solution.py:219
  82.7 20.5 %collective-permute-start.10 = (bf16[960,768]{1,0:T(8,128)(2,1)S(1)}, bf16[960,768]{1,0:T(8,128)(2,1)S(1)}, u32[]{:S(2)}, u32[]{:S(2)}) collective-permute-start(bf16[960,768]{1,0:T(8,128)(2,1)S(1)} %shard_map.91.refs_0_), channel_id=1, source_target_pairs={{0,384},{8,56},{16,400},{24,8},{32,416},{40,24},{48,432},{56,40},{... | collective-permute-start | bytes 4423688 | tf_op jit(solution)/shard_map/ppermute | solution.py:219
  85.1 21.6 %collective-permute-start.9 = (bf16[960,768]{1,0:T(8,128)(2,1)S(1)}, bf16[960,768]{1,0:T(8,128)(2,1)S(1)}, u32[]{:S(2)}, u32[]{:S(2)}) collective-permute-start(bf16[960,768]{1,0:T(8,128)(2,1)S(1)} %shard_map.91.refs_0_), channel_id=1, source_target_pairs={{0,128},{8,24},{16,144},{24,40},{32,160},{40,56},{48,176},{56,8},{... | collective-permute-start | bytes 4423688 | tf_op jit(solution)/shard_map/ppermute | solution.py:219
  90.9 17.0 %copy-start.3 = (bf16[960,768]{1,0:T(8,128)(2,1)}, bf16[960,768]{1,0:T(8,128)(2,1)S(1)}, u32[]{:S(2)}) copy-start(bf16[960,768]{1,0:T(8,128)(2,1)S(1)} %shard_map.93.refs_5_) | copy-start | bytes 4423684
  90.9 28.1 %collective-permute-start.16 = (bf16[960,768]{1,0:T(8,128)(2,1)S(1)}, bf16[960,768]{1,0:T(8,128)(2,1)S(1)}, u32[]{:S(2)}, u32[]{:S(2)}) collective-permute-start(bf16[960,768]{1,0:T(8,128)(2,1)S(1)} %shard_map.93.refs_5_), channel_id=1, source_target_pairs={{0,384},{8,56},{16,400},{24,8},{32,416},{40,24},{48,432},{56,40},{... | collective-permute-start | bytes 4423688 | tf_op jit(solution)/shard_map/ppermute | solution.py:219
  93.2 29.3 %collective-permute-start.15 = (bf16[960,768]{1,0:T(8,128)(2,1)S(1)}, bf16[960,768]{1,0:T(8,128)(2,1)S(1)}, u32[]{:S(2)}, u32[]{:S(2)}) collective-permute-start(bf16[960,768]{1,0:T(8,128)(2,1)S(1)} %shard_map.93.refs_5_), channel_id=1, source_target_pairs={{0,128},{8,24},{16,144},{24,40},{32,160},{40,56},{48,176},{56,8},{... | collective-permute-start | bytes 4423688 | tf_op jit(solution)/shard_map/ppermute | solution.py:219
  103.2 4.2 %copy-start.1 = (bf16[960,768]{1,0:T(8,128)(2,1)}, bf16[960,768]{1,0:T(8,128)(2,1)S(1)}, u32[]{:S(2)}) copy-start(bf16[960,768]{1,0:T(8,128)(2,1)S(1)} %collective-permute-done.10.refs_1_.refs_2_) | copy-start | bytes 4423684
  106.7 1.2 copy-start.2
  107.9 23.0 %collective-permute-start.11 = (bf16[480,768]{1,0:T(8,128)(2,1)S(1)}, bf16[480,768]{1,0:T(8,128)(2,1)}, u32[]{:S(2)}, u32[]{:S(2)}) collective-permute-start(bf16[480,768]{1,0:T(8,128)(2,1)S(1)} %get-tuple-element.28), channel_id=1, source_target_pairs={{0,128},{8,24},{16,144},{24,40},{32,160},{40,56},{48,176},{56,8},{... | collective-permute-start | bytes 2211848 | tf_op jit(solution)/shard_map/ppermute | solution.py:219
  109.8 21.1 %collective-permute-start.12 = (bf16[480,768]{1,0:T(8,128)(2,1)S(1)}, bf16[480,768]{1,0:T(8,128)(2,1)}, u32[]{:S(2)}, u32[]{:S(2)}) collective-permute-start(bf16[480,768]{1,0:T(8,128)(2,1)S(1)} %get-tuple-element.29), channel_id=1, source_target_pairs={{0,384},{8,56},{16,400},{24,8},{32,416},{40,24},{48,432},{56,40},{... | collective-permute-start | bytes 2211848 | tf_op jit(solution)/shard_map/ppermute | solution.py:219
  119.0 4.3 %copy-start.4 = (bf16[960,768]{1,0:T(8,128)(2,1)}, bf16[960,768]{1,0:T(8,128)(2,1)S(1)}, u32[]{:S(2)}) copy-start(bf16[960,768]{1,0:T(8,128)(2,1)S(1)} %collective-permute-done.16.refs_1_.refs_7_) | copy-start | bytes 4423684
  122.6 1.2 copy-start.5
  123.7 14.6 %collective-permute-start.17 = (bf16[480,768]{1,0:T(8,128)(2,1)S(1)}, bf16[480,768]{1,0:T(8,128)(2,1)}, u32[]{:S(2)}, u32[]{:S(2)}) collective-permute-start(bf16[480,768]{1,0:T(8,128)(2,1)S(1)} %get-tuple-element.30), channel_id=1, source_target_pairs={{0,128},{8,24},{16,144},{24,40},{32,160},{40,56},{48,176},{56,8},{... | collective-permute-start | bytes 2211848 | tf_op jit(solution)/shard_map/ppermute | solution.py:219
  125.7 13.0 %collective-permute-start.18 = (bf16[480,768]{1,0:T(8,128)(2,1)S(1)}, bf16[480,768]{1,0:T(8,128)(2,1)}, u32[]{:S(2)}, u32[]{:S(2)}) collective-permute-start(bf16[480,768]{1,0:T(8,128)(2,1)S(1)} %get-tuple-element.31), channel_id=1, source_target_pairs={{0,384},{8,56},{16,400},{24,8},{32,416},{40,24},{48,432},{56,40},{... | collective-permute-start | bytes 2211848 | tf_op jit(solution)/shard_map/ppermute | solution.py:219
  150.4 42.1 %copy-start.7 = (bf16[256,256]{1,0:T(8,128)(2,1)S(1)}, bf16[256,256]{1,0:T(8,128)(2,1)}, u32[]{:S(2)}) copy-start(bf16[256,256]{1,0:T(8,128)(2,1)} %get-tuple-element.18.sel_ref) | copy-start | bytes 393220
  150.4 42.1 %copy-start.8 = (s32[256,6]{0,1:T(8,128)S(1)}, s32[256,6]{0,1:T(8,128)}, u32[]{:S(2)}) copy-start(s32[256,6]{0,1:T(8,128)} %param.9) | copy-start | bytes 18436
  150.4 42.1 %copy-start.9 = (bf16[256,6]{0,1:T(8,128)(2,1)S(1)}, bf16[256,6]{0,1:T(8,128)(2,1)}, u32[]{:S(2)}) copy-start(bf16[256,6]{0,1:T(8,128)(2,1)} %param.10) | copy-start | bytes 9220

commit v8 on v7

--- a/solution.py
+++ b/solution.py
@@ -43,11 +43,19 @@
         out_ref[:, first : first + 32, :] = rows.reshape(8, 32, step)
 
 
-def combine_kernel(routes_ref, gates_ref, sel_ref, back_ref, grad_ref, score_ref):
+def combine_kernel(where_ref, routes_ref, gates_ref, sel_ref, *refs):
+    back_refs, (grad_ref, score_ref) = refs[:8], refs[8:]
     width = grad_ref.shape[1]
     window = routes_ref[...] < 8
     gate = jnp.sum(jnp.where(window, gates_ref[...].astype(F32), 0.0), axis=0, keepdims=True)
-    sel = sel_ref[...]
+    core, place = where_ref[2], where_ref[4]
+    sel = jnp.concatenate(
+        [
+            sel_ref[pl.ds(pl.multiple_of(partner(core, place, r) * 32, 32), 32), :]
+            for r in range(8)
+        ],
+        axis=0,
+    )
     scaled = (sel.astype(F32) * gate).astype(BF)
     down = (((0,), (0,)), ((), ()))
     step = 512
@@ -55,12 +63,12 @@
     @pl.loop(0, width // step)
     def _(i):
         cols = pl.ds(pl.multiple_of(i * step, step), step)
-        rows = back_ref[:, :, cols].reshape(256, step)
+        rows = jnp.concatenate([ref[:, cols] for ref in back_refs], axis=0)
         grad_ref[:, cols] = lax.dot_general(
             scaled, rows, down, preferred_element_type=F32
         ).astype(BF)
 
-    tail = back_ref[:, :, width : width + PAD].reshape(256, PAD)
+    tail = jnp.concatenate([ref[:, width : width + PAD] for ref in back_refs], axis=0)
     score = lax.dot_general(tail, sel, down, preferred_element_type=F32)[0:1]
     score_ref[...] = jnp.where(window, score, 0.0).astype(BF)
 
@@ -79,10 +87,8 @@
             out_ref[row : row + 40] = jnp.where(swap == (k == 0), mine, theirs)
 
 
-def near_kernel(source_ref, mine, low, high, out_ref, top_ref, bottom_ref):
-    cut = top_ref.shape[0]
-    top_ref[...] = low[:cut]
-    bottom_ref[...] = high[cut:]
+def near_kernel(source_ref, mine, low, out_ref, top_ref):
+    top_ref[...] = low[: top_ref.shape[0]]
     out_ref[...] = jnp.where(source_ref[0] == 1, mine[...], low[...])
 
 
@@ -93,13 +99,17 @@
     out_ref[cut:] = jnp.where(source, bottom[...], high[cut:])
 
 
+def partner(core, place, r):
+    return jnp.bitwise_xor(core, r // 4) * 4 + jnp.bitwise_xor(place, r % 4)
+
+
 def expert_kernel(pieces, where_ref, rows_ref, *refs):
     sources = refs[: pieces[-1][0] + 1]
-    out_ref = refs[len(sources)]
+    out_refs = refs[len(sources) : len(sources) + 8]
     gate_w, up_w, down_w, tok_v, cot_v, result, grad_a, grad_b, pre_g, pre_u, pre_b, sems, out_sems = refs[
-        len(sources) + 1 :
+        len(sources) + 8 :
     ]
-    my_x, my_y, core, first_half = where_ref[0], where_ref[1], where_ref[2], where_ref[3]
+    my_x, my_y, core, first_half, place = (where_ref[i] for i in range(5))
     width, hidden_width = gate_w.shape
 
     gate_copies, up_copies, down_copies = [], [], []
@@ -162,8 +172,12 @@
         rows = rows + lax.dot_general(b, up_w[i * dstep : (i + 1) * dstep, :], dims, preferred_element_type=F32)
         result[:, :, i * dstep : (i + 1) * dstep] = rows.astype(BF).reshape(8, 32, dstep)
         part = pl.ds(i * dstep, dstep if i == 0 else dstep + PAD)
-        outs.append(pltpu.make_async_copy(result.at[:, :, part], out_ref.at[:, :, part], out_sems.at[i]))
-        outs[i].start()
+        for r, out_ref in enumerate(out_refs):
+            copy = pltpu.make_async_copy(
+                result.at[partner(core, place, r), :, part], out_ref.at[:, part], out_sems.at[i]
+            )
+            copy.start()
+            outs.append(copy)
     for copy in outs:
         copy.wait()
 
@@ -273,6 +287,11 @@
 
     source = ic == zq
     low, high = zmove(pair, True, 1), zmove(pair, True, -1)
+    first, top = small(near_kernel, source, (pair, low), (240, SPLIT))
+    far0, far1 = zmove(top, False, 1), zmove(high[SPLIT:], False, -1)
+    (second,) = small(far_kernel, source, (far0, far1, high), (240,))
+    first_half = jnp.where(source, zh, jnp.where((ring == 1) | (ring == 2), 0, 1))
+
     step = 512
     columns = pl.BlockSpec((256, step), lambda i: (0, i))
     payload, sel = pl.pallas_call(
@@ -291,24 +310,19 @@
         cost_estimate=cost(2 * 256 * 512 * width, 8 * 256 * width),
     )(routes.T, tokens_in, cotangent)
 
-    low, high, payload = lax.optimization_barrier((low, high, payload))
-    first, top, bottom = small(near_kernel, source, (pair, low, high), (240, SPLIT, 240 - SPLIT))
-    far0, far1 = zmove(top, False, 1), zmove(bottom, False, -1)
-    (second,) = small(far_kernel, source, (far0, far1, high), (240,))
-    first_half = jnp.where(source, zh, jnp.where((ring == 1) | (ring == 2), 0, 1))
-
     arrays, pieces, near = torus_gather(first, 0, 0)
-    second, *_ = lax.optimization_barrier((second, near[0]))
-    more_arrays, more_pieces, near2 = torus_gather(second, 1, len(arrays))
-    payload, *_ = lax.optimization_barrier((payload, far0, far1, near2[0], arrays[0]))
+    payload, *_ = lax.optimization_barrier((payload, far0, far1, *near[:2]))
     rows = lax.all_to_all(payload, ("c", "zr"), split_axis=0, concat_axis=0, tiled=True)
+    second, *_ = lax.optimization_barrier((second, *near[:2]))
+    more_arrays, more_pieces, _ = torus_gather(second, 1, len(arrays))
     arrays, pieces = arrays + more_arrays, pieces + more_pieces
 
+    where = jnp.stack([ix, iy, ic, first_half, lax.axis_index("zr")]).astype(jnp.int32)
     back = pl.pallas_call(
         functools.partial(expert_kernel, pieces),
-        out_shape=jax.ShapeDtypeStruct((8, 32, width + PAD), BF),
+        out_shape=[jax.ShapeDtypeStruct((32, width + PAD), BF)] * 8,
         in_specs=[smem] + [ANY] * (1 + len(arrays)),
-        out_specs=ANY,
+        out_specs=[ANY] * 8,
         scratch_shapes=[pltpu.VMEM((width, hidden_width), BF)] * 3
         + [pltpu.VMEM((8, 32, width), BF)] * 2
         + [pltpu.VMEM((8, 32, width + PAD), BF)]
@@ -317,9 +331,13 @@
         + [pltpu.SemaphoreType.DMA((5,)), pltpu.SemaphoreType.DMA((2,))],
         compiler_params=params(56),
         cost_estimate=cost(10 * 256 * width * hidden_width, 6 * width * hidden_width),
-    )(jnp.stack([ix, iy, ic, first_half]).astype(jnp.int32), rows, *arrays)
-
-    home = lax.all_to_all(back, ("c", "zr"), split_axis=0, concat_axis=0, tiled=True)
+    )(where, rows, *arrays)
+
+    home = {0: back[0]}
+    for r in (4, 3, 7, 2, 6, 1, 5):
+        pairs = [(d, (d // 4 ^ r // 4) * 4 + (d % 4 ^ r % 4)) for d in range(8)]
+        home[r] = lax.ppermute(back[r], ("c", "zr"), pairs)
+    home = [home[r] for r in range(8)]
 
     grad_tokens, grad_gates = pl.pallas_call(
         combine_kernel,
@@ -327,11 +345,11 @@
             jax.ShapeDtypeStruct(tokens_in.shape, BF),
             jax.ShapeDtypeStruct((6, 256), BF),
         ),
-        in_specs=[VM] * 4,
+        in_specs=[smem] + [VM] * 11,
         out_specs=(VM, VM),
         compiler_params=params(),
         cost_estimate=cost(2 * 256 * 256 * width, 4 * 256 * width),
-    )(routes.T, gate_weights.T, sel, home)
+    )(where, routes.T, gate_weights.T, sel, *home)
     return grad_tokens, grad_gates.T
 
 

time: 196 us -> 186 us (0.949)
  blocking collectives: 42.1 us -> 0 us
  starting transfers between devices: 72.6 us -> 105 us
  waiting for transfers between devices: 52.7 us -> 49.3 us
    all_to_all x1 -> x0, blocking collectives: 42.1 us -> none  [on_device(): lax.all_to_all(back, ('c', 'zr'), split_axis=0, concat_axis=0, tiled=True)]
    ppermute x0 -> x7, starting transfers between devices: none -> 26.3 us  [on_device(): home[r] = lax.ppermute(back[r], ('c', 'zr'), pairs)]
    ppermute x0 -> x7, waiting for transfers between devices: none -> 9.36 us  [on_device(): home[r] = lax.ppermute(back[r], ('c', 'zr'), pairs)]
    ppermute x14, waiting for transfers between devices: 35.7 us -> 26.9 us  [shift(): return lax.ppermute(v, ('x', 'y', 'c'), pairs)]
    ppermute x4, starting transfers between devices: 10.9 us -> 18.2 us  [zmove(): return lax.ppermute(v, ('zh', 'c', 'zq'), pairs)]
    ppermute x4, waiting for transfers between devices: 15.8 us -> 11.8 us  [zmove(): return lax.ppermute(v, ('zh', 'c', 'zq'), pairs)]
    all_to_all x1, starting transfers between devices: 10.5 us -> 7.1 us  [on_device(): lax.all_to_all(payload, ('c', 'zr'), split_axis=0, concat_axis=0, tiled=T...]
    ppermute x14, starting transfers between devices: 42.4 us -> 45 us  [shift(): return lax.ppermute(v, ('x', 'y', 'c'), pairs)]
  transfers between devices with their start and end apart: 20 -> 27, of which waited for: 13 -> 13; matrix products, arithmetic and copies ran while one was open for 0% -> 0% of each run, Pallas kernels for 4% -> 4%
where the time goes in v8:
time: 186 us; the launch traced here: 184 us
  starting transfers between devices  105 us (56%)
  waiting for transfers between devices  49.3 us (27%)
  Pallas kernels  24.4 us (13%)
  local copies, waits for them, and re-layouts  3.59 us (2%)
    ppermute x14, starting transfers between devices, shift(): return lax.ppermute(v, ('x', 'y', 'c'), pairs)  45 us
    ppermute x14, waiting for transfers between devices, shift(): return lax.ppermute(v, ('x', 'y', 'c'), pairs)  26.9 us
    ppermute x7, starting transfers between devices, on_device(): home[r] = lax.ppermute(back[r], ('c', 'zr'), pairs)  26.3 us
    ppermute x4, starting transfers between devices, zmove(): return lax.ppermute(v, ('zh', 'c', 'zq'), pairs)  18.2 us
    ppermute x4, waiting for transfers between devices, zmove(): return lax.ppermute(v, ('zh', 'c', 'zq'), pairs)  11.8 us
    pallas_call x1, Pallas kernels, on_device(): pl.pallas_call(functools.partial(expert_kernel, pieces), out_shape=[jax.S...  11.7 us
    ppermute x7, waiting for transfers between devices, on_device(): home[r] = lax.ppermute(back[r], ('c', 'zr'), pairs)  9.36 us
    ppermute x1, starting transfers between devices, on_device(): other = lax.ppermute(shard, ('c', 'zq'), [(2, 0), (1, 3)])  8.78 us
  transfers between devices with their start and end apart: 27, of which 13 were waited for; matrix products, arithmetic and copies ran while one was open for 0% of the time, Pallas kernels for 4%

profile of v8, /device:TPU:1, one launch (start us, length us, event | category | flops | bytes accessed | tf_op | source)
XLA Modules:
  0.0 183.7 jit_solution(2824493029390800063)
XLA Ops:
  2.2 8.8 %collective-permute-start = (bf16[3,40,768]{2,1,0:T(8,128)(2,1)}, bf16[3,40,768]{2,1,0:T(8,128)(2,1)S(1)}, u32[]{:S(2)}, u32[]{:S(2)}) collective-permute-start(bf16[3,40,768]{2,1,0:T(8,128)(2,1)} %shard_map.87.shard_ref), channel_id=1, source_target_pairs={{8,0},{4,12},{9,1},{5,13},{10,2},{6,14},{11,3},{7,15},{24,16},{20,... | collective-permute-start | bytes 552968 | tf_op jit(solution)/shard_map/ppermute | solution.py:267
  15.8 11.5 %collective-permute-done.1.low = bf16[240,768]{1,0:T(8,128)(2,1)S(1)} collective-permute-done((bf16[240,768]{1,0:T(8,128)(2,1)S(1)}, bf16[240,768]{1,0:T(8,128)(2,1)S(1)}, u32[]{:S(2)}, u32[]{:S(2)}) %collective-permute-start.1) | collective-permute-done | bytes 368672 | tf_op jit(solution)/shard_map/ppermute | solution.py:286
  27.3 1.9 %collective-permute-start.5 = (bf16[240,768]{1,0:T(8,128)(2,1)S(1)}, bf16[240,768]{1,0:T(8,128)(2,1)S(1)}, u32[]{:S(2)}, u32[]{:S(2)}) collective-permute-start(bf16[240,768]{1,0:T(8,128)(2,1)S(1)} %get-tuple-element.25.refs_0_), channel_id=1, source_target_pairs={{0,16},{8,136},{16,32},{24,152},{32,48},{40,168},{48,0},{56,184},{... | collective-permute-start | bytes 1105928 | tf_op jit(solution)/shard_map/ppermute | solution.py:233
  29.2 4.6 %collective-permute-start.6 = (bf16[240,768]{1,0:T(8,128)(2,1)S(1)}, bf16[240,768]{1,0:T(8,128)(2,1)S(1)}, u32[]{:S(2)}, u32[]{:S(2)}) collective-permute-start(bf16[240,768]{1,0:T(8,128)(2,1)S(1)} %get-tuple-element.25.refs_0_), channel_id=1, source_target_pairs={{0,48},{8,392},{16,0},{24,408},{32,16},{40,424},{48,32},{56,440},{... | collective-permute-start | bytes 1105928 | tf_op jit(solution)/shard_map/ppermute | solution.py:233
  33.8 14.3 %collective-permute-start.2 = (bf16[128,768]{1,0:T(8,128)(2,1)S(1)}, bf16[128,768]{1,0:T(8,128)(2,1)S(1)}, u32[]{:S(2)}, u32[]{:S(2)}) collective-permute-start(bf16[128,768]{1,0:T(8,128)(2,1)S(1)} %get-tuple-element.24), channel_id=1, source_target_pairs={{4,64},{68,0},{8,12},{72,76},{5,65},{69,1},{9,13},{73,77},{6,66},{... | collective-permute-start | bytes 589832 | tf_op jit(solution)/shard_map/ppermute | solution.py:286
  49.5 5.6 %shard_map.86 = (bf16[8,64,2560]{2,1,0:T(8,128)(2,1)}, bf16[256,256]{1,0:T(8,128)(2,1)}) custom-call(s32[6,256]{1,0:T(8,128)} %bitcast.9, bf16[256,2560]{1,0:T(8,128)(2,1)} %tok_ref.1, bf16[256,2560]{1,0:T(8,128)(2,1)} %cot_ref.1), custom_call_target="tpu_custom_call" | custom-call | flops 671088640 | bytes 5242880 | tf_op jit(solution)/shard_map/pallas_call | solution.py:297
  55.4 7.1 %all-to-all-start = ((bf16[8,64,2560]{2,1,0:T(8,128)(2,1)}), bf16[8,64,2560]{2,1,0:T(8,128)(2,1)}, u32[]{:S(2)}, u32[]{:S(2)}) async-start(bf16[8,64,2560]{2,1,0:T(8,128)(2,1)} %get-tuple-element.26), calls=%async_computation | async-start | bytes 5242880 | tf_op jit(solution)/shard_map/all_to_all | solution.py:315
  62.5 2.6 %collective-permute-start.12 = (bf16[240,768]{1,0:T(8,128)(2,1)S(1)}, bf16[240,768]{1,0:T(8,128)(2,1)S(1)}, u32[]{:S(2)}, u32[]{:S(2)}) collective-permute-start(bf16[240,768]{1,0:T(8,128)(2,1)S(1)} %shard_map.92.refs_0_), channel_id=1, source_target_pairs={{0,16},{8,136},{16,32},{24,152},{32,48},{40,168},{48,0},{56,184},{... | collective-permute-start | bytes 1105928 | tf_op jit(solution)/shard_map/ppermute | solution.py:233
  65.1 3.1 %collective-permute-start.7 = (bf16[240,768]{1,0:T(8,128)(2,1)S(1)}, bf16[240,768]{1,0:T(8,128)(2,1)S(1)}, u32[]{:S(2)}, u32[]{:S(2)}) collective-permute-start(bf16[240,768]{1,0:T(8,128)(2,1)S(1)} %collective-permute-done.5.refs_1_), channel_id=1, source_target_pairs={{0,16},{8,136},{16,32},{24,152},{32,48},{40,168},{48,0},{56,184},{... | collective-permute-start | bytes 1105928 | tf_op jit(solution)/shard_map/ppermute | solution.py:233
  68.3 3.4 %collective-permute-start.13 = (bf16[240,768]{1,0:T(8,128)(2,1)S(1)}, bf16[240,768]{1,0:T(8,128)(2,1)S(1)}, u32[]{:S(2)}, u32[]{:S(2)}) collective-permute-start(bf16[240,768]{1,0:T(8,128)(2,1)S(1)} %shard_map.92.refs_0_), channel_id=1, source_target_pairs={{0,48},{8,392},{16,0},{24,408},{32,16},{40,424},{48,32},{56,440},{... | collective-permute-start | bytes 1105928 | tf_op jit(solution)/shard_map/ppermute | solution.py:233
  74.2 2.0 %collective-permute-done.7.refs_3_ = bf16[240,768]{1,0:T(8,128)(2,1)S(1)} collective-permute-done((bf16[240,768]{1,0:T(8,128)(2,1)S(1)}, bf16[240,768]{1,0:T(8,128)(2,1)S(1)}, u32[]{:S(2)}, u32[]{:S(2)}) %collective-permute-start.7) | collective-permute-done | bytes 368672 | tf_op jit(solution)/shard_map/ppermute | solution.py:233
  76.9 2.3 %collective-permute-start.8 = (bf16[960,768]{1,0:T(8,128)(2,1)S(1)}, bf16[960,768]{1,0:T(8,128)(2,1)S(1)}, u32[]{:S(2)}, u32[]{:S(2)}) collective-permute-start(bf16[960,768]{1,0:T(8,128)(2,1)S(1)} %shard_map.90.refs_0_), channel_id=1, source_target_pairs={{0,128},{8,24},{16,144},{24,40},{32,160},{40,56},{48,176},{56,8},{... | collective-permute-start | bytes 4423688 | tf_op jit(solution)/shard_map/ppermute | solution.py:233
  79.2 4.2 %collective-permute-start.9 = (bf16[960,768]{1,0:T(8,128)(2,1)S(1)}, bf16[960,768]{1,0:T(8,128)(2,1)S(1)}, u32[]{:S(2)}, u32[]{:S(2)}) collective-permute-start(bf16[960,768]{1,0:T(8,128)(2,1)S(1)} %shard_map.90.refs_0_), channel_id=1, source_target_pairs={{0,384},{8,56},{16,400},{24,8},{32,416},{40,24},{48,432},{56,40},{... | collective-permute-start | bytes 4423688 | tf_op jit(solution)/shard_map/ppermute | solution.py:233
  84.1 1.9 %collective-permute-start.15 = (bf16[960,768]{1,0:T(8,128)(2,1)S(1)}, bf16[960,768]{1,0:T(8,128)(2,1)S(1)}, u32[]{:S(2)}, u32[]{:S(2)}) collective-permute-start(bf16[960,768]{1,0:T(8,128)(2,1)S(1)} %shard_map.93.refs_5_), channel_id=1, source_target_pairs={{0,128},{8,24},{16,144},{24,40},{32,160},{40,56},{48,176},{56,8},{... | collective-permute-start | bytes 4423688 | tf_op jit(solution)/shard_map/ppermute | solution.py:233
  86.0 4.6 %collective-permute-start.16 = (bf16[960,768]{1,0:T(8,128)(2,1)S(1)}, bf16[960,768]{1,0:T(8,128)(2,1)S(1)}, u32[]{:S(2)}, u32[]{:S(2)}) collective-permute-start(bf16[960,768]{1,0:T(8,128)(2,1)S(1)} %shard_map.93.refs_5_), channel_id=1, source_target_pairs={{0,384},{8,56},{16,400},{24,8},{32,416},{40,24},{48,432},{56,40},{... | collective-permute-start | bytes 4423688 | tf_op jit(solution)/shard_map/ppermute | solution.py:233
  90.6 8.7 %collective-permute-done.8.refs_0_.refs_1_ = bf16[960,768]{1,0:T(8,128)(2,1)S(1)} collective-permute-done((bf16[960,768]{1,0:T(8,128)(2,1)S(1)}, bf16[960,768]{1,0:T(8,128)(2,1)S(1)}, u32[]{:S(2)}, u32[]{:S(2)}) %collective-permute-start.8) | collective-permute-done | bytes 1474592 | tf_op jit(solution)/shard_map/ppermute | solution.py:233
  100.9 3.1 %collective-permute-start.10 = (bf16[480,768]{1,0:T(8,128)(2,1)S(1)}, bf16[480,768]{1,0:T(8,128)(2,1)}, u32[]{:S(2)}, u32[]{:S(2)}) collective-permute-start(bf16[480,768]{1,0:T(8,128)(2,1)S(1)} %get-tuple-element.27), channel_id=1, source_target_pairs={{0,128},{8,24},{16,144},{24,40},{32,160},{40,56},{48,176},{56,8},{... | collective-permute-start | bytes 2211848 | tf_op jit(solution)/shard_map/ppermute | solution.py:233
  104.0 4.1 %collective-permute-start.11 = (bf16[480,768]{1,0:T(8,128)(2,1)S(1)}, bf16[480,768]{1,0:T(8,128)(2,1)}, u32[]{:S(2)}, u32[]{:S(2)}) collective-permute-start(bf16[480,768]{1,0:T(8,128)(2,1)S(1)} %get-tuple-element.28), channel_id=1, source_target_pairs={{0,384},{8,56},{16,400},{24,8},{32,416},{40,24},{48,432},{56,40},{... | collective-permute-start | bytes 2211848 | tf_op jit(solution)/shard_map/ppermute | solution.py:233
  108.2 6.8 %collective-permute-done.15.refs_0_.refs_6_ = bf16[960,768]{1,0:T(8,128)(2,1)S(1)} collective-permute-done((bf16[960,768]{1,0:T(8,128)(2,1)S(1)}, bf16[960,768]{1,0:T(8,128)(2,1)S(1)}, u32[]{:S(2)}, u32[]{:S(2)}) %collective-permute-start.15) | collective-permute-done | bytes 1474592 | tf_op jit(solution)/shard_map/ppermute | solution.py:233
  116.6 3.2 %collective-permute-start.17 = (bf16[480,768]{1,0:T(8,128)(2,1)S(1)}, bf16[480,768]{1,0:T(8,128)(2,1)}, u32[]{:S(2)}, u32[]{:S(2)}) collective-permute-start(bf16[480,768]{1,0:T(8,128)(2,1)S(1)} %get-tuple-element.30), channel_id=1, source_target_pairs={{0,128},{8,24},{16,144},{24,40},{32,160},{40,56},{48,176},{56,8},{... | collective-permute-start | bytes 2211848 | tf_op jit(solution)/shard_map/ppermute | solution.py:233
  119.8 4.1 %collective-permute-start.18 = (bf16[480,768]{1,0:T(8,128)(2,1)S(1)}, bf16[480,768]{1,0:T(8,128)(2,1)}, u32[]{:S(2)}, u32[]{:S(2)}) collective-permute-start(bf16[480,768]{1,0:T(8,128)(2,1)S(1)} %get-tuple-element.31), channel_id=1, source_target_pairs={{0,384},{8,56},{16,400},{24,8},{32,416},{40,24},{48,432},{56,40},{... | collective-permute-start | bytes 2211848 | tf_op jit(solution)/shard_map/ppermute | solution.py:233
  124.6 6.6 %collective-permute-done.17.refs_8_ = bf16[480,768]{1,0:T(8,128)(2,1)} collective-permute-done((bf16[480,768]{1,0:T(8,128)(2,1)S(1)}, bf16[480,768]{1,0:T(8,128)(2,1)}, u32[]{:S(2)}, u32[]{:S(2)}) %collective-permute-start.17) | collective-permute-done | bytes 737312 | tf_op jit(solution)/shard_map/ppermute | solution.py:233
  132.4 11.7 %shard_map.95 = (bf16[32,2688]{1,0:T(8,128)(2,1)}, bf16[32,2688]{1,0:T(8,128)(2,1)}, bf16[32,2688]{1,0:T(8,128)(2,1)}, bf16[32,2688]{1,0:T(8,128)(2,1)}, bf16[32...) custom-call(s32[5]{0:T(128)} %stack.23.where_ref, ...), custom_call_target="tpu_custom_call" | custom-call | flops 5033164800 | bytes 11796480 | tf_op jit(solution)/shard_map/pallas_call | solution.py:321
  144.2 3.3 %collective-permute-start.19 = (bf16[32,2688]{1,0:T(8,128)(2,1)}, bf16[32,2688]{1,0:T(8,128)(2,1)S(1)}, u32[]{:S(2)}, u32[]{:S(2)}) collective-permute-start(bf16[32,2688]{1,0:T(8,128)(2,1)} %get-tuple-element.33), channel_id=1, source_target_pairs={{0,1},{1,0},{2,3},{3,2},{8,9},{9,8},{10,11},{11,10},{4,5},{5,4},{6... | collective-permute-start | bytes 516104 | tf_op jit(solution)/shard_map/ppermute | solution.py:339
  147.5 4.4 %collective-permute-start.20 = (bf16[32,2688]{1,0:T(8,128)(2,1)}, bf16[32,2688]{1,0:T(8,128)(2,1)S(1)}, u32[]{:S(2)}, u32[]{:S(2)}) collective-permute-start(bf16[32,2688]{1,0:T(8,128)(2,1)} %get-tuple-element.34), channel_id=1, source_target_pairs={{0,2},{1,3},{2,0},{3,1},{8,10},{9,11},{10,8},{11,9},{4,6},{5,7},{6... | collective-permute-start | bytes 516104 | tf_op jit(solution)/shard_map/ppermute | solution.py:339
  151.9 1.9 %collective-permute-start.21 = (bf16[32,2688]{1,0:T(8,128)(2,1)}, bf16[32,2688]{1,0:T(8,128)(2,1)S(1)}, u32[]{:S(2)}, u32[]{:S(2)}) collective-permute-start(bf16[32,2688]{1,0:T(8,128)(2,1)} %get-tuple-element.35), channel_id=1, source_target_pairs={{0,3},{1,2},{2,1},{3,0},{8,11},{9,10},{10,9},{11,8},{4,7},{5,6},{6... | collective-permute-start | bytes 516104 | tf_op jit(solution)/shard_map/ppermute | solution.py:339
  153.8 5.7 %collective-permute-start.22 = (bf16[32,2688]{1,0:T(8,128)(2,1)}, bf16[32,2688]{1,0:T(8,128)(2,1)S(1)}, u32[]{:S(2)}, u32[]{:S(2)}) collective-permute-start(bf16[32,2688]{1,0:T(8,128)(2,1)} %get-tuple-element.36), channel_id=1, source_target_pairs={{0,8},{1,9},{2,10},{3,11},{8,0},{9,1},{10,2},{11,3},{4,12},{5,13},... | collective-permute-start | bytes 516104 | tf_op jit(solution)/shard_map/ppermute | solution.py:339
  159.5 2.6 %collective-permute-start.23 = (bf16[32,2688]{1,0:T(8,128)(2,1)}, bf16[32,2688]{1,0:T(8,128)(2,1)S(1)}, u32[]{:S(2)}, u32[]{:S(2)}) collective-permute-start(bf16[32,2688]{1,0:T(8,128)(2,1)} %get-tuple-element.37), channel_id=1, source_target_pairs={{0,9},{1,8},{2,11},{3,10},{8,1},{9,0},{10,3},{11,2},{4,13},{5,12},... | collective-permute-start | bytes 516104 | tf_op jit(solution)/shard_map/ppermute | solution.py:339
  162.1 5.3 %collective-permute-start.24 = (bf16[32,2688]{1,0:T(8,128)(2,1)}, bf16[32,2688]{1,0:T(8,128)(2,1)S(1)}, u32[]{:S(2)}, u32[]{:S(2)}) collective-permute-start(bf16[32,2688]{1,0:T(8,128)(2,1)} %get-tuple-element.38), channel_id=1, source_target_pairs={{0,10},{1,11},{2,8},{3,9},{8,2},{9,3},{10,0},{11,1},{4,14},{5,15},... | collective-permute-start | bytes 516104 | tf_op jit(solution)/shard_map/ppermute | solution.py:339
  167.4 3.1 %collective-permute-start.25 = (bf16[32,2688]{1,0:T(8,128)(2,1)}, bf16[32,2688]{1,0:T(8,128)(2,1)S(1)}, u32[]{:S(2)}, u32[]{:S(2)}) collective-permute-start(bf16[32,2688]{1,0:T(8,128)(2,1)} %get-tuple-element.39), channel_id=1, source_target_pairs={{0,11},{1,10},{2,9},{3,8},{8,3},{9,2},{10,1},{11,0},{4,15},{5,14},... | collective-permute-start | bytes 516104 | tf_op jit(solution)/shard_map/ppermute | solution.py:339
  170.8 9.1 %collective-permute-done.24.refs_6_ = bf16[32,2688]{1,0:T(8,128)(2,1)S(1)} collective-permute-done((bf16[32,2688]{1,0:T(8,128)(2,1)}, bf16[32,2688]{1,0:T(8,128)(2,1)S(1)}, u32[]{:S(2)}, u32[]{:S(2)}) %collective-permute-start.24) | collective-permute-done | bytes 172064 | tf_op jit(solution)/shard_map/ppermute | solution.py:339
  180.8 2.9 %shard_map.96 = (bf16[256,2560]{1,0:T(8,128)(2,1)}, bf16[6,256]{1,0:T(8,128)(2,1)}) custom-call(s32[5]{0:T(128)S(1)} %copy-done.11, s32[6,256]{1,0:T(8,128)S(1)} %bitcast.10, bf16[6,256]{1,0:T(8,128)(2,1)S(1)} %bitcast.11, bf16[256,256]{1,0:T(8,128)(2,1)S(1)} %copy-done.8, bf16[32,2688]{1,0:T(8,128)(2,1)S(1)} %copy-done.7, ...), custom_call_target="tpu_custom_call" | custom-call | flops 335544320 | bytes 2621440 | tf_op jit(solution)/shard_map/pallas_call | solution.py:342
  (59 shorter events, 18.2 us)
Async XLA Ops:
  2.2 10.0 %collective-permute-start = (bf16[3,40,768]{2,1,0:T(8,128)(2,1)}, bf16[3,40,768]{2,1,0:T(8,128)(2,1)S(1)}, u32[]{:S(2)}, u32[]{:S(2)}) collective-permute-start(bf16[3,40,768]{2,1,0:T(8,128)(2,1)} %shard_map.87.shard_ref), channel_id=1, source_target_pairs={{8,0},{4,12},{9,1},{5,13},{10,2},{6,14},{11,3},{7,15},{24,16},{20,... | collective-permute-start | bytes 552968 | tf_op jit(solution)/shard_map/ppermute | solution.py:267
  13.2 14.1 %collective-permute-start.1 = (bf16[240,768]{1,0:T(8,128)(2,1)S(1)}, bf16[240,768]{1,0:T(8,128)(2,1)S(1)}, u32[]{:S(2)}, u32[]{:S(2)}) collective-permute-start(bf16[240,768]{1,0:T(8,128)(2,1)S(1)} %shard_map.88.mine), channel_id=1, source_target_pairs={{0,4},{64,68},{12,72},{76,8},{1,5},{65,69},{13,73},{77,9},{2,6},{6... | collective-permute-start | bytes 1105928 | tf_op jit(solution)/shard_map/ppermute | solution.py:286
  14.5 33.6 %collective-permute-start.3 = (bf16[240,768]{1,0:T(8,128)(2,1)S(1)}, bf16[240,768]{1,0:T(8,128)(2,1)S(1)}, u32[]{:S(2)}, u32[]{:S(2)}) collective-permute-start(bf16[240,768]{1,0:T(8,128)(2,1)S(1)} %shard_map.88.mine), channel_id=1, source_target_pairs={{0,68},{64,4},{12,8},{76,72},{1,69},{65,5},{13,9},{77,73},{2,70},{... | collective-permute-start | bytes 1105928 | tf_op jit(solution)/shard_map/ppermute | solution.py:286
  27.3 28.1 %collective-permute-start.5 = (bf16[240,768]{1,0:T(8,128)(2,1)S(1)}, bf16[240,768]{1,0:T(8,128)(2,1)S(1)}, u32[]{:S(2)}, u32[]{:S(2)}) collective-permute-start(bf16[240,768]{1,0:T(8,128)(2,1)S(1)} %get-tuple-element.25.refs_0_), channel_id=1, source_target_pairs={{0,16},{8,136},{16,32},{24,152},{32,48},{40,168},{48,0},{56,184},{... | collective-permute-start | bytes 1105928 | tf_op jit(solution)/shard_map/ppermute | solution.py:233
  29.2 26.1 %collective-permute-start.6 = (bf16[240,768]{1,0:T(8,128)(2,1)S(1)}, bf16[240,768]{1,0:T(8,128)(2,1)S(1)}, u32[]{:S(2)}, u32[]{:S(2)}) collective-permute-start(bf16[240,768]{1,0:T(8,128)(2,1)S(1)} %get-tuple-element.25.refs_0_), channel_id=1, source_target_pairs={{0,48},{8,392},{16,0},{24,408},{32,16},{40,424},{48,32},{56,440},{... | collective-permute-start | bytes 1105928 | tf_op jit(solution)/shard_map/ppermute | solution.py:233
  33.8 21.5 %collective-permute-start.2 = (bf16[128,768]{1,0:T(8,128)(2,1)S(1)}, bf16[128,768]{1,0:T(8,128)(2,1)S(1)}, u32[]{:S(2)}, u32[]{:S(2)}) collective-permute-start(bf16[128,768]{1,0:T(8,128)(2,1)S(1)} %get-tuple-element.24), channel_id=1, source_target_pairs={{4,64},{68,0},{8,12},{72,76},{5,65},{69,1},{9,13},{73,77},{6,66},{... | collective-permute-start | bytes 589832 | tf_op jit(solution)/shard_map/ppermute | solution.py:286
  48.2 6.9 %collective-permute-start.4 = (bf16[112,768]{1,0:T(8,128)(2,1)S(1)}, bf16[112,768]{1,0:T(8,128)(2,1)S(1)}, u32[]{:S(2)}, u32[]{:S(2)}) collective-permute-start(bf16[112,768]{1,0:T(8,128)(2,1)S(1)} %slice.4), channel_id=1, source_target_pairs={{4,0},{68,64},{8,76},{72,12},{5,1},{69,65},{9,77},{73,13},{6,2},{7... | collective-permute-start | bytes 516104 | tf_op jit(solution)/shard_map/ppermute | solution.py:286
  55.4 77.0 %all-to-all-start = ((bf16[8,64,2560]{2,1,0:T(8,128)(2,1)}), bf16[8,64,2560]{2,1,0:T(8,128)(2,1)}, u32[]{:S(2)}, u32[]{:S(2)}) async-start(bf16[8,64,2560]{2,1,0:T(8,128)(2,1)} %get-tuple-element.26), calls=%async_computation | async-start | bytes 5242880 | tf_op jit(solution)/shard_map/all_to_all | solution.py:315
  62.5 9.8 %collective-permute-start.12 = (bf16[240,768]{1,0:T(8,128)(2,1)S(1)}, bf16[240,768]{1,0:T(8,128)(2,1)S(1)}, u32[]{:S(2)}, u32[]{:S(2)}) collective-permute-start(bf16[240,768]{1,0:T(8,128)(2,1)S(1)} %shard_map.92.refs_0_), channel_id=1, source_target_pairs={{0,16},{8,136},{16,32},{24,152},{32,48},{40,168},{48,0},{56,184},{... | collective-permute-start | bytes 1105928 | tf_op jit(solution)/shard_map/ppermute | solution.py:233
  65.1 11.1 %collective-permute-start.7 = (bf16[240,768]{1,0:T(8,128)(2,1)S(1)}, bf16[240,768]{1,0:T(8,128)(2,1)S(1)}, u32[]{:S(2)}, u32[]{:S(2)}) collective-permute-start(bf16[240,768]{1,0:T(8,128)(2,1)S(1)} %collective-permute-done.5.refs_1_), channel_id=1, source_target_pairs={{0,16},{8,136},{16,32},{24,152},{32,48},{40,168},{48,0},{56,184},{... | collective-permute-start | bytes 1105928 | tf_op jit(solution)/shard_map/ppermute | solution.py:233
  68.3 15.1 %collective-permute-start.13 = (bf16[240,768]{1,0:T(8,128)(2,1)S(1)}, bf16[240,768]{1,0:T(8,128)(2,1)S(1)}, u32[]{:S(2)}, u32[]{:S(2)}) collective-permute-start(bf16[240,768]{1,0:T(8,128)(2,1)S(1)} %shard_map.92.refs_0_), channel_id=1, source_target_pairs={{0,48},{8,392},{16,0},{24,408},{32,16},{40,424},{48,32},{56,440},{... | collective-permute-start | bytes 1105928 | tf_op jit(solution)/shard_map/ppermute | solution.py:233
  72.3 11.1 %collective-permute-start.14 = (bf16[240,768]{1,0:T(8,128)(2,1)S(1)}, bf16[240,768]{1,0:T(8,128)(2,1)S(1)}, u32[]{:S(2)}, u32[]{:S(2)}) collective-permute-start(bf16[240,768]{1,0:T(8,128)(2,1)S(1)} %collective-permute-done.12.refs_1_), channel_id=1, source_target_pairs={{0,16},{8,136},{16,32},{24,152},{32,48},{40,168},{48,0},{56,184},{... | collective-permute-start | bytes 1105928 | tf_op jit(solution)/shard_map/ppermute | solution.py:233
  76.9 23.4 %copy-start = (bf16[960,768]{1,0:T(8,128)(2,1)}, bf16[960,768]{1,0:T(8,128)(2,1)S(1)}, u32[]{:S(2)}) copy-start(bf16[960,768]{1,0:T(8,128)(2,1)S(1)} %shard_map.90.refs_0_) | copy-start | bytes 4423684
  76.9 22.4 %collective-permute-start.8 = (bf16[960,768]{1,0:T(8,128)(2,1)S(1)}, bf16[960,768]{1,0:T(8,128)(2,1)S(1)}, u32[]{:S(2)}, u32[]{:S(2)}) collective-permute-start(bf16[960,768]{1,0:T(8,128)(2,1)S(1)} %shard_map.90.refs_0_), channel_id=1, source_target_pairs={{0,128},{8,24},{16,144},{24,40},{32,160},{40,56},{48,176},{56,8},{... | collective-permute-start | bytes 4423688 | tf_op jit(solution)/shard_map/ppermute | solution.py:233
  79.2 20.5 %collective-permute-start.9 = (bf16[960,768]{1,0:T(8,128)(2,1)S(1)}, bf16[960,768]{1,0:T(8,128)(2,1)S(1)}, u32[]{:S(2)}, u32[]{:S(2)}) collective-permute-start(bf16[960,768]{1,0:T(8,128)(2,1)S(1)} %shard_map.90.refs_0_), channel_id=1, source_target_pairs={{0,384},{8,56},{16,400},{24,8},{32,416},{40,24},{48,432},{56,40},{... | collective-permute-start | bytes 4423688 | tf_op jit(solution)/shard_map/ppermute | solution.py:233
  84.1 30.9 %collective-permute-start.15 = (bf16[960,768]{1,0:T(8,128)(2,1)S(1)}, bf16[960,768]{1,0:T(8,128)(2,1)S(1)}, u32[]{:S(2)}, u32[]{:S(2)}) collective-permute-start(bf16[960,768]{1,0:T(8,128)(2,1)S(1)} %shard_map.93.refs_5_), channel_id=1, source_target_pairs={{0,128},{8,24},{16,144},{24,40},{32,160},{40,56},{48,176},{56,8},{... | collective-permute-start | bytes 4423688 | tf_op jit(solution)/shard_map/ppermute | solution.py:233
  86.0 29.5 %collective-permute-start.16 = (bf16[960,768]{1,0:T(8,128)(2,1)S(1)}, bf16[960,768]{1,0:T(8,128)(2,1)S(1)}, u32[]{:S(2)}, u32[]{:S(2)}) collective-permute-start(bf16[960,768]{1,0:T(8,128)(2,1)S(1)} %shard_map.93.refs_5_), channel_id=1, source_target_pairs={{0,384},{8,56},{16,400},{24,8},{32,416},{40,24},{48,432},{56,40},{... | collective-permute-start | bytes 4423688 | tf_op jit(solution)/shard_map/ppermute | solution.py:233
  100.9 23.7 %collective-permute-start.10 = (bf16[480,768]{1,0:T(8,128)(2,1)S(1)}, bf16[480,768]{1,0:T(8,128)(2,1)}, u32[]{:S(2)}, u32[]{:S(2)}) collective-permute-start(bf16[480,768]{1,0:T(8,128)(2,1)S(1)} %get-tuple-element.27), channel_id=1, source_target_pairs={{0,128},{8,24},{16,144},{24,40},{32,160},{40,56},{48,176},{56,8},{... | collective-permute-start | bytes 2211848 | tf_op jit(solution)/shard_map/ppermute | solution.py:233
  104.0 20.6 %collective-permute-start.11 = (bf16[480,768]{1,0:T(8,128)(2,1)S(1)}, bf16[480,768]{1,0:T(8,128)(2,1)}, u32[]{:S(2)}, u32[]{:S(2)}) collective-permute-start(bf16[480,768]{1,0:T(8,128)(2,1)S(1)} %get-tuple-element.28), channel_id=1, source_target_pairs={{0,384},{8,56},{16,400},{24,8},{32,416},{40,24},{48,432},{56,40},{... | collective-permute-start | bytes 2211848 | tf_op jit(solution)/shard_map/ppermute | solution.py:233
  116.6 14.6 %collective-permute-start.17 = (bf16[480,768]{1,0:T(8,128)(2,1)S(1)}, bf16[480,768]{1,0:T(8,128)(2,1)}, u32[]{:S(2)}, u32[]{:S(2)}) collective-permute-start(bf16[480,768]{1,0:T(8,128)(2,1)S(1)} %get-tuple-element.30), channel_id=1, source_target_pairs={{0,128},{8,24},{16,144},{24,40},{32,160},{40,56},{48,176},{56,8},{... | collective-permute-start | bytes 2211848 | tf_op jit(solution)/shard_map/ppermute | solution.py:233
  119.8 12.6 %collective-permute-start.18 = (bf16[480,768]{1,0:T(8,128)(2,1)S(1)}, bf16[480,768]{1,0:T(8,128)(2,1)}, u32[]{:S(2)}, u32[]{:S(2)}) collective-permute-start(bf16[480,768]{1,0:T(8,128)(2,1)S(1)} %get-tuple-element.31), channel_id=1, source_target_pairs={{0,384},{8,56},{16,400},{24,8},{32,416},{40,24},{48,432},{56,40},{... | collective-permute-start | bytes 2211848 | tf_op jit(solution)/shard_map/ppermute | solution.py:233
  124.6 55.3 %copy-start.8 = (bf16[256,256]{1,0:T(8,128)(2,1)S(1)}, bf16[256,256]{1,0:T(8,128)(2,1)}, u32[]{:S(2)}) copy-start(bf16[256,256]{1,0:T(8,128)(2,1)} %get-tuple-element.22.sel_ref) | copy-start | bytes 393220
  124.6 55.3 %copy-start.9 = (s32[256,6]{0,1:T(8,128)S(1)}, s32[256,6]{0,1:T(8,128)}, u32[]{:S(2)}) copy-start(s32[256,6]{0,1:T(8,128)} %param.9) | copy-start | bytes 18436
  124.6 55.3 %copy-start.10 = (bf16[256,6]{0,1:T(8,128)(2,1)S(1)}, bf16[256,6]{0,1:T(8,128)(2,1)}, u32[]{:S(2)}) copy-start(bf16[256,6]{0,1:T(8,128)(2,1)} %param.10) | copy-start | bytes 9220
  124.6 55.3 %copy-start.11 = (s32[5]{0:T(128)S(1)}, s32[5]{0:T(128)}, u32[]{:S(2)}) copy-start(s32[5]{0:T(128)} %stack.23.where_ref) | copy-start | bytes 64
  144.2 17.9 %collective-permute-start.19 = (bf16[32,2688]{1,0:T(8,128)(2,1)}, bf16[32,2688]{1,0:T(8,128)(2,1)S(1)}, u32[]{:S(2)}, u32[]{:S(2)}) collective-permute-start(bf16[32,2688]{1,0:T(8,128)(2,1)} %get-tuple-element.33), channel_id=1, source_target_pairs={{0,1},{1,0},{2,3},{3,2},{8,9},{9,8},{10,11},{11,10},{4,5},{5,4},{6... | collective-permute-start | bytes 516104 | tf_op jit(solution)/shard_map/ppermute | solution.py:339
  147.5 19.9 %collective-permute-start.20 = (bf16[32,2688]{1,0:T(8,128)(2,1)}, bf16[32,2688]{1,0:T(8,128)(2,1)S(1)}, u32[]{:S(2)}, u32[]{:S(2)}) collective-permute-start(bf16[32,2688]{1,0:T(8,128)(2,1)} %get-tuple-element.34), channel_id=1, source_target_pairs={{0,2},{1,3},{2,0},{3,1},{8,10},{9,11},{10,8},{11,9},{4,6},{5,7},{6... | collective-permute-start | bytes 516104 | tf_op jit(solution)/shard_map/ppermute | solution.py:339
  151.9 18.7 %collective-permute-start.21 = (bf16[32,2688]{1,0:T(8,128)(2,1)}, bf16[32,2688]{1,0:T(8,128)(2,1)S(1)}, u32[]{:S(2)}, u32[]{:S(2)}) collective-permute-start(bf16[32,2688]{1,0:T(8,128)(2,1)} %get-tuple-element.35), channel_id=1, source_target_pairs={{0,3},{1,2},{2,1},{3,0},{8,11},{9,10},{10,9},{11,8},{4,7},{5,6},{6... | collective-permute-start | bytes 516104 | tf_op jit(solution)/shard_map/ppermute | solution.py:339
  153.8 16.8 %collective-permute-start.22 = (bf16[32,2688]{1,0:T(8,128)(2,1)}, bf16[32,2688]{1,0:T(8,128)(2,1)S(1)}, u32[]{:S(2)}, u32[]{:S(2)}) collective-permute-start(bf16[32,2688]{1,0:T(8,128)(2,1)} %get-tuple-element.36), channel_id=1, source_target_pairs={{0,8},{1,9},{2,10},{3,11},{8,0},{9,1},{10,2},{11,3},{4,12},{5,13},... | collective-permute-start | bytes 516104 | tf_op jit(solution)/shard_map/ppermute | solution.py:339
  159.5 11.3 %collective-permute-start.23 = (bf16[32,2688]{1,0:T(8,128)(2,1)}, bf16[32,2688]{1,0:T(8,128)(2,1)S(1)}, u32[]{:S(2)}, u32[]{:S(2)}) collective-permute-start(bf16[32,2688]{1,0:T(8,128)(2,1)} %get-tuple-element.37), channel_id=1, source_target_pairs={{0,9},{1,8},{2,11},{3,10},{8,1},{9,0},{10,3},{11,2},{4,13},{5,12},... | collective-permute-start | bytes 516104 | tf_op jit(solution)/shard_map/ppermute | solution.py:339
  162.1 17.8 %collective-permute-start.24 = (bf16[32,2688]{1,0:T(8,128)(2,1)}, bf16[32,2688]{1,0:T(8,128)(2,1)S(1)}, u32[]{:S(2)}, u32[]{:S(2)}) collective-permute-start(bf16[32,2688]{1,0:T(8,128)(2,1)} %get-tuple-element.38), channel_id=1, source_target_pairs={{0,10},{1,11},{2,8},{3,9},{8,2},{9,3},{10,0},{11,1},{4,14},{5,15},... | collective-permute-start | bytes 516104 | tf_op jit(solution)/shard_map/ppermute | solution.py:339
  167.4 12.5 %collective-permute-start.25 = (bf16[32,2688]{1,0:T(8,128)(2,1)}, bf16[32,2688]{1,0:T(8,128)(2,1)S(1)}, u32[]{:S(2)}, u32[]{:S(2)}) collective-permute-start(bf16[32,2688]{1,0:T(8,128)(2,1)} %get-tuple-element.39), channel_id=1, source_target_pairs={{0,11},{1,10},{2,9},{3,8},{8,3},{9,2},{10,1},{11,0},{4,15},{5,14},... | collective-permute-start | bytes 516104 | tf_op jit(solution)/shard_map/ppermute | solution.py:339
  (7 other events, 23.5 us)

commit v9 on v8

--- a/solution.py
+++ b/solution.py
@@ -114,8 +114,8 @@
 
     gate_copies, up_copies, down_copies = [], [], []
     for number, row, chain, far, near in pieces:
-        xx = lax.rem(my_x + jnp.where(core == 0, far, near), 4)
-        yy = lax.rem(my_y + jnp.where(core == 0, near, far), 4)
+        xx = jnp.where(core == 0, lax.rem(my_x + far, 4), jnp.bitwise_xor(my_x, near))
+        yy = jnp.where(core == 0, jnp.bitwise_xor(my_y, near), lax.rem(my_y + far, 4))
         half = first_half if chain == 0 else 1 - first_half
         target = pl.multiple_of(((xx * 2 + half) * 4 + yy) * 80, 16)
         for m, (weights, copies) in enumerate(
@@ -222,33 +222,39 @@
     )(*arrays)
 
 
-def shift(v, far, by):
+def shift(v, by):
     pairs = []
     for x in range(4):
         for y in range(4):
-            for c in range(2):
-                along_x = (c == 0) == far
-                tx, ty = ((x + by) % 4, y) if along_x else (x, (y + by) % 4)
-                pairs.append(((x * 4 + y) * 2 + c, (tx * 4 + ty) * 2 + c))
+            pairs.append(((x * 4 + y) * 2, ((x + by) % 4 * 4 + y) * 2))
+            pairs.append(((x * 4 + y) * 2 + 1, (x * 4 + (y + by) % 4) * 2 + 1))
+    return lax.ppermute(v, ("x", "y", "c"), pairs)
+
+
+def exchange(v, by):
+    pairs = []
+    for x in range(4):
+        for y in range(4):
+            pairs.append(((x * 4 + y) * 2, (x * 4 + (y ^ by)) * 2))
+            pairs.append(((x * 4 + y) * 2 + 1, ((x ^ by) * 4 + y) * 2 + 1))
     return lax.ppermute(v, ("x", "y", "c"), pairs)
 
 
 def torus_gather(own, chain, first):
     count = own.shape[0]
-    low, high = shift(own, False, 1), shift(own, False, -1)
-    opposite = shift(low, False, 1)
-    (line,) = join(
-        [4 * count], [(n, 0, count, 0, n * count) for n in range(4)], own, low, high, opposite
-    )
-    line_low, line_high = shift(line, True, 1), shift(line, True, -1)
+    beside = exchange(own, 1)
+    (half,) = join([2 * count], [(n, 0, count, 0, n * count) for n in range(2)], own, beside)
+    across = exchange(half, 3)
+    (line,) = join([4 * count], [(n, 0, 2 * count, 0, 2 * n * count) for n in range(2)], half, across)
+    line_low, line_high = shift(line, 1), shift(line, -1)
     far0, far1 = join(
         [2 * count] * 2, [(0, 0, 2 * count, 0, 0), (1, 2 * count, 2 * count, 1, 0)], line_low, line_high
     )
-    far0, far1 = shift(far0, True, 1), shift(far1, True, -1)
-    near = (0, 3, 1, 2)
+    far0, far1 = shift(far0, 1), shift(far1, -1)
+    near = (0, 1, 3, 2)
     pieces = [(first + n, k * count, chain, far, near[k]) for n, far in enumerate((0, 3, 1)) for k in range(4)]
     pieces += [(first + 3 + k // 2, k % 2 * count, chain, 2, near[k]) for k in range(4)]
-    return (line, line_low, line_high, far0, far1), pieces, (low, high, opposite)
+    return (line, line_low, line_high, far0, far1), pieces, beside
 
 
 def on_device(tokens_in, cotangent, routes, gate_weights, gate_proj, up_proj, down_proj):
@@ -287,11 +293,6 @@
 
     source = ic == zq
     low, high = zmove(pair, True, 1), zmove(pair, True, -1)
-    first, top = small(near_kernel, source, (pair, low), (240, SPLIT))
-    far0, far1 = zmove(top, False, 1), zmove(high[SPLIT:], False, -1)
-    (second,) = small(far_kernel, source, (far0, far1, high), (240,))
-    first_half = jnp.where(source, zh, jnp.where((ring == 1) | (ring == 2), 0, 1))
-
     step = 512
     columns = pl.BlockSpec((256, step), lambda i: (0, i))
     payload, sel = pl.pallas_call(
@@ -310,10 +311,16 @@
         cost_estimate=cost(2 * 256 * 512 * width, 8 * 256 * width),
     )(routes.T, tokens_in, cotangent)
 
+    low, payload = lax.optimization_barrier((low, payload))
+    first, top = small(near_kernel, source, (pair, low), (240, SPLIT))
+    far0, far1 = zmove(top, False, 1), zmove(high[SPLIT:], False, -1)
+    (second,) = small(far_kernel, source, (far0, far1, high), (240,))
+    first_half = jnp.where(source, zh, jnp.where((ring == 1) | (ring == 2), 0, 1))
+
     arrays, pieces, near = torus_gather(first, 0, 0)
-    payload, *_ = lax.optimization_barrier((payload, far0, far1, *near[:2]))
+    payload, *_ = lax.optimization_barrier((payload, far0, far1, near))
     rows = lax.all_to_all(payload, ("c", "zr"), split_axis=0, concat_axis=0, tiled=True)
-    second, *_ = lax.optimization_barrier((second, *near[:2]))
+    second, *_ = lax.optimization_barrier((second, near))
     more_arrays, more_pieces, _ = torus_gather(second, 1, len(arrays))
     arrays, pieces = arrays + more_arrays, pieces + more_pieces
 

time: 186 us -> 188 us (1.011)
  waiting for transfers between devices: 49.3 us -> 57.3 us
  starting transfers between devices: 105 us -> 98.2 us
    ppermute x14 -> x8, starting transfers between devices: 45 us -> 25 us  [shift(): return lax.ppermute(v, ('x', 'y', 'c'), pairs)]
    ppermute x0 -> x4, starting transfers between devices: none -> 12.3 us  [exchange(): return lax.ppermute(v, ('x', 'y', 'c'), pairs)]
    ppermute x0 -> x4, waiting for transfers between devices: none -> 7.34 us  [exchange(): return lax.ppermute(v, ('x', 'y', 'c'), pairs)]
    ppermute x14 -> x8, waiting for transfers between devices: 26.9 us -> 27.5 us  [shift(): return lax.ppermute(v, ('x', 'y', 'c'), pairs)]
  transfers between devices with their start and end apart: 27 -> 25, of which waited for: 13 -> 15; matrix products, arithmetic and copies ran while one was open for 0% -> 0% of each run, Pallas kernels for 4% -> 5%
where the time goes in v9:
time: 188 us; the launch traced here: 185 us
  starting transfers between devices  98.2 us (52%)
  waiting for transfers between devices  57.3 us (30%)
  Pallas kernels  25 us (13%)
  local copies, waits for them, and re-layouts  3.66 us (2%)
    ppermute x8, waiting for transfers between devices, shift(): return lax.ppermute(v, ('x', 'y', 'c'), pairs)  27.5 us
    ppermute x7, starting transfers between devices, on_device(): home[r] = lax.ppermute(back[r], ('c', 'zr'), pairs)  26.2 us
    ppermute x8, starting transfers between devices, shift(): return lax.ppermute(v, ('x', 'y', 'c'), pairs)  25 us
    ppermute x4, starting transfers between devices, zmove(): return lax.ppermute(v, ('zh', 'c', 'zq'), pairs)  19.3 us
    ppermute x4, starting transfers between devices, exchange(): return lax.ppermute(v, ('x', 'y', 'c'), pairs)  12.3 us
    pallas_call x1, Pallas kernels, on_device(): pl.pallas_call(functools.partial(expert_kernel, pieces), out_shape=[jax.S...  11.7 us
    ppermute x4, waiting for transfers between devices, zmove(): return lax.ppermute(v, ('zh', 'c', 'zq'), pairs)  11.7 us
    ppermute x7, waiting for transfers between devices, on_device(): home[r] = lax.ppermute(back[r], ('c', 'zr'), pairs)  9.49 us
  transfers between devices with their start and end apart: 25, of which 15 were waited for; matrix products, arithmetic and copies ran while one was open for 0% of the time, Pallas kernels for 5%

profile of v9, /device:TPU:1, one launch (start us, length us, event | category | flops | bytes accessed | tf_op | source)
XLA Modules:
  0.0 185.2 jit_solution(14100151820939524711)
XLA Ops:
  2.2 8.8 %collective-permute-start = (bf16[3,40,768]{2,1,0:T(8,128)(2,1)}, bf16[3,40,768]{2,1,0:T(8,128)(2,1)S(1)}, u32[]{:S(2)}, u32[]{:S(2)}) collective-permute-start(bf16[3,40,768]{2,1,0:T(8,128)(2,1)} %shard_map.87.shard_ref), channel_id=1, source_target_pairs={{8,0},{4,12},{9,1},{5,13},{10,2},{6,14},{11,3},{7,15},{24,16},{20,... | collective-permute-start | bytes 552968 | tf_op jit(solution)/shard_map/ppermute | solution.py:273
  15.8 5.6 %shard_map.86 = (bf16[8,64,2560]{2,1,0:T(8,128)(2,1)}, bf16[256,256]{1,0:T(8,128)(2,1)}) custom-call(s32[6,256]{1,0:T(8,128)} %bitcast.9, bf16[256,2560]{1,0:T(8,128)(2,1)} %tok_ref.1, bf16[256,2560]{1,0:T(8,128)(2,1)} %cot_ref.1), custom_call_target="tpu_custom_call" | custom-call | flops 671088640 | bytes 5242880 | tf_op jit(solution)/shard_map/pallas_call | solution.py:298
  21.4 5.9 %collective-permute-done.1.low = bf16[240,768]{1,0:T(8,128)(2,1)S(1)} collective-permute-done((bf16[240,768]{1,0:T(8,128)(2,1)S(1)}, bf16[240,768]{1,0:T(8,128)(2,1)S(1)}, u32[]{:S(2)}, u32[]{:S(2)}) %collective-permute-start.1) | collective-permute-done | bytes 368672 | tf_op jit(solution)/shard_map/ppermute | solution.py:292
  27.3 1.9 %collective-permute-start.5 = (bf16[240,768]{1,0:T(8,128)(2,1)S(1)}, bf16[240,768]{1,0:T(8,128)(2,1)S(1)}, u32[]{:S(2)}, u32[]{:S(2)}) collective-permute-start(bf16[240,768]{1,0:T(8,128)(2,1)S(1)} %get-tuple-element.29.refs_0_), channel_id=1, source_target_pairs={{0,16},{8,136},{16,0},{24,152},{32,48},{40,168},{48,32},{56,184},{... | collective-permute-start | bytes 1105928 | tf_op jit(solution)/shard_map/ppermute | solution.py:240
  29.2 15.4 %collective-permute-start.2 = (bf16[128,768]{1,0:T(8,128)(2,1)S(1)}, bf16[128,768]{1,0:T(8,128)(2,1)S(1)}, u32[]{:S(2)}, u32[]{:S(2)}) collective-permute-start(bf16[128,768]{1,0:T(8,128)(2,1)S(1)} %get-tuple-element.28), channel_id=1, source_target_pairs={{4,64},{68,0},{8,12},{72,76},{5,65},{69,1},{9,13},{73,77},{6,66},{... | collective-permute-start | bytes 589832 | tf_op jit(solution)/shard_map/ppermute | solution.py:292
  46.0 2.4 %collective-permute-done.4.bottom = bf16[112,768]{1,0:T(8,128)(2,1)S(1)} collective-permute-done((bf16[112,768]{1,0:T(8,128)(2,1)S(1)}, bf16[112,768]{1,0:T(8,128)(2,1)S(1)}, u32[]{:S(2)}, u32[]{:S(2)}) %collective-permute-start.4) | collective-permute-done | bytes 172064 | tf_op jit(solution)/shard_map/ppermute | solution.py:292
  48.4 3.4 %collective-permute-done.2.top = bf16[128,768]{1,0:T(8,128)(2,1)S(1)} collective-permute-done((bf16[128,768]{1,0:T(8,128)(2,1)S(1)}, bf16[128,768]{1,0:T(8,128)(2,1)S(1)}, u32[]{:S(2)}, u32[]{:S(2)}) %collective-permute-start.2) | collective-permute-done | bytes 196640 | tf_op jit(solution)/shard_map/ppermute | solution.py:292
  51.8 6.7 %all-to-all-start = ((bf16[8,64,2560]{2,1,0:T(8,128)(2,1)}), bf16[8,64,2560]{2,1,0:T(8,128)(2,1)}, u32[]{:S(2)}, u32[]{:S(2)}) async-start(bf16[8,64,2560]{2,1,0:T(8,128)(2,1)} %get-tuple-element.30), calls=%async_computation | async-start | bytes 5242880 | tf_op jit(solution)/shard_map/all_to_all | solution.py:322
  58.5 3.1 %collective-permute-start.11 = (bf16[240,768]{1,0:T(8,128)(2,1)S(1)}, bf16[240,768]{1,0:T(8,128)(2,1)S(1)}, u32[]{:S(2)}, u32[]{:S(2)}) collective-permute-start(bf16[240,768]{1,0:T(8,128)(2,1)S(1)} %shard_map.93.refs_0_), channel_id=1, source_target_pairs={{0,16},{8,136},{16,0},{24,152},{32,48},{40,168},{48,32},{56,184},{... | collective-permute-start | bytes 1105928 | tf_op jit(solution)/shard_map/ppermute | solution.py:240
  61.9 3.3 %collective-permute-start.6 = (bf16[480,768]{1,0:T(8,128)(2,1)S(1)}, bf16[480,768]{1,0:T(8,128)(2,1)S(1)}, u32[]{:S(2)}, u32[]{:S(2)}) collective-permute-start(bf16[480,768]{1,0:T(8,128)(2,1)S(1)} %shard_map.90.refs_0_), channel_id=1, source_target_pairs={{0,48},{8,392},{16,32},{24,408},{32,16},{40,424},{48,0},{56,440},{... | collective-permute-start | bytes 2211848 | tf_op jit(solution)/shard_map/ppermute | solution.py:240
  65.2 2.0 %collective-permute-done.11.refs_1_ = bf16[240,768]{1,0:T(8,128)(2,1)S(1)} collective-permute-done((bf16[240,768]{1,0:T(8,128)(2,1)S(1)}, bf16[240,768]{1,0:T(8,128)(2,1)S(1)}, u32[]{:S(2)}, u32[]{:S(2)}) %collective-permute-start.11) | collective-permute-done | bytes 368672 | tf_op jit(solution)/shard_map/ppermute | solution.py:240
  67.5 4.0 %collective-permute-start.12 = (bf16[480,768]{1,0:T(8,128)(2,1)S(1)}, bf16[480,768]{1,0:T(8,128)(2,1)S(1)}, u32[]{:S(2)}, u32[]{:S(2)}) collective-permute-start(bf16[480,768]{1,0:T(8,128)(2,1)S(1)} %shard_map.94.refs_0_), channel_id=1, source_target_pairs={{0,48},{8,392},{16,32},{24,408},{32,16},{40,424},{48,0},{56,440},{... | collective-permute-start | bytes 2211848 | tf_op jit(solution)/shard_map/ppermute | solution.py:240
  71.5 4.1 %collective-permute-done.6.refs_1_ = bf16[480,768]{1,0:T(8,128)(2,1)S(1)} collective-permute-done((bf16[480,768]{1,0:T(8,128)(2,1)S(1)}, bf16[480,768]{1,0:T(8,128)(2,1)S(1)}, u32[]{:S(2)}, u32[]{:S(2)}) %collective-permute-start.6) | collective-permute-done | bytes 737312 | tf_op jit(solution)/shard_map/ppermute | solution.py:240
  76.3 4.1 %collective-permute-start.8 = (bf16[960,768]{1,0:T(8,128)(2,1)S(1)}, bf16[960,768]{1,0:T(8,128)(2,1)S(1)}, u32[]{:S(2)}, u32[]{:S(2)}) collective-permute-start(bf16[960,768]{1,0:T(8,128)(2,1)S(1)} %shard_map.91.refs_0_), channel_id=1, source_target_pairs={{0,384},{8,56},{16,400},{24,8},{32,416},{40,24},{48,432},{56,40},{... | collective-permute-start | bytes 4423688 | tf_op jit(solution)/shard_map/ppermute | solution.py:231
  84.2 4.1 %collective-permute-start.14 = (bf16[960,768]{1,0:T(8,128)(2,1)S(1)}, bf16[960,768]{1,0:T(8,128)(2,1)S(1)}, u32[]{:S(2)}, u32[]{:S(2)}) collective-permute-start(bf16[960,768]{1,0:T(8,128)(2,1)S(1)} %shard_map.95.refs_5_), channel_id=1, source_target_pairs={{0,384},{8,56},{16,400},{24,8},{32,416},{40,24},{48,432},{56,40},{... | collective-permute-start | bytes 4423688 | tf_op jit(solution)/shard_map/ppermute | solution.py:231
  90.2 8.6 %collective-permute-done.8.refs_1_.refs_2_ = bf16[960,768]{1,0:T(8,128)(2,1)S(1)} collective-permute-done((bf16[960,768]{1,0:T(8,128)(2,1)S(1)}, bf16[960,768]{1,0:T(8,128)(2,1)S(1)}, u32[]{:S(2)}, u32[]{:S(2)}) %collective-permute-start.8) | collective-permute-done | bytes 1474592 | tf_op jit(solution)/shard_map/ppermute | solution.py:231
  98.8 3.3 %collective-permute-done.7.refs_0_.refs_1_ = bf16[960,768]{1,0:T(8,128)(2,1)S(1)} collective-permute-done((bf16[960,768]{1,0:T(8,128)(2,1)S(1)}, bf16[960,768]{1,0:T(8,128)(2,1)S(1)}, u32[]{:S(2)}, u32[]{:S(2)}) %collective-permute-start.7) | collective-permute-done | bytes 1474592 | tf_op jit(solution)/shard_map/ppermute | solution.py:231
  105.2 4.6 %collective-permute-start.10 = (bf16[480,768]{1,0:T(8,128)(2,1)S(1)}, bf16[480,768]{1,0:T(8,128)(2,1)}, u32[]{:S(2)}, u32[]{:S(2)}) collective-permute-start(bf16[480,768]{1,0:T(8,128)(2,1)S(1)} %get-tuple-element.32), channel_id=1, source_target_pairs={{0,384},{8,56},{16,400},{24,8},{32,416},{40,24},{48,432},{56,40},{... | collective-permute-start | bytes 2211848 | tf_op jit(solution)/shard_map/ppermute | solution.py:231
  109.8 4.8 %collective-permute-done.14.refs_1_.refs_7_ = bf16[960,768]{1,0:T(8,128)(2,1)S(1)} collective-permute-done((bf16[960,768]{1,0:T(8,128)(2,1)S(1)}, bf16[960,768]{1,0:T(8,128)(2,1)S(1)}, u32[]{:S(2)}, u32[]{:S(2)}) %collective-permute-start.14) | collective-permute-done | bytes 1474592 | tf_op jit(solution)/shard_map/ppermute | solution.py:231
  114.6 3.2 %collective-permute-done.13.refs_0_.refs_6_ = bf16[960,768]{1,0:T(8,128)(2,1)S(1)} collective-permute-done((bf16[960,768]{1,0:T(8,128)(2,1)S(1)}, bf16[960,768]{1,0:T(8,128)(2,1)S(1)}, u32[]{:S(2)}, u32[]{:S(2)}) %collective-permute-start.13) | collective-permute-done | bytes 1474592 | tf_op jit(solution)/shard_map/ppermute | solution.py:231
  120.9 4.6 %collective-permute-start.16 = (bf16[480,768]{1,0:T(8,128)(2,1)S(1)}, bf16[480,768]{1,0:T(8,128)(2,1)}, u32[]{:S(2)}, u32[]{:S(2)}) collective-permute-start(bf16[480,768]{1,0:T(8,128)(2,1)S(1)} %get-tuple-element.35), channel_id=1, source_target_pairs={{0,384},{8,56},{16,400},{24,8},{32,416},{40,24},{48,432},{56,40},{... | collective-permute-start | bytes 2211848 | tf_op jit(solution)/shard_map/ppermute | solution.py:231
  126.2 7.5 %collective-permute-done.15.refs_8_ = bf16[480,768]{1,0:T(8,128)(2,1)} collective-permute-done((bf16[480,768]{1,0:T(8,128)(2,1)S(1)}, bf16[480,768]{1,0:T(8,128)(2,1)}, u32[]{:S(2)}, u32[]{:S(2)}) %collective-permute-start.15) | collective-permute-done | bytes 737312 | tf_op jit(solution)/shard_map/ppermute | solution.py:231
  133.9 11.7 %shard_map.97 = (bf16[32,2688]{1,0:T(8,128)(2,1)}, bf16[32,2688]{1,0:T(8,128)(2,1)}, bf16[32,2688]{1,0:T(8,128)(2,1)}, bf16[32,2688]{1,0:T(8,128)(2,1)}, bf16[32...) custom-call(s32[5]{0:T(128)} %stack.23.where_ref, ...), custom_call_target="tpu_custom_call" | custom-call | flops 5033164800 | bytes 11796480 | tf_op jit(solution)/shard_map/pallas_call | solution.py:328
  145.6 3.3 %collective-permute-start.17 = (bf16[32,2688]{1,0:T(8,128)(2,1)}, bf16[32,2688]{1,0:T(8,128)(2,1)S(1)}, u32[]{:S(2)}, u32[]{:S(2)}) collective-permute-start(bf16[32,2688]{1,0:T(8,128)(2,1)} %get-tuple-element.37), channel_id=1, source_target_pairs={{0,1},{1,0},{2,3},{3,2},{8,9},{9,8},{10,11},{11,10},{4,5},{5,4},{6... | collective-permute-start | bytes 516104 | tf_op jit(solution)/shard_map/ppermute | solution.py:346
  148.9 4.0 %collective-permute-start.18 = (bf16[32,2688]{1,0:T(8,128)(2,1)}, bf16[32,2688]{1,0:T(8,128)(2,1)S(1)}, u32[]{:S(2)}, u32[]{:S(2)}) collective-permute-start(bf16[32,2688]{1,0:T(8,128)(2,1)} %get-tuple-element.38), channel_id=1, source_target_pairs={{0,2},{1,3},{2,0},{3,1},{8,10},{9,11},{10,8},{11,9},{4,6},{5,7},{6... | collective-permute-start | bytes 516104 | tf_op jit(solution)/shard_map/ppermute | solution.py:346
  152.9 2.0 %collective-permute-start.19 = (bf16[32,2688]{1,0:T(8,128)(2,1)}, bf16[32,2688]{1,0:T(8,128)(2,1)S(1)}, u32[]{:S(2)}, u32[]{:S(2)}) collective-permute-start(bf16[32,2688]{1,0:T(8,128)(2,1)} %get-tuple-element.39), channel_id=1, source_target_pairs={{0,3},{1,2},{2,1},{3,0},{8,11},{9,10},{10,9},{11,8},{4,7},{5,6},{6... | collective-permute-start | bytes 516104 | tf_op jit(solution)/shard_map/ppermute | solution.py:346
  154.9 6.0 %collective-permute-start.20 = (bf16[32,2688]{1,0:T(8,128)(2,1)}, bf16[32,2688]{1,0:T(8,128)(2,1)S(1)}, u32[]{:S(2)}, u32[]{:S(2)}) collective-permute-start(bf16[32,2688]{1,0:T(8,128)(2,1)} %get-tuple-element.40), channel_id=1, source_target_pairs={{0,8},{1,9},{2,10},{3,11},{8,0},{9,1},{10,2},{11,3},{4,12},{5,13},... | collective-permute-start | bytes 516104 | tf_op jit(solution)/shard_map/ppermute | solution.py:346
  160.9 2.6 %collective-permute-start.21 = (bf16[32,2688]{1,0:T(8,128)(2,1)}, bf16[32,2688]{1,0:T(8,128)(2,1)S(1)}, u32[]{:S(2)}, u32[]{:S(2)}) collective-permute-start(bf16[32,2688]{1,0:T(8,128)(2,1)} %get-tuple-element.41), channel_id=1, source_target_pairs={{0,9},{1,8},{2,11},{3,10},{8,1},{9,0},{10,3},{11,2},{4,13},{5,12},... | collective-permute-start | bytes 516104 | tf_op jit(solution)/shard_map/ppermute | solution.py:346
  163.6 5.3 %collective-permute-start.22 = (bf16[32,2688]{1,0:T(8,128)(2,1)}, bf16[32,2688]{1,0:T(8,128)(2,1)S(1)}, u32[]{:S(2)}, u32[]{:S(2)}) collective-permute-start(bf16[32,2688]{1,0:T(8,128)(2,1)} %get-tuple-element.42), channel_id=1, source_target_pairs={{0,10},{1,11},{2,8},{3,9},{8,2},{9,3},{10,0},{11,1},{4,14},{5,15},... | collective-permute-start | bytes 516104 | tf_op jit(solution)/shard_map/ppermute | solution.py:346
  168.8 3.0 %collective-permute-start.23 = (bf16[32,2688]{1,0:T(8,128)(2,1)}, bf16[32,2688]{1,0:T(8,128)(2,1)S(1)}, u32[]{:S(2)}, u32[]{:S(2)}) collective-permute-start(bf16[32,2688]{1,0:T(8,128)(2,1)} %get-tuple-element.43), channel_id=1, source_target_pairs={{0,11},{1,10},{2,9},{3,8},{8,3},{9,2},{10,1},{11,0},{4,15},{5,14},... | collective-permute-start | bytes 516104 | tf_op jit(solution)/shard_map/ppermute | solution.py:346
  172.2 9.1 %collective-permute-done.22.refs_6_ = bf16[32,2688]{1,0:T(8,128)(2,1)S(1)} collective-permute-done((bf16[32,2688]{1,0:T(8,128)(2,1)}, bf16[32,2688]{1,0:T(8,128)(2,1)S(1)}, u32[]{:S(2)}, u32[]{:S(2)}) %collective-permute-start.22) | collective-permute-done | bytes 172064 | tf_op jit(solution)/shard_map/ppermute | solution.py:346
  182.3 2.9 %shard_map.98 = (bf16[256,2560]{1,0:T(8,128)(2,1)}, bf16[6,256]{1,0:T(8,128)(2,1)}) custom-call(s32[5]{0:T(128)S(1)} %copy-done.11, s32[6,256]{1,0:T(8,128)S(1)} %bitcast.10, bf16[6,256]{1,0:T(8,128)(2,1)S(1)} %bitcast.11, bf16[256,256]{1,0:T(8,128)(2,1)S(1)} %copy-done.8, bf16[32,2688]{1,0:T(8,128)(2,1)S(1)} %copy-done.7, ...), custom_call_target="tpu_custom_call" | custom-call | flops 335544320 | bytes 2621440 | tf_op jit(solution)/shard_map/pallas_call | solution.py:349
  (57 shorter events, 23.1 us)
Async XLA Ops:
  2.2 10.0 %collective-permute-start = (bf16[3,40,768]{2,1,0:T(8,128)(2,1)}, bf16[3,40,768]{2,1,0:T(8,128)(2,1)S(1)}, u32[]{:S(2)}, u32[]{:S(2)}) collective-permute-start(bf16[3,40,768]{2,1,0:T(8,128)(2,1)} %shard_map.87.shard_ref), channel_id=1, source_target_pairs={{8,0},{4,12},{9,1},{5,13},{10,2},{6,14},{11,3},{7,15},{24,16},{20,... | collective-permute-start | bytes 552968 | tf_op jit(solution)/shard_map/ppermute | solution.py:273
  13.2 14.1 %collective-permute-start.1 = (bf16[240,768]{1,0:T(8,128)(2,1)S(1)}, bf16[240,768]{1,0:T(8,128)(2,1)S(1)}, u32[]{:S(2)}, u32[]{:S(2)}) collective-permute-start(bf16[240,768]{1,0:T(8,128)(2,1)S(1)} %shard_map.88.mine), channel_id=1, source_target_pairs={{0,4},{64,68},{12,72},{76,8},{1,5},{65,69},{13,73},{77,9},{2,6},{6... | collective-permute-start | bytes 1105928 | tf_op jit(solution)/shard_map/ppermute | solution.py:292
  14.5 30.2 %collective-permute-start.3 = (bf16[240,768]{1,0:T(8,128)(2,1)S(1)}, bf16[240,768]{1,0:T(8,128)(2,1)S(1)}, u32[]{:S(2)}, u32[]{:S(2)}) collective-permute-start(bf16[240,768]{1,0:T(8,128)(2,1)S(1)} %shard_map.88.mine), channel_id=1, source_target_pairs={{0,68},{64,4},{12,8},{76,72},{1,69},{65,5},{13,9},{77,73},{2,70},{... | collective-permute-start | bytes 1105928 | tf_op jit(solution)/shard_map/ppermute | solution.py:292
  27.3 24.5 %collective-permute-start.5 = (bf16[240,768]{1,0:T(8,128)(2,1)S(1)}, bf16[240,768]{1,0:T(8,128)(2,1)S(1)}, u32[]{:S(2)}, u32[]{:S(2)}) collective-permute-start(bf16[240,768]{1,0:T(8,128)(2,1)S(1)} %get-tuple-element.29.refs_0_), channel_id=1, source_target_pairs={{0,16},{8,136},{16,0},{24,152},{32,48},{40,168},{48,32},{56,184},{... | collective-permute-start | bytes 1105928 | tf_op jit(solution)/shard_map/ppermute | solution.py:240
  29.2 22.5 %collective-permute-start.2 = (bf16[128,768]{1,0:T(8,128)(2,1)S(1)}, bf16[128,768]{1,0:T(8,128)(2,1)S(1)}, u32[]{:S(2)}, u32[]{:S(2)}) collective-permute-start(bf16[128,768]{1,0:T(8,128)(2,1)S(1)} %get-tuple-element.28), channel_id=1, source_target_pairs={{4,64},{68,0},{8,12},{72,76},{5,65},{69,1},{9,13},{73,77},{6,66},{... | collective-permute-start | bytes 589832 | tf_op jit(solution)/shard_map/ppermute | solution.py:292
  44.7 3.7 %collective-permute-start.4 = (bf16[112,768]{1,0:T(8,128)(2,1)S(1)}, bf16[112,768]{1,0:T(8,128)(2,1)S(1)}, u32[]{:S(2)}, u32[]{:S(2)}) collective-permute-start(bf16[112,768]{1,0:T(8,128)(2,1)S(1)} %slice.4), channel_id=1, source_target_pairs={{4,0},{68,64},{8,76},{72,12},{5,1},{69,65},{9,77},{73,13},{6,2},{7... | collective-permute-start | bytes 516104 | tf_op jit(solution)/shard_map/ppermute | solution.py:292
  51.8 82.1 %all-to-all-start = ((bf16[8,64,2560]{2,1,0:T(8,128)(2,1)}), bf16[8,64,2560]{2,1,0:T(8,128)(2,1)}, u32[]{:S(2)}, u32[]{:S(2)}) async-start(bf16[8,64,2560]{2,1,0:T(8,128)(2,1)} %get-tuple-element.30), calls=%async_computation | async-start | bytes 5242880 | tf_op jit(solution)/shard_map/all_to_all | solution.py:322
  58.5 8.7 %collective-permute-start.11 = (bf16[240,768]{1,0:T(8,128)(2,1)S(1)}, bf16[240,768]{1,0:T(8,128)(2,1)S(1)}, u32[]{:S(2)}, u32[]{:S(2)}) collective-permute-start(bf16[240,768]{1,0:T(8,128)(2,1)S(1)} %shard_map.93.refs_0_), channel_id=1, source_target_pairs={{0,16},{8,136},{16,0},{24,152},{32,48},{40,168},{48,32},{56,184},{... | collective-permute-start | bytes 1105928 | tf_op jit(solution)/shard_map/ppermute | solution.py:240
  61.9 13.7 %collective-permute-start.6 = (bf16[480,768]{1,0:T(8,128)(2,1)S(1)}, bf16[480,768]{1,0:T(8,128)(2,1)S(1)}, u32[]{:S(2)}, u32[]{:S(2)}) collective-permute-start(bf16[480,768]{1,0:T(8,128)(2,1)S(1)} %shard_map.90.refs_0_), channel_id=1, source_target_pairs={{0,48},{8,392},{16,32},{24,408},{32,16},{40,424},{48,0},{56,440},{... | collective-permute-start | bytes 2211848 | tf_op jit(solution)/shard_map/ppermute | solution.py:240
  67.5 16.1 %collective-permute-start.12 = (bf16[480,768]{1,0:T(8,128)(2,1)S(1)}, bf16[480,768]{1,0:T(8,128)(2,1)S(1)}, u32[]{:S(2)}, u32[]{:S(2)}) collective-permute-start(bf16[480,768]{1,0:T(8,128)(2,1)S(1)} %shard_map.94.refs_0_), channel_id=1, source_target_pairs={{0,48},{8,392},{16,32},{24,408},{32,16},{40,424},{48,0},{56,440},{... | collective-permute-start | bytes 2211848 | tf_op jit(solution)/shard_map/ppermute | solution.py:240
  76.3 7.9 %copy-start = (bf16[960,768]{1,0:T(8,128)(2,1)}, bf16[960,768]{1,0:T(8,128)(2,1)S(1)}, u32[]{:S(2)}) copy-start(bf16[960,768]{1,0:T(8,128)(2,1)S(1)} %shard_map.91.refs_0_) | copy-start | bytes 4423684
  76.3 22.5 %collective-permute-start.8 = (bf16[960,768]{1,0:T(8,128)(2,1)S(1)}, bf16[960,768]{1,0:T(8,128)(2,1)S(1)}, u32[]{:S(2)}, u32[]{:S(2)}) collective-permute-start(bf16[960,768]{1,0:T(8,128)(2,1)S(1)} %shard_map.91.refs_0_), channel_id=1, source_target_pairs={{0,384},{8,56},{16,400},{24,8},{32,416},{40,24},{48,432},{56,40},{... | collective-permute-start | bytes 4423688 | tf_op jit(solution)/shard_map/ppermute | solution.py:231
  80.4 21.7 %collective-permute-start.7 = (bf16[960,768]{1,0:T(8,128)(2,1)S(1)}, bf16[960,768]{1,0:T(8,128)(2,1)S(1)}, u32[]{:S(2)}, u32[]{:S(2)}) collective-permute-start(bf16[960,768]{1,0:T(8,128)(2,1)S(1)} %shard_map.91.refs_0_), channel_id=1, source_target_pairs={{0,128},{8,24},{16,144},{24,40},{32,160},{40,56},{48,176},{56,8},{... | collective-permute-start | bytes 4423688 | tf_op jit(solution)/shard_map/ppermute | solution.py:231
  84.2 19.1 %copy-start.3 = (bf16[960,768]{1,0:T(8,128)(2,1)}, bf16[960,768]{1,0:T(8,128)(2,1)S(1)}, u32[]{:S(2)}) copy-start(bf16[960,768]{1,0:T(8,128)(2,1)S(1)} %shard_map.95.refs_5_) | copy-start | bytes 4423684
  84.2 30.4 %collective-permute-start.14 = (bf16[960,768]{1,0:T(8,128)(2,1)S(1)}, bf16[960,768]{1,0:T(8,128)(2,1)S(1)}, u32[]{:S(2)}, u32[]{:S(2)}) collective-permute-start(bf16[960,768]{1,0:T(8,128)(2,1)S(1)} %shard_map.95.refs_5_), channel_id=1, source_target_pairs={{0,384},{8,56},{16,400},{24,8},{32,416},{40,24},{48,432},{56,40},{... | collective-permute-start | bytes 4423688 | tf_op jit(solution)/shard_map/ppermute | solution.py:231
  88.3 29.5 %collective-permute-start.13 = (bf16[960,768]{1,0:T(8,128)(2,1)S(1)}, bf16[960,768]{1,0:T(8,128)(2,1)S(1)}, u32[]{:S(2)}, u32[]{:S(2)}) collective-permute-start(bf16[960,768]{1,0:T(8,128)(2,1)S(1)} %shard_map.95.refs_5_), channel_id=1, source_target_pairs={{0,128},{8,24},{16,144},{24,40},{32,160},{40,56},{48,176},{56,8},{... | collective-permute-start | bytes 4423688 | tf_op jit(solution)/shard_map/ppermute | solution.py:231
  98.8 3.9 %copy-start.1 = (bf16[960,768]{1,0:T(8,128)(2,1)}, bf16[960,768]{1,0:T(8,128)(2,1)S(1)}, u32[]{:S(2)}) copy-start(bf16[960,768]{1,0:T(8,128)(2,1)S(1)} %collective-permute-done.8.refs_1_.refs_2_) | copy-start | bytes 4423684
  103.3 22.9 %collective-permute-start.9 = (bf16[480,768]{1,0:T(8,128)(2,1)S(1)}, bf16[480,768]{1,0:T(8,128)(2,1)}, u32[]{:S(2)}, u32[]{:S(2)}) collective-permute-start(bf16[480,768]{1,0:T(8,128)(2,1)S(1)} %get-tuple-element.31), channel_id=1, source_target_pairs={{0,128},{8,24},{16,144},{24,40},{32,160},{40,56},{48,176},{56,8},{... | collective-permute-start | bytes 2211848 | tf_op jit(solution)/shard_map/ppermute | solution.py:231
  105.2 21.0 %collective-permute-start.10 = (bf16[480,768]{1,0:T(8,128)(2,1)S(1)}, bf16[480,768]{1,0:T(8,128)(2,1)}, u32[]{:S(2)}, u32[]{:S(2)}) collective-permute-start(bf16[480,768]{1,0:T(8,128)(2,1)S(1)} %get-tuple-element.32), channel_id=1, source_target_pairs={{0,384},{8,56},{16,400},{24,8},{32,416},{40,24},{48,432},{56,40},{... | collective-permute-start | bytes 2211848 | tf_op jit(solution)/shard_map/ppermute | solution.py:231
  119.0 14.7 %collective-permute-start.15 = (bf16[480,768]{1,0:T(8,128)(2,1)S(1)}, bf16[480,768]{1,0:T(8,128)(2,1)}, u32[]{:S(2)}, u32[]{:S(2)}) collective-permute-start(bf16[480,768]{1,0:T(8,128)(2,1)S(1)} %get-tuple-element.34), channel_id=1, source_target_pairs={{0,128},{8,24},{16,144},{24,40},{32,160},{40,56},{48,176},{56,8},{... | collective-permute-start | bytes 2211848 | tf_op jit(solution)/shard_map/ppermute | solution.py:231
  120.9 13.0 %collective-permute-start.16 = (bf16[480,768]{1,0:T(8,128)(2,1)S(1)}, bf16[480,768]{1,0:T(8,128)(2,1)}, u32[]{:S(2)}, u32[]{:S(2)}) collective-permute-start(bf16[480,768]{1,0:T(8,128)(2,1)S(1)} %get-tuple-element.35), channel_id=1, source_target_pairs={{0,384},{8,56},{16,400},{24,8},{32,416},{40,24},{48,432},{56,40},{... | collective-permute-start | bytes 2211848 | tf_op jit(solution)/shard_map/ppermute | solution.py:231
  126.2 55.2 %copy-start.8 = (bf16[256,256]{1,0:T(8,128)(2,1)S(1)}, bf16[256,256]{1,0:T(8,128)(2,1)}, u32[]{:S(2)}) copy-start(bf16[256,256]{1,0:T(8,128)(2,1)} %get-tuple-element.24.sel_ref) | copy-start | bytes 393220
  126.2 55.2 %copy-start.9 = (s32[256,6]{0,1:T(8,128)S(1)}, s32[256,6]{0,1:T(8,128)}, u32[]{:S(2)}) copy-start(s32[256,6]{0,1:T(8,128)} %param.9) | copy-start | bytes 18436
  126.2 55.2 %copy-start.10 = (bf16[256,6]{0,1:T(8,128)(2,1)S(1)}, bf16[256,6]{0,1:T(8,128)(2,1)}, u32[]{:S(2)}) copy-start(bf16[256,6]{0,1:T(8,128)(2,1)} %param.10) | copy-start | bytes 9220
  126.2 55.2 %copy-start.11 = (s32[5]{0:T(128)S(1)}, s32[5]{0:T(128)}, u32[]{:S(2)}) copy-start(s32[5]{0:T(128)} %stack.23.where_ref) | copy-start | bytes 64
  145.6 17.9 %collective-permute-start.17 = (bf16[32,2688]{1,0:T(8,128)(2,1)}, bf16[32,2688]{1,0:T(8,128)(2,1)S(1)}, u32[]{:S(2)}, u32[]{:S(2)}) collective-permute-start(bf16[32,2688]{1,0:T(8,128)(2,1)} %get-tuple-element.37), channel_id=1, source_target_pairs={{0,1},{1,0},{2,3},{3,2},{8,9},{9,8},{10,11},{11,10},{4,5},{5,4},{6... | collective-permute-start | bytes 516104 | tf_op jit(solution)/shard_map/ppermute | solution.py:346
  148.9 19.9 %collective-permute-start.18 = (bf16[32,2688]{1,0:T(8,128)(2,1)}, bf16[32,2688]{1,0:T(8,128)(2,1)S(1)}, u32[]{:S(2)}, u32[]{:S(2)}) collective-permute-start(bf16[32,2688]{1,0:T(8,128)(2,1)} %get-tuple-element.38), channel_id=1, source_target_pairs={{0,2},{1,3},{2,0},{3,1},{8,10},{9,11},{10,8},{11,9},{4,6},{5,7},{6... | collective-permute-start | bytes 516104 | tf_op jit(solution)/shard_map/ppermute | solution.py:346
  152.9 18.9 %collective-permute-start.19 = (bf16[32,2688]{1,0:T(8,128)(2,1)}, bf16[32,2688]{1,0:T(8,128)(2,1)S(1)}, u32[]{:S(2)}, u32[]{:S(2)}) collective-permute-start(bf16[32,2688]{1,0:T(8,128)(2,1)} %get-tuple-element.39), channel_id=1, source_target_pairs={{0,3},{1,2},{2,1},{3,0},{8,11},{9,10},{10,9},{11,8},{4,7},{5,6},{6... | collective-permute-start | bytes 516104 | tf_op jit(solution)/shard_map/ppermute | solution.py:346
  154.9 16.9 %collective-permute-start.20 = (bf16[32,2688]{1,0:T(8,128)(2,1)}, bf16[32,2688]{1,0:T(8,128)(2,1)S(1)}, u32[]{:S(2)}, u32[]{:S(2)}) collective-permute-start(bf16[32,2688]{1,0:T(8,128)(2,1)} %get-tuple-element.40), channel_id=1, source_target_pairs={{0,8},{1,9},{2,10},{3,11},{8,0},{9,1},{10,2},{11,3},{4,12},{5,13},... | collective-permute-start | bytes 516104 | tf_op jit(solution)/shard_map/ppermute | solution.py:346
  160.9 11.3 %collective-permute-start.21 = (bf16[32,2688]{1,0:T(8,128)(2,1)}, bf16[32,2688]{1,0:T(8,128)(2,1)S(1)}, u32[]{:S(2)}, u32[]{:S(2)}) collective-permute-start(bf16[32,2688]{1,0:T(8,128)(2,1)} %get-tuple-element.41), channel_id=1, source_target_pairs={{0,9},{1,8},{2,11},{3,10},{8,1},{9,0},{10,3},{11,2},{4,13},{5,12},... | collective-permute-start | bytes 516104 | tf_op jit(solution)/shard_map/ppermute | solution.py:346
  163.6 17.8 %collective-permute-start.22 = (bf16[32,2688]{1,0:T(8,128)(2,1)}, bf16[32,2688]{1,0:T(8,128)(2,1)S(1)}, u32[]{:S(2)}, u32[]{:S(2)}) collective-permute-start(bf16[32,2688]{1,0:T(8,128)(2,1)} %get-tuple-element.42), channel_id=1, source_target_pairs={{0,10},{1,11},{2,8},{3,9},{8,2},{9,3},{10,0},{11,1},{4,14},{5,15},... | collective-permute-start | bytes 516104 | tf_op jit(solution)/shard_map/ppermute | solution.py:346
  168.8 12.5 %collective-permute-start.23 = (bf16[32,2688]{1,0:T(8,128)(2,1)}, bf16[32,2688]{1,0:T(8,128)(2,1)S(1)}, u32[]{:S(2)}, u32[]{:S(2)}) collective-permute-start(bf16[32,2688]{1,0:T(8,128)(2,1)} %get-tuple-element.43), channel_id=1, source_target_pairs={{0,11},{1,10},{2,9},{3,8},{8,3},{9,2},{10,1},{11,0},{4,15},{5,14},... | collective-permute-start | bytes 516104 | tf_op jit(solution)/shard_map/ppermute | solution.py:346
  (5 other events, 8.0 us)

commit v10 on v9

--- a/solution.py
+++ b/solution.py
@@ -245,16 +245,16 @@
     beside = exchange(own, 1)
     (half,) = join([2 * count], [(n, 0, count, 0, n * count) for n in range(2)], own, beside)
     across = exchange(half, 3)
-    (line,) = join([4 * count], [(n, 0, 2 * count, 0, 2 * n * count) for n in range(2)], half, across)
-    line_low, line_high = shift(line, 1), shift(line, -1)
-    far0, far1 = join(
-        [2 * count] * 2, [(0, 0, 2 * count, 0, 0), (1, 2 * count, 2 * count, 1, 0)], line_low, line_high
-    )
-    far0, far1 = shift(far0, 1), shift(far1, -1)
+    half_low, half_high = shift(half, 1), shift(half, -1)
+    across_high, across_low = shift(across, -1), shift(across, 1)
+    half_far, across_far = shift(half_low, 1), shift(across_high, -1)
+    arrays = (half, across, half_low, across_low, half_high, across_high, half_far, across_far)
+    fars = (0, 0, 3, 3, 1, 1, 2, 2)
     near = (0, 1, 3, 2)
-    pieces = [(first + n, k * count, chain, far, near[k]) for n, far in enumerate((0, 3, 1)) for k in range(4)]
-    pieces += [(first + 3 + k // 2, k % 2 * count, chain, 2, near[k]) for k in range(4)]
-    return (line, line_low, line_high, far0, far1), pieces, beside
+    pieces = [
+        (first + n, k * count, chain, fars[n], near[n % 2 * 2 + k]) for n in range(8) for k in range(2)
+    ]
+    return arrays, pieces, beside
 
 
 def on_device(tokens_in, cotangent, routes, gate_weights, gate_proj, up_proj, down_proj):

time: 188 us -> 192 us (1.021)
  starting transfers between devices: 98.2 us -> 108 us
  Pallas kernels: 25 us -> 22.6 us
    ppermute x8 -> x12, starting transfers between devices: 25 us -> 36.1 us  [shift(): return lax.ppermute(v, ('x', 'y', 'c'), pairs)]
    ppermute x8 -> x12, waiting for transfers between devices: 27.5 us -> 18.7 us  [shift(): return lax.ppermute(v, ('x', 'y', 'c'), pairs)]
    ppermute x4, waiting for transfers between devices: 7.34 us -> 14.7 us  [exchange(): return lax.ppermute(v, ('x', 'y', 'c'), pairs)]
    pallas_call x6 -> x2, Pallas kernels: 3.14 us -> 0.64 us  [join(): pl.pallas_call(functools.partial(join_kernel, plan, len(arrays)), out_sha...]
  transfers between devices with their start and end apart: 25 -> 29, of which waited for: 15 -> 9; matrix products, arithmetic and copies ran while one was open for 0% -> 0% of each run, Pallas kernels for 5% -> 3%
where the time goes in v10:
time: 192 us; the launch traced here: 191 us
  starting transfers between devices  108 us (56%)
  waiting for transfers between devices  56.5 us (29%)
  Pallas kernels  22.6 us (12%)
  local copies, waits for them, and re-layouts  2.52 us (1%)
    ppermute x12, starting transfers between devices, shift(): return lax.ppermute(v, ('x', 'y', 'c'), pairs)  36.1 us
    ppermute x7, starting transfers between devices, on_device(): home[r] = lax.ppermute(back[r], ('c', 'zr'), pairs)  25.7 us
    ppermute x4, starting transfers between devices, zmove(): return lax.ppermute(v, ('zh', 'c', 'zq'), pairs)  19.3 us
    ppermute x12, waiting for transfers between devices, shift(): return lax.ppermute(v, ('x', 'y', 'c'), pairs)  18.7 us
    ppermute x4, waiting for transfers between devices, exchange(): return lax.ppermute(v, ('x', 'y', 'c'), pairs)  14.7 us
    pallas_call x1, Pallas kernels, on_device(): pl.pallas_call(functools.partial(expert_kernel, pieces), out_shape=[jax.S...  11.8 us
    ppermute x4, waiting for transfers between devices, zmove(): return lax.ppermute(v, ('zh', 'c', 'zq'), pairs)  11.7 us
    ppermute x4, starting transfers between devices, exchange(): return lax.ppermute(v, ('x', 'y', 'c'), pairs)  11.5 us
  transfers between devices with their start and end apart: 29, of which 9 were waited for; matrix products, arithmetic and copies ran while one was open for 0% of the time, Pallas kernels for 3%

profile of v10, /device:TPU:1, one launch (start us, length us, event | category | flops | bytes accessed | tf_op | source)
XLA Modules:
  0.0 190.8 jit_solution(632897508656732287)
XLA Ops:
  2.2 8.8 %collective-permute-start = (bf16[3,40,768]{2,1,0:T(8,128)(2,1)}, bf16[3,40,768]{2,1,0:T(8,128)(2,1)S(1)}, u32[]{:S(2)}, u32[]{:S(2)}) collective-permute-start(bf16[3,40,768]{2,1,0:T(8,128)(2,1)} %shard_map.87.shard_ref), channel_id=1, source_target_pairs={{8,0},{4,12},{9,1},{5,13},{10,2},{6,14},{11,3},{7,15},{24,16},{20,... | collective-permute-start | bytes 552968 | tf_op jit(solution)/shard_map/ppermute | solution.py:273
  15.8 5.6 %shard_map.86 = (bf16[8,64,2560]{2,1,0:T(8,128)(2,1)}, bf16[256,256]{1,0:T(8,128)(2,1)}) custom-call(s32[6,256]{1,0:T(8,128)} %bitcast.9, bf16[256,2560]{1,0:T(8,128)(2,1)} %tok_ref.1, bf16[256,2560]{1,0:T(8,128)(2,1)} %cot_ref.1), custom_call_target="tpu_custom_call" | custom-call | flops 671088640 | bytes 5242880 | tf_op jit(solution)/shard_map/pallas_call | solution.py:298
  21.4 5.9 %collective-permute-done.1.low = bf16[240,768]{1,0:T(8,128)(2,1)S(1)} collective-permute-done((bf16[240,768]{1,0:T(8,128)(2,1)S(1)}, bf16[240,768]{1,0:T(8,128)(2,1)S(1)}, u32[]{:S(2)}, u32[]{:S(2)}) %collective-permute-start.1) | collective-permute-done | bytes 368672 | tf_op jit(solution)/shard_map/ppermute | solution.py:292
  29.2 15.4 %collective-permute-start.2 = (bf16[128,768]{1,0:T(8,128)(2,1)S(1)}, bf16[128,768]{1,0:T(8,128)(2,1)S(1)}, u32[]{:S(2)}, u32[]{:S(2)}) collective-permute-start(bf16[128,768]{1,0:T(8,128)(2,1)S(1)} %get-tuple-element.24), channel_id=1, source_target_pairs={{4,64},{68,0},{8,12},{72,76},{5,65},{69,1},{9,13},{73,77},{6,66},{... | collective-permute-start | bytes 589832 | tf_op jit(solution)/shard_map/ppermute | solution.py:292
  46.0 2.4 %collective-permute-done.4.bottom = bf16[112,768]{1,0:T(8,128)(2,1)S(1)} collective-permute-done((bf16[112,768]{1,0:T(8,128)(2,1)S(1)}, bf16[112,768]{1,0:T(8,128)(2,1)S(1)}, u32[]{:S(2)}, u32[]{:S(2)}) %collective-permute-start.4) | collective-permute-done | bytes 172064 | tf_op jit(solution)/shard_map/ppermute | solution.py:292
  48.4 3.4 %collective-permute-done.2.top = bf16[128,768]{1,0:T(8,128)(2,1)S(1)} collective-permute-done((bf16[128,768]{1,0:T(8,128)(2,1)S(1)}, bf16[128,768]{1,0:T(8,128)(2,1)S(1)}, u32[]{:S(2)}, u32[]{:S(2)}) %collective-permute-start.2) | collective-permute-done | bytes 196640 | tf_op jit(solution)/shard_map/ppermute | solution.py:292
  51.8 6.7 %all-to-all-start = ((bf16[8,64,2560]{2,1,0:T(8,128)(2,1)}), bf16[8,64,2560]{2,1,0:T(8,128)(2,1)}, u32[]{:S(2)}, u32[]{:S(2)}) async-start(bf16[8,64,2560]{2,1,0:T(8,128)(2,1)} %get-tuple-element.26), calls=%async_computation | async-start | bytes 5242880 | tf_op jit(solution)/shard_map/all_to_all | solution.py:322
  58.5 3.1 %collective-permute-start.13 = (bf16[240,768]{1,0:T(8,128)(2,1)S(1)}, bf16[240,768]{1,0:T(8,128)(2,1)S(1)}, u32[]{:S(2)}, u32[]{:S(2)}) collective-permute-start(bf16[240,768]{1,0:T(8,128)(2,1)S(1)} %shard_map.91.refs_0_), channel_id=1, source_target_pairs={{0,16},{8,136},{16,0},{24,152},{32,48},{40,168},{48,32},{56,184},{... | collective-permute-start | bytes 1105928 | tf_op jit(solution)/shard_map/ppermute | solution.py:240
  61.9 4.1 %collective-permute-start.9 = (bf16[480,768]{1,0:T(8,128)(2,1)S(1)}, bf16[480,768]{1,0:T(8,128)(2,1)S(1)}, u32[]{:S(2)}, u32[]{:S(2)}) collective-permute-start(bf16[480,768]{1,0:T(8,128)(2,1)S(1)} %shard_map.90.refs_0_), channel_id=1, source_target_pairs={{0,384},{8,56},{16,400},{24,8},{32,416},{40,24},{48,432},{56,40},{... | collective-permute-start | bytes 2211848 | tf_op jit(solution)/shard_map/ppermute | solution.py:231
  68.0 3.8 %collective-permute-start.6 = (bf16[480,768]{1,0:T(8,128)(2,1)S(1)}, bf16[480,768]{1,0:T(8,128)(2,1)}, u32[]{:S(2)}, u32[]{:S(2)}) collective-permute-start(bf16[480,768]{1,0:T(8,128)(2,1)S(1)} %shard_map.90.refs_0_), channel_id=1, source_target_pairs={{0,48},{8,392},{16,32},{24,408},{32,16},{40,424},{48,0},{56,440},{... | collective-permute-start | bytes 2211848 | tf_op jit(solution)/shard_map/ppermute | solution.py:240
  72.1 2.7 %collective-permute-start.14 = (bf16[480,768]{1,0:T(8,128)(2,1)S(1)}, bf16[480,768]{1,0:T(8,128)(2,1)}, u32[]{:S(2)}, u32[]{:S(2)}) collective-permute-start(bf16[480,768]{1,0:T(8,128)(2,1)S(1)} %shard_map.92.refs_8_), channel_id=1, source_target_pairs={{0,48},{8,392},{16,32},{24,408},{32,16},{40,424},{48,0},{56,440},{... | collective-permute-start | bytes 2211848 | tf_op jit(solution)/shard_map/ppermute | solution.py:240
  74.8 4.6 %collective-permute-start.17 = (bf16[480,768]{1,0:T(8,128)(2,1)S(1)}, bf16[480,768]{1,0:T(8,128)(2,1)S(1)}, u32[]{:S(2)}, u32[]{:S(2)}) collective-permute-start(bf16[480,768]{1,0:T(8,128)(2,1)S(1)} %shard_map.92.refs_8_), channel_id=1, source_target_pairs={{0,384},{8,56},{16,400},{24,8},{32,416},{40,24},{48,432},{56,40},{... | collective-permute-start | bytes 2211848 | tf_op jit(solution)/shard_map/ppermute | solution.py:231
  79.4 1.9 %collective-permute-start.15 = (bf16[480,768]{1,0:T(8,128)(2,1)S(1)}, bf16[480,768]{1,0:T(8,128)(2,1)}, u32[]{:S(2)}, u32[]{:S(2)}) collective-permute-start(bf16[480,768]{1,0:T(8,128)(2,1)S(1)} %shard_map.92.refs_8_), channel_id=1, source_target_pairs={{0,128},{8,24},{16,144},{24,40},{32,160},{40,56},{48,176},{56,8},{... | collective-permute-start | bytes 2211848 | tf_op jit(solution)/shard_map/ppermute | solution.py:231
  81.4 3.5 %collective-permute-done.7.refs_2_ = bf16[480,768]{1,0:T(8,128)(2,1)S(1)} collective-permute-done((bf16[480,768]{1,0:T(8,128)(2,1)S(1)}, bf16[480,768]{1,0:T(8,128)(2,1)S(1)}, u32[]{:S(2)}, u32[]{:S(2)}) %collective-permute-start.7) | collective-permute-done | bytes 737312 | tf_op jit(solution)/shard_map/ppermute | solution.py:231
  86.8 2.9 %collective-permute-done.6.refs_1_ = bf16[480,768]{1,0:T(8,128)(2,1)} collective-permute-done((bf16[480,768]{1,0:T(8,128)(2,1)S(1)}, bf16[480,768]{1,0:T(8,128)(2,1)}, u32[]{:S(2)}, u32[]{:S(2)}) %collective-permute-start.6) | collective-permute-done | bytes 737312 | tf_op jit(solution)/shard_map/ppermute | solution.py:240
  89.7 3.9 %collective-permute-start.10 = (bf16[480,768]{1,0:T(8,128)(2,1)}, bf16[480,768]{1,0:T(8,128)(2,1)}, u32[]{:S(2)}, u32[]{:S(2)}) collective-permute-start(bf16[480,768]{1,0:T(8,128)(2,1)} %collective-permute-done.6.refs_1_), channel_id=1, source_target_pairs={{0,384},{8,56},{16,400},{24,8},{32,416},{40,24},{48,432},{56,40},{... | collective-permute-start | bytes 2211848 | tf_op jit(solution)/shard_map/ppermute | solution.py:231
  93.6 11.8 %collective-permute-done.14.refs_9_ = bf16[480,768]{1,0:T(8,128)(2,1)} collective-permute-done((bf16[480,768]{1,0:T(8,128)(2,1)S(1)}, bf16[480,768]{1,0:T(8,128)(2,1)}, u32[]{:S(2)}, u32[]{:S(2)}) %collective-permute-start.14) | collective-permute-done | bytes 737312 | tf_op jit(solution)/shard_map/ppermute | solution.py:240
  105.5 3.8 %collective-permute-start.18 = (bf16[480,768]{1,0:T(8,128)(2,1)}, bf16[480,768]{1,0:T(8,128)(2,1)}, u32[]{:S(2)}, u32[]{:S(2)}) collective-permute-start(bf16[480,768]{1,0:T(8,128)(2,1)} %collective-permute-done.14.refs_9_), channel_id=1, source_target_pairs={{0,384},{8,56},{16,400},{24,8},{32,416},{40,24},{48,432},{56,40},{... | collective-permute-start | bytes 2211848 | tf_op jit(solution)/shard_map/ppermute | solution.py:231
  109.4 1.9 %collective-permute-start.8 = (bf16[480,768]{1,0:T(8,128)(2,1)}, bf16[480,768]{1,0:T(8,128)(2,1)}, u32[]{:S(2)}, u32[]{:S(2)}) collective-permute-start(bf16[480,768]{1,0:T(8,128)(2,1)} %collective-permute-done.6.refs_1_), channel_id=1, source_target_pairs={{0,128},{8,24},{16,144},{24,40},{32,160},{40,56},{48,176},{56,8},{... | collective-permute-start | bytes 2211848 | tf_op jit(solution)/shard_map/ppermute | solution.py:231
  113.3 2.9 %collective-permute-start.19 = (bf16[480,768]{1,0:T(8,128)(2,1)}, bf16[480,768]{1,0:T(8,128)(2,1)}, u32[]{:S(2)}, u32[]{:S(2)}) collective-permute-start(bf16[480,768]{1,0:T(8,128)(2,1)} %collective-permute-done.15.refs_10_), channel_id=1, source_target_pairs={{0,128},{8,24},{16,144},{24,40},{32,160},{40,56},{48,176},{56,8},{... | collective-permute-start | bytes 2211848 | tf_op jit(solution)/shard_map/ppermute | solution.py:231
  116.2 3.6 %collective-permute-start.12 = (bf16[480,768]{1,0:T(8,128)(2,1)}, bf16[480,768]{1,0:T(8,128)(2,1)}, u32[]{:S(2)}, u32[]{:S(2)}) collective-permute-start(bf16[480,768]{1,0:T(8,128)(2,1)} %collective-permute-done.10.refs_5_), channel_id=1, source_target_pairs={{0,384},{8,56},{16,400},{24,8},{32,416},{40,24},{48,432},{56,40},{... | collective-permute-start | bytes 2211848 | tf_op jit(solution)/shard_map/ppermute | solution.py:231
  119.8 3.5 %collective-permute-start.20 = (bf16[480,768]{1,0:T(8,128)(2,1)}, bf16[480,768]{1,0:T(8,128)(2,1)}, u32[]{:S(2)}, u32[]{:S(2)}) collective-permute-start(bf16[480,768]{1,0:T(8,128)(2,1)} %collective-permute-done.18.refs_13_), channel_id=1, source_target_pairs={{0,384},{8,56},{16,400},{24,8},{32,416},{40,24},{48,432},{56,40},{... | collective-permute-start | bytes 2211848 | tf_op jit(solution)/shard_map/ppermute | solution.py:231
  124.0 15.2 %collective-permute-done.19.refs_14_ = bf16[480,768]{1,0:T(8,128)(2,1)} collective-permute-done((bf16[480,768]{1,0:T(8,128)(2,1)}, bf16[480,768]{1,0:T(8,128)(2,1)}, u32[]{:S(2)}, u32[]{:S(2)}) %collective-permute-start.19) | collective-permute-done | bytes 737312 | tf_op jit(solution)/shard_map/ppermute | solution.py:231
  139.3 11.8 %shard_map.93 = (bf16[32,2688]{1,0:T(8,128)(2,1)}, bf16[32,2688]{1,0:T(8,128)(2,1)}, bf16[32,2688]{1,0:T(8,128)(2,1)}, bf16[32,2688]{1,0:T(8,128)(2,1)}, bf16[32...) custom-call(s32[5]{0:T(128)} %stack.23.where_ref, ...), custom_call_target="tpu_custom_call" | custom-call | flops 5033164800 | bytes 11796480 | tf_op jit(solution)/shard_map/pallas_call | solution.py:328
  151.1 3.7 %collective-permute-start.21 = (bf16[32,2688]{1,0:T(8,128)(2,1)}, bf16[32,2688]{1,0:T(8,128)(2,1)S(1)}, u32[]{:S(2)}, u32[]{:S(2)}) collective-permute-start(bf16[32,2688]{1,0:T(8,128)(2,1)} %get-tuple-element.29), channel_id=1, source_target_pairs={{0,1},{1,0},{2,3},{3,2},{8,9},{9,8},{10,11},{11,10},{4,5},{5,4},{6... | collective-permute-start | bytes 516104 | tf_op jit(solution)/shard_map/ppermute | solution.py:346
  154.7 4.0 %collective-permute-start.22 = (bf16[32,2688]{1,0:T(8,128)(2,1)}, bf16[32,2688]{1,0:T(8,128)(2,1)S(1)}, u32[]{:S(2)}, u32[]{:S(2)}) collective-permute-start(bf16[32,2688]{1,0:T(8,128)(2,1)} %get-tuple-element.30), channel_id=1, source_target_pairs={{0,2},{1,3},{2,0},{3,1},{8,10},{9,11},{10,8},{11,9},{4,6},{5,7},{6... | collective-permute-start | bytes 516104 | tf_op jit(solution)/shard_map/ppermute | solution.py:346
  160.6 4.3 %collective-permute-start.24 = (bf16[32,2688]{1,0:T(8,128)(2,1)}, bf16[32,2688]{1,0:T(8,128)(2,1)S(1)}, u32[]{:S(2)}, u32[]{:S(2)}) collective-permute-start(bf16[32,2688]{1,0:T(8,128)(2,1)} %get-tuple-element.32), channel_id=1, source_target_pairs={{0,8},{1,9},{2,10},{3,11},{8,0},{9,1},{10,2},{11,3},{4,12},{5,13},... | collective-permute-start | bytes 516104 | tf_op jit(solution)/shard_map/ppermute | solution.py:346
  165.0 2.3 %collective-permute-start.25 = (bf16[32,2688]{1,0:T(8,128)(2,1)}, bf16[32,2688]{1,0:T(8,128)(2,1)S(1)}, u32[]{:S(2)}, u32[]{:S(2)}) collective-permute-start(bf16[32,2688]{1,0:T(8,128)(2,1)} %get-tuple-element.33), channel_id=1, source_target_pairs={{0,9},{1,8},{2,11},{3,10},{8,1},{9,0},{10,3},{11,2},{4,13},{5,12},... | collective-permute-start | bytes 516104 | tf_op jit(solution)/shard_map/ppermute | solution.py:346
  167.3 5.3 %collective-permute-start.26 = (bf16[32,2688]{1,0:T(8,128)(2,1)}, bf16[32,2688]{1,0:T(8,128)(2,1)S(1)}, u32[]{:S(2)}, u32[]{:S(2)}) collective-permute-start(bf16[32,2688]{1,0:T(8,128)(2,1)} %get-tuple-element.34), channel_id=1, source_target_pairs={{0,10},{1,11},{2,8},{3,9},{8,2},{9,3},{10,0},{11,1},{4,14},{5,15},... | collective-permute-start | bytes 516104 | tf_op jit(solution)/shard_map/ppermute | solution.py:346
  172.6 4.3 %collective-permute-start.27 = (bf16[32,2688]{1,0:T(8,128)(2,1)}, bf16[32,2688]{1,0:T(8,128)(2,1)S(1)}, u32[]{:S(2)}, u32[]{:S(2)}) collective-permute-start(bf16[32,2688]{1,0:T(8,128)(2,1)} %get-tuple-element.35), channel_id=1, source_target_pairs={{0,11},{1,10},{2,9},{3,8},{8,3},{9,2},{10,1},{11,0},{4,15},{5,14},... | collective-permute-start | bytes 516104 | tf_op jit(solution)/shard_map/ppermute | solution.py:346
  176.8 10.1 %collective-permute-done.26.refs_6_ = bf16[32,2688]{1,0:T(8,128)(2,1)S(1)} collective-permute-done((bf16[32,2688]{1,0:T(8,128)(2,1)}, bf16[32,2688]{1,0:T(8,128)(2,1)S(1)}, u32[]{:S(2)}, u32[]{:S(2)}) %collective-permute-start.26) | collective-permute-done | bytes 172064 | tf_op jit(solution)/shard_map/ppermute | solution.py:346
  187.9 2.9 %shard_map.94 = (bf16[256,2560]{1,0:T(8,128)(2,1)}, bf16[6,256]{1,0:T(8,128)(2,1)}) custom-call(s32[5]{0:T(128)S(1)} %copy-done.7, s32[6,256]{1,0:T(8,128)S(1)} %bitcast.10, bf16[6,256]{1,0:T(8,128)(2,1)S(1)} %bitcast.11, bf16[256,256]{1,0:T(8,128)(2,1)S(1)} %copy-done.4, bf16[32,2688]{1,0:T(8,128)(2,1)S(1)} %copy-done.3, ...), custom_call_target="tpu_custom_call" | custom-call | flops 335544320 | bytes 2621440 | tf_op jit(solution)/shard_map/pallas_call | solution.py:349
  (61 shorter events, 19.6 us)
Async XLA Ops:
  2.2 10.0 %collective-permute-start = (bf16[3,40,768]{2,1,0:T(8,128)(2,1)}, bf16[3,40,768]{2,1,0:T(8,128)(2,1)S(1)}, u32[]{:S(2)}, u32[]{:S(2)}) collective-permute-start(bf16[3,40,768]{2,1,0:T(8,128)(2,1)} %shard_map.87.shard_ref), channel_id=1, source_target_pairs={{8,0},{4,12},{9,1},{5,13},{10,2},{6,14},{11,3},{7,15},{24,16},{20,... | collective-permute-start | bytes 552968 | tf_op jit(solution)/shard_map/ppermute | solution.py:273
  13.2 14.1 %collective-permute-start.1 = (bf16[240,768]{1,0:T(8,128)(2,1)S(1)}, bf16[240,768]{1,0:T(8,128)(2,1)S(1)}, u32[]{:S(2)}, u32[]{:S(2)}) collective-permute-start(bf16[240,768]{1,0:T(8,128)(2,1)S(1)} %shard_map.88.mine), channel_id=1, source_target_pairs={{0,4},{64,68},{12,72},{76,8},{1,5},{65,69},{13,73},{77,9},{2,6},{6... | collective-permute-start | bytes 1105928 | tf_op jit(solution)/shard_map/ppermute | solution.py:292
  14.5 30.2 %collective-permute-start.3 = (bf16[240,768]{1,0:T(8,128)(2,1)S(1)}, bf16[240,768]{1,0:T(8,128)(2,1)S(1)}, u32[]{:S(2)}, u32[]{:S(2)}) collective-permute-start(bf16[240,768]{1,0:T(8,128)(2,1)S(1)} %shard_map.88.mine), channel_id=1, source_target_pairs={{0,68},{64,4},{12,8},{76,72},{1,69},{65,5},{13,9},{77,73},{2,70},{... | collective-permute-start | bytes 1105928 | tf_op jit(solution)/shard_map/ppermute | solution.py:292
  27.3 24.5 %collective-permute-start.5 = (bf16[240,768]{1,0:T(8,128)(2,1)S(1)}, bf16[240,768]{1,0:T(8,128)(2,1)S(1)}, u32[]{:S(2)}, u32[]{:S(2)}) collective-permute-start(bf16[240,768]{1,0:T(8,128)(2,1)S(1)} %get-tuple-element.25.refs_0_), channel_id=1, source_target_pairs={{0,16},{8,136},{16,0},{24,152},{32,48},{40,168},{48,32},{56,184},{... | collective-permute-start | bytes 1105928 | tf_op jit(solution)/shard_map/ppermute | solution.py:240
  29.2 22.5 %collective-permute-start.2 = (bf16[128,768]{1,0:T(8,128)(2,1)S(1)}, bf16[128,768]{1,0:T(8,128)(2,1)S(1)}, u32[]{:S(2)}, u32[]{:S(2)}) collective-permute-start(bf16[128,768]{1,0:T(8,128)(2,1)S(1)} %get-tuple-element.24), channel_id=1, source_target_pairs={{4,64},{68,0},{8,12},{72,76},{5,65},{69,1},{9,13},{73,77},{6,66},{... | collective-permute-start | bytes 589832 | tf_op jit(solution)/shard_map/ppermute | solution.py:292
  44.7 3.7 %collective-permute-start.4 = (bf16[112,768]{1,0:T(8,128)(2,1)S(1)}, bf16[112,768]{1,0:T(8,128)(2,1)S(1)}, u32[]{:S(2)}, u32[]{:S(2)}) collective-permute-start(bf16[112,768]{1,0:T(8,128)(2,1)S(1)} %slice.4), channel_id=1, source_target_pairs={{4,0},{68,64},{8,76},{72,12},{5,1},{69,65},{9,77},{73,13},{6,2},{7... | collective-permute-start | bytes 516104 | tf_op jit(solution)/shard_map/ppermute | solution.py:292
  51.8 87.4 %all-to-all-start = ((bf16[8,64,2560]{2,1,0:T(8,128)(2,1)}), bf16[8,64,2560]{2,1,0:T(8,128)(2,1)}, u32[]{:S(2)}, u32[]{:S(2)}) async-start(bf16[8,64,2560]{2,1,0:T(8,128)(2,1)} %get-tuple-element.26), calls=%async_computation | async-start | bytes 5242880 | tf_op jit(solution)/shard_map/all_to_all | solution.py:322
  58.5 13.2 %collective-permute-start.13 = (bf16[240,768]{1,0:T(8,128)(2,1)S(1)}, bf16[240,768]{1,0:T(8,128)(2,1)S(1)}, u32[]{:S(2)}, u32[]{:S(2)}) collective-permute-start(bf16[240,768]{1,0:T(8,128)(2,1)S(1)} %shard_map.91.refs_0_), channel_id=1, source_target_pairs={{0,16},{8,136},{16,0},{24,152},{32,48},{40,168},{48,32},{56,184},{... | collective-permute-start | bytes 1105928 | tf_op jit(solution)/shard_map/ppermute | solution.py:240
  61.9 77.3 %copy-start = (bf16[480,768]{1,0:T(8,128)(2,1)}, bf16[480,768]{1,0:T(8,128)(2,1)S(1)}, u32[]{:S(2)}) copy-start(bf16[480,768]{1,0:T(8,128)(2,1)S(1)} %shard_map.90.refs_0_) | copy-start | bytes 2211844
  61.9 17.5 %collective-permute-start.9 = (bf16[480,768]{1,0:T(8,128)(2,1)S(1)}, bf16[480,768]{1,0:T(8,128)(2,1)S(1)}, u32[]{:S(2)}, u32[]{:S(2)}) collective-permute-start(bf16[480,768]{1,0:T(8,128)(2,1)S(1)} %shard_map.90.refs_0_), channel_id=1, source_target_pairs={{0,384},{8,56},{16,400},{24,8},{32,416},{40,24},{48,432},{56,40},{... | collective-permute-start | bytes 2211848 | tf_op jit(solution)/shard_map/ppermute | solution.py:231
  66.0 18.9 %collective-permute-start.7 = (bf16[480,768]{1,0:T(8,128)(2,1)S(1)}, bf16[480,768]{1,0:T(8,128)(2,1)S(1)}, u32[]{:S(2)}, u32[]{:S(2)}) collective-permute-start(bf16[480,768]{1,0:T(8,128)(2,1)S(1)} %shard_map.90.refs_0_), channel_id=1, source_target_pairs={{0,128},{8,24},{16,144},{24,40},{32,160},{40,56},{48,176},{56,8},{... | collective-permute-start | bytes 2211848 | tf_op jit(solution)/shard_map/ppermute | solution.py:231
  68.0 21.7 %collective-permute-start.6 = (bf16[480,768]{1,0:T(8,128)(2,1)S(1)}, bf16[480,768]{1,0:T(8,128)(2,1)}, u32[]{:S(2)}, u32[]{:S(2)}) collective-permute-start(bf16[480,768]{1,0:T(8,128)(2,1)S(1)} %shard_map.90.refs_0_), channel_id=1, source_target_pairs={{0,48},{8,392},{16,32},{24,408},{32,16},{40,424},{48,0},{56,440},{... | collective-permute-start | bytes 2211848 | tf_op jit(solution)/shard_map/ppermute | solution.py:240
  72.1 67.1 %copy-start.1 = (bf16[480,768]{1,0:T(8,128)(2,1)}, bf16[480,768]{1,0:T(8,128)(2,1)S(1)}, u32[]{:S(2)}) copy-start(bf16[480,768]{1,0:T(8,128)(2,1)S(1)} %shard_map.92.refs_8_) | copy-start | bytes 2211844
  72.1 33.4 %collective-permute-start.14 = (bf16[480,768]{1,0:T(8,128)(2,1)S(1)}, bf16[480,768]{1,0:T(8,128)(2,1)}, u32[]{:S(2)}, u32[]{:S(2)}) collective-permute-start(bf16[480,768]{1,0:T(8,128)(2,1)S(1)} %shard_map.92.refs_8_), channel_id=1, source_target_pairs={{0,48},{8,392},{16,32},{24,408},{32,16},{40,424},{48,0},{56,440},{... | collective-permute-start | bytes 2211848 | tf_op jit(solution)/shard_map/ppermute | solution.py:240
  74.8 34.5 %collective-permute-start.17 = (bf16[480,768]{1,0:T(8,128)(2,1)S(1)}, bf16[480,768]{1,0:T(8,128)(2,1)S(1)}, u32[]{:S(2)}, u32[]{:S(2)}) collective-permute-start(bf16[480,768]{1,0:T(8,128)(2,1)S(1)} %shard_map.92.refs_8_), channel_id=1, source_target_pairs={{0,384},{8,56},{16,400},{24,8},{32,416},{40,24},{48,432},{56,40},{... | collective-permute-start | bytes 2211848 | tf_op jit(solution)/shard_map/ppermute | solution.py:231
  79.4 31.9 %collective-permute-start.15 = (bf16[480,768]{1,0:T(8,128)(2,1)S(1)}, bf16[480,768]{1,0:T(8,128)(2,1)}, u32[]{:S(2)}, u32[]{:S(2)}) collective-permute-start(bf16[480,768]{1,0:T(8,128)(2,1)S(1)} %shard_map.92.refs_8_), channel_id=1, source_target_pairs={{0,128},{8,24},{16,144},{24,40},{32,160},{40,56},{48,176},{56,8},{... | collective-permute-start | bytes 2211848 | tf_op jit(solution)/shard_map/ppermute | solution.py:231
  84.9 28.3 %collective-permute-start.11 = (bf16[480,768]{1,0:T(8,128)(2,1)S(1)}, bf16[480,768]{1,0:T(8,128)(2,1)S(1)}, u32[]{:S(2)}, u32[]{:S(2)}) collective-permute-start(bf16[480,768]{1,0:T(8,128)(2,1)S(1)} %collective-permute-done.7.refs_2_), channel_id=1, source_target_pairs={{0,128},{8,24},{16,144},{24,40},{32,160},{40,56},{48,176},{56,8},{... | collective-permute-start | bytes 2211848 | tf_op jit(solution)/shard_map/ppermute | solution.py:231
  89.7 26.5 %collective-permute-start.10 = (bf16[480,768]{1,0:T(8,128)(2,1)}, bf16[480,768]{1,0:T(8,128)(2,1)}, u32[]{:S(2)}, u32[]{:S(2)}) collective-permute-start(bf16[480,768]{1,0:T(8,128)(2,1)} %collective-permute-done.6.refs_1_), channel_id=1, source_target_pairs={{0,384},{8,56},{16,400},{24,8},{32,416},{40,24},{48,432},{56,40},{... | collective-permute-start | bytes 2211848 | tf_op jit(solution)/shard_map/ppermute | solution.py:231
  105.5 14.3 %collective-permute-start.18 = (bf16[480,768]{1,0:T(8,128)(2,1)}, bf16[480,768]{1,0:T(8,128)(2,1)}, u32[]{:S(2)}, u32[]{:S(2)}) collective-permute-start(bf16[480,768]{1,0:T(8,128)(2,1)} %collective-permute-done.14.refs_9_), channel_id=1, source_target_pairs={{0,384},{8,56},{16,400},{24,8},{32,416},{40,24},{48,432},{56,40},{... | collective-permute-start | bytes 2211848 | tf_op jit(solution)/shard_map/ppermute | solution.py:231
  109.4 14.7 %collective-permute-start.8 = (bf16[480,768]{1,0:T(8,128)(2,1)}, bf16[480,768]{1,0:T(8,128)(2,1)}, u32[]{:S(2)}, u32[]{:S(2)}) collective-permute-start(bf16[480,768]{1,0:T(8,128)(2,1)} %collective-permute-done.6.refs_1_), channel_id=1, source_target_pairs={{0,128},{8,24},{16,144},{24,40},{32,160},{40,56},{48,176},{56,8},{... | collective-permute-start | bytes 2211848 | tf_op jit(solution)/shard_map/ppermute | solution.py:231
  111.3 27.9 %collective-permute-start.16 = (bf16[480,768]{1,0:T(8,128)(2,1)}, bf16[480,768]{1,0:T(8,128)(2,1)}, u32[]{:S(2)}, u32[]{:S(2)}) collective-permute-start(bf16[480,768]{1,0:T(8,128)(2,1)} %collective-permute-done.14.refs_9_), channel_id=1, source_target_pairs={{0,128},{8,24},{16,144},{24,40},{32,160},{40,56},{48,176},{56,8},{... | collective-permute-start | bytes 2211848 | tf_op jit(solution)/shard_map/ppermute | solution.py:231
  113.3 25.9 %collective-permute-start.19 = (bf16[480,768]{1,0:T(8,128)(2,1)}, bf16[480,768]{1,0:T(8,128)(2,1)}, u32[]{:S(2)}, u32[]{:S(2)}) collective-permute-start(bf16[480,768]{1,0:T(8,128)(2,1)} %collective-permute-done.15.refs_10_), channel_id=1, source_target_pairs={{0,128},{8,24},{16,144},{24,40},{32,160},{40,56},{48,176},{56,8},{... | collective-permute-start | bytes 2211848 | tf_op jit(solution)/shard_map/ppermute | solution.py:231
  116.2 23.0 %collective-permute-start.12 = (bf16[480,768]{1,0:T(8,128)(2,1)}, bf16[480,768]{1,0:T(8,128)(2,1)}, u32[]{:S(2)}, u32[]{:S(2)}) collective-permute-start(bf16[480,768]{1,0:T(8,128)(2,1)} %collective-permute-done.10.refs_5_), channel_id=1, source_target_pairs={{0,384},{8,56},{16,400},{24,8},{32,416},{40,24},{48,432},{56,40},{... | collective-permute-start | bytes 2211848 | tf_op jit(solution)/shard_map/ppermute | solution.py:231
  119.8 19.4 %collective-permute-start.20 = (bf16[480,768]{1,0:T(8,128)(2,1)}, bf16[480,768]{1,0:T(8,128)(2,1)}, u32[]{:S(2)}, u32[]{:S(2)}) collective-permute-start(bf16[480,768]{1,0:T(8,128)(2,1)} %collective-permute-done.18.refs_13_), channel_id=1, source_target_pairs={{0,384},{8,56},{16,400},{24,8},{32,416},{40,24},{48,432},{56,40},{... | collective-permute-start | bytes 2211848 | tf_op jit(solution)/shard_map/ppermute | solution.py:231
  124.0 63.0 %copy-start.7 = (s32[5]{0:T(128)S(1)}, s32[5]{0:T(128)}, u32[]{:S(2)}) copy-start(s32[5]{0:T(128)} %stack.23.where_ref) | copy-start | bytes 64
  151.1 16.2 %collective-permute-start.21 = (bf16[32,2688]{1,0:T(8,128)(2,1)}, bf16[32,2688]{1,0:T(8,128)(2,1)S(1)}, u32[]{:S(2)}, u32[]{:S(2)}) collective-permute-start(bf16[32,2688]{1,0:T(8,128)(2,1)} %get-tuple-element.29), channel_id=1, source_target_pairs={{0,1},{1,0},{2,3},{3,2},{8,9},{9,8},{10,11},{11,10},{4,5},{5,4},{6... | collective-permute-start | bytes 516104 | tf_op jit(solution)/shard_map/ppermute | solution.py:346
  154.7 17.8 %collective-permute-start.22 = (bf16[32,2688]{1,0:T(8,128)(2,1)}, bf16[32,2688]{1,0:T(8,128)(2,1)S(1)}, u32[]{:S(2)}, u32[]{:S(2)}) collective-permute-start(bf16[32,2688]{1,0:T(8,128)(2,1)} %get-tuple-element.30), channel_id=1, source_target_pairs={{0,2},{1,3},{2,0},{3,1},{8,10},{9,11},{10,8},{11,9},{4,6},{5,7},{6... | collective-permute-start | bytes 516104 | tf_op jit(solution)/shard_map/ppermute | solution.py:346
  158.7 18.1 %collective-permute-start.23 = (bf16[32,2688]{1,0:T(8,128)(2,1)}, bf16[32,2688]{1,0:T(8,128)(2,1)S(1)}, u32[]{:S(2)}, u32[]{:S(2)}) collective-permute-start(bf16[32,2688]{1,0:T(8,128)(2,1)} %get-tuple-element.31), channel_id=1, source_target_pairs={{0,3},{1,2},{2,1},{3,0},{8,11},{9,10},{10,9},{11,8},{4,7},{5,6},{6... | collective-permute-start | bytes 516104 | tf_op jit(solution)/shard_map/ppermute | solution.py:346
  160.6 16.2 %collective-permute-start.24 = (bf16[32,2688]{1,0:T(8,128)(2,1)}, bf16[32,2688]{1,0:T(8,128)(2,1)S(1)}, u32[]{:S(2)}, u32[]{:S(2)}) collective-permute-start(bf16[32,2688]{1,0:T(8,128)(2,1)} %get-tuple-element.32), channel_id=1, source_target_pairs={{0,8},{1,9},{2,10},{3,11},{8,0},{9,1},{10,2},{11,3},{4,12},{5,13},... | collective-permute-start | bytes 516104 | tf_op jit(solution)/shard_map/ppermute | solution.py:346
  165.0 11.9 %collective-permute-start.25 = (bf16[32,2688]{1,0:T(8,128)(2,1)}, bf16[32,2688]{1,0:T(8,128)(2,1)S(1)}, u32[]{:S(2)}, u32[]{:S(2)}) collective-permute-start(bf16[32,2688]{1,0:T(8,128)(2,1)} %get-tuple-element.33), channel_id=1, source_target_pairs={{0,9},{1,8},{2,11},{3,10},{8,1},{9,0},{10,3},{11,2},{4,13},{5,12},... | collective-permute-start | bytes 516104 | tf_op jit(solution)/shard_map/ppermute | solution.py:346
  167.3 19.7 %collective-permute-start.26 = (bf16[32,2688]{1,0:T(8,128)(2,1)}, bf16[32,2688]{1,0:T(8,128)(2,1)S(1)}, u32[]{:S(2)}, u32[]{:S(2)}) collective-permute-start(bf16[32,2688]{1,0:T(8,128)(2,1)} %get-tuple-element.34), channel_id=1, source_target_pairs={{0,10},{1,11},{2,8},{3,9},{8,2},{9,3},{10,0},{11,1},{4,14},{5,15},... | collective-permute-start | bytes 516104 | tf_op jit(solution)/shard_map/ppermute | solution.py:346
  172.6 14.4 %collective-permute-start.27 = (bf16[32,2688]{1,0:T(8,128)(2,1)}, bf16[32,2688]{1,0:T(8,128)(2,1)S(1)}, u32[]{:S(2)}, u32[]{:S(2)}) collective-permute-start(bf16[32,2688]{1,0:T(8,128)(2,1)} %get-tuple-element.35), channel_id=1, source_target_pairs={{0,11},{1,10},{2,9},{3,8},{8,3},{9,2},{10,1},{11,0},{4,15},{5,14},... | collective-permute-start | bytes 516104 | tf_op jit(solution)/shard_map/ppermute | solution.py:346
  (9 other events, 311.7 us)

commit v11 on v8

--- a/solution.py
+++ b/solution.py
@@ -287,11 +287,6 @@
 
     source = ic == zq
     low, high = zmove(pair, True, 1), zmove(pair, True, -1)
-    first, top = small(near_kernel, source, (pair, low), (240, SPLIT))
-    far0, far1 = zmove(top, False, 1), zmove(high[SPLIT:], False, -1)
-    (second,) = small(far_kernel, source, (far0, far1, high), (240,))
-    first_half = jnp.where(source, zh, jnp.where((ring == 1) | (ring == 2), 0, 1))
-
     step = 512
     columns = pl.BlockSpec((256, step), lambda i: (0, i))
     payload, sel = pl.pallas_call(
@@ -310,6 +305,12 @@
         cost_estimate=cost(2 * 256 * 512 * width, 8 * 256 * width),
     )(routes.T, tokens_in, cotangent)
 
+    low, payload = lax.optimization_barrier((low, payload))
+    first, top = small(near_kernel, source, (pair, low), (240, SPLIT))
+    far0, far1 = zmove(top, False, 1), zmove(high[SPLIT:], False, -1)
+    (second,) = small(far_kernel, source, (far0, far1, high), (240,))
+    first_half = jnp.where(source, zh, jnp.where((ring == 1) | (ring == 2), 0, 1))
+
     arrays, pieces, near = torus_gather(first, 0, 0)
     payload, *_ = lax.optimization_barrier((payload, far0, far1, *near[:2]))
     rows = lax.all_to_all(payload, ("c", "zr"), split_axis=0, concat_axis=0, tiled=True)

time: 186 us -> 189 us (1.016)
  waiting for transfers between devices: 49.3 us -> 53.6 us
  starting transfers between devices: 105 us -> 103 us
    ppermute x14, waiting for transfers between devices: 26.9 us -> 31 us  [shift(): return lax.ppermute(v, ('x', 'y', 'c'), pairs)]
    ppermute x14, starting transfers between devices: 45 us -> 42.1 us  [shift(): return lax.ppermute(v, ('x', 'y', 'c'), pairs)]
  transfers between devices with their start and end apart: 27 -> 27, of which waited for: 13 -> 14; matrix products, arithmetic and copies ran while one was open for 0% -> 0% of each run, Pallas kernels for 4% -> 4%
where the time goes in v11:
time: 189 us; the launch traced here: 186 us
  starting transfers between devices  103 us (54%)
  waiting for transfers between devices  53.6 us (28%)
  Pallas kernels  24.4 us (13%)
  local copies, waits for them, and re-layouts  3.63 us (2%)
    ppermute x14, starting transfers between devices, shift(): return lax.ppermute(v, ('x', 'y', 'c'), pairs)  42.1 us
    ppermute x14, waiting for transfers between devices, shift(): return lax.ppermute(v, ('x', 'y', 'c'), pairs)  31 us
    ppermute x7, starting transfers between devices, on_device(): home[r] = lax.ppermute(back[r], ('c', 'zr'), pairs)  26.1 us
    ppermute x4, starting transfers between devices, zmove(): return lax.ppermute(v, ('zh', 'c', 'zq'), pairs)  19.1 us
    ppermute x4, waiting for transfers between devices, zmove(): return lax.ppermute(v, ('zh', 'c', 'zq'), pairs)  11.9 us
    pallas_call x1, Pallas kernels, on_device(): pl.pallas_call(functools.partial(expert_kernel, pieces), out_shape=[jax.S...  11.7 us
    ppermute x7, waiting for transfers between devices, on_device(): home[r] = lax.ppermute(back[r], ('c', 'zr'), pairs)  9.53 us
    ppermute x1, starting transfers between devices, on_device(): other = lax.ppermute(shard, ('c', 'zq'), [(2, 0), (1, 3)])  8.78 us
  transfers between devices with their start and end apart: 27, of which 14 were waited for; matrix products, arithmetic and copies ran while one was open for 0% of the time, Pallas kernels for 4%

profile of v11, /device:TPU:1, one launch (start us, length us, event | category | flops | bytes accessed | tf_op | source)
XLA Modules:
  0.0 186.1 jit_solution(16580073163320628032)
XLA Ops:
  2.2 8.8 %collective-permute-start = (bf16[3,40,768]{2,1,0:T(8,128)(2,1)}, bf16[3,40,768]{2,1,0:T(8,128)(2,1)S(1)}, u32[]{:S(2)}, u32[]{:S(2)}) collective-permute-start(bf16[3,40,768]{2,1,0:T(8,128)(2,1)} %shard_map.87.shard_ref), channel_id=1, source_target_pairs={{8,0},{4,12},{9,1},{5,13},{10,2},{6,14},{11,3},{7,15},{24,16},{20,... | collective-permute-start | bytes 552968 | tf_op jit(solution)/shard_map/ppermute | solution.py:267
  15.8 5.6 %shard_map.86 = (bf16[8,64,2560]{2,1,0:T(8,128)(2,1)}, bf16[256,256]{1,0:T(8,128)(2,1)}) custom-call(s32[6,256]{1,0:T(8,128)} %bitcast.9, bf16[256,2560]{1,0:T(8,128)(2,1)} %tok_ref.1, bf16[256,2560]{1,0:T(8,128)(2,1)} %cot_ref.1), custom_call_target="tpu_custom_call" | custom-call | flops 671088640 | bytes 5242880 | tf_op jit(solution)/shard_map/pallas_call | solution.py:292
  21.4 5.9 %collective-permute-done.1.low = bf16[240,768]{1,0:T(8,128)(2,1)S(1)} collective-permute-done((bf16[240,768]{1,0:T(8,128)(2,1)S(1)}, bf16[240,768]{1,0:T(8,128)(2,1)S(1)}, u32[]{:S(2)}, u32[]{:S(2)}) %collective-permute-start.1) | collective-permute-done | bytes 368672 | tf_op jit(solution)/shard_map/ppermute | solution.py:286
  27.3 1.9 %collective-permute-start.6 = (bf16[240,768]{1,0:T(8,128)(2,1)S(1)}, bf16[240,768]{1,0:T(8,128)(2,1)S(1)}, u32[]{:S(2)}, u32[]{:S(2)}) collective-permute-start(bf16[240,768]{1,0:T(8,128)(2,1)S(1)} %get-tuple-element.29.refs_0_), channel_id=1, source_target_pairs={{0,48},{8,392},{16,0},{24,408},{32,16},{40,424},{48,32},{56,440},{... | collective-permute-start | bytes 1105928 | tf_op jit(solution)/shard_map/ppermute | solution.py:233
  29.2 3.4 %collective-permute-start.5 = (bf16[240,768]{1,0:T(8,128)(2,1)S(1)}, bf16[240,768]{1,0:T(8,128)(2,1)S(1)}, u32[]{:S(2)}, u32[]{:S(2)}) collective-permute-start(bf16[240,768]{1,0:T(8,128)(2,1)S(1)} %get-tuple-element.29.refs_0_), channel_id=1, source_target_pairs={{0,16},{8,136},{16,32},{24,152},{32,48},{40,168},{48,0},{56,184},{... | collective-permute-start | bytes 1105928 | tf_op jit(solution)/shard_map/ppermute | solution.py:233
  32.6 15.3 %collective-permute-start.2 = (bf16[128,768]{1,0:T(8,128)(2,1)S(1)}, bf16[128,768]{1,0:T(8,128)(2,1)S(1)}, u32[]{:S(2)}, u32[]{:S(2)}) collective-permute-start(bf16[128,768]{1,0:T(8,128)(2,1)S(1)} %get-tuple-element.28), channel_id=1, source_target_pairs={{4,64},{68,0},{8,12},{72,76},{5,65},{69,1},{9,13},{73,77},{6,66},{... | collective-permute-start | bytes 589832 | tf_op jit(solution)/shard_map/ppermute | solution.py:286
  49.2 4.4 %collective-permute-done.4.bottom = bf16[112,768]{1,0:T(8,128)(2,1)S(1)} collective-permute-done((bf16[112,768]{1,0:T(8,128)(2,1)S(1)}, bf16[112,768]{1,0:T(8,128)(2,1)S(1)}, u32[]{:S(2)}, u32[]{:S(2)}) %collective-permute-start.4) | collective-permute-done | bytes 172064 | tf_op jit(solution)/shard_map/ppermute | solution.py:286
  55.2 7.3 %all-to-all-start = ((bf16[8,64,2560]{2,1,0:T(8,128)(2,1)}), bf16[8,64,2560]{2,1,0:T(8,128)(2,1)}, u32[]{:S(2)}, u32[]{:S(2)}) async-start(bf16[8,64,2560]{2,1,0:T(8,128)(2,1)} %get-tuple-element.30), calls=%async_computation | async-start | bytes 5242880 | tf_op jit(solution)/shard_map/all_to_all | solution.py:316
  62.5 2.6 %collective-permute-start.12 = (bf16[240,768]{1,0:T(8,128)(2,1)S(1)}, bf16[240,768]{1,0:T(8,128)(2,1)S(1)}, u32[]{:S(2)}, u32[]{:S(2)}) collective-permute-start(bf16[240,768]{1,0:T(8,128)(2,1)S(1)} %shard_map.92.refs_0_), channel_id=1, source_target_pairs={{0,16},{8,136},{16,32},{24,152},{32,48},{40,168},{48,0},{56,184},{... | collective-permute-start | bytes 1105928 | tf_op jit(solution)/shard_map/ppermute | solution.py:233
  65.1 3.1 %collective-permute-start.7 = (bf16[240,768]{1,0:T(8,128)(2,1)S(1)}, bf16[240,768]{1,0:T(8,128)(2,1)S(1)}, u32[]{:S(2)}, u32[]{:S(2)}) collective-permute-start(bf16[240,768]{1,0:T(8,128)(2,1)S(1)} %collective-permute-done.5.refs_1_), channel_id=1, source_target_pairs={{0,16},{8,136},{16,32},{24,152},{32,48},{40,168},{48,0},{56,184},{... | collective-permute-start | bytes 1105928 | tf_op jit(solution)/shard_map/ppermute | solution.py:233
  68.2 3.4 %collective-permute-start.13 = (bf16[240,768]{1,0:T(8,128)(2,1)S(1)}, bf16[240,768]{1,0:T(8,128)(2,1)S(1)}, u32[]{:S(2)}, u32[]{:S(2)}) collective-permute-start(bf16[240,768]{1,0:T(8,128)(2,1)S(1)} %shard_map.92.refs_0_), channel_id=1, source_target_pairs={{0,48},{8,392},{16,0},{24,408},{32,16},{40,424},{48,32},{56,440},{... | collective-permute-start | bytes 1105928 | tf_op jit(solution)/shard_map/ppermute | solution.py:233
  74.2 2.0 %collective-permute-done.7.refs_3_ = bf16[240,768]{1,0:T(8,128)(2,1)S(1)} collective-permute-done((bf16[240,768]{1,0:T(8,128)(2,1)S(1)}, bf16[240,768]{1,0:T(8,128)(2,1)S(1)}, u32[]{:S(2)}, u32[]{:S(2)}) %collective-permute-start.7) | collective-permute-done | bytes 368672 | tf_op jit(solution)/shard_map/ppermute | solution.py:233
  76.9 4.4 %collective-permute-start.9 = (bf16[960,768]{1,0:T(8,128)(2,1)S(1)}, bf16[960,768]{1,0:T(8,128)(2,1)S(1)}, u32[]{:S(2)}, u32[]{:S(2)}) collective-permute-start(bf16[960,768]{1,0:T(8,128)(2,1)S(1)} %shard_map.90.refs_0_), channel_id=1, source_target_pairs={{0,384},{8,56},{16,400},{24,8},{32,416},{40,24},{48,432},{56,40},{... | collective-permute-start | bytes 4423688 | tf_op jit(solution)/shard_map/ppermute | solution.py:233
  81.3 1.9 %collective-permute-start.8 = (bf16[960,768]{1,0:T(8,128)(2,1)S(1)}, bf16[960,768]{1,0:T(8,128)(2,1)S(1)}, u32[]{:S(2)}, u32[]{:S(2)}) collective-permute-start(bf16[960,768]{1,0:T(8,128)(2,1)S(1)} %shard_map.90.refs_0_), channel_id=1, source_target_pairs={{0,128},{8,24},{16,144},{24,40},{32,160},{40,56},{48,176},{56,8},{... | collective-permute-start | bytes 4423688 | tf_op jit(solution)/shard_map/ppermute | solution.py:233
  83.9 4.6 %collective-permute-start.16 = (bf16[960,768]{1,0:T(8,128)(2,1)S(1)}, bf16[960,768]{1,0:T(8,128)(2,1)S(1)}, u32[]{:S(2)}, u32[]{:S(2)}) collective-permute-start(bf16[960,768]{1,0:T(8,128)(2,1)S(1)} %shard_map.93.refs_5_), channel_id=1, source_target_pairs={{0,384},{8,56},{16,400},{24,8},{32,416},{40,24},{48,432},{56,40},{... | collective-permute-start | bytes 4423688 | tf_op jit(solution)/shard_map/ppermute | solution.py:233
  88.5 1.9 %collective-permute-start.15 = (bf16[960,768]{1,0:T(8,128)(2,1)S(1)}, bf16[960,768]{1,0:T(8,128)(2,1)S(1)}, u32[]{:S(2)}, u32[]{:S(2)}) collective-permute-start(bf16[960,768]{1,0:T(8,128)(2,1)S(1)} %shard_map.93.refs_5_), channel_id=1, source_target_pairs={{0,128},{8,24},{16,144},{24,40},{32,160},{40,56},{48,176},{56,8},{... | collective-permute-start | bytes 4423688 | tf_op jit(solution)/shard_map/ppermute | solution.py:233
  90.4 7.2 %collective-permute-done.9.refs_1_.refs_2_ = bf16[960,768]{1,0:T(8,128)(2,1)S(1)} collective-permute-done((bf16[960,768]{1,0:T(8,128)(2,1)S(1)}, bf16[960,768]{1,0:T(8,128)(2,1)S(1)}, u32[]{:S(2)}, u32[]{:S(2)}) %collective-permute-start.9) | collective-permute-done | bytes 1474592 | tf_op jit(solution)/shard_map/ppermute | solution.py:233
  97.6 5.4 %collective-permute-done.8.refs_0_.refs_1_ = bf16[960,768]{1,0:T(8,128)(2,1)S(1)} collective-permute-done((bf16[960,768]{1,0:T(8,128)(2,1)S(1)}, bf16[960,768]{1,0:T(8,128)(2,1)S(1)}, u32[]{:S(2)}, u32[]{:S(2)}) %collective-permute-start.8) | collective-permute-done | bytes 1474592 | tf_op jit(solution)/shard_map/ppermute | solution.py:233
  106.2 4.6 %collective-permute-start.11 = (bf16[480,768]{1,0:T(8,128)(2,1)S(1)}, bf16[480,768]{1,0:T(8,128)(2,1)}, u32[]{:S(2)}, u32[]{:S(2)}) collective-permute-start(bf16[480,768]{1,0:T(8,128)(2,1)S(1)} %get-tuple-element.32), channel_id=1, source_target_pairs={{0,384},{8,56},{16,400},{24,8},{32,416},{40,24},{48,432},{56,40},{... | collective-permute-start | bytes 2211848 | tf_op jit(solution)/shard_map/ppermute | solution.py:233
  110.7 2.7 %collective-permute-done.16.refs_1_.refs_7_ = bf16[960,768]{1,0:T(8,128)(2,1)S(1)} collective-permute-done((bf16[960,768]{1,0:T(8,128)(2,1)S(1)}, bf16[960,768]{1,0:T(8,128)(2,1)S(1)}, u32[]{:S(2)}, u32[]{:S(2)}) %collective-permute-start.16) | collective-permute-done | bytes 1474592 | tf_op jit(solution)/shard_map/ppermute | solution.py:233
  113.4 5.3 %collective-permute-done.15.refs_0_.refs_6_ = bf16[960,768]{1,0:T(8,128)(2,1)S(1)} collective-permute-done((bf16[960,768]{1,0:T(8,128)(2,1)S(1)}, bf16[960,768]{1,0:T(8,128)(2,1)S(1)}, u32[]{:S(2)}, u32[]{:S(2)}) %collective-permute-start.15) | collective-permute-done | bytes 1474592 | tf_op jit(solution)/shard_map/ppermute | solution.py:233
  121.8 4.6 %collective-permute-start.18 = (bf16[480,768]{1,0:T(8,128)(2,1)S(1)}, bf16[480,768]{1,0:T(8,128)(2,1)}, u32[]{:S(2)}, u32[]{:S(2)}) collective-permute-start(bf16[480,768]{1,0:T(8,128)(2,1)S(1)} %get-tuple-element.35), channel_id=1, source_target_pairs={{0,384},{8,56},{16,400},{24,8},{32,416},{40,24},{48,432},{56,40},{... | collective-permute-start | bytes 2211848 | tf_op jit(solution)/shard_map/ppermute | solution.py:233
  127.1 7.5 %collective-permute-done.17.refs_8_ = bf16[480,768]{1,0:T(8,128)(2,1)} collective-permute-done((bf16[480,768]{1,0:T(8,128)(2,1)S(1)}, bf16[480,768]{1,0:T(8,128)(2,1)}, u32[]{:S(2)}, u32[]{:S(2)}) %collective-permute-start.17) | collective-permute-done | bytes 737312 | tf_op jit(solution)/shard_map/ppermute | solution.py:233
  134.8 11.7 %shard_map.95 = (bf16[32,2688]{1,0:T(8,128)(2,1)}, bf16[32,2688]{1,0:T(8,128)(2,1)}, bf16[32,2688]{1,0:T(8,128)(2,1)}, bf16[32,2688]{1,0:T(8,128)(2,1)}, bf16[32...) custom-call(s32[5]{0:T(128)} %stack.23.where_ref, ...), custom_call_target="tpu_custom_call" | custom-call | flops 5033164800 | bytes 11796480 | tf_op jit(solution)/shard_map/pallas_call | solution.py:322
  146.5 3.3 %collective-permute-start.19 = (bf16[32,2688]{1,0:T(8,128)(2,1)}, bf16[32,2688]{1,0:T(8,128)(2,1)S(1)}, u32[]{:S(2)}, u32[]{:S(2)}) collective-permute-start(bf16[32,2688]{1,0:T(8,128)(2,1)} %get-tuple-element.37), channel_id=1, source_target_pairs={{0,1},{1,0},{2,3},{3,2},{8,9},{9,8},{10,11},{11,10},{4,5},{5,4},{6... | collective-permute-start | bytes 516104 | tf_op jit(solution)/shard_map/ppermute | solution.py:340
  149.8 4.1 %collective-permute-start.20 = (bf16[32,2688]{1,0:T(8,128)(2,1)}, bf16[32,2688]{1,0:T(8,128)(2,1)S(1)}, u32[]{:S(2)}, u32[]{:S(2)}) collective-permute-start(bf16[32,2688]{1,0:T(8,128)(2,1)} %get-tuple-element.38), channel_id=1, source_target_pairs={{0,2},{1,3},{2,0},{3,1},{8,10},{9,11},{10,8},{11,9},{4,6},{5,7},{6... | collective-permute-start | bytes 516104 | tf_op jit(solution)/shard_map/ppermute | solution.py:340
  155.9 6.0 %collective-permute-start.22 = (bf16[32,2688]{1,0:T(8,128)(2,1)}, bf16[32,2688]{1,0:T(8,128)(2,1)S(1)}, u32[]{:S(2)}, u32[]{:S(2)}) collective-permute-start(bf16[32,2688]{1,0:T(8,128)(2,1)} %get-tuple-element.40), channel_id=1, source_target_pairs={{0,8},{1,9},{2,10},{3,11},{8,0},{9,1},{10,2},{11,3},{4,12},{5,13},... | collective-permute-start | bytes 516104 | tf_op jit(solution)/shard_map/ppermute | solution.py:340
  161.9 2.6 %collective-permute-start.23 = (bf16[32,2688]{1,0:T(8,128)(2,1)}, bf16[32,2688]{1,0:T(8,128)(2,1)S(1)}, u32[]{:S(2)}, u32[]{:S(2)}) collective-permute-start(bf16[32,2688]{1,0:T(8,128)(2,1)} %get-tuple-element.41), channel_id=1, source_target_pairs={{0,9},{1,8},{2,11},{3,10},{8,1},{9,0},{10,3},{11,2},{4,13},{5,12},... | collective-permute-start | bytes 516104 | tf_op jit(solution)/shard_map/ppermute | solution.py:340
  164.5 5.3 %collective-permute-start.24 = (bf16[32,2688]{1,0:T(8,128)(2,1)}, bf16[32,2688]{1,0:T(8,128)(2,1)S(1)}, u32[]{:S(2)}, u32[]{:S(2)}) collective-permute-start(bf16[32,2688]{1,0:T(8,128)(2,1)} %get-tuple-element.42), channel_id=1, source_target_pairs={{0,10},{1,11},{2,8},{3,9},{8,2},{9,3},{10,0},{11,1},{4,14},{5,15},... | collective-permute-start | bytes 516104 | tf_op jit(solution)/shard_map/ppermute | solution.py:340
  169.8 2.9 %collective-permute-start.25 = (bf16[32,2688]{1,0:T(8,128)(2,1)}, bf16[32,2688]{1,0:T(8,128)(2,1)S(1)}, u32[]{:S(2)}, u32[]{:S(2)}) collective-permute-start(bf16[32,2688]{1,0:T(8,128)(2,1)} %get-tuple-element.43), channel_id=1, source_target_pairs={{0,11},{1,10},{2,9},{3,8},{8,3},{9,2},{10,1},{11,0},{4,15},{5,14},... | collective-permute-start | bytes 516104 | tf_op jit(solution)/shard_map/ppermute | solution.py:340
  173.2 9.1 %collective-permute-done.24.refs_6_ = bf16[32,2688]{1,0:T(8,128)(2,1)S(1)} collective-permute-done((bf16[32,2688]{1,0:T(8,128)(2,1)}, bf16[32,2688]{1,0:T(8,128)(2,1)S(1)}, u32[]{:S(2)}, u32[]{:S(2)}) %collective-permute-start.24) | collective-permute-done | bytes 172064 | tf_op jit(solution)/shard_map/ppermute | solution.py:340
  183.3 2.9 %shard_map.96 = (bf16[256,2560]{1,0:T(8,128)(2,1)}, bf16[6,256]{1,0:T(8,128)(2,1)}) custom-call(s32[5]{0:T(128)S(1)} %copy-done.11, s32[6,256]{1,0:T(8,128)S(1)} %bitcast.10, bf16[6,256]{1,0:T(8,128)(2,1)S(1)} %bitcast.11, bf16[256,256]{1,0:T(8,128)(2,1)S(1)} %copy-done.8, bf16[32,2688]{1,0:T(8,128)(2,1)S(1)} %copy-done.7, ...), custom_call_target="tpu_custom_call" | custom-call | flops 335544320 | bytes 2621440 | tf_op jit(solution)/shard_map/pallas_call | solution.py:343
  (59 shorter events, 23.4 us)
Async XLA Ops:
  2.2 10.0 %collective-permute-start = (bf16[3,40,768]{2,1,0:T(8,128)(2,1)}, bf16[3,40,768]{2,1,0:T(8,128)(2,1)S(1)}, u32[]{:S(2)}, u32[]{:S(2)}) collective-permute-start(bf16[3,40,768]{2,1,0:T(8,128)(2,1)} %shard_map.87.shard_ref), channel_id=1, source_target_pairs={{8,0},{4,12},{9,1},{5,13},{10,2},{6,14},{11,3},{7,15},{24,16},{20,... | collective-permute-start | bytes 552968 | tf_op jit(solution)/shard_map/ppermute | solution.py:267
  13.2 14.1 %collective-permute-start.1 = (bf16[240,768]{1,0:T(8,128)(2,1)S(1)}, bf16[240,768]{1,0:T(8,128)(2,1)S(1)}, u32[]{:S(2)}, u32[]{:S(2)}) collective-permute-start(bf16[240,768]{1,0:T(8,128)(2,1)S(1)} %shard_map.88.mine), channel_id=1, source_target_pairs={{0,4},{64,68},{12,72},{76,8},{1,5},{65,69},{13,73},{77,9},{2,6},{6... | collective-permute-start | bytes 1105928 | tf_op jit(solution)/shard_map/ppermute | solution.py:286
  14.5 33.4 %collective-permute-start.3 = (bf16[240,768]{1,0:T(8,128)(2,1)S(1)}, bf16[240,768]{1,0:T(8,128)(2,1)S(1)}, u32[]{:S(2)}, u32[]{:S(2)}) collective-permute-start(bf16[240,768]{1,0:T(8,128)(2,1)S(1)} %shard_map.88.mine), channel_id=1, source_target_pairs={{0,68},{64,4},{12,8},{76,72},{1,69},{65,5},{13,9},{77,73},{2,70},{... | collective-permute-start | bytes 1105928 | tf_op jit(solution)/shard_map/ppermute | solution.py:286
  27.3 27.8 %collective-permute-start.6 = (bf16[240,768]{1,0:T(8,128)(2,1)S(1)}, bf16[240,768]{1,0:T(8,128)(2,1)S(1)}, u32[]{:S(2)}, u32[]{:S(2)}) collective-permute-start(bf16[240,768]{1,0:T(8,128)(2,1)S(1)} %get-tuple-element.29.refs_0_), channel_id=1, source_target_pairs={{0,48},{8,392},{16,0},{24,408},{32,16},{40,424},{48,32},{56,440},{... | collective-permute-start | bytes 1105928 | tf_op jit(solution)/shard_map/ppermute | solution.py:233
  29.2 25.9 %collective-permute-start.5 = (bf16[240,768]{1,0:T(8,128)(2,1)S(1)}, bf16[240,768]{1,0:T(8,128)(2,1)S(1)}, u32[]{:S(2)}, u32[]{:S(2)}) collective-permute-start(bf16[240,768]{1,0:T(8,128)(2,1)S(1)} %get-tuple-element.29.refs_0_), channel_id=1, source_target_pairs={{0,16},{8,136},{16,32},{24,152},{32,48},{40,168},{48,0},{56,184},{... | collective-permute-start | bytes 1105928 | tf_op jit(solution)/shard_map/ppermute | solution.py:233
  32.6 22.5 %collective-permute-start.2 = (bf16[128,768]{1,0:T(8,128)(2,1)S(1)}, bf16[128,768]{1,0:T(8,128)(2,1)S(1)}, u32[]{:S(2)}, u32[]{:S(2)}) collective-permute-start(bf16[128,768]{1,0:T(8,128)(2,1)S(1)} %get-tuple-element.28), channel_id=1, source_target_pairs={{4,64},{68,0},{8,12},{72,76},{5,65},{69,1},{9,13},{73,77},{6,66},{... | collective-permute-start | bytes 589832 | tf_op jit(solution)/shard_map/ppermute | solution.py:286
  47.9 5.7 %collective-permute-start.4 = (bf16[112,768]{1,0:T(8,128)(2,1)S(1)}, bf16[112,768]{1,0:T(8,128)(2,1)S(1)}, u32[]{:S(2)}, u32[]{:S(2)}) collective-permute-start(bf16[112,768]{1,0:T(8,128)(2,1)S(1)} %slice.4), channel_id=1, source_target_pairs={{4,0},{68,64},{8,76},{72,12},{5,1},{69,65},{9,77},{73,13},{6,2},{7... | collective-permute-start | bytes 516104 | tf_op jit(solution)/shard_map/ppermute | solution.py:286
  55.2 79.6 %all-to-all-start = ((bf16[8,64,2560]{2,1,0:T(8,128)(2,1)}), bf16[8,64,2560]{2,1,0:T(8,128)(2,1)}, u32[]{:S(2)}, u32[]{:S(2)}) async-start(bf16[8,64,2560]{2,1,0:T(8,128)(2,1)} %get-tuple-element.30), calls=%async_computation | async-start | bytes 5242880 | tf_op jit(solution)/shard_map/all_to_all | solution.py:316
  62.5 9.8 %collective-permute-start.12 = (bf16[240,768]{1,0:T(8,128)(2,1)S(1)}, bf16[240,768]{1,0:T(8,128)(2,1)S(1)}, u32[]{:S(2)}, u32[]{:S(2)}) collective-permute-start(bf16[240,768]{1,0:T(8,128)(2,1)S(1)} %shard_map.92.refs_0_), channel_id=1, source_target_pairs={{0,16},{8,136},{16,32},{24,152},{32,48},{40,168},{48,0},{56,184},{... | collective-permute-start | bytes 1105928 | tf_op jit(solution)/shard_map/ppermute | solution.py:233
  65.1 11.1 %collective-permute-start.7 = (bf16[240,768]{1,0:T(8,128)(2,1)S(1)}, bf16[240,768]{1,0:T(8,128)(2,1)S(1)}, u32[]{:S(2)}, u32[]{:S(2)}) collective-permute-start(bf16[240,768]{1,0:T(8,128)(2,1)S(1)} %collective-permute-done.5.refs_1_), channel_id=1, source_target_pairs={{0,16},{8,136},{16,32},{24,152},{32,48},{40,168},{48,0},{56,184},{... | collective-permute-start | bytes 1105928 | tf_op jit(solution)/shard_map/ppermute | solution.py:233
  68.2 15.0 %collective-permute-start.13 = (bf16[240,768]{1,0:T(8,128)(2,1)S(1)}, bf16[240,768]{1,0:T(8,128)(2,1)S(1)}, u32[]{:S(2)}, u32[]{:S(2)}) collective-permute-start(bf16[240,768]{1,0:T(8,128)(2,1)S(1)} %shard_map.92.refs_0_), channel_id=1, source_target_pairs={{0,48},{8,392},{16,0},{24,408},{32,16},{40,424},{48,32},{56,440},{... | collective-permute-start | bytes 1105928 | tf_op jit(solution)/shard_map/ppermute | solution.py:233
  72.3 11.0 %collective-permute-start.14 = (bf16[240,768]{1,0:T(8,128)(2,1)S(1)}, bf16[240,768]{1,0:T(8,128)(2,1)S(1)}, u32[]{:S(2)}, u32[]{:S(2)}) collective-permute-start(bf16[240,768]{1,0:T(8,128)(2,1)S(1)} %collective-permute-done.12.refs_1_), channel_id=1, source_target_pairs={{0,16},{8,136},{16,32},{24,152},{32,48},{40,168},{48,0},{56,184},{... | collective-permute-start | bytes 1105928 | tf_op jit(solution)/shard_map/ppermute | solution.py:233
  76.9 20.7 %collective-permute-start.9 = (bf16[960,768]{1,0:T(8,128)(2,1)S(1)}, bf16[960,768]{1,0:T(8,128)(2,1)S(1)}, u32[]{:S(2)}, u32[]{:S(2)}) collective-permute-start(bf16[960,768]{1,0:T(8,128)(2,1)S(1)} %shard_map.90.refs_0_), channel_id=1, source_target_pairs={{0,384},{8,56},{16,400},{24,8},{32,416},{40,24},{48,432},{56,40},{... | collective-permute-start | bytes 4423688 | tf_op jit(solution)/shard_map/ppermute | solution.py:233
  81.3 21.7 %collective-permute-start.8 = (bf16[960,768]{1,0:T(8,128)(2,1)S(1)}, bf16[960,768]{1,0:T(8,128)(2,1)S(1)}, u32[]{:S(2)}, u32[]{:S(2)}) collective-permute-start(bf16[960,768]{1,0:T(8,128)(2,1)S(1)} %shard_map.90.refs_0_), channel_id=1, source_target_pairs={{0,128},{8,24},{16,144},{24,40},{32,160},{40,56},{48,176},{56,8},{... | collective-permute-start | bytes 4423688 | tf_op jit(solution)/shard_map/ppermute | solution.py:233
  83.9 20.3 %copy-start.3 = (bf16[960,768]{1,0:T(8,128)(2,1)}, bf16[960,768]{1,0:T(8,128)(2,1)S(1)}, u32[]{:S(2)}) copy-start(bf16[960,768]{1,0:T(8,128)(2,1)S(1)} %shard_map.93.refs_5_) | copy-start | bytes 4423684
  83.9 29.5 %collective-permute-start.16 = (bf16[960,768]{1,0:T(8,128)(2,1)S(1)}, bf16[960,768]{1,0:T(8,128)(2,1)S(1)}, u32[]{:S(2)}, u32[]{:S(2)}) collective-permute-start(bf16[960,768]{1,0:T(8,128)(2,1)S(1)} %shard_map.93.refs_5_), channel_id=1, source_target_pairs={{0,384},{8,56},{16,400},{24,8},{32,416},{40,24},{48,432},{56,40},{... | collective-permute-start | bytes 4423688 | tf_op jit(solution)/shard_map/ppermute | solution.py:233
  88.5 30.2 %collective-permute-start.15 = (bf16[960,768]{1,0:T(8,128)(2,1)S(1)}, bf16[960,768]{1,0:T(8,128)(2,1)S(1)}, u32[]{:S(2)}, u32[]{:S(2)}) collective-permute-start(bf16[960,768]{1,0:T(8,128)(2,1)S(1)} %shard_map.93.refs_5_), channel_id=1, source_target_pairs={{0,128},{8,24},{16,144},{24,40},{32,160},{40,56},{48,176},{56,8},{... | collective-permute-start | bytes 4423688 | tf_op jit(solution)/shard_map/ppermute | solution.py:233
  104.2 22.8 %collective-permute-start.10 = (bf16[480,768]{1,0:T(8,128)(2,1)S(1)}, bf16[480,768]{1,0:T(8,128)(2,1)}, u32[]{:S(2)}, u32[]{:S(2)}) collective-permute-start(bf16[480,768]{1,0:T(8,128)(2,1)S(1)} %get-tuple-element.31), channel_id=1, source_target_pairs={{0,128},{8,24},{16,144},{24,40},{32,160},{40,56},{48,176},{56,8},{... | collective-permute-start | bytes 2211848 | tf_op jit(solution)/shard_map/ppermute | solution.py:233
  106.2 20.9 %collective-permute-start.11 = (bf16[480,768]{1,0:T(8,128)(2,1)S(1)}, bf16[480,768]{1,0:T(8,128)(2,1)}, u32[]{:S(2)}, u32[]{:S(2)}) collective-permute-start(bf16[480,768]{1,0:T(8,128)(2,1)S(1)} %get-tuple-element.32), channel_id=1, source_target_pairs={{0,384},{8,56},{16,400},{24,8},{32,416},{40,24},{48,432},{56,40},{... | collective-permute-start | bytes 2211848 | tf_op jit(solution)/shard_map/ppermute | solution.py:233
  119.9 14.7 %collective-permute-start.17 = (bf16[480,768]{1,0:T(8,128)(2,1)S(1)}, bf16[480,768]{1,0:T(8,128)(2,1)}, u32[]{:S(2)}, u32[]{:S(2)}) collective-permute-start(bf16[480,768]{1,0:T(8,128)(2,1)S(1)} %get-tuple-element.34), channel_id=1, source_target_pairs={{0,128},{8,24},{16,144},{24,40},{32,160},{40,56},{48,176},{56,8},{... | collective-permute-start | bytes 2211848 | tf_op jit(solution)/shard_map/ppermute | solution.py:233
  121.8 13.0 %collective-permute-start.18 = (bf16[480,768]{1,0:T(8,128)(2,1)S(1)}, bf16[480,768]{1,0:T(8,128)(2,1)}, u32[]{:S(2)}, u32[]{:S(2)}) collective-permute-start(bf16[480,768]{1,0:T(8,128)(2,1)S(1)} %get-tuple-element.35), channel_id=1, source_target_pairs={{0,384},{8,56},{16,400},{24,8},{32,416},{40,24},{48,432},{56,40},{... | collective-permute-start | bytes 2211848 | tf_op jit(solution)/shard_map/ppermute | solution.py:233
  127.1 55.2 %copy-start.8 = (bf16[256,256]{1,0:T(8,128)(2,1)S(1)}, bf16[256,256]{1,0:T(8,128)(2,1)}, u32[]{:S(2)}) copy-start(bf16[256,256]{1,0:T(8,128)(2,1)} %get-tuple-element.24.sel_ref) | copy-start | bytes 393220
  127.1 55.2 %copy-start.9 = (s32[256,6]{0,1:T(8,128)S(1)}, s32[256,6]{0,1:T(8,128)}, u32[]{:S(2)}) copy-start(s32[256,6]{0,1:T(8,128)} %param.9) | copy-start | bytes 18436
  127.1 55.2 %copy-start.10 = (bf16[256,6]{0,1:T(8,128)(2,1)S(1)}, bf16[256,6]{0,1:T(8,128)(2,1)}, u32[]{:S(2)}) copy-start(bf16[256,6]{0,1:T(8,128)(2,1)} %param.10) | copy-start | bytes 9220
  127.1 55.3 %copy-start.11 = (s32[5]{0:T(128)S(1)}, s32[5]{0:T(128)}, u32[]{:S(2)}) copy-start(s32[5]{0:T(128)} %stack.23.where_ref) | copy-start | bytes 64
  146.5 18.0 %collective-permute-start.19 = (bf16[32,2688]{1,0:T(8,128)(2,1)}, bf16[32,2688]{1,0:T(8,128)(2,1)S(1)}, u32[]{:S(2)}, u32[]{:S(2)}) collective-permute-start(bf16[32,2688]{1,0:T(8,128)(2,1)} %get-tuple-element.37), channel_id=1, source_target_pairs={{0,1},{1,0},{2,3},{3,2},{8,9},{9,8},{10,11},{11,10},{4,5},{5,4},{6... | collective-permute-start | bytes 516104 | tf_op jit(solution)/shard_map/ppermute | solution.py:340
  149.8 20.0 %collective-permute-start.20 = (bf16[32,2688]{1,0:T(8,128)(2,1)}, bf16[32,2688]{1,0:T(8,128)(2,1)S(1)}, u32[]{:S(2)}, u32[]{:S(2)}) collective-permute-start(bf16[32,2688]{1,0:T(8,128)(2,1)} %get-tuple-element.38), channel_id=1, source_target_pairs={{0,2},{1,3},{2,0},{3,1},{8,10},{9,11},{10,8},{11,9},{4,6},{5,7},{6... | collective-permute-start | bytes 516104 | tf_op jit(solution)/shard_map/ppermute | solution.py:340
  153.9 18.8 %collective-permute-start.21 = (bf16[32,2688]{1,0:T(8,128)(2,1)}, bf16[32,2688]{1,0:T(8,128)(2,1)S(1)}, u32[]{:S(2)}, u32[]{:S(2)}) collective-permute-start(bf16[32,2688]{1,0:T(8,128)(2,1)} %get-tuple-element.39), channel_id=1, source_target_pairs={{0,3},{1,2},{2,1},{3,0},{8,11},{9,10},{10,9},{11,8},{4,7},{5,6},{6... | collective-permute-start | bytes 516104 | tf_op jit(solution)/shard_map/ppermute | solution.py:340
  155.9 16.9 %collective-permute-start.22 = (bf16[32,2688]{1,0:T(8,128)(2,1)}, bf16[32,2688]{1,0:T(8,128)(2,1)S(1)}, u32[]{:S(2)}, u32[]{:S(2)}) collective-permute-start(bf16[32,2688]{1,0:T(8,128)(2,1)} %get-tuple-element.40), channel_id=1, source_target_pairs={{0,8},{1,9},{2,10},{3,11},{8,0},{9,1},{10,2},{11,3},{4,12},{5,13},... | collective-permute-start | bytes 516104 | tf_op jit(solution)/shard_map/ppermute | solution.py:340
  161.9 11.3 %collective-permute-start.23 = (bf16[32,2688]{1,0:T(8,128)(2,1)}, bf16[32,2688]{1,0:T(8,128)(2,1)S(1)}, u32[]{:S(2)}, u32[]{:S(2)}) collective-permute-start(bf16[32,2688]{1,0:T(8,128)(2,1)} %get-tuple-element.41), channel_id=1, source_target_pairs={{0,9},{1,8},{2,11},{3,10},{8,1},{9,0},{10,3},{11,2},{4,13},{5,12},... | collective-permute-start | bytes 516104 | tf_op jit(solution)/shard_map/ppermute | solution.py:340
  164.5 17.8 %collective-permute-start.24 = (bf16[32,2688]{1,0:T(8,128)(2,1)}, bf16[32,2688]{1,0:T(8,128)(2,1)S(1)}, u32[]{:S(2)}, u32[]{:S(2)}) collective-permute-start(bf16[32,2688]{1,0:T(8,128)(2,1)} %get-tuple-element.42), channel_id=1, source_target_pairs={{0,10},{1,11},{2,8},{3,9},{8,2},{9,3},{10,0},{11,1},{4,14},{5,15},... | collective-permute-start | bytes 516104 | tf_op jit(solution)/shard_map/ppermute | solution.py:340
  169.8 12.5 %collective-permute-start.25 = (bf16[32,2688]{1,0:T(8,128)(2,1)}, bf16[32,2688]{1,0:T(8,128)(2,1)S(1)}, u32[]{:S(2)}, u32[]{:S(2)}) collective-permute-start(bf16[32,2688]{1,0:T(8,128)(2,1)} %get-tuple-element.43), channel_id=1, source_target_pairs={{0,11},{1,10},{2,9},{3,8},{8,3},{9,2},{10,1},{11,0},{4,15},{5,14},... | collective-permute-start | bytes 516104 | tf_op jit(solution)/shard_map/ppermute | solution.py:340
  (7 other events, 23.3 us)

commit v12 on v8

--- a/solution.py
+++ b/solution.py
@@ -43,6 +43,10 @@
         out_ref[:, first : first + 32, :] = rows.reshape(8, 32, step)
 
 
+def copy_kernel(in_ref, out_ref):
+    out_ref[...] = in_ref[...]
+
+
 def combine_kernel(where_ref, routes_ref, gates_ref, sel_ref, *refs):
     back_refs, (grad_ref, score_ref) = refs[:8], refs[8:]
     width = grad_ref.shape[1]
@@ -106,7 +110,7 @@
 def expert_kernel(pieces, where_ref, rows_ref, *refs):
     sources = refs[: pieces[-1][0] + 1]
     out_refs = refs[len(sources) : len(sources) + 8]
-    gate_w, up_w, down_w, tok_v, cot_v, result, grad_a, grad_b, pre_g, pre_u, pre_b, sems, out_sems = refs[
+    gate_w, up_w, down_w, tok_v, cot_v, result, grad_a, grad_b, pre_g, pre_u, pre_b, slope, sems, out_sems = refs[
         len(sources) + 8 :
     ]
     my_x, my_y, core, first_half, place = (where_ref[i] for i in range(5))
@@ -142,20 +146,27 @@
         copy.wait()
     tok = tok_v[...].reshape(256, width)
     pre_g[...] = jnp.dot(tok, gate_w[...], preferred_element_type=F32)
+    cstep = 256
+
+    @pl.loop(0, hidden_width // cstep)
+    def _(i):
+        cols = pl.ds(pl.multiple_of(i * cstep, cstep), cstep)
+        gate, back_hidden = pre_g[:, cols], pre_b[:, cols]
+        sig = jax.nn.sigmoid(gate)
+        act = gate * sig
+        grad_b[:, cols] = (back_hidden * act).astype(BF)
+        slope[:, cols] = sig * (1.0 + gate * (1.0 - sig))
+        pre_g[:, cols] = act
+
     for copy in up_copies:
         copy.wait()
     pre_u[...] = jnp.dot(tok, up_w[...], preferred_element_type=F32)
-
-    cstep = 256
 
     def middle(i, score):
         cols = pl.ds(pl.multiple_of(i * cstep, cstep), cstep)
-        gate, up, back_hidden = pre_g[:, cols], pre_u[:, cols], pre_b[:, cols]
-        sig = jax.nn.sigmoid(gate)
-        act = gate * sig
+        act, up, back_hidden = pre_g[:, cols], pre_u[:, cols], pre_b[:, cols]
         hidden = (act * up).astype(BF).astype(F32)
-        grad_a[:, cols] = (back_hidden * up * (sig * (1.0 + gate * (1.0 - sig)))).astype(BF)
-        grad_b[:, cols] = (back_hidden * act).astype(BF)
+        grad_a[:, cols] = (back_hidden * up * slope[:, cols]).astype(BF)
         return score + jnp.sum(hidden * back_hidden, axis=1, keepdims=True)
 
     score = lax.fori_loop(0, hidden_width // cstep, middle, jnp.zeros((256, 1), F32))
@@ -327,13 +338,22 @@
         + [pltpu.VMEM((8, 32, width), BF)] * 2
         + [pltpu.VMEM((8, 32, width + PAD), BF)]
         + [pltpu.VMEM((256, hidden_width), BF)] * 2
-        + [pltpu.VMEM((256, hidden_width), F32)] * 3
+        + [pltpu.VMEM((256, hidden_width), F32)] * 4
         + [pltpu.SemaphoreType.DMA((5,)), pltpu.SemaphoreType.DMA((2,))],
         compiler_params=params(56),
         cost_estimate=cost(10 * 256 * width * hidden_width, 6 * width * hidden_width),
     )(where, rows, *arrays)
 
-    home = {0: back[0]}
+    home = {
+        0: pl.pallas_call(
+            copy_kernel,
+            out_shape=jax.ShapeDtypeStruct((32, width + PAD), BF),
+            in_specs=[VM],
+            out_specs=VM,
+            compiler_params=params(4),
+            cost_estimate=cost(0, 4 * 32 * (width + PAD)),
+        )(back[0])
+    }
     for r in (4, 3, 7, 2, 6, 1, 5):
         pairs = [(d, (d // 4 ^ r // 4) * 4 + (d % 4 ^ r % 4)) for d in range(8)]
         home[r] = lax.ppermute(back[r], ("c", "zr"), pairs)

time: 186 us -> 185 us (level)
  transfers between devices with their start and end apart: 27 -> 27, of which waited for: 13 -> 12; matrix products, arithmetic and copies ran while one was open for 0% -> 0% of each run, Pallas kernels for 4% -> 4%
where the time goes in v12:
time: 185 us; the launch traced here: 183 us
  starting transfers between devices  105 us (57%)
  waiting for transfers between devices  48.4 us (26%)
  Pallas kernels  24.5 us (13%)
  local copies, waits for them, and re-layouts  3.59 us (2%)
    ppermute x14, starting transfers between devices, shift(): return lax.ppermute(v, ('x', 'y', 'c'), pairs)  45 us
    ppermute x14, waiting for transfers between devices, shift(): return lax.ppermute(v, ('x', 'y', 'c'), pairs)  26.9 us
    ppermute x7, starting transfers between devices, on_device(): home[r] = lax.ppermute(back[r], ('c', 'zr'), pairs)  26.3 us
    ppermute x4, starting transfers between devices, zmove(): return lax.ppermute(v, ('zh', 'c', 'zq'), pairs)  18.2 us
    ppermute x4, waiting for transfers between devices, zmove(): return lax.ppermute(v, ('zh', 'c', 'zq'), pairs)  11.8 us
    pallas_call x1, Pallas kernels, on_device(): pl.pallas_call(functools.partial(expert_kernel, pieces), out_shape=[jax.S...  11.8 us
    ppermute x1, starting transfers between devices, on_device(): other = lax.ppermute(shard, ('c', 'zq'), [(2, 0), (1, 3)])  8.78 us
    ppermute x7, waiting for transfers between devices, on_device(): home[r] = lax.ppermute(back[r], ('c', 'zr'), pairs)  8.41 us
  transfers between devices with their start and end apart: 27, of which 12 were waited for; matrix products, arithmetic and copies ran while one was open for 0% of the time, Pallas kernels for 4%

profile of v12, /device:TPU:1, one launch (start us, length us, event | category | flops | bytes accessed | tf_op | source)
XLA Modules:
  0.0 182.9 jit_solution(18130575167490263217)
XLA Ops:
  2.2 8.8 %collective-permute-start = (bf16[3,40,768]{2,1,0:T(8,128)(2,1)}, bf16[3,40,768]{2,1,0:T(8,128)(2,1)S(1)}, u32[]{:S(2)}, u32[]{:S(2)}) collective-permute-start(bf16[3,40,768]{2,1,0:T(8,128)(2,1)} %shard_map.87.shard_ref), channel_id=1, source_target_pairs={{8,0},{4,12},{9,1},{5,13},{10,2},{6,14},{11,3},{7,15},{24,16},{20,... | collective-permute-start | bytes 552968 | tf_op jit(solution)/shard_map/ppermute | solution.py:278
  15.8 11.5 %collective-permute-done.1.low = bf16[240,768]{1,0:T(8,128)(2,1)S(1)} collective-permute-done((bf16[240,768]{1,0:T(8,128)(2,1)S(1)}, bf16[240,768]{1,0:T(8,128)(2,1)S(1)}, u32[]{:S(2)}, u32[]{:S(2)}) %collective-permute-start.1) | collective-permute-done | bytes 368672 | tf_op jit(solution)/shard_map/ppermute | solution.py:297
  27.3 1.9 %collective-permute-start.5 = (bf16[240,768]{1,0:T(8,128)(2,1)S(1)}, bf16[240,768]{1,0:T(8,128)(2,1)S(1)}, u32[]{:S(2)}, u32[]{:S(2)}) collective-permute-start(bf16[240,768]{1,0:T(8,128)(2,1)S(1)} %get-tuple-element.25.refs_0_), channel_id=1, source_target_pairs={{0,16},{8,136},{16,32},{24,152},{32,48},{40,168},{48,0},{56,184},{... | collective-permute-start | bytes 1105928 | tf_op jit(solution)/shard_map/ppermute | solution.py:244
  29.2 4.6 %collective-permute-start.6 = (bf16[240,768]{1,0:T(8,128)(2,1)S(1)}, bf16[240,768]{1,0:T(8,128)(2,1)S(1)}, u32[]{:S(2)}, u32[]{:S(2)}) collective-permute-start(bf16[240,768]{1,0:T(8,128)(2,1)S(1)} %get-tuple-element.25.refs_0_), channel_id=1, source_target_pairs={{0,48},{8,392},{16,0},{24,408},{32,16},{40,424},{48,32},{56,440},{... | collective-permute-start | bytes 1105928 | tf_op jit(solution)/shard_map/ppermute | solution.py:244
  33.8 14.3 %collective-permute-start.2 = (bf16[128,768]{1,0:T(8,128)(2,1)S(1)}, bf16[128,768]{1,0:T(8,128)(2,1)S(1)}, u32[]{:S(2)}, u32[]{:S(2)}) collective-permute-start(bf16[128,768]{1,0:T(8,128)(2,1)S(1)} %get-tuple-element.24), channel_id=1, source_target_pairs={{4,64},{68,0},{8,12},{72,76},{5,65},{69,1},{9,13},{73,77},{6,66},{... | collective-permute-start | bytes 589832 | tf_op jit(solution)/shard_map/ppermute | solution.py:297
  49.5 5.6 %shard_map.86 = (bf16[8,64,2560]{2,1,0:T(8,128)(2,1)}, bf16[256,256]{1,0:T(8,128)(2,1)}) custom-call(s32[6,256]{1,0:T(8,128)} %bitcast.9, bf16[256,2560]{1,0:T(8,128)(2,1)} %tok_ref.1, bf16[256,2560]{1,0:T(8,128)(2,1)} %cot_ref.1), custom_call_target="tpu_custom_call" | custom-call | flops 671088640 | bytes 5242880 | tf_op jit(solution)/shard_map/pallas_call | solution.py:308
  55.4 7.1 %all-to-all-start = ((bf16[8,64,2560]{2,1,0:T(8,128)(2,1)}), bf16[8,64,2560]{2,1,0:T(8,128)(2,1)}, u32[]{:S(2)}, u32[]{:S(2)}) async-start(bf16[8,64,2560]{2,1,0:T(8,128)(2,1)} %get-tuple-element.26), calls=%async_computation | async-start | bytes 5242880 | tf_op jit(solution)/shard_map/all_to_all | solution.py:326
  62.5 2.6 %collective-permute-start.12 = (bf16[240,768]{1,0:T(8,128)(2,1)S(1)}, bf16[240,768]{1,0:T(8,128)(2,1)S(1)}, u32[]{:S(2)}, u32[]{:S(2)}) collective-permute-start(bf16[240,768]{1,0:T(8,128)(2,1)S(1)} %shard_map.92.refs_0_), channel_id=1, source_target_pairs={{0,16},{8,136},{16,32},{24,152},{32,48},{40,168},{48,0},{56,184},{... | collective-permute-start | bytes 1105928 | tf_op jit(solution)/shard_map/ppermute | solution.py:244
  65.1 3.1 %collective-permute-start.7 = (bf16[240,768]{1,0:T(8,128)(2,1)S(1)}, bf16[240,768]{1,0:T(8,128)(2,1)S(1)}, u32[]{:S(2)}, u32[]{:S(2)}) collective-permute-start(bf16[240,768]{1,0:T(8,128)(2,1)S(1)} %collective-permute-done.5.refs_1_), channel_id=1, source_target_pairs={{0,16},{8,136},{16,32},{24,152},{32,48},{40,168},{48,0},{56,184},{... | collective-permute-start | bytes 1105928 | tf_op jit(solution)/shard_map/ppermute | solution.py:244
  68.3 3.4 %collective-permute-start.13 = (bf16[240,768]{1,0:T(8,128)(2,1)S(1)}, bf16[240,768]{1,0:T(8,128)(2,1)S(1)}, u32[]{:S(2)}, u32[]{:S(2)}) collective-permute-start(bf16[240,768]{1,0:T(8,128)(2,1)S(1)} %shard_map.92.refs_0_), channel_id=1, source_target_pairs={{0,48},{8,392},{16,0},{24,408},{32,16},{40,424},{48,32},{56,440},{... | collective-permute-start | bytes 1105928 | tf_op jit(solution)/shard_map/ppermute | solution.py:244
  74.2 2.0 %collective-permute-done.7.refs_3_ = bf16[240,768]{1,0:T(8,128)(2,1)S(1)} collective-permute-done((bf16[240,768]{1,0:T(8,128)(2,1)S(1)}, bf16[240,768]{1,0:T(8,128)(2,1)S(1)}, u32[]{:S(2)}, u32[]{:S(2)}) %collective-permute-start.7) | collective-permute-done | bytes 368672 | tf_op jit(solution)/shard_map/ppermute | solution.py:244
  76.9 2.3 %collective-permute-start.8 = (bf16[960,768]{1,0:T(8,128)(2,1)S(1)}, bf16[960,768]{1,0:T(8,128)(2,1)S(1)}, u32[]{:S(2)}, u32[]{:S(2)}) collective-permute-start(bf16[960,768]{1,0:T(8,128)(2,1)S(1)} %shard_map.90.refs_0_), channel_id=1, source_target_pairs={{0,128},{8,24},{16,144},{24,40},{32,160},{40,56},{48,176},{56,8},{... | collective-permute-start | bytes 4423688 | tf_op jit(solution)/shard_map/ppermute | solution.py:244
  79.2 4.2 %collective-permute-start.9 = (bf16[960,768]{1,0:T(8,128)(2,1)S(1)}, bf16[960,768]{1,0:T(8,128)(2,1)S(1)}, u32[]{:S(2)}, u32[]{:S(2)}) collective-permute-start(bf16[960,768]{1,0:T(8,128)(2,1)S(1)} %shard_map.90.refs_0_), channel_id=1, source_target_pairs={{0,384},{8,56},{16,400},{24,8},{32,416},{40,24},{48,432},{56,40},{... | collective-permute-start | bytes 4423688 | tf_op jit(solution)/shard_map/ppermute | solution.py:244
  84.1 1.9 %collective-permute-start.15 = (bf16[960,768]{1,0:T(8,128)(2,1)S(1)}, bf16[960,768]{1,0:T(8,128)(2,1)S(1)}, u32[]{:S(2)}, u32[]{:S(2)}) collective-permute-start(bf16[960,768]{1,0:T(8,128)(2,1)S(1)} %shard_map.93.refs_5_), channel_id=1, source_target_pairs={{0,128},{8,24},{16,144},{24,40},{32,160},{40,56},{48,176},{56,8},{... | collective-permute-start | bytes 4423688 | tf_op jit(solution)/shard_map/ppermute | solution.py:244
  86.0 4.6 %collective-permute-start.16 = (bf16[960,768]{1,0:T(8,128)(2,1)S(1)}, bf16[960,768]{1,0:T(8,128)(2,1)S(1)}, u32[]{:S(2)}, u32[]{:S(2)}) collective-permute-start(bf16[960,768]{1,0:T(8,128)(2,1)S(1)} %shard_map.93.refs_5_), channel_id=1, source_target_pairs={{0,384},{8,56},{16,400},{24,8},{32,416},{40,24},{48,432},{56,40},{... | collective-permute-start | bytes 4423688 | tf_op jit(solution)/shard_map/ppermute | solution.py:244
  90.6 8.7 %collective-permute-done.8.refs_0_.refs_1_ = bf16[960,768]{1,0:T(8,128)(2,1)S(1)} collective-permute-done((bf16[960,768]{1,0:T(8,128)(2,1)S(1)}, bf16[960,768]{1,0:T(8,128)(2,1)S(1)}, u32[]{:S(2)}, u32[]{:S(2)}) %collective-permute-start.8) | collective-permute-done | bytes 1474592 | tf_op jit(solution)/shard_map/ppermute | solution.py:244
  100.9 3.1 %collective-permute-start.10 = (bf16[480,768]{1,0:T(8,128)(2,1)S(1)}, bf16[480,768]{1,0:T(8,128)(2,1)}, u32[]{:S(2)}, u32[]{:S(2)}) collective-permute-start(bf16[480,768]{1,0:T(8,128)(2,1)S(1)} %get-tuple-element.27), channel_id=1, source_target_pairs={{0,128},{8,24},{16,144},{24,40},{32,160},{40,56},{48,176},{56,8},{... | collective-permute-start | bytes 2211848 | tf_op jit(solution)/shard_map/ppermute | solution.py:244
  104.0 4.1 %collective-permute-start.11 = (bf16[480,768]{1,0:T(8,128)(2,1)S(1)}, bf16[480,768]{1,0:T(8,128)(2,1)}, u32[]{:S(2)}, u32[]{:S(2)}) collective-permute-start(bf16[480,768]{1,0:T(8,128)(2,1)S(1)} %get-tuple-element.28), channel_id=1, source_target_pairs={{0,384},{8,56},{16,400},{24,8},{32,416},{40,24},{48,432},{56,40},{... | collective-permute-start | bytes 2211848 | tf_op jit(solution)/shard_map/ppermute | solution.py:244
  108.2 6.8 %collective-permute-done.15.refs_0_.refs_6_ = bf16[960,768]{1,0:T(8,128)(2,1)S(1)} collective-permute-done((bf16[960,768]{1,0:T(8,128)(2,1)S(1)}, bf16[960,768]{1,0:T(8,128)(2,1)S(1)}, u32[]{:S(2)}, u32[]{:S(2)}) %collective-permute-start.15) | collective-permute-done | bytes 1474592 | tf_op jit(solution)/shard_map/ppermute | solution.py:244
  116.6 3.2 %collective-permute-start.17 = (bf16[480,768]{1,0:T(8,128)(2,1)S(1)}, bf16[480,768]{1,0:T(8,128)(2,1)}, u32[]{:S(2)}, u32[]{:S(2)}) collective-permute-start(bf16[480,768]{1,0:T(8,128)(2,1)S(1)} %get-tuple-element.30), channel_id=1, source_target_pairs={{0,128},{8,24},{16,144},{24,40},{32,160},{40,56},{48,176},{56,8},{... | collective-permute-start | bytes 2211848 | tf_op jit(solution)/shard_map/ppermute | solution.py:244
  119.8 4.1 %collective-permute-start.18 = (bf16[480,768]{1,0:T(8,128)(2,1)S(1)}, bf16[480,768]{1,0:T(8,128)(2,1)}, u32[]{:S(2)}, u32[]{:S(2)}) collective-permute-start(bf16[480,768]{1,0:T(8,128)(2,1)S(1)} %get-tuple-element.31), channel_id=1, source_target_pairs={{0,384},{8,56},{16,400},{24,8},{32,416},{40,24},{48,432},{56,40},{... | collective-permute-start | bytes 2211848 | tf_op jit(solution)/shard_map/ppermute | solution.py:244
  124.6 6.6 %collective-permute-done.17.refs_8_ = bf16[480,768]{1,0:T(8,128)(2,1)} collective-permute-done((bf16[480,768]{1,0:T(8,128)(2,1)S(1)}, bf16[480,768]{1,0:T(8,128)(2,1)}, u32[]{:S(2)}, u32[]{:S(2)}) %collective-permute-start.17) | collective-permute-done | bytes 737312 | tf_op jit(solution)/shard_map/ppermute | solution.py:244
  132.4 11.8 %shard_map.95 = (bf16[32,2688]{1,0:T(8,128)(2,1)}, bf16[32,2688]{1,0:T(8,128)(2,1)}, bf16[32,2688]{1,0:T(8,128)(2,1)}, bf16[32,2688]{1,0:T(8,128)(2,1)}, bf16[32...) custom-call(s32[5]{0:T(128)} %stack.23.where_ref, ...), custom_call_target="tpu_custom_call" | custom-call | flops 5033164800 | bytes 11796480 | tf_op jit(solution)/shard_map/pallas_call | solution.py:332
  144.2 3.3 %collective-permute-start.19 = (bf16[32,2688]{1,0:T(8,128)(2,1)}, bf16[32,2688]{1,0:T(8,128)(2,1)S(1)}, u32[]{:S(2)}, u32[]{:S(2)}) collective-permute-start(bf16[32,2688]{1,0:T(8,128)(2,1)} %get-tuple-element.33), channel_id=1, source_target_pairs={{0,1},{1,0},{2,3},{3,2},{8,9},{9,8},{10,11},{11,10},{4,5},{5,4},{6... | collective-permute-start | bytes 516104 | tf_op jit(solution)/shard_map/ppermute | solution.py:359
  147.5 4.4 %collective-permute-start.20 = (bf16[32,2688]{1,0:T(8,128)(2,1)}, bf16[32,2688]{1,0:T(8,128)(2,1)S(1)}, u32[]{:S(2)}, u32[]{:S(2)}) collective-permute-start(bf16[32,2688]{1,0:T(8,128)(2,1)} %get-tuple-element.34), channel_id=1, source_target_pairs={{0,2},{1,3},{2,0},{3,1},{8,10},{9,11},{10,8},{11,9},{4,6},{5,7},{6... | collective-permute-start | bytes 516104 | tf_op jit(solution)/shard_map/ppermute | solution.py:359
  151.9 1.9 %collective-permute-start.21 = (bf16[32,2688]{1,0:T(8,128)(2,1)}, bf16[32,2688]{1,0:T(8,128)(2,1)S(1)}, u32[]{:S(2)}, u32[]{:S(2)}) collective-permute-start(bf16[32,2688]{1,0:T(8,128)(2,1)} %get-tuple-element.35), channel_id=1, source_target_pairs={{0,3},{1,2},{2,1},{3,0},{8,11},{9,10},{10,9},{11,8},{4,7},{5,6},{6... | collective-permute-start | bytes 516104 | tf_op jit(solution)/shard_map/ppermute | solution.py:359
  153.8 5.7 %collective-permute-start.22 = (bf16[32,2688]{1,0:T(8,128)(2,1)}, bf16[32,2688]{1,0:T(8,128)(2,1)S(1)}, u32[]{:S(2)}, u32[]{:S(2)}) collective-permute-start(bf16[32,2688]{1,0:T(8,128)(2,1)} %get-tuple-element.36), channel_id=1, source_target_pairs={{0,8},{1,9},{2,10},{3,11},{8,0},{9,1},{10,2},{11,3},{4,12},{5,13},... | collective-permute-start | bytes 516104 | tf_op jit(solution)/shard_map/ppermute | solution.py:359
  159.5 2.6 %collective-permute-start.23 = (bf16[32,2688]{1,0:T(8,128)(2,1)}, bf16[32,2688]{1,0:T(8,128)(2,1)S(1)}, u32[]{:S(2)}, u32[]{:S(2)}) collective-permute-start(bf16[32,2688]{1,0:T(8,128)(2,1)} %get-tuple-element.37), channel_id=1, source_target_pairs={{0,9},{1,8},{2,11},{3,10},{8,1},{9,0},{10,3},{11,2},{4,13},{5,12},... | collective-permute-start | bytes 516104 | tf_op jit(solution)/shard_map/ppermute | solution.py:359
  162.2 5.3 %collective-permute-start.24 = (bf16[32,2688]{1,0:T(8,128)(2,1)}, bf16[32,2688]{1,0:T(8,128)(2,1)S(1)}, u32[]{:S(2)}, u32[]{:S(2)}) collective-permute-start(bf16[32,2688]{1,0:T(8,128)(2,1)} %get-tuple-element.38), channel_id=1, source_target_pairs={{0,10},{1,11},{2,8},{3,9},{8,2},{9,3},{10,0},{11,1},{4,14},{5,15},... | collective-permute-start | bytes 516104 | tf_op jit(solution)/shard_map/ppermute | solution.py:359
  167.5 3.1 %collective-permute-start.25 = (bf16[32,2688]{1,0:T(8,128)(2,1)}, bf16[32,2688]{1,0:T(8,128)(2,1)S(1)}, u32[]{:S(2)}, u32[]{:S(2)}) collective-permute-start(bf16[32,2688]{1,0:T(8,128)(2,1)} %get-tuple-element.39), channel_id=1, source_target_pairs={{0,11},{1,10},{2,9},{3,8},{8,3},{9,2},{10,1},{11,0},{4,15},{5,14},... | collective-permute-start | bytes 516104 | tf_op jit(solution)/shard_map/ppermute | solution.py:359
  171.6 8.4 %collective-permute-done.24.refs_6_ = bf16[32,2688]{1,0:T(8,128)(2,1)S(1)} collective-permute-done((bf16[32,2688]{1,0:T(8,128)(2,1)}, bf16[32,2688]{1,0:T(8,128)(2,1)S(1)}, u32[]{:S(2)}, u32[]{:S(2)}) %collective-permute-start.24) | collective-permute-done | bytes 172064 | tf_op jit(solution)/shard_map/ppermute | solution.py:359
  180.0 2.9 %shard_map.97 = (bf16[256,2560]{1,0:T(8,128)(2,1)}, bf16[6,256]{1,0:T(8,128)(2,1)}) custom-call(s32[5]{0:T(128)S(1)} %copy-done.11, s32[6,256]{1,0:T(8,128)S(1)} %bitcast.10, bf16[6,256]{1,0:T(8,128)(2,1)S(1)} %bitcast.11, bf16[256,256]{1,0:T(8,128)(2,1)S(1)} %copy-done.8, bf16[32,2688]{1,0:T(8,128)(2,1)S(1)} %shard_map.96.refs_0_, ...), custom_call_target="tpu_custom_call" | custom-call | flops 335544320 | bytes 2621440 | tf_op jit(solution)/shard_map/pallas_call | solution.py:362
  (60 shorter events, 18.0 us)
Async XLA Ops:
  2.2 10.0 %collective-permute-start = (bf16[3,40,768]{2,1,0:T(8,128)(2,1)}, bf16[3,40,768]{2,1,0:T(8,128)(2,1)S(1)}, u32[]{:S(2)}, u32[]{:S(2)}) collective-permute-start(bf16[3,40,768]{2,1,0:T(8,128)(2,1)} %shard_map.87.shard_ref), channel_id=1, source_target_pairs={{8,0},{4,12},{9,1},{5,13},{10,2},{6,14},{11,3},{7,15},{24,16},{20,... | collective-permute-start | bytes 552968 | tf_op jit(solution)/shard_map/ppermute | solution.py:278
  13.2 14.1 %collective-permute-start.1 = (bf16[240,768]{1,0:T(8,128)(2,1)S(1)}, bf16[240,768]{1,0:T(8,128)(2,1)S(1)}, u32[]{:S(2)}, u32[]{:S(2)}) collective-permute-start(bf16[240,768]{1,0:T(8,128)(2,1)S(1)} %shard_map.88.mine), channel_id=1, source_target_pairs={{0,4},{64,68},{12,72},{76,8},{1,5},{65,69},{13,73},{77,9},{2,6},{6... | collective-permute-start | bytes 1105928 | tf_op jit(solution)/shard_map/ppermute | solution.py:297
  14.5 33.6 %collective-permute-start.3 = (bf16[240,768]{1,0:T(8,128)(2,1)S(1)}, bf16[240,768]{1,0:T(8,128)(2,1)S(1)}, u32[]{:S(2)}, u32[]{:S(2)}) collective-permute-start(bf16[240,768]{1,0:T(8,128)(2,1)S(1)} %shard_map.88.mine), channel_id=1, source_target_pairs={{0,68},{64,4},{12,8},{76,72},{1,69},{65,5},{13,9},{77,73},{2,70},{... | collective-permute-start | bytes 1105928 | tf_op jit(solution)/shard_map/ppermute | solution.py:297
  27.3 28.1 %collective-permute-start.5 = (bf16[240,768]{1,0:T(8,128)(2,1)S(1)}, bf16[240,768]{1,0:T(8,128)(2,1)S(1)}, u32[]{:S(2)}, u32[]{:S(2)}) collective-permute-start(bf16[240,768]{1,0:T(8,128)(2,1)S(1)} %get-tuple-element.25.refs_0_), channel_id=1, source_target_pairs={{0,16},{8,136},{16,32},{24,152},{32,48},{40,168},{48,0},{56,184},{... | collective-permute-start | bytes 1105928 | tf_op jit(solution)/shard_map/ppermute | solution.py:244
  29.2 26.1 %collective-permute-start.6 = (bf16[240,768]{1,0:T(8,128)(2,1)S(1)}, bf16[240,768]{1,0:T(8,128)(2,1)S(1)}, u32[]{:S(2)}, u32[]{:S(2)}) collective-permute-start(bf16[240,768]{1,0:T(8,128)(2,1)S(1)} %get-tuple-element.25.refs_0_), channel_id=1, source_target_pairs={{0,48},{8,392},{16,0},{24,408},{32,16},{40,424},{48,32},{56,440},{... | collective-permute-start | bytes 1105928 | tf_op jit(solution)/shard_map/ppermute | solution.py:244
  33.8 21.5 %collective-permute-start.2 = (bf16[128,768]{1,0:T(8,128)(2,1)S(1)}, bf16[128,768]{1,0:T(8,128)(2,1)S(1)}, u32[]{:S(2)}, u32[]{:S(2)}) collective-permute-start(bf16[128,768]{1,0:T(8,128)(2,1)S(1)} %get-tuple-element.24), channel_id=1, source_target_pairs={{4,64},{68,0},{8,12},{72,76},{5,65},{69,1},{9,13},{73,77},{6,66},{... | collective-permute-start | bytes 589832 | tf_op jit(solution)/shard_map/ppermute | solution.py:297
  48.2 6.9 %collective-permute-start.4 = (bf16[112,768]{1,0:T(8,128)(2,1)S(1)}, bf16[112,768]{1,0:T(8,128)(2,1)S(1)}, u32[]{:S(2)}, u32[]{:S(2)}) collective-permute-start(bf16[112,768]{1,0:T(8,128)(2,1)S(1)} %slice.4), channel_id=1, source_target_pairs={{4,0},{68,64},{8,76},{72,12},{5,1},{69,65},{9,77},{73,13},{6,2},{7... | collective-permute-start | bytes 516104 | tf_op jit(solution)/shard_map/ppermute | solution.py:297
  55.4 77.0 %all-to-all-start = ((bf16[8,64,2560]{2,1,0:T(8,128)(2,1)}), bf16[8,64,2560]{2,1,0:T(8,128)(2,1)}, u32[]{:S(2)}, u32[]{:S(2)}) async-start(bf16[8,64,2560]{2,1,0:T(8,128)(2,1)} %get-tuple-element.26), calls=%async_computation | async-start | bytes 5242880 | tf_op jit(solution)/shard_map/all_to_all | solution.py:326
  62.5 9.8 %collective-permute-start.12 = (bf16[240,768]{1,0:T(8,128)(2,1)S(1)}, bf16[240,768]{1,0:T(8,128)(2,1)S(1)}, u32[]{:S(2)}, u32[]{:S(2)}) collective-permute-start(bf16[240,768]{1,0:T(8,128)(2,1)S(1)} %shard_map.92.refs_0_), channel_id=1, source_target_pairs={{0,16},{8,136},{16,32},{24,152},{32,48},{40,168},{48,0},{56,184},{... | collective-permute-start | bytes 1105928 | tf_op jit(solution)/shard_map/ppermute | solution.py:244
  65.1 11.1 %collective-permute-start.7 = (bf16[240,768]{1,0:T(8,128)(2,1)S(1)}, bf16[240,768]{1,0:T(8,128)(2,1)S(1)}, u32[]{:S(2)}, u32[]{:S(2)}) collective-permute-start(bf16[240,768]{1,0:T(8,128)(2,1)S(1)} %collective-permute-done.5.refs_1_), channel_id=1, source_target_pairs={{0,16},{8,136},{16,32},{24,152},{32,48},{40,168},{48,0},{56,184},{... | collective-permute-start | bytes 1105928 | tf_op jit(solution)/shard_map/ppermute | solution.py:244
  68.3 15.1 %collective-permute-start.13 = (bf16[240,768]{1,0:T(8,128)(2,1)S(1)}, bf16[240,768]{1,0:T(8,128)(2,1)S(1)}, u32[]{:S(2)}, u32[]{:S(2)}) collective-permute-start(bf16[240,768]{1,0:T(8,128)(2,1)S(1)} %shard_map.92.refs_0_), channel_id=1, source_target_pairs={{0,48},{8,392},{16,0},{24,408},{32,16},{40,424},{48,32},{56,440},{... | collective-permute-start | bytes 1105928 | tf_op jit(solution)/shard_map/ppermute | solution.py:244
  72.3 11.1 %collective-permute-start.14 = (bf16[240,768]{1,0:T(8,128)(2,1)S(1)}, bf16[240,768]{1,0:T(8,128)(2,1)S(1)}, u32[]{:S(2)}, u32[]{:S(2)}) collective-permute-start(bf16[240,768]{1,0:T(8,128)(2,1)S(1)} %collective-permute-done.12.refs_1_), channel_id=1, source_target_pairs={{0,16},{8,136},{16,32},{24,152},{32,48},{40,168},{48,0},{56,184},{... | collective-permute-start | bytes 1105928 | tf_op jit(solution)/shard_map/ppermute | solution.py:244
  76.9 23.4 %copy-start = (bf16[960,768]{1,0:T(8,128)(2,1)}, bf16[960,768]{1,0:T(8,128)(2,1)S(1)}, u32[]{:S(2)}) copy-start(bf16[960,768]{1,0:T(8,128)(2,1)S(1)} %shard_map.90.refs_0_) | copy-start | bytes 4423684
  76.9 22.4 %collective-permute-start.8 = (bf16[960,768]{1,0:T(8,128)(2,1)S(1)}, bf16[960,768]{1,0:T(8,128)(2,1)S(1)}, u32[]{:S(2)}, u32[]{:S(2)}) collective-permute-start(bf16[960,768]{1,0:T(8,128)(2,1)S(1)} %shard_map.90.refs_0_), channel_id=1, source_target_pairs={{0,128},{8,24},{16,144},{24,40},{32,160},{40,56},{48,176},{56,8},{... | collective-permute-start | bytes 4423688 | tf_op jit(solution)/shard_map/ppermute | solution.py:244
  79.2 20.5 %collective-permute-start.9 = (bf16[960,768]{1,0:T(8,128)(2,1)S(1)}, bf16[960,768]{1,0:T(8,128)(2,1)S(1)}, u32[]{:S(2)}, u32[]{:S(2)}) collective-permute-start(bf16[960,768]{1,0:T(8,128)(2,1)S(1)} %shard_map.90.refs_0_), channel_id=1, source_target_pairs={{0,384},{8,56},{16,400},{24,8},{32,416},{40,24},{48,432},{56,40},{... | collective-permute-start | bytes 4423688 | tf_op jit(solution)/shard_map/ppermute | solution.py:244
  84.1 30.9 %collective-permute-start.15 = (bf16[960,768]{1,0:T(8,128)(2,1)S(1)}, bf16[960,768]{1,0:T(8,128)(2,1)S(1)}, u32[]{:S(2)}, u32[]{:S(2)}) collective-permute-start(bf16[960,768]{1,0:T(8,128)(2,1)S(1)} %shard_map.93.refs_5_), channel_id=1, source_target_pairs={{0,128},{8,24},{16,144},{24,40},{32,160},{40,56},{48,176},{56,8},{... | collective-permute-start | bytes 4423688 | tf_op jit(solution)/shard_map/ppermute | solution.py:244
  86.0 29.5 %collective-permute-start.16 = (bf16[960,768]{1,0:T(8,128)(2,1)S(1)}, bf16[960,768]{1,0:T(8,128)(2,1)S(1)}, u32[]{:S(2)}, u32[]{:S(2)}) collective-permute-start(bf16[960,768]{1,0:T(8,128)(2,1)S(1)} %shard_map.93.refs_5_), channel_id=1, source_target_pairs={{0,384},{8,56},{16,400},{24,8},{32,416},{40,24},{48,432},{56,40},{... | collective-permute-start | bytes 4423688 | tf_op jit(solution)/shard_map/ppermute | solution.py:244
  100.9 23.7 %collective-permute-start.10 = (bf16[480,768]{1,0:T(8,128)(2,1)S(1)}, bf16[480,768]{1,0:T(8,128)(2,1)}, u32[]{:S(2)}, u32[]{:S(2)}) collective-permute-start(bf16[480,768]{1,0:T(8,128)(2,1)S(1)} %get-tuple-element.27), channel_id=1, source_target_pairs={{0,128},{8,24},{16,144},{24,40},{32,160},{40,56},{48,176},{56,8},{... | collective-permute-start | bytes 2211848 | tf_op jit(solution)/shard_map/ppermute | solution.py:244
  104.0 20.6 %collective-permute-start.11 = (bf16[480,768]{1,0:T(8,128)(2,1)S(1)}, bf16[480,768]{1,0:T(8,128)(2,1)}, u32[]{:S(2)}, u32[]{:S(2)}) collective-permute-start(bf16[480,768]{1,0:T(8,128)(2,1)S(1)} %get-tuple-element.28), channel_id=1, source_target_pairs={{0,384},{8,56},{16,400},{24,8},{32,416},{40,24},{48,432},{56,40},{... | collective-permute-start | bytes 2211848 | tf_op jit(solution)/shard_map/ppermute | solution.py:244
  116.6 14.6 %collective-permute-start.17 = (bf16[480,768]{1,0:T(8,128)(2,1)S(1)}, bf16[480,768]{1,0:T(8,128)(2,1)}, u32[]{:S(2)}, u32[]{:S(2)}) collective-permute-start(bf16[480,768]{1,0:T(8,128)(2,1)S(1)} %get-tuple-element.30), channel_id=1, source_target_pairs={{0,128},{8,24},{16,144},{24,40},{32,160},{40,56},{48,176},{56,8},{... | collective-permute-start | bytes 2211848 | tf_op jit(solution)/shard_map/ppermute | solution.py:244
  119.8 12.6 %collective-permute-start.18 = (bf16[480,768]{1,0:T(8,128)(2,1)S(1)}, bf16[480,768]{1,0:T(8,128)(2,1)}, u32[]{:S(2)}, u32[]{:S(2)}) collective-permute-start(bf16[480,768]{1,0:T(8,128)(2,1)S(1)} %get-tuple-element.31), channel_id=1, source_target_pairs={{0,384},{8,56},{16,400},{24,8},{32,416},{40,24},{48,432},{56,40},{... | collective-permute-start | bytes 2211848 | tf_op jit(solution)/shard_map/ppermute | solution.py:244
  124.6 55.4 %copy-start.8 = (bf16[256,256]{1,0:T(8,128)(2,1)S(1)}, bf16[256,256]{1,0:T(8,128)(2,1)}, u32[]{:S(2)}) copy-start(bf16[256,256]{1,0:T(8,128)(2,1)} %get-tuple-element.22.sel_ref) | copy-start | bytes 393220
  124.6 55.4 %copy-start.9 = (s32[256,6]{0,1:T(8,128)S(1)}, s32[256,6]{0,1:T(8,128)}, u32[]{:S(2)}) copy-start(s32[256,6]{0,1:T(8,128)} %param.9) | copy-start | bytes 18436
  124.6 55.4 %copy-start.10 = (bf16[256,6]{0,1:T(8,128)(2,1)S(1)}, bf16[256,6]{0,1:T(8,128)(2,1)}, u32[]{:S(2)}) copy-start(bf16[256,6]{0,1:T(8,128)(2,1)} %param.10) | copy-start | bytes 9220
  124.6 55.4 %copy-start.11 = (s32[5]{0:T(128)S(1)}, s32[5]{0:T(128)}, u32[]{:S(2)}) copy-start(s32[5]{0:T(128)} %stack.23.where_ref) | copy-start | bytes 64
  144.2 17.9 %collective-permute-start.19 = (bf16[32,2688]{1,0:T(8,128)(2,1)}, bf16[32,2688]{1,0:T(8,128)(2,1)S(1)}, u32[]{:S(2)}, u32[]{:S(2)}) collective-permute-start(bf16[32,2688]{1,0:T(8,128)(2,1)} %get-tuple-element.33), channel_id=1, source_target_pairs={{0,1},{1,0},{2,3},{3,2},{8,9},{9,8},{10,11},{11,10},{4,5},{5,4},{6... | collective-permute-start | bytes 516104 | tf_op jit(solution)/shard_map/ppermute | solution.py:359
  147.5 19.9 %collective-permute-start.20 = (bf16[32,2688]{1,0:T(8,128)(2,1)}, bf16[32,2688]{1,0:T(8,128)(2,1)S(1)}, u32[]{:S(2)}, u32[]{:S(2)}) collective-permute-start(bf16[32,2688]{1,0:T(8,128)(2,1)} %get-tuple-element.34), channel_id=1, source_target_pairs={{0,2},{1,3},{2,0},{3,1},{8,10},{9,11},{10,8},{11,9},{4,6},{5,7},{6... | collective-permute-start | bytes 516104 | tf_op jit(solution)/shard_map/ppermute | solution.py:359
  151.9 19.6 %collective-permute-start.21 = (bf16[32,2688]{1,0:T(8,128)(2,1)}, bf16[32,2688]{1,0:T(8,128)(2,1)S(1)}, u32[]{:S(2)}, u32[]{:S(2)}) collective-permute-start(bf16[32,2688]{1,0:T(8,128)(2,1)} %get-tuple-element.35), channel_id=1, source_target_pairs={{0,3},{1,2},{2,1},{3,0},{8,11},{9,10},{10,9},{11,8},{4,7},{5,6},{6... | collective-permute-start | bytes 516104 | tf_op jit(solution)/shard_map/ppermute | solution.py:359
  153.8 17.7 %collective-permute-start.22 = (bf16[32,2688]{1,0:T(8,128)(2,1)}, bf16[32,2688]{1,0:T(8,128)(2,1)S(1)}, u32[]{:S(2)}, u32[]{:S(2)}) collective-permute-start(bf16[32,2688]{1,0:T(8,128)(2,1)} %get-tuple-element.36), channel_id=1, source_target_pairs={{0,8},{1,9},{2,10},{3,11},{8,0},{9,1},{10,2},{11,3},{4,12},{5,13},... | collective-permute-start | bytes 516104 | tf_op jit(solution)/shard_map/ppermute | solution.py:359
  159.5 12.0 %collective-permute-start.23 = (bf16[32,2688]{1,0:T(8,128)(2,1)}, bf16[32,2688]{1,0:T(8,128)(2,1)S(1)}, u32[]{:S(2)}, u32[]{:S(2)}) collective-permute-start(bf16[32,2688]{1,0:T(8,128)(2,1)} %get-tuple-element.37), channel_id=1, source_target_pairs={{0,9},{1,8},{2,11},{3,10},{8,1},{9,0},{10,3},{11,2},{4,13},{5,12},... | collective-permute-start | bytes 516104 | tf_op jit(solution)/shard_map/ppermute | solution.py:359
  162.2 17.8 %collective-permute-start.24 = (bf16[32,2688]{1,0:T(8,128)(2,1)}, bf16[32,2688]{1,0:T(8,128)(2,1)S(1)}, u32[]{:S(2)}, u32[]{:S(2)}) collective-permute-start(bf16[32,2688]{1,0:T(8,128)(2,1)} %get-tuple-element.38), channel_id=1, source_target_pairs={{0,10},{1,11},{2,8},{3,9},{8,2},{9,3},{10,0},{11,1},{4,14},{5,15},... | collective-permute-start | bytes 516104 | tf_op jit(solution)/shard_map/ppermute | solution.py:359
  167.5 12.5 %collective-permute-start.25 = (bf16[32,2688]{1,0:T(8,128)(2,1)}, bf16[32,2688]{1,0:T(8,128)(2,1)S(1)}, u32[]{:S(2)}, u32[]{:S(2)}) collective-permute-start(bf16[32,2688]{1,0:T(8,128)(2,1)} %get-tuple-element.39), channel_id=1, source_target_pairs={{0,11},{1,10},{2,9},{3,8},{8,3},{9,2},{10,1},{11,0},{4,15},{5,14},... | collective-permute-start | bytes 516104 | tf_op jit(solution)/shard_map/ppermute | solution.py:359
  (7 other events, 23.5 us)

commit v13 on v8

--- a/solution.py
+++ b/solution.py
@@ -43,6 +43,10 @@
         out_ref[:, first : first + 32, :] = rows.reshape(8, 32, step)
 
 
+def copy_kernel(in_ref, out_ref):
+    out_ref[...] = in_ref[...]
+
+
 def combine_kernel(where_ref, routes_ref, gates_ref, sel_ref, *refs):
     back_refs, (grad_ref, score_ref) = refs[:8], refs[8:]
     width = grad_ref.shape[1]
@@ -58,7 +62,7 @@
     )
     scaled = (sel.astype(F32) * gate).astype(BF)
     down = (((0,), (0,)), ((), ()))
-    step = 512
+    step = width // 2
 
     @pl.loop(0, width // step)
     def _(i):
@@ -333,7 +337,16 @@
         cost_estimate=cost(10 * 256 * width * hidden_width, 6 * width * hidden_width),
     )(where, rows, *arrays)
 
-    home = {0: back[0]}
+    home = {
+        0: pl.pallas_call(
+            copy_kernel,
+            out_shape=jax.ShapeDtypeStruct((32, width + PAD), BF),
+            in_specs=[VM],
+            out_specs=VM,
+            compiler_params=params(4),
+            cost_estimate=cost(0, 4 * 32 * (width + PAD)),
+        )(back[0])
+    }
     for r in (4, 3, 7, 2, 6, 1, 5):
         pairs = [(d, (d // 4 ^ r // 4) * 4 + (d % 4 ^ r % 4)) for d in range(8)]
         home[r] = lax.ppermute(back[r], ("c", "zr"), pairs)

time: 186 us -> 185 us (level)
  transfers between devices with their start and end apart: 27 -> 27, of which waited for: 13 -> 12; matrix products, arithmetic and copies ran while one was open for 0% -> 0% of each run, Pallas kernels for 4% -> 4%
where the time goes in v13:
time: 185 us; the launch traced here: 182 us
  starting transfers between devices  105 us (57%)
  waiting for transfers between devices  48.4 us (26%)
  Pallas kernels  23.9 us (13%)
  local copies, waits for them, and re-layouts  3.59 us (2%)
    ppermute x14, starting transfers between devices, shift(): return lax.ppermute(v, ('x', 'y', 'c'), pairs)  45 us
    ppermute x14, waiting for transfers between devices, shift(): return lax.ppermute(v, ('x', 'y', 'c'), pairs)  26.9 us
    ppermute x7, starting transfers between devices, on_device(): home[r] = lax.ppermute(back[r], ('c', 'zr'), pairs)  26.3 us
    ppermute x4, starting transfers between devices, zmove(): return lax.ppermute(v, ('zh', 'c', 'zq'), pairs)  18.2 us
    ppermute x4, waiting for transfers between devices, zmove(): return lax.ppermute(v, ('zh', 'c', 'zq'), pairs)  11.8 us
    pallas_call x1, Pallas kernels, on_device(): pl.pallas_call(functools.partial(expert_kernel, pieces), out_shape=[jax.S...  11.7 us
    ppermute x1, starting transfers between devices, on_device(): other = lax.ppermute(shard, ('c', 'zq'), [(2, 0), (1, 3)])  8.78 us
    ppermute x7, waiting for transfers between devices, on_device(): home[r] = lax.ppermute(back[r], ('c', 'zr'), pairs)  8.41 us
  transfers between devices with their start and end apart: 27, of which 12 were waited for; matrix products, arithmetic and copies ran while one was open for 0% of the time, Pallas kernels for 4%

profile of v13, /device:TPU:1, one launch (start us, length us, event | category | flops | bytes accessed | tf_op | source)
XLA Modules:
  0.0 182.3 jit_solution(8437001772944367813)
XLA Ops:
  2.2 8.8 %collective-permute-start = (bf16[3,40,768]{2,1,0:T(8,128)(2,1)}, bf16[3,40,768]{2,1,0:T(8,128)(2,1)S(1)}, u32[]{:S(2)}, u32[]{:S(2)}) collective-permute-start(bf16[3,40,768]{2,1,0:T(8,128)(2,1)} %shard_map.87.shard_ref), channel_id=1, source_target_pairs={{8,0},{4,12},{9,1},{5,13},{10,2},{6,14},{11,3},{7,15},{24,16},{20,... | collective-permute-start | bytes 552968 | tf_op jit(solution)/shard_map/ppermute | solution.py:271
  15.8 11.5 %collective-permute-done.1.low = bf16[240,768]{1,0:T(8,128)(2,1)S(1)} collective-permute-done((bf16[240,768]{1,0:T(8,128)(2,1)S(1)}, bf16[240,768]{1,0:T(8,128)(2,1)S(1)}, u32[]{:S(2)}, u32[]{:S(2)}) %collective-permute-start.1) | collective-permute-done | bytes 368672 | tf_op jit(solution)/shard_map/ppermute | solution.py:290
  27.3 1.9 %collective-permute-start.5 = (bf16[240,768]{1,0:T(8,128)(2,1)S(1)}, bf16[240,768]{1,0:T(8,128)(2,1)S(1)}, u32[]{:S(2)}, u32[]{:S(2)}) collective-permute-start(bf16[240,768]{1,0:T(8,128)(2,1)S(1)} %get-tuple-element.25.refs_0_), channel_id=1, source_target_pairs={{0,16},{8,136},{16,32},{24,152},{32,48},{40,168},{48,0},{56,184},{... | collective-permute-start | bytes 1105928 | tf_op jit(solution)/shard_map/ppermute | solution.py:237
  29.2 4.6 %collective-permute-start.6 = (bf16[240,768]{1,0:T(8,128)(2,1)S(1)}, bf16[240,768]{1,0:T(8,128)(2,1)S(1)}, u32[]{:S(2)}, u32[]{:S(2)}) collective-permute-start(bf16[240,768]{1,0:T(8,128)(2,1)S(1)} %get-tuple-element.25.refs_0_), channel_id=1, source_target_pairs={{0,48},{8,392},{16,0},{24,408},{32,16},{40,424},{48,32},{56,440},{... | collective-permute-start | bytes 1105928 | tf_op jit(solution)/shard_map/ppermute | solution.py:237
  33.8 14.3 %collective-permute-start.2 = (bf16[128,768]{1,0:T(8,128)(2,1)S(1)}, bf16[128,768]{1,0:T(8,128)(2,1)S(1)}, u32[]{:S(2)}, u32[]{:S(2)}) collective-permute-start(bf16[128,768]{1,0:T(8,128)(2,1)S(1)} %get-tuple-element.24), channel_id=1, source_target_pairs={{4,64},{68,0},{8,12},{72,76},{5,65},{69,1},{9,13},{73,77},{6,66},{... | collective-permute-start | bytes 589832 | tf_op jit(solution)/shard_map/ppermute | solution.py:290
  49.5 5.6 %shard_map.86 = (bf16[8,64,2560]{2,1,0:T(8,128)(2,1)}, bf16[256,256]{1,0:T(8,128)(2,1)}) custom-call(s32[6,256]{1,0:T(8,128)} %bitcast.9, bf16[256,2560]{1,0:T(8,128)(2,1)} %tok_ref.1, bf16[256,2560]{1,0:T(8,128)(2,1)} %cot_ref.1), custom_call_target="tpu_custom_call" | custom-call | flops 671088640 | bytes 5242880 | tf_op jit(solution)/shard_map/pallas_call | solution.py:301
  55.4 7.1 %all-to-all-start = ((bf16[8,64,2560]{2,1,0:T(8,128)(2,1)}), bf16[8,64,2560]{2,1,0:T(8,128)(2,1)}, u32[]{:S(2)}, u32[]{:S(2)}) async-start(bf16[8,64,2560]{2,1,0:T(8,128)(2,1)} %get-tuple-element.26), calls=%async_computation | async-start | bytes 5242880 | tf_op jit(solution)/shard_map/all_to_all | solution.py:319
  62.5 2.6 %collective-permute-start.12 = (bf16[240,768]{1,0:T(8,128)(2,1)S(1)}, bf16[240,768]{1,0:T(8,128)(2,1)S(1)}, u32[]{:S(2)}, u32[]{:S(2)}) collective-permute-start(bf16[240,768]{1,0:T(8,128)(2,1)S(1)} %shard_map.92.refs_0_), channel_id=1, source_target_pairs={{0,16},{8,136},{16,32},{24,152},{32,48},{40,168},{48,0},{56,184},{... | collective-permute-start | bytes 1105928 | tf_op jit(solution)/shard_map/ppermute | solution.py:237
  65.1 3.1 %collective-permute-start.7 = (bf16[240,768]{1,0:T(8,128)(2,1)S(1)}, bf16[240,768]{1,0:T(8,128)(2,1)S(1)}, u32[]{:S(2)}, u32[]{:S(2)}) collective-permute-start(bf16[240,768]{1,0:T(8,128)(2,1)S(1)} %collective-permute-done.5.refs_1_), channel_id=1, source_target_pairs={{0,16},{8,136},{16,32},{24,152},{32,48},{40,168},{48,0},{56,184},{... | collective-permute-start | bytes 1105928 | tf_op jit(solution)/shard_map/ppermute | solution.py:237
  68.3 3.4 %collective-permute-start.13 = (bf16[240,768]{1,0:T(8,128)(2,1)S(1)}, bf16[240,768]{1,0:T(8,128)(2,1)S(1)}, u32[]{:S(2)}, u32[]{:S(2)}) collective-permute-start(bf16[240,768]{1,0:T(8,128)(2,1)S(1)} %shard_map.92.refs_0_), channel_id=1, source_target_pairs={{0,48},{8,392},{16,0},{24,408},{32,16},{40,424},{48,32},{56,440},{... | collective-permute-start | bytes 1105928 | tf_op jit(solution)/shard_map/ppermute | solution.py:237
  74.2 2.0 %collective-permute-done.7.refs_3_ = bf16[240,768]{1,0:T(8,128)(2,1)S(1)} collective-permute-done((bf16[240,768]{1,0:T(8,128)(2,1)S(1)}, bf16[240,768]{1,0:T(8,128)(2,1)S(1)}, u32[]{:S(2)}, u32[]{:S(2)}) %collective-permute-start.7) | collective-permute-done | bytes 368672 | tf_op jit(solution)/shard_map/ppermute | solution.py:237
  76.9 2.3 %collective-permute-start.8 = (bf16[960,768]{1,0:T(8,128)(2,1)S(1)}, bf16[960,768]{1,0:T(8,128)(2,1)S(1)}, u32[]{:S(2)}, u32[]{:S(2)}) collective-permute-start(bf16[960,768]{1,0:T(8,128)(2,1)S(1)} %shard_map.90.refs_0_), channel_id=1, source_target_pairs={{0,128},{8,24},{16,144},{24,40},{32,160},{40,56},{48,176},{56,8},{... | collective-permute-start | bytes 4423688 | tf_op jit(solution)/shard_map/ppermute | solution.py:237
  79.2 4.2 %collective-permute-start.9 = (bf16[960,768]{1,0:T(8,128)(2,1)S(1)}, bf16[960,768]{1,0:T(8,128)(2,1)S(1)}, u32[]{:S(2)}, u32[]{:S(2)}) collective-permute-start(bf16[960,768]{1,0:T(8,128)(2,1)S(1)} %shard_map.90.refs_0_), channel_id=1, source_target_pairs={{0,384},{8,56},{16,400},{24,8},{32,416},{40,24},{48,432},{56,40},{... | collective-permute-start | bytes 4423688 | tf_op jit(solution)/shard_map/ppermute | solution.py:237
  84.1 1.9 %collective-permute-start.15 = (bf16[960,768]{1,0:T(8,128)(2,1)S(1)}, bf16[960,768]{1,0:T(8,128)(2,1)S(1)}, u32[]{:S(2)}, u32[]{:S(2)}) collective-permute-start(bf16[960,768]{1,0:T(8,128)(2,1)S(1)} %shard_map.93.refs_5_), channel_id=1, source_target_pairs={{0,128},{8,24},{16,144},{24,40},{32,160},{40,56},{48,176},{56,8},{... | collective-permute-start | bytes 4423688 | tf_op jit(solution)/shard_map/ppermute | solution.py:237
  86.0 4.6 %collective-permute-start.16 = (bf16[960,768]{1,0:T(8,128)(2,1)S(1)}, bf16[960,768]{1,0:T(8,128)(2,1)S(1)}, u32[]{:S(2)}, u32[]{:S(2)}) collective-permute-start(bf16[960,768]{1,0:T(8,128)(2,1)S(1)} %shard_map.93.refs_5_), channel_id=1, source_target_pairs={{0,384},{8,56},{16,400},{24,8},{32,416},{40,24},{48,432},{56,40},{... | collective-permute-start | bytes 4423688 | tf_op jit(solution)/shard_map/ppermute | solution.py:237
  90.6 8.7 %collective-permute-done.8.refs_0_.refs_1_ = bf16[960,768]{1,0:T(8,128)(2,1)S(1)} collective-permute-done((bf16[960,768]{1,0:T(8,128)(2,1)S(1)}, bf16[960,768]{1,0:T(8,128)(2,1)S(1)}, u32[]{:S(2)}, u32[]{:S(2)}) %collective-permute-start.8) | collective-permute-done | bytes 1474592 | tf_op jit(solution)/shard_map/ppermute | solution.py:237
  100.9 3.1 %collective-permute-start.10 = (bf16[480,768]{1,0:T(8,128)(2,1)S(1)}, bf16[480,768]{1,0:T(8,128)(2,1)}, u32[]{:S(2)}, u32[]{:S(2)}) collective-permute-start(bf16[480,768]{1,0:T(8,128)(2,1)S(1)} %get-tuple-element.27), channel_id=1, source_target_pairs={{0,128},{8,24},{16,144},{24,40},{32,160},{40,56},{48,176},{56,8},{... | collective-permute-start | bytes 2211848 | tf_op jit(solution)/shard_map/ppermute | solution.py:237
  104.0 4.1 %collective-permute-start.11 = (bf16[480,768]{1,0:T(8,128)(2,1)S(1)}, bf16[480,768]{1,0:T(8,128)(2,1)}, u32[]{:S(2)}, u32[]{:S(2)}) collective-permute-start(bf16[480,768]{1,0:T(8,128)(2,1)S(1)} %get-tuple-element.28), channel_id=1, source_target_pairs={{0,384},{8,56},{16,400},{24,8},{32,416},{40,24},{48,432},{56,40},{... | collective-permute-start | bytes 2211848 | tf_op jit(solution)/shard_map/ppermute | solution.py:237
  108.2 6.8 %collective-permute-done.15.refs_0_.refs_6_ = bf16[960,768]{1,0:T(8,128)(2,1)S(1)} collective-permute-done((bf16[960,768]{1,0:T(8,128)(2,1)S(1)}, bf16[960,768]{1,0:T(8,128)(2,1)S(1)}, u32[]{:S(2)}, u32[]{:S(2)}) %collective-permute-start.15) | collective-permute-done | bytes 1474592 | tf_op jit(solution)/shard_map/ppermute | solution.py:237
  116.6 3.2 %collective-permute-start.17 = (bf16[480,768]{1,0:T(8,128)(2,1)S(1)}, bf16[480,768]{1,0:T(8,128)(2,1)}, u32[]{:S(2)}, u32[]{:S(2)}) collective-permute-start(bf16[480,768]{1,0:T(8,128)(2,1)S(1)} %get-tuple-element.30), channel_id=1, source_target_pairs={{0,128},{8,24},{16,144},{24,40},{32,160},{40,56},{48,176},{56,8},{... | collective-permute-start | bytes 2211848 | tf_op jit(solution)/shard_map/ppermute | solution.py:237
  119.8 4.1 %collective-permute-start.18 = (bf16[480,768]{1,0:T(8,128)(2,1)S(1)}, bf16[480,768]{1,0:T(8,128)(2,1)}, u32[]{:S(2)}, u32[]{:S(2)}) collective-permute-start(bf16[480,768]{1,0:T(8,128)(2,1)S(1)} %get-tuple-element.31), channel_id=1, source_target_pairs={{0,384},{8,56},{16,400},{24,8},{32,416},{40,24},{48,432},{56,40},{... | collective-permute-start | bytes 2211848 | tf_op jit(solution)/shard_map/ppermute | solution.py:237
  124.6 6.6 %collective-permute-done.17.refs_8_ = bf16[480,768]{1,0:T(8,128)(2,1)} collective-permute-done((bf16[480,768]{1,0:T(8,128)(2,1)S(1)}, bf16[480,768]{1,0:T(8,128)(2,1)}, u32[]{:S(2)}, u32[]{:S(2)}) %collective-permute-start.17) | collective-permute-done | bytes 737312 | tf_op jit(solution)/shard_map/ppermute | solution.py:237
  132.4 11.7 %shard_map.95 = (bf16[32,2688]{1,0:T(8,128)(2,1)}, bf16[32,2688]{1,0:T(8,128)(2,1)}, bf16[32,2688]{1,0:T(8,128)(2,1)}, bf16[32,2688]{1,0:T(8,128)(2,1)}, bf16[32...) custom-call(s32[5]{0:T(128)} %stack.23.where_ref, ...), custom_call_target="tpu_custom_call" | custom-call | flops 5033164800 | bytes 11796480 | tf_op jit(solution)/shard_map/pallas_call | solution.py:325
  144.2 3.3 %collective-permute-start.19 = (bf16[32,2688]{1,0:T(8,128)(2,1)}, bf16[32,2688]{1,0:T(8,128)(2,1)S(1)}, u32[]{:S(2)}, u32[]{:S(2)}) collective-permute-start(bf16[32,2688]{1,0:T(8,128)(2,1)} %get-tuple-element.33), channel_id=1, source_target_pairs={{0,1},{1,0},{2,3},{3,2},{8,9},{9,8},{10,11},{11,10},{4,5},{5,4},{6... | collective-permute-start | bytes 516104 | tf_op jit(solution)/shard_map/ppermute | solution.py:352
  147.5 4.4 %collective-permute-start.20 = (bf16[32,2688]{1,0:T(8,128)(2,1)}, bf16[32,2688]{1,0:T(8,128)(2,1)S(1)}, u32[]{:S(2)}, u32[]{:S(2)}) collective-permute-start(bf16[32,2688]{1,0:T(8,128)(2,1)} %get-tuple-element.34), channel_id=1, source_target_pairs={{0,2},{1,3},{2,0},{3,1},{8,10},{9,11},{10,8},{11,9},{4,6},{5,7},{6... | collective-permute-start | bytes 516104 | tf_op jit(solution)/shard_map/ppermute | solution.py:352
  151.9 1.9 %collective-permute-start.21 = (bf16[32,2688]{1,0:T(8,128)(2,1)}, bf16[32,2688]{1,0:T(8,128)(2,1)S(1)}, u32[]{:S(2)}, u32[]{:S(2)}) collective-permute-start(bf16[32,2688]{1,0:T(8,128)(2,1)} %get-tuple-element.35), channel_id=1, source_target_pairs={{0,3},{1,2},{2,1},{3,0},{8,11},{9,10},{10,9},{11,8},{4,7},{5,6},{6... | collective-permute-start | bytes 516104 | tf_op jit(solution)/shard_map/ppermute | solution.py:352
  153.8 5.7 %collective-permute-start.22 = (bf16[32,2688]{1,0:T(8,128)(2,1)}, bf16[32,2688]{1,0:T(8,128)(2,1)S(1)}, u32[]{:S(2)}, u32[]{:S(2)}) collective-permute-start(bf16[32,2688]{1,0:T(8,128)(2,1)} %get-tuple-element.36), channel_id=1, source_target_pairs={{0,8},{1,9},{2,10},{3,11},{8,0},{9,1},{10,2},{11,3},{4,12},{5,13},... | collective-permute-start | bytes 516104 | tf_op jit(solution)/shard_map/ppermute | solution.py:352
  159.5 2.6 %collective-permute-start.23 = (bf16[32,2688]{1,0:T(8,128)(2,1)}, bf16[32,2688]{1,0:T(8,128)(2,1)S(1)}, u32[]{:S(2)}, u32[]{:S(2)}) collective-permute-start(bf16[32,2688]{1,0:T(8,128)(2,1)} %get-tuple-element.37), channel_id=1, source_target_pairs={{0,9},{1,8},{2,11},{3,10},{8,1},{9,0},{10,3},{11,2},{4,13},{5,12},... | collective-permute-start | bytes 516104 | tf_op jit(solution)/shard_map/ppermute | solution.py:352
  162.1 5.3 %collective-permute-start.24 = (bf16[32,2688]{1,0:T(8,128)(2,1)}, bf16[32,2688]{1,0:T(8,128)(2,1)S(1)}, u32[]{:S(2)}, u32[]{:S(2)}) collective-permute-start(bf16[32,2688]{1,0:T(8,128)(2,1)} %get-tuple-element.38), channel_id=1, source_target_pairs={{0,10},{1,11},{2,8},{3,9},{8,2},{9,3},{10,0},{11,1},{4,14},{5,15},... | collective-permute-start | bytes 516104 | tf_op jit(solution)/shard_map/ppermute | solution.py:352
  167.4 3.1 %collective-permute-start.25 = (bf16[32,2688]{1,0:T(8,128)(2,1)}, bf16[32,2688]{1,0:T(8,128)(2,1)S(1)}, u32[]{:S(2)}, u32[]{:S(2)}) collective-permute-start(bf16[32,2688]{1,0:T(8,128)(2,1)} %get-tuple-element.39), channel_id=1, source_target_pairs={{0,11},{1,10},{2,9},{3,8},{8,3},{9,2},{10,1},{11,0},{4,15},{5,14},... | collective-permute-start | bytes 516104 | tf_op jit(solution)/shard_map/ppermute | solution.py:352
  171.5 8.4 %collective-permute-done.24.refs_6_ = bf16[32,2688]{1,0:T(8,128)(2,1)S(1)} collective-permute-done((bf16[32,2688]{1,0:T(8,128)(2,1)}, bf16[32,2688]{1,0:T(8,128)(2,1)S(1)}, u32[]{:S(2)}, u32[]{:S(2)}) %collective-permute-start.24) | collective-permute-done | bytes 172064 | tf_op jit(solution)/shard_map/ppermute | solution.py:352
  179.9 2.4 %shard_map.97 = (bf16[256,2560]{1,0:T(8,128)(2,1)}, bf16[6,256]{1,0:T(8,128)(2,1)}) custom-call(s32[5]{0:T(128)S(1)} %copy-done.11, s32[6,256]{1,0:T(8,128)S(1)} %bitcast.10, bf16[6,256]{1,0:T(8,128)(2,1)S(1)} %bitcast.11, bf16[256,256]{1,0:T(8,128)(2,1)S(1)} %copy-done.8, bf16[32,2688]{1,0:T(8,128)(2,1)S(1)} %shard_map.96.refs_0_, ...), custom_call_target="tpu_custom_call" | custom-call | flops 335544320 | bytes 2621440 | tf_op jit(solution)/shard_map/pallas_call | solution.py:355
  (60 shorter events, 18.0 us)
Async XLA Ops:
  2.2 10.0 %collective-permute-start = (bf16[3,40,768]{2,1,0:T(8,128)(2,1)}, bf16[3,40,768]{2,1,0:T(8,128)(2,1)S(1)}, u32[]{:S(2)}, u32[]{:S(2)}) collective-permute-start(bf16[3,40,768]{2,1,0:T(8,128)(2,1)} %shard_map.87.shard_ref), channel_id=1, source_target_pairs={{8,0},{4,12},{9,1},{5,13},{10,2},{6,14},{11,3},{7,15},{24,16},{20,... | collective-permute-start | bytes 552968 | tf_op jit(solution)/shard_map/ppermute | solution.py:271
  13.2 14.1 %collective-permute-start.1 = (bf16[240,768]{1,0:T(8,128)(2,1)S(1)}, bf16[240,768]{1,0:T(8,128)(2,1)S(1)}, u32[]{:S(2)}, u32[]{:S(2)}) collective-permute-start(bf16[240,768]{1,0:T(8,128)(2,1)S(1)} %shard_map.88.mine), channel_id=1, source_target_pairs={{0,4},{64,68},{12,72},{76,8},{1,5},{65,69},{13,73},{77,9},{2,6},{6... | collective-permute-start | bytes 1105928 | tf_op jit(solution)/shard_map/ppermute | solution.py:290
  14.5 33.6 %collective-permute-start.3 = (bf16[240,768]{1,0:T(8,128)(2,1)S(1)}, bf16[240,768]{1,0:T(8,128)(2,1)S(1)}, u32[]{:S(2)}, u32[]{:S(2)}) collective-permute-start(bf16[240,768]{1,0:T(8,128)(2,1)S(1)} %shard_map.88.mine), channel_id=1, source_target_pairs={{0,68},{64,4},{12,8},{76,72},{1,69},{65,5},{13,9},{77,73},{2,70},{... | collective-permute-start | bytes 1105928 | tf_op jit(solution)/shard_map/ppermute | solution.py:290
  27.3 28.1 %collective-permute-start.5 = (bf16[240,768]{1,0:T(8,128)(2,1)S(1)}, bf16[240,768]{1,0:T(8,128)(2,1)S(1)}, u32[]{:S(2)}, u32[]{:S(2)}) collective-permute-start(bf16[240,768]{1,0:T(8,128)(2,1)S(1)} %get-tuple-element.25.refs_0_), channel_id=1, source_target_pairs={{0,16},{8,136},{16,32},{24,152},{32,48},{40,168},{48,0},{56,184},{... | collective-permute-start | bytes 1105928 | tf_op jit(solution)/shard_map/ppermute | solution.py:237
  29.2 26.1 %collective-permute-start.6 = (bf16[240,768]{1,0:T(8,128)(2,1)S(1)}, bf16[240,768]{1,0:T(8,128)(2,1)S(1)}, u32[]{:S(2)}, u32[]{:S(2)}) collective-permute-start(bf16[240,768]{1,0:T(8,128)(2,1)S(1)} %get-tuple-element.25.refs_0_), channel_id=1, source_target_pairs={{0,48},{8,392},{16,0},{24,408},{32,16},{40,424},{48,32},{56,440},{... | collective-permute-start | bytes 1105928 | tf_op jit(solution)/shard_map/ppermute | solution.py:237
  33.8 21.5 %collective-permute-start.2 = (bf16[128,768]{1,0:T(8,128)(2,1)S(1)}, bf16[128,768]{1,0:T(8,128)(2,1)S(1)}, u32[]{:S(2)}, u32[]{:S(2)}) collective-permute-start(bf16[128,768]{1,0:T(8,128)(2,1)S(1)} %get-tuple-element.24), channel_id=1, source_target_pairs={{4,64},{68,0},{8,12},{72,76},{5,65},{69,1},{9,13},{73,77},{6,66},{... | collective-permute-start | bytes 589832 | tf_op jit(solution)/shard_map/ppermute | solution.py:290
  48.2 6.9 %collective-permute-start.4 = (bf16[112,768]{1,0:T(8,128)(2,1)S(1)}, bf16[112,768]{1,0:T(8,128)(2,1)S(1)}, u32[]{:S(2)}, u32[]{:S(2)}) collective-permute-start(bf16[112,768]{1,0:T(8,128)(2,1)S(1)} %slice.4), channel_id=1, source_target_pairs={{4,0},{68,64},{8,76},{72,12},{5,1},{69,65},{9,77},{73,13},{6,2},{7... | collective-permute-start | bytes 516104 | tf_op jit(solution)/shard_map/ppermute | solution.py:290
  55.4 77.0 %all-to-all-start = ((bf16[8,64,2560]{2,1,0:T(8,128)(2,1)}), bf16[8,64,2560]{2,1,0:T(8,128)(2,1)}, u32[]{:S(2)}, u32[]{:S(2)}) async-start(bf16[8,64,2560]{2,1,0:T(8,128)(2,1)} %get-tuple-element.26), calls=%async_computation | async-start | bytes 5242880 | tf_op jit(solution)/shard_map/all_to_all | solution.py:319
  62.5 9.8 %collective-permute-start.12 = (bf16[240,768]{1,0:T(8,128)(2,1)S(1)}, bf16[240,768]{1,0:T(8,128)(2,1)S(1)}, u32[]{:S(2)}, u32[]{:S(2)}) collective-permute-start(bf16[240,768]{1,0:T(8,128)(2,1)S(1)} %shard_map.92.refs_0_), channel_id=1, source_target_pairs={{0,16},{8,136},{16,32},{24,152},{32,48},{40,168},{48,0},{56,184},{... | collective-permute-start | bytes 1105928 | tf_op jit(solution)/shard_map/ppermute | solution.py:237
  65.1 11.1 %collective-permute-start.7 = (bf16[240,768]{1,0:T(8,128)(2,1)S(1)}, bf16[240,768]{1,0:T(8,128)(2,1)S(1)}, u32[]{:S(2)}, u32[]{:S(2)}) collective-permute-start(bf16[240,768]{1,0:T(8,128)(2,1)S(1)} %collective-permute-done.5.refs_1_), channel_id=1, source_target_pairs={{0,16},{8,136},{16,32},{24,152},{32,48},{40,168},{48,0},{56,184},{... | collective-permute-start | bytes 1105928 | tf_op jit(solution)/shard_map/ppermute | solution.py:237
  68.3 15.1 %collective-permute-start.13 = (bf16[240,768]{1,0:T(8,128)(2,1)S(1)}, bf16[240,768]{1,0:T(8,128)(2,1)S(1)}, u32[]{:S(2)}, u32[]{:S(2)}) collective-permute-start(bf16[240,768]{1,0:T(8,128)(2,1)S(1)} %shard_map.92.refs_0_), channel_id=1, source_target_pairs={{0,48},{8,392},{16,0},{24,408},{32,16},{40,424},{48,32},{56,440},{... | collective-permute-start | bytes 1105928 | tf_op jit(solution)/shard_map/ppermute | solution.py:237
  72.3 11.1 %collective-permute-start.14 = (bf16[240,768]{1,0:T(8,128)(2,1)S(1)}, bf16[240,768]{1,0:T(8,128)(2,1)S(1)}, u32[]{:S(2)}, u32[]{:S(2)}) collective-permute-start(bf16[240,768]{1,0:T(8,128)(2,1)S(1)} %collective-permute-done.12.refs_1_), channel_id=1, source_target_pairs={{0,16},{8,136},{16,32},{24,152},{32,48},{40,168},{48,0},{56,184},{... | collective-permute-start | bytes 1105928 | tf_op jit(solution)/shard_map/ppermute | solution.py:237
  76.9 23.4 %copy-start = (bf16[960,768]{1,0:T(8,128)(2,1)}, bf16[960,768]{1,0:T(8,128)(2,1)S(1)}, u32[]{:S(2)}) copy-start(bf16[960,768]{1,0:T(8,128)(2,1)S(1)} %shard_map.90.refs_0_) | copy-start | bytes 4423684
  76.9 22.4 %collective-permute-start.8 = (bf16[960,768]{1,0:T(8,128)(2,1)S(1)}, bf16[960,768]{1,0:T(8,128)(2,1)S(1)}, u32[]{:S(2)}, u32[]{:S(2)}) collective-permute-start(bf16[960,768]{1,0:T(8,128)(2,1)S(1)} %shard_map.90.refs_0_), channel_id=1, source_target_pairs={{0,128},{8,24},{16,144},{24,40},{32,160},{40,56},{48,176},{56,8},{... | collective-permute-start | bytes 4423688 | tf_op jit(solution)/shard_map/ppermute | solution.py:237
  79.2 20.5 %collective-permute-start.9 = (bf16[960,768]{1,0:T(8,128)(2,1)S(1)}, bf16[960,768]{1,0:T(8,128)(2,1)S(1)}, u32[]{:S(2)}, u32[]{:S(2)}) collective-permute-start(bf16[960,768]{1,0:T(8,128)(2,1)S(1)} %shard_map.90.refs_0_), channel_id=1, source_target_pairs={{0,384},{8,56},{16,400},{24,8},{32,416},{40,24},{48,432},{56,40},{... | collective-permute-start | bytes 4423688 | tf_op jit(solution)/shard_map/ppermute | solution.py:237
  84.1 30.9 %collective-permute-start.15 = (bf16[960,768]{1,0:T(8,128)(2,1)S(1)}, bf16[960,768]{1,0:T(8,128)(2,1)S(1)}, u32[]{:S(2)}, u32[]{:S(2)}) collective-permute-start(bf16[960,768]{1,0:T(8,128)(2,1)S(1)} %shard_map.93.refs_5_), channel_id=1, source_target_pairs={{0,128},{8,24},{16,144},{24,40},{32,160},{40,56},{48,176},{56,8},{... | collective-permute-start | bytes 4423688 | tf_op jit(solution)/shard_map/ppermute | solution.py:237
  86.0 29.5 %collective-permute-start.16 = (bf16[960,768]{1,0:T(8,128)(2,1)S(1)}, bf16[960,768]{1,0:T(8,128)(2,1)S(1)}, u32[]{:S(2)}, u32[]{:S(2)}) collective-permute-start(bf16[960,768]{1,0:T(8,128)(2,1)S(1)} %shard_map.93.refs_5_), channel_id=1, source_target_pairs={{0,384},{8,56},{16,400},{24,8},{32,416},{40,24},{48,432},{56,40},{... | collective-permute-start | bytes 4423688 | tf_op jit(solution)/shard_map/ppermute | solution.py:237
  100.9 23.7 %collective-permute-start.10 = (bf16[480,768]{1,0:T(8,128)(2,1)S(1)}, bf16[480,768]{1,0:T(8,128)(2,1)}, u32[]{:S(2)}, u32[]{:S(2)}) collective-permute-start(bf16[480,768]{1,0:T(8,128)(2,1)S(1)} %get-tuple-element.27), channel_id=1, source_target_pairs={{0,128},{8,24},{16,144},{24,40},{32,160},{40,56},{48,176},{56,8},{... | collective-permute-start | bytes 2211848 | tf_op jit(solution)/shard_map/ppermute | solution.py:237
  104.0 20.6 %collective-permute-start.11 = (bf16[480,768]{1,0:T(8,128)(2,1)S(1)}, bf16[480,768]{1,0:T(8,128)(2,1)}, u32[]{:S(2)}, u32[]{:S(2)}) collective-permute-start(bf16[480,768]{1,0:T(8,128)(2,1)S(1)} %get-tuple-element.28), channel_id=1, source_target_pairs={{0,384},{8,56},{16,400},{24,8},{32,416},{40,24},{48,432},{56,40},{... | collective-permute-start | bytes 2211848 | tf_op jit(solution)/shard_map/ppermute | solution.py:237
  116.6 14.6 %collective-permute-start.17 = (bf16[480,768]{1,0:T(8,128)(2,1)S(1)}, bf16[480,768]{1,0:T(8,128)(2,1)}, u32[]{:S(2)}, u32[]{:S(2)}) collective-permute-start(bf16[480,768]{1,0:T(8,128)(2,1)S(1)} %get-tuple-element.30), channel_id=1, source_target_pairs={{0,128},{8,24},{16,144},{24,40},{32,160},{40,56},{48,176},{56,8},{... | collective-permute-start | bytes 2211848 | tf_op jit(solution)/shard_map/ppermute | solution.py:237
  119.8 12.6 %collective-permute-start.18 = (bf16[480,768]{1,0:T(8,128)(2,1)S(1)}, bf16[480,768]{1,0:T(8,128)(2,1)}, u32[]{:S(2)}, u32[]{:S(2)}) collective-permute-start(bf16[480,768]{1,0:T(8,128)(2,1)S(1)} %get-tuple-element.31), channel_id=1, source_target_pairs={{0,384},{8,56},{16,400},{24,8},{32,416},{40,24},{48,432},{56,40},{... | collective-permute-start | bytes 2211848 | tf_op jit(solution)/shard_map/ppermute | solution.py:237
  124.6 55.3 %copy-start.8 = (bf16[256,256]{1,0:T(8,128)(2,1)S(1)}, bf16[256,256]{1,0:T(8,128)(2,1)}, u32[]{:S(2)}) copy-start(bf16[256,256]{1,0:T(8,128)(2,1)} %get-tuple-element.22.sel_ref) | copy-start | bytes 393220
  124.6 55.3 %copy-start.9 = (s32[256,6]{0,1:T(8,128)S(1)}, s32[256,6]{0,1:T(8,128)}, u32[]{:S(2)}) copy-start(s32[256,6]{0,1:T(8,128)} %param.9) | copy-start | bytes 18436
  124.6 55.3 %copy-start.10 = (bf16[256,6]{0,1:T(8,128)(2,1)S(1)}, bf16[256,6]{0,1:T(8,128)(2,1)}, u32[]{:S(2)}) copy-start(bf16[256,6]{0,1:T(8,128)(2,1)} %param.10) | copy-start | bytes 9220
  124.6 55.3 %copy-start.11 = (s32[5]{0:T(128)S(1)}, s32[5]{0:T(128)}, u32[]{:S(2)}) copy-start(s32[5]{0:T(128)} %stack.23.where_ref) | copy-start | bytes 64
  144.2 17.9 %collective-permute-start.19 = (bf16[32,2688]{1,0:T(8,128)(2,1)}, bf16[32,2688]{1,0:T(8,128)(2,1)S(1)}, u32[]{:S(2)}, u32[]{:S(2)}) collective-permute-start(bf16[32,2688]{1,0:T(8,128)(2,1)} %get-tuple-element.33), channel_id=1, source_target_pairs={{0,1},{1,0},{2,3},{3,2},{8,9},{9,8},{10,11},{11,10},{4,5},{5,4},{6... | collective-permute-start | bytes 516104 | tf_op jit(solution)/shard_map/ppermute | solution.py:352
  147.5 19.9 %collective-permute-start.20 = (bf16[32,2688]{1,0:T(8,128)(2,1)}, bf16[32,2688]{1,0:T(8,128)(2,1)S(1)}, u32[]{:S(2)}, u32[]{:S(2)}) collective-permute-start(bf16[32,2688]{1,0:T(8,128)(2,1)} %get-tuple-element.34), channel_id=1, source_target_pairs={{0,2},{1,3},{2,0},{3,1},{8,10},{9,11},{10,8},{11,9},{4,6},{5,7},{6... | collective-permute-start | bytes 516104 | tf_op jit(solution)/shard_map/ppermute | solution.py:352
  151.9 19.6 %collective-permute-start.21 = (bf16[32,2688]{1,0:T(8,128)(2,1)}, bf16[32,2688]{1,0:T(8,128)(2,1)S(1)}, u32[]{:S(2)}, u32[]{:S(2)}) collective-permute-start(bf16[32,2688]{1,0:T(8,128)(2,1)} %get-tuple-element.35), channel_id=1, source_target_pairs={{0,3},{1,2},{2,1},{3,0},{8,11},{9,10},{10,9},{11,8},{4,7},{5,6},{6... | collective-permute-start | bytes 516104 | tf_op jit(solution)/shard_map/ppermute | solution.py:352
  153.8 17.7 %collective-permute-start.22 = (bf16[32,2688]{1,0:T(8,128)(2,1)}, bf16[32,2688]{1,0:T(8,128)(2,1)S(1)}, u32[]{:S(2)}, u32[]{:S(2)}) collective-permute-start(bf16[32,2688]{1,0:T(8,128)(2,1)} %get-tuple-element.36), channel_id=1, source_target_pairs={{0,8},{1,9},{2,10},{3,11},{8,0},{9,1},{10,2},{11,3},{4,12},{5,13},... | collective-permute-start | bytes 516104 | tf_op jit(solution)/shard_map/ppermute | solution.py:352
  159.5 12.0 %collective-permute-start.23 = (bf16[32,2688]{1,0:T(8,128)(2,1)}, bf16[32,2688]{1,0:T(8,128)(2,1)S(1)}, u32[]{:S(2)}, u32[]{:S(2)}) collective-permute-start(bf16[32,2688]{1,0:T(8,128)(2,1)} %get-tuple-element.37), channel_id=1, source_target_pairs={{0,9},{1,8},{2,11},{3,10},{8,1},{9,0},{10,3},{11,2},{4,13},{5,12},... | collective-permute-start | bytes 516104 | tf_op jit(solution)/shard_map/ppermute | solution.py:352
  162.1 17.8 %collective-permute-start.24 = (bf16[32,2688]{1,0:T(8,128)(2,1)}, bf16[32,2688]{1,0:T(8,128)(2,1)S(1)}, u32[]{:S(2)}, u32[]{:S(2)}) collective-permute-start(bf16[32,2688]{1,0:T(8,128)(2,1)} %get-tuple-element.38), channel_id=1, source_target_pairs={{0,10},{1,11},{2,8},{3,9},{8,2},{9,3},{10,0},{11,1},{4,14},{5,15},... | collective-permute-start | bytes 516104 | tf_op jit(solution)/shard_map/ppermute | solution.py:352
  167.4 12.5 %collective-permute-start.25 = (bf16[32,2688]{1,0:T(8,128)(2,1)}, bf16[32,2688]{1,0:T(8,128)(2,1)S(1)}, u32[]{:S(2)}, u32[]{:S(2)}) collective-permute-start(bf16[32,2688]{1,0:T(8,128)(2,1)} %get-tuple-element.39), channel_id=1, source_target_pairs={{0,11},{1,10},{2,9},{3,8},{8,3},{9,2},{10,1},{11,0},{4,15},{5,14},... | collective-permute-start | bytes 516104 | tf_op jit(solution)/shard_map/ppermute | solution.py:352
  (7 other events, 23.5 us)
